TPU v7x, 32 devices: a whole 2x2x4 slice. The times are simulated.
32 devices in a mesh: img: 16 (over z, y, core), txt: 2 (over x).
Axes of the slice: x: 2, y: 2, z: 4, core: 2. Of those that a mesh axis runs over, the one named last changes fastest.
Arguments:
- tokens: bfloat16 [4096, 1536], P('img'), may hold values from -6 to 6
- cotangent: bfloat16 [4096, 1536], P('img'), may hold values from -6 to 6
- text_states: bfloat16 [256, 4096], P('img'), may hold values from -6 to 6
- conditions: bfloat16 [16, 1024], replicated, may hold values from -6 to 6
- image_sides: int32 [16, 2], replicated, may hold values from 16 to 32, as said below
- master: float32 [16, 2, 1572864], P('img', 'txt')
- moment_one: float32 [16, 2, 1572864], P('img', 'txt'), may hold values from -0.0008457003 to 0.0008457003
- moment_two: float32 [16, 2, 1572864], P('img', 'txt'), may hold values from 1.9866917e-08 to 7.946767e-08
- average: float32 [16, 2, 1572864], P('img', 'txt')
- small_master: float32 [3288], replicated
- small_one: float32 [3288], replicated, may hold values from -0.0033828013 to 0.0033828013
- small_two: float32 [3288], replicated, may hold values from 3.1787067e-07 to 1.2714827e-06
- small_average: float32 [3288], replicated
Outputs:
- block_out: float32 [4096, 1536], P('img')
- d_tokens: float32 [4096, 1536], P('img')
- grad_square: float32 [], replicated
- moment_one_new: float32 [16, 2, 1572864], P('img', 'txt')
- moment_two_new: float32 [16, 2, 1572864], P('img', 'txt')
- master_new: float32 [16, 2, 1572864], P('img', 'txt')
- average_new: float32 [16, 2, 1572864], P('img', 'txt')
- master_low: bfloat16 [16, 2, 1572864], P('img', 'txt')
- small_one_new: float32 [3288], replicated
- small_two_new: float32 [3288], replicated
- small_new: float32 [3288], replicated
- small_average_new: float32 [3288], replicated
Inputs may be any that keep to these rules, and one draw needn't show every extreme that they name: `image_sides`: row s gives image s's height and width in patches; its h * (w + 1) tokens follow those of image s - 1 in the packed rows; one of the first two images is 32 by 32; the images together hold 4096 tokens or more, and the rows after the last token are unused.
All inputs are finite; a program needn't handle non-finite values.
Results may differ from a plain program's by a relative error of at most 0.008.
The roundings to bfloat16 on the way count: a program that leaves them out, or rounds other values in their place, can miss the bound.
Values may be sent and summed in bfloat16 or wider, within the bound.
No kernel may reach another device: no remote copies, remote signals or barrier semaphores. Data moves between devices by JAX's collectives and lax.ppermute only.
A program may use at most 448 MiB of HBM per device.

v0:
```python
import math

import jax
import jax.numpy as jnp
from jax import lax
from jax.sharding import PartitionSpec as P

D = 1536
HEADS = 24
HD = 64
FF = 4096
TXT_D = 4096
COND = 1024
SIDE_MIN = 16
SIDE_MAX = 32
STEP = 10


HIGH = lax.Precision.HIGHEST
EPS_NORM = 1e-06
MAX_NORM = 1.0
BETA_ONE = 0.5
BETA_TWO = 0.5
RATE_MATRIX = 0.01
RATE_SMALL = 0.1
DECAY_WEIGHT = 0.01
ADAM_EPS = 1e-08
EMA_DECAY = 0.8


def from_behind(x, axis, by):
    count = lax.axis_size(axis)
    pairs = [(i, i + by) for i in range(count) if 0 <= i + by < count]
    return lax.ppermute(x, axis, pairs)


def segment_table(n_txt):
    half_d = D // n_txt
    return [
        ((D, 2, FF // n_txt), 2),
        ((FF // n_txt, D), 0),
        ((D, 3, half_d), 2),
        ((TXT_D, 2, half_d), 2),
        ((half_d, D), 0),
        ((COND, 6, half_d), 2),
    ]


def token_places(row_index, image_sides):
    heights = image_sides[:, 0]
    widths = image_sides[:, 1]
    lengths = heights * (widths + 1)
    sample_ends = jnp.cumsum(lengths, dtype=jnp.int32)
    starts = sample_ends - lengths
    sample_ids = jnp.sum(
        (sample_ends[None, :] <= row_index[:, None]).astype(jnp.int32), axis=1, dtype=jnp.int32
    )
    matched = jnp.arange(image_sides.shape[0], dtype=jnp.int32)[None, :] == sample_ids[:, None]
    first_row = jnp.sum(jnp.where(matched, starts[None, :], 0), axis=1, dtype=jnp.int32)
    row_width = jnp.sum(jnp.where(matched, widths[None, :] + 1, 0), axis=1, dtype=jnp.int32)
    row_width = jnp.maximum(row_width, 1)
    offset = row_index - first_row
    return (sample_ids, offset // row_width, offset % row_width)


def rotate(tensor, row_pos, col_pos, direction):
    head_dim = tensor.shape[-1]
    quarter = head_dim // 4
    frequency = 10000.0 ** (-jnp.arange(quarter, dtype=jnp.float32) / quarter)
    angles = jnp.concatenate(
        [
            row_pos.astype(jnp.float32)[:, None] * frequency[None, :],
            col_pos.astype(jnp.float32)[:, None] * frequency[None, :],
        ],
        axis=1,
    )
    cosine = jnp.cos(angles)[:, None, :]
    sine_part = direction * jnp.sin(angles)[:, None, :]
    first_part = tensor[..., : head_dim // 2]
    second_part = tensor[..., head_dim // 2 :]
    return jnp.concatenate(
        [
            first_part * cosine - second_part * sine_part,
            first_part * sine_part + second_part * cosine,
        ],
        axis=-1,
    )


def rms_norm(values):
    return values * lax.rsqrt(jnp.mean(values * values, axis=-1, keepdims=True) + EPS_NORM)


def rms_back(values, d_normed):
    inverse = lax.rsqrt(jnp.mean(values * values, axis=-1, keepdims=True) + EPS_NORM)
    normed = values * inverse
    return inverse * (d_normed - normed * jnp.mean(d_normed * normed, axis=-1, keepdims=True))


def adam_update(gradient, first_moment, second_moment, weight, moving, rate, decay):
    first_new = BETA_ONE * first_moment + (1.0 - BETA_ONE) * gradient
    second_new = BETA_TWO * second_moment + (1.0 - BETA_TWO) * gradient * gradient
    corr_one = 1.0 - BETA_ONE**STEP
    corr_two = 1.0 - BETA_TWO**STEP
    step_dir = first_new / corr_one / (jnp.sqrt(second_new / corr_two) + ADAM_EPS)
    weight_new = weight - rate * (step_dir + decay * weight)
    moving_new = EMA_DECAY * moving + (1.0 - EMA_DECAY) * weight_new
    return (first_new, second_new, weight_new, moving_new)


def on_device(
    tokens,
    cotangent,
    text_states,
    conditions,
    image_sides,
    master,
    moment_one,
    moment_two,
    average,
    small_master,
    small_one,
    small_two,
    small_average,
):
    n_img = lax.axis_size("img")
    n_txt = lax.axis_size("txt")
    img_index = lax.axis_index("img")
    txt_index = lax.axis_index("txt")
    tok_dev = tokens.shape[0]
    samples = image_sides.shape[0]
    half_d = D // n_txt
    local_heads = half_d // HD
    score_scale = HD ** (-0.5)
    layout_table = segment_table(n_txt)
    item_counts = [math.prod(shape_dims) // n_img for shape_dims, join_axis in layout_table]
    bf16 = jnp.bfloat16
    f32 = jnp.float32
    gathered = lax.all_gather(master.reshape(1, -1).astype(bf16), "img", axis=0, tiled=True)
    weight_list = []
    offset = 0
    for (shape_dims, join_axis), item_count in zip(layout_table, item_counts):
        weight_list.append(gathered[:, offset : offset + item_count].reshape(shape_dims))
        offset += item_count
    w_updown, w_down, w_project, w_text, w_output, w_modulate = weight_list
    gain_attn = small_master[:D]
    gain_ffn = small_master[D : 2 * D]
    gain_query = small_master[2 * D : 2 * D + HD]
    gain_key = small_master[2 * D + HD : 2 * D + 2 * HD]
    gain_text = small_master[2 * D + 2 * HD : 2 * D + 3 * HD]
    gate_heads = small_master[2 * D + 3 * HD :]
    gate_local = lax.dynamic_slice_in_dim(gate_heads, txt_index * local_heads, local_heads)
    row_index = img_index * tok_dev + jnp.arange(tok_dev, dtype=jnp.int32)
    sample_ids, row_pos, col_pos = token_places(row_index, image_sides)
    min_len = SIDE_MIN * (SIDE_MIN + 1)
    near_count = min(tok_dev // min_len + 2, samples)
    base_sample = jnp.minimum(sample_ids[0], samples - near_count)
    cond_near = lax.dynamic_slice_in_dim(conditions, base_sample, near_count, 0)
    silu_low = jax.nn.silu(cond_near.astype(f32)).astype(bf16)
    mod_half = jnp.dot(silu_low, w_modulate.reshape(COND, 6 * half_d), preferred_element_type=f32)
    mod_half = mod_half.astype(bf16).reshape(near_count, 6, half_d)
    mod_full = lax.all_gather(mod_half, "txt", axis=2, tiled=True)
    one_hot = (
        sample_ids[:, None] == base_sample + jnp.arange(near_count, dtype=jnp.int32)[None, :]
    ).astype(f32)
    per_token = jnp.einsum("tk,kcd->tcd", one_hot, mod_full.astype(f32), precision=HIGH)
    shift_one = per_token[:, 0]
    scale_one = per_token[:, 1]
    gate_one = per_token[:, 2]
    shift_two = per_token[:, 3]
    scale_two = per_token[:, 4]
    gate_two = per_token[:, 5]
    x_float = tokens.astype(f32)
    x_normed = rms_norm(x_float)
    normed_one = x_normed * gain_attn
    attn_in = (normed_one * (1.0 + scale_one) + shift_one).astype(bf16)
    projected = jnp.einsum("td,dcn->tcn", attn_in, w_project, preferred_element_type=f32)
    heads_shape = (tok_dev, local_heads, HD)
    q_normed = rms_norm(projected[:, 0].reshape(heads_shape))
    k_normed = rms_norm(projected[:, 1].reshape(heads_shape))
    queries = rotate(q_normed * gain_query, row_pos, col_pos, 1.0).astype(bf16)
    key_rows = rotate(k_normed * gain_key, row_pos, col_pos, 1.0).astype(bf16)
    value_rows = projected[:, 2].astype(bf16)
    text_rows = text_states.shape[0]
    text_proj = jnp.einsum("sd,dcn->scn", text_states, w_text, preferred_element_type=f32)
    text_shape = (text_rows, local_heads, HD)
    text_normed = rms_norm(text_proj[:, 0].reshape(text_shape))
    text_key_low = (text_normed * gain_text).reshape(text_rows, half_d).astype(bf16)
    text_value_low = text_proj[:, 1].astype(bf16)
    all_text_keys, all_text_values = (
        lax.all_gather(text_key_low, "img", axis=0, tiled=True),
        lax.all_gather(text_value_low, "img", axis=0, tiled=True),
    )
    text_len = all_text_keys.shape[0]
    reach = min((SIDE_MAX * (SIDE_MAX + 1) - 1 + tok_dev - 1) // tok_dev, n_img - 1)
    own_pair = jnp.stack([key_rows.reshape(tok_dev, half_d), value_rows])
    offsets = list(range(reach, 0, -1)) + list(range(-1, -reach - 1, -1))
    received = {}
    for distance in offsets:
        received[distance] = from_behind(own_pair, "img", distance)
    ordered = [received[distance] for distance in range(reach, 0, -1)] + [own_pair]
    ordered = ordered + [received[-distance] for distance in range(1, reach + 1)]
    near_pair = jnp.concatenate(ordered, axis=1)
    key_count = (2 * reach + 1) * tok_dev
    key_global = (img_index - reach) * tok_dev + jnp.arange(key_count, dtype=jnp.int32)
    sample_ends = jnp.cumsum(image_sides[:, 0] * (image_sides[:, 1] + 1), dtype=jnp.int32)
    key_ids = jnp.sum(
        (sample_ends[None, :] <= key_global[:, None]).astype(jnp.int32), axis=1, dtype=jnp.int32
    )
    inside = (key_global >= 0) & (key_global < n_img * tok_dev)
    key_ids = jnp.where(inside, key_ids, -1)
    same_sample = sample_ids[:, None] == key_ids[None, :]

    def to_heads(values, row_count):
        return values.reshape(row_count, local_heads, HD).transpose(1, 0, 2)

    q_heads = to_heads(queries, tok_dev)
    k_heads = to_heads(near_pair[0], key_count)
    v_heads = to_heads(near_pair[1], key_count)
    tk_heads = to_heads(all_text_keys, text_len)
    tv_heads = to_heads(all_text_values, text_len)

    def attend(operands):
        query, key_block, value_block, text_key, text_value = operands
        scores = jnp.dot(query, key_block.T, preferred_element_type=f32) * score_scale
        scores = jnp.where(same_sample, scores, -1e30)
        row_max = jnp.max(scores, axis=1, keepdims=True)
        exponent = jnp.exp(scores - row_max)
        row_total = jnp.sum(exponent, axis=1, keepdims=True)
        self_part = jnp.dot(
            (exponent / row_total).astype(bf16), value_block, preferred_element_type=f32
        )
        cross_scores = jnp.dot(query, text_key.T, preferred_element_type=f32) * score_scale
        cross_max = jnp.max(cross_scores, axis=1, keepdims=True)
        cross_exp = jnp.exp(cross_scores - cross_max)
        cross_total = jnp.sum(cross_exp, axis=1, keepdims=True)
        cross_part = jnp.dot(
            (cross_exp / cross_total).astype(bf16), text_value, preferred_element_type=f32
        )
        return (
            self_part,
            cross_part,
            row_max + jnp.log(row_total),
            cross_max + jnp.log(cross_total),
        )

    self_out, cross_out, log_self, log_cross = lax.map(
        attend, (q_heads, k_heads, v_heads, tk_heads, tv_heads)
    )
    tanh_gate = jnp.tanh(gate_local)[:, None, None]
    mixed_heads = self_out + tanh_gate * cross_out
    mixed_low = mixed_heads.transpose(1, 0, 2).reshape(tok_dev, half_d).astype(bf16)
    attn_out = lax.psum(jnp.dot(mixed_low, w_output, preferred_element_type=f32), "txt")
    hidden = x_float + gate_one * attn_out
    h_normed = rms_norm(hidden)
    normed_two = h_normed * gain_ffn
    ffn_in = (normed_two * (1.0 + scale_two) + shift_two).astype(bf16)
    gate_up = jnp.einsum("td,dcf->tcf", ffn_in, w_updown, preferred_element_type=f32)
    activated = jax.nn.silu(gate_up[:, 0])
    hidden_units = (activated * gate_up[:, 1]).astype(bf16)
    branch = lax.psum(jnp.dot(hidden_units, w_down, preferred_element_type=f32), "txt")
    block_out = hidden + gate_two * branch
    d_out = cotangent.astype(f32)
    d_gate_two = d_out * branch
    d_branch = (d_out * gate_two).astype(bf16)
    grad_down = jnp.dot(hidden_units.T, d_branch, preferred_element_type=f32)
    d_units = jnp.dot(d_branch, w_down.T, preferred_element_type=f32)
    sigmoid = jax.nn.sigmoid(gate_up[:, 0])
    d_gate = d_units * gate_up[:, 1] * sigmoid * (1.0 + gate_up[:, 0] * (1.0 - sigmoid))
    d_up = d_units * activated
    d_gate_up = jnp.stack([d_gate, d_up], axis=1).astype(bf16)
    grad_updown = jnp.einsum("td,tcf->dcf", ffn_in, d_gate_up, preferred_element_type=f32)
    d_ffn_part = jnp.einsum("tcf,dcf->td", d_gate_up, w_updown, preferred_element_type=f32)
    d_ffn_in = lax.psum(d_ffn_part, "txt")
    d_scale_two = d_ffn_in * normed_two
    d_normed_two = d_ffn_in * (1.0 + scale_two)
    d_gain_ffn = jnp.sum(d_normed_two * h_normed, axis=0)
    d_hidden = d_out + rms_back(hidden, d_normed_two * gain_ffn)
    d_gate_one = d_hidden * attn_out
    d_attn = (d_hidden * gate_one).astype(bf16)
    grad_output = jnp.dot(mixed_low.T, d_attn, preferred_element_type=f32)
    d_mixed = to_heads(jnp.dot(d_attn, w_output.T, preferred_element_type=f32), tok_dev)
    d_gate_local = jnp.sum(d_mixed * cross_out, axis=(1, 2)) * (1.0 - jnp.tanh(gate_local) ** 2)
    d_self_low = d_mixed.astype(bf16)
    d_cross_low = (tanh_gate * d_mixed).astype(bf16)

    def attend_back(operands):
        (
            query,
            key_block,
            value_block,
            text_key,
            text_value,
            d_self,
            d_cross,
            lse_self,
            lse_cross,
        ) = operands
        scores = jnp.dot(query, key_block.T, preferred_element_type=f32) * score_scale
        scores = jnp.where(same_sample, scores, -1e30)
        weights_p = jnp.exp(scores - lse_self)
        d_value = jnp.dot(weights_p.astype(bf16).T, d_self, preferred_element_type=f32)
        d_weights = jnp.dot(d_self, value_block.T, preferred_element_type=f32)
        row_dot = jnp.sum(d_weights * weights_p, axis=1, keepdims=True)
        d_scores = (weights_p * (d_weights - row_dot) * score_scale).astype(bf16)
        d_query = jnp.dot(d_scores, key_block, preferred_element_type=f32)
        d_key = jnp.dot(d_scores.T, query, preferred_element_type=f32)
        cross_scores = jnp.dot(query, text_key.T, preferred_element_type=f32) * score_scale
        cross_p = jnp.exp(cross_scores - lse_cross)
        d_text_value = jnp.dot(cross_p.astype(bf16).T, d_cross, preferred_element_type=f32)
        d_cross_p = jnp.dot(d_cross, text_value.T, preferred_element_type=f32)
        cross_dot = jnp.sum(d_cross_p * cross_p, axis=1, keepdims=True)
        d_cross_scores = (cross_p * (d_cross_p - cross_dot) * score_scale).astype(bf16)
        d_query = d_query + jnp.dot(d_cross_scores, text_key, preferred_element_type=f32)
        d_text_key = jnp.dot(d_cross_scores.T, query, preferred_element_type=f32)
        return (d_query, d_key, d_value, d_text_key, d_text_value)

    d_query, d_key, d_value, d_text_key, d_text_value = lax.map(
        attend_back,
        (
            q_heads,
            k_heads,
            v_heads,
            tk_heads,
            tv_heads,
            d_self_low,
            d_cross_low,
            log_self,
            log_cross,
        ),
    )
    key_grads = jnp.stack(
        [
            d_key.transpose(1, 0, 2).reshape(key_count, half_d),
            d_value.transpose(1, 0, 2).reshape(key_count, half_d),
        ]
    )
    key_sum = key_grads[:, reach * tok_dev : (reach + 1) * tok_dev]
    for distance in offsets:
        slot = reach - distance
        piece_grads = key_grads[:, slot * tok_dev : (slot + 1) * tok_dev]
        key_sum = key_sum + from_behind(piece_grads, "img", -distance)
    text_grads = jnp.stack(
        [
            d_text_key.transpose(1, 0, 2).reshape(text_len, half_d),
            d_text_value.transpose(1, 0, 2).reshape(text_len, half_d),
        ]
    )
    text_own = lax.psum_scatter(text_grads, "img", scatter_dimension=1, tiled=True)
    d_text_scaled = text_own[0].reshape(text_shape)
    d_gain_text = jnp.sum(d_text_scaled * text_normed, axis=(0, 1))
    d_text_raw = rms_back(text_proj[:, 0].reshape(text_shape), d_text_scaled * gain_text).reshape(
        text_rows, half_d
    )
    d_text_proj = jnp.stack([d_text_raw, text_own[1]], axis=1).astype(bf16)
    grad_text = jnp.einsum("sd,scn->dcn", text_states, d_text_proj, preferred_element_type=f32)
    d_q_rot = rotate(d_query.transpose(1, 0, 2), row_pos, col_pos, -1.0)
    d_gain_query = jnp.sum(d_q_rot * q_normed, axis=(0, 1))
    d_q_raw = rms_back(projected[:, 0].reshape(heads_shape), d_q_rot * gain_query)
    d_k_rot = rotate(key_sum[0].reshape(heads_shape), row_pos, col_pos, -1.0)
    d_gain_key = jnp.sum(d_k_rot * k_normed, axis=(0, 1))
    d_k_raw = rms_back(projected[:, 1].reshape(heads_shape), d_k_rot * gain_key)
    d_projected = jnp.stack(
        [d_q_raw.reshape(tok_dev, half_d), d_k_raw.reshape(tok_dev, half_d), key_sum[1]], axis=1
    ).astype(bf16)
    grad_project = jnp.einsum("td,tcn->dcn", attn_in, d_projected, preferred_element_type=f32)
    d_attn_part = jnp.einsum("tcn,dcn->td", d_projected, w_project, preferred_element_type=f32)
    d_attn_in = lax.psum(d_attn_part, "txt")
    d_scale_one = d_attn_in * normed_one
    d_normed_one = d_attn_in * (1.0 + scale_one)
    d_gain_attn = jnp.sum(d_normed_one * x_normed, axis=0)
    d_tokens = d_hidden + rms_back(x_float, d_normed_one * gain_attn)
    d_per_token = jnp.stack(
        [d_attn_in, d_scale_one, d_gate_one, d_ffn_in, d_scale_two, d_gate_two], axis=1
    )
    d_mod = jnp.einsum("tk,tcd->kcd", one_hot, d_per_token, precision=HIGH)
    d_mod_half = lax.dynamic_slice_in_dim(d_mod, txt_index * half_d, half_d, 2)
    grad_modulate = jnp.einsum(
        "kc,kn->cn",
        silu_low.astype(f32),
        d_mod_half.reshape(near_count, 6 * half_d),
        precision=HIGH,
    ).reshape(COND, 6, half_d)
    all_terms = jnp.concatenate(
        [
            grad_updown.reshape(n_img, -1),
            grad_down.reshape(n_img, -1),
            grad_project.reshape(n_img, -1),
            grad_text.reshape(n_img, -1),
            grad_output.reshape(n_img, -1),
            grad_modulate.reshape(n_img, -1),
        ],
        axis=1,
    )
    all_pieces = lax.all_to_all(all_terms, "img", split_axis=0, concat_axis=0, tiled=True)
    reduced = jnp.sum(all_pieces, axis=0, keepdims=True)
    replica = (txt_index == 0).astype(f32)
    gate_full = lax.dynamic_update_slice(
        jnp.zeros((HEADS,), f32), d_gate_local, (txt_index * local_heads,)
    )
    small_terms = jnp.concatenate(
        [
            d_gain_attn * replica,
            d_gain_ffn * replica,
            d_gain_query,
            d_gain_key,
            d_gain_text,
            gate_full,
        ]
    )
    local_square = jnp.sum(reduced * reduced)
    small_grad, square_big = lax.psum((small_terms, local_square), ("img", "txt"))
    grad_square = square_big + jnp.sum(small_grad * small_grad)
    clip_factor = MAX_NORM / jnp.maximum(jnp.sqrt(grad_square), MAX_NORM)
    one_new, two_new, master_new, average_new = adam_update(
        reduced.reshape(master.shape) * clip_factor,
        moment_one,
        moment_two,
        master,
        average,
        RATE_MATRIX,
        DECAY_WEIGHT,
    )
    small_one_new, small_two_new, small_new, small_average_new = adam_update(
        small_grad * clip_factor, small_one, small_two, small_master, small_average, RATE_SMALL, 0.0
    )
    return (
        block_out,
        d_tokens,
        grad_square,
        one_new,
        two_new,
        master_new,
        average_new,
        master_new.astype(bf16),
        small_one_new,
        small_two_new,
        small_new,
        small_average_new,
    )


def solution(mesh):
    in_specs = (
        P("img", None),
        P("img", None),
        P("img", None),
        P(),
        P(),
        P("img", "txt", None),
        P("img", "txt", None),
        P("img", "txt", None),
        P("img", "txt", None),
        P(),
        P(),
        P(),
        P(),
    )
    out_specs = (
        P("img", None),
        P("img", None),
        P(),
        P("img", "txt", None),
        P("img", "txt", None),
        P("img", "txt", None),
        P("img", "txt", None),
        P("img", "txt", None),
        P(),
        P(),
        P(),
        P(),
    )
    return jax.shard_map(
        on_device, mesh=mesh, in_specs=in_specs, out_specs=out_specs, check_vma=False
    )
```

profile of v0, /device:TPU:0, one launch (start us, length us, event | category | flops | bytes accessed | tf_op | source)
XLA Modules:
  0.0 4404.3 jit_solution(14116964235732254643)
XLA Ops:
  19.1 481.9 %all-gather.4.cloned.1.call-done = bf16[16,1,1572864]{2,1,0:T(2,128)(2,1)} async-done(((bf16[1,1,1572864]{2,1,0:T(2,128)(2,1)}), bf16[16,1,1572864]{2,1,0:T(2,128)(2,1)}) %all-gather.4.cloned.1.call-update) | async-done | bytes 50331664 | tf_op jit(solution)/shard_map/all_gather | solution.py:139
  501.0 81.9 %copy.261 = bf16[16,1,1572864]{2,0,1:T(8,128)(2,1)} copy(bf16[16,1,1572864]{2,1,0:T(2,128)(2,1)} %all-gather.4.cloned.1.call-done) | data formatting | bytes 100663296
  720.3 26.8 all_gather.14
  753.0 25.9 all-gather.1
  798.6 23.2 collective-permute-done.6
  824.8 29.9 collective-permute-done.8
  894.6 75.2 %while.36 = (s32[]{:T(128)}, f32[12,256,64]{1,2,0:T(8,128)}, f32[12,256,64]{1,2,0:T(8,128)S(1)}, f32[12,256,1]{1,2,0:T(1,128)S(1)}, f32[12,256,1]{1,2,0:T(1,128)...) while((s32[]{:T(128)}, f32[12,256,64]{1,2,0:T(8,128)}, ...), condition=%wide.region_14.15_spmd.clone, body=%wide.region_9.14_spmd.clone.sunk | while | flops 208272896 | bytes 11310217 | solution.py:247
  982.6 22.8 reshape.619
  1011.8 27.2 all-reduce.6.cloned.1.call-done
  1101.5 41.9 copy.230
  1143.4 43.3 reshape.621
  1197.3 179.3 %while.37 = (s32[]{:T(128)}, f32[12,256,64]{1,2,0:T(8,128)}, f32[12,2816,64]{1,2,0:T(8,128)}, f32[12,2816,64]{1,2,0:T(8,128)}, f32[12,256,64]{1,2,0:T(8,128)S(1)...) while((s32[]{:T(128)}, f32[12,256,64]{1,2,0:T(8,128)}, ...), condition=%wide.region_23.24_spmd.clone, body=%wide.region_20.23_spmd.clone.sunk | while | flops 511852032 | bytes 28146868 | solution.py:318
  1484.4 73.1 %collective-permute-done.16 = f32[2,256,768]{2,1,0:T(8,128)} collective-permute-done((f32[2,256,768]{2,1,0:T(8,128)}, f32[2,256,768]{2,1,0:T(8,128)}, u32[]{:S(2)}, u32[]{:S(2)}) %collective-permute-start.16) | collective-permute-done | bytes 1572896 | tf_op jit(solution)/shard_map/ppermute | solution.py:34
  1634.9 34.4 copy.232
  1669.3 23.0 reshape.623
  1725.1 37.2 copy.235
  1762.3 43.0 reshape.624
  1826.5 27.7 all-reduce.10.cloned.1.call-done
  1905.3 110.7 %copy.236 = f32[16,1,1572864]{2,1,0:T(1,128)} copy(f32[16,1,1572864]{2,0,1:T(8,128)} %bitcast.73) | data formatting | bytes 201326592 | tf_op jit(solution)/shard_map/all_to_all | solution.py:395
  2016.0 34.0 all-to-all-start
  2052.6 1755.1 %all-to-all-done = f32[16,1,1572864]{2,1,0:T(1,128)} async-done(((f32[16,1,1572864]{2,1,0:T(1,128)}), f32[16,1,1572864]{2,1,0:T(1,128)}, u32[]{:S(2)}, u32[]{:S(2)}) %all-to-all-start) | async-done | bytes 100663328 | tf_op jit(solution)/shard_map/all_to_all | solution.py:395
  3807.8 74.3 %reduce_sum.298 = f32[1572864]{0:T(1024)} reduce(f32[16,1,1572864]{2,1,0:T(1,128)} %all-to-all-done, f32[]{:T(128)} %constant.150.clone.1), dimensions={0,1}, to_apply=%region_30.31 | reduce | flops 23592960 | bytes 106954752 | tf_op jit(solution)/shard_map/reduce_sum | solution.py:396
  3890.6 442.8 %all-reduce = (f32[]{:T(128)}, f32[3288]{0:T(1024)S(1)}) all-reduce(f32[]{:T(128)} %multiply_reduce_fusion.2, f32[3288]{0:T(1024)S(1)} %concatenate.53), channel_id=1, replica_groups=mesh['img'=16,'txt'=2] {'img','txt'}, use_global_device_ids=true, to_apply=%region_32.33 | all-reduce | flops 3289 | bytes 26312 | tf_op jit(solution)/shard_map/psum | solution.py:412
  4340.2 42.0 fusion.213
  (718 shorter events, 882.1 us)
Async XLA Ops:
  7.2 493.8 %all-gather.4.cloned.1.call-start = ((), (), s32[]{:S(2)}) async-start(), calls=%async_computation.5 | async-start | bytes 106954752 | tf_op jit(solution)/shard_map/all_gather | solution.py:139
  14.0 1024.9 %all-reduce.6.cloned.1.call-start = ((), (), s32[]{:S(2)}) async-start(), calls=%async_computation.2 | async-start | bytes 3145728 | tf_op jit(solution)/shard_map/psum | solution.py:253
  654.9 130.5 %collective-permute-start = (bf16[2,256,768]{2,1,0:T(8,128)(2,1)}, bf16[2,256,768]{2,1,0:T(8,128)(2,1)}, u32[]{:S(2)}, u32[]{:S(2)}) collective-permute-start(bf16[2,256,768]{2,1,0:T(8,128)(2,1)} %pad_maximum_fusion.6), channel_id=1, source_target_pairs={{0,10},{2,12},{4,14},{6,16},{8,18},{10,20},{12,22},{14,24},{16,26}... | collective-permute-start | bytes 2359304 | tf_op jit(solution)/shard_map/ppermute | solution.py:34
  657.9 130.0 %collective-permute-start.1 = (bf16[2,256,768]{2,1,0:T(8,128)(2,1)}, bf16[2,256,768]{2,1,0:T(8,128)(2,1)}, u32[]{:S(2)}, u32[]{:S(2)}) collective-permute-start(bf16[2,256,768]{2,1,0:T(8,128)(2,1)} %pad_maximum_fusion.6), channel_id=1, source_target_pairs={{0,8},{2,10},{4,12},{6,14},{8,16},{10,18},{12,20},{14,22},{16,24},... | collective-permute-start | bytes 2359304 | tf_op jit(solution)/shard_map/ppermute | solution.py:34
  662.2 128.4 %collective-permute-start.2 = (bf16[2,256,768]{2,1,0:T(8,128)(2,1)}, bf16[2,256,768]{2,1,0:T(8,128)(2,1)}, u32[]{:S(2)}, u32[]{:S(2)}) collective-permute-start(bf16[2,256,768]{2,1,0:T(8,128)(2,1)} %pad_maximum_fusion.6), channel_id=1, source_target_pairs={{0,6},{2,8},{4,10},{6,12},{8,14},{10,16},{12,18},{14,20},{16,22},{... | collective-permute-start | bytes 2359304 | tf_op jit(solution)/shard_map/ppermute | solution.py:34
  667.2 125.8 %collective-permute-start.3 = (bf16[2,256,768]{2,1,0:T(8,128)(2,1)}, bf16[2,256,768]{2,1,0:T(8,128)(2,1)}, u32[]{:S(2)}, u32[]{:S(2)}) collective-permute-start(bf16[2,256,768]{2,1,0:T(8,128)(2,1)} %pad_maximum_fusion.6), channel_id=1, source_target_pairs={{0,4},{2,6},{4,8},{6,10},{8,12},{10,14},{12,16},{14,18},{16,20},{1... | collective-permute-start | bytes 2359304 | tf_op jit(solution)/shard_map/ppermute | solution.py:34
  669.7 125.9 %collective-permute-start.4 = (bf16[2,256,768]{2,1,0:T(8,128)(2,1)}, bf16[2,256,768]{2,1,0:T(8,128)(2,1)}, u32[]{:S(2)}, u32[]{:S(2)}) collective-permute-start(bf16[2,256,768]{2,1,0:T(8,128)(2,1)} %pad_maximum_fusion.6), channel_id=1, source_target_pairs={{0,2},{2,4},{4,6},{6,8},{8,10},{10,12},{12,14},{14,16},{16,18},{18... | collective-permute-start | bytes 2359304 | tf_op jit(solution)/shard_map/ppermute | solution.py:34
  790.6 34.2 collective-permute-start.7
  793.1 61.7 %collective-permute-start.8 = (bf16[2,256,768]{2,1,0:T(8,128)(2,1)}, bf16[2,256,768]{2,1,0:T(8,128)(2,1)S(1)}, u32[]{:S(2)}, u32[]{:S(2)}) collective-permute-start(bf16[2,256,768]{2,1,0:T(8,128)(2,1)} %pad_maximum_fusion.6), channel_id=1, source_target_pairs={{8,0},{10,2},{12,4},{14,6},{16,8},{18,10},{20,12},{22,14},{24,16},... | collective-permute-start | bytes 2359304 | tf_op jit(solution)/shard_map/ppermute | solution.py:34
  795.6 63.1 %collective-permute-start.9 = (bf16[2,256,768]{2,1,0:T(8,128)(2,1)}, bf16[2,256,768]{2,1,0:T(8,128)(2,1)S(1)}, u32[]{:S(2)}, u32[]{:S(2)}) collective-permute-start(bf16[2,256,768]{2,1,0:T(8,128)(2,1)} %pad_maximum_fusion.6), channel_id=1, source_target_pairs={{10,0},{12,2},{14,4},{16,6},{18,8},{20,10},{22,12},{24,14},{26,16}... | collective-permute-start | bytes 2359304 | tf_op jit(solution)/shard_map/ppermute | solution.py:34
  976.1 210.7 %all-reduce.8.cloned.1.call-start = ((), (), s32[]{:S(2)}) async-start(), calls=%async_computation.3 | async-start | bytes 3145728 | tf_op jit(solution)/shard_map/psum | solution.py:274
  1076.8 633.8 %reduce-scatter.2.cloned.1.call-start = ((), (), s32[]{:S(2)}) async-start(), calls=%async_computation.4 | async-start | bytes 1671168 | tf_op jit(solution)/shard_map/reduce_scatter | solution.py:349
  1411.1 56.8 %collective-permute-start.19 = (f32[2,256,768]{2,1,0:T(8,128)}, f32[2,256,768]{2,1,0:T(8,128)}, u32[]{:S(2)}, u32[]{:S(2)}) collective-permute-start(f32[2,256,768]{2,1,0:T(8,128)} %get-tuple-element.482), channel_id=1, source_target_pairs={{0,10},{2,12},{4,14},{6,16},{8,18},{10,20},{12,22},{14,24},{16,26}... | collective-permute-start | bytes 4718600 | tf_op jit(solution)/shard_map/ppermute | solution.py:34
  1415.1 66.7 %collective-permute-start.18 = (f32[2,256,768]{2,1,0:T(8,128)}, f32[2,256,768]{2,1,0:T(8,128)}, u32[]{:S(2)}, u32[]{:S(2)}) collective-permute-start(f32[2,256,768]{2,1,0:T(8,128)} %fusion.127), channel_id=1, source_target_pairs={{0,8},{2,10},{4,12},{6,14},{8,16},{10,18},{12,20},{14,22},{16,24},... | collective-permute-start | bytes 4718600 | tf_op jit(solution)/shard_map/ppermute | solution.py:34
  1419.7 63.5 %collective-permute-start.17 = (f32[2,256,768]{2,1,0:T(8,128)}, f32[2,256,768]{2,1,0:T(8,128)}, u32[]{:S(2)}, u32[]{:S(2)}) collective-permute-start(f32[2,256,768]{2,1,0:T(8,128)} %get-tuple-element.481), channel_id=1, source_target_pairs={{0,6},{2,8},{4,10},{6,12},{8,14},{10,16},{12,18},{14,20},{16,22},{... | collective-permute-start | bytes 4718600 | tf_op jit(solution)/shard_map/ppermute | solution.py:34
  1423.9 133.6 %collective-permute-start.16 = (f32[2,256,768]{2,1,0:T(8,128)}, f32[2,256,768]{2,1,0:T(8,128)}, u32[]{:S(2)}, u32[]{:S(2)}) collective-permute-start(f32[2,256,768]{2,1,0:T(8,128)} %get-tuple-element.480), channel_id=1, source_target_pairs={{0,4},{2,6},{4,8},{6,10},{8,12},{10,14},{12,16},{14,18},{16,20},{1... | collective-permute-start | bytes 4718600 | tf_op jit(solution)/shard_map/ppermute | solution.py:34
  1427.3 131.5 %collective-permute-start.15 = (f32[2,256,768]{2,1,0:T(8,128)}, f32[2,256,768]{2,1,0:T(8,128)}, u32[]{:S(2)}, u32[]{:S(2)}) collective-permute-start(f32[2,256,768]{2,1,0:T(8,128)} %get-tuple-element.479), channel_id=1, source_target_pairs={{0,2},{2,4},{4,6},{6,8},{8,10},{10,12},{12,14},{14,16},{16,18},{18... | collective-permute-start | bytes 4718600 | tf_op jit(solution)/shard_map/ppermute | solution.py:34
  1467.9 120.8 %collective-permute-start.14 = (f32[2,256,768]{2,1,0:T(8,128)}, f32[2,256,768]{2,1,0:T(8,128)}, u32[]{:S(2)}, u32[]{:S(2)}) collective-permute-start(f32[2,256,768]{2,1,0:T(8,128)} %get-tuple-element.478), channel_id=1, source_target_pairs={{2,0},{4,2},{6,4},{8,6},{10,8},{12,10},{14,12},{16,14},{18,16},{20... | collective-permute-start | bytes 4718600 | tf_op jit(solution)/shard_map/ppermute | solution.py:34
  1481.8 106.9 %collective-permute-start.13 = (f32[2,256,768]{2,1,0:T(8,128)}, f32[2,256,768]{2,1,0:T(8,128)}, u32[]{:S(2)}, u32[]{:S(2)}) collective-permute-start(f32[2,256,768]{2,1,0:T(8,128)} %get-tuple-element.477), channel_id=1, source_target_pairs={{4,0},{6,2},{8,4},{10,6},{12,8},{14,10},{16,12},{18,14},{20,16},{2... | collective-permute-start | bytes 4718600 | tf_op jit(solution)/shard_map/ppermute | solution.py:34
  1483.1 105.6 %collective-permute-start.12 = (f32[2,256,768]{2,1,0:T(8,128)}, f32[2,256,768]{2,1,0:T(8,128)}, u32[]{:S(2)}, u32[]{:S(2)}) collective-permute-start(f32[2,256,768]{2,1,0:T(8,128)} %get-tuple-element.476), channel_id=1, source_target_pairs={{6,0},{8,2},{10,4},{12,6},{14,8},{16,10},{18,12},{20,14},{22,16},{... | collective-permute-start | bytes 4718600 | tf_op jit(solution)/shard_map/ppermute | solution.py:34
  1557.6 48.1 %collective-permute-start.11 = (f32[2,256,768]{2,1,0:T(8,128)}, f32[2,256,768]{2,1,0:T(8,128)}, u32[]{:S(2)}, u32[]{:S(2)}) collective-permute-start(f32[2,256,768]{2,1,0:T(8,128)} %get-tuple-element.475), channel_id=1, source_target_pairs={{8,0},{10,2},{12,4},{14,6},{16,8},{18,10},{20,12},{22,14},{24,16},... | collective-permute-start | bytes 4718600 | tf_op jit(solution)/shard_map/ppermute | solution.py:34
  1558.9 48.2 %collective-permute-start.10 = (f32[2,256,768]{2,1,0:T(8,128)}, f32[2,256,768]{2,1,0:T(8,128)}, u32[]{:S(2)}, u32[]{:S(2)}) collective-permute-start(f32[2,256,768]{2,1,0:T(8,128)} %get-tuple-element.474), channel_id=1, source_target_pairs={{10,0},{12,2},{14,4},{16,6},{18,8},{20,10},{22,12},{24,14},{26,16}... | collective-permute-start | bytes 4718600 | tf_op jit(solution)/shard_map/ppermute | solution.py:34
  1581.0 273.2 %all-reduce.10.cloned.1.call-start = ((), (), s32[]{:S(2)}) async-start(), calls=%async_computation.6 | async-start | bytes 6291456 | tf_op jit(solution)/shard_map/psum | solution.py:261
  2016.0 1791.8 %all-to-all-start = ((f32[16,1,1572864]{2,1,0:T(1,128)}), f32[16,1,1572864]{2,1,0:T(1,128)}, u32[]{:S(2)}, u32[]{:S(2)}) async-start(f32[16,1,1572864]{2,1,0:T(1,128)} %copy.236), calls=%async_computation.1 | async-start | bytes 201326592 | tf_op jit(solution)/shard_map/all_to_all | solution.py:395
  (107 other events, 8757.7 us)
Sparse Core Ops, SparseCore 0:
  14.1 486.8 all-gather.3
  976.2 62.6 all-reduce.5
  1076.9 51.4 all-reduce.7
  1581.2 86.7 reduce-scatter.1
  1710.7 143.4 all-reduce.9
where the time goes:
time: 4420 us; the launch traced here: 4400 us
  waiting for transfers between devices  2460 us (56%)
  local copies, waits for them, and re-layouts  776 us (18%)
  blocking collectives  501 us (11%)
  matrix products  351 us (8%)
  other arithmetic  216 us (5%)
  starting transfers between devices  84 us (2%)
    all_to_all x1, waiting for transfers between devices, on_device(): lax.all_to_all(all_terms, 'img', split_axis=0, concat_axis=0, tiled=True)  1760 us
    all_gather x1, waiting for transfers between devices, on_device(): lax.all_gather(master.reshape(1, -1).astype(bf16), 'img', axis=0, tiled=T...  482 us
    psum x1, blocking collectives, on_device(): lax.psum((small_terms, local_square), ('img', 'txt'))  443 us
    unnamed x232, local copies, waits for them, and re-layouts  190 us
    ppermute x20, waiting for transfers between devices, from_behind(): return lax.ppermute(x, axis, pairs)  164 us
    all_to_all x1, local copies, waits for them, and re-layouts, on_device(): lax.all_to_all(all_terms, 'img', split_axis=0, concat_axis=0, tiled=True)  111 us
  transfers between devices with their start and end apart: 26, of which 12 were waited for; matrix products, arithmetic and copies ran while one was open for 11% of the time, Pallas kernels for 0%

commit v1 on v0

v1 whole, which is shorter than its diff:
```python
import functools
import math

import jax
import jax.numpy as jnp
from jax import lax
from jax.experimental import pallas as pl
from jax.experimental.pallas import tpu as pltpu
from jax.sharding import PartitionSpec as P

D = 1536
HEADS = 24
HD = 64
FF = 4096
TXT_D = 4096
COND = 1024
SIDE_MAX = 32
STEP = 10

HIGH = lax.Precision.HIGHEST
EPS_NORM = 1e-06
MAX_NORM = 1.0
BETA_ONE = 0.5
BETA_TWO = 0.5
RATE_MATRIX = 0.01
RATE_SMALL = 0.1
DECAY_WEIGHT = 0.01
ADAM_EPS = 1e-08
EMA_DECAY = 0.8

LANES = 128
EDGE = 128
PACK = 16
PIECES = 14
MASKED = -1e30
VMEM = 48 * 1024 * 1024

bf16 = jnp.bfloat16
f32 = jnp.float32


def mm(a, b, on_a, on_b):
    return lax.dot_general(a, b, (((on_a,), (on_b,)), ((), ())), preferred_element_type=f32)


def lane_index(rows):
    return lax.broadcasted_iota(jnp.int32, (rows, LANES), 1)


def head_sum(values):
    low = lane_index(values.shape[0]) < HD
    first = jnp.sum(jnp.where(low, values, 0.0), axis=1, keepdims=True)
    second = jnp.sum(jnp.where(low, 0.0, values), axis=1, keepdims=True)
    return jnp.where(low, first, second)


def swap_halves(values):
    first = lane_index(values.shape[0]) % HD < HD // 2
    return jnp.where(
        first, pltpu.roll(values, LANES - HD // 2, 1), pltpu.roll(values, HD // 2, 1)
    )


def two_heads(pair):
    low = lane_index(pair.shape[0]) < HD
    zero = jnp.zeros_like(pair)
    return jnp.concatenate([jnp.where(low, pair, zero), jnp.where(low, zero, pair)], axis=0)


def one_pair(stacked):
    rows = stacked.shape[0] // 2
    low = lane_index(rows) < HD
    return jnp.where(low, stacked[:rows], stacked[rows:])


def columns_of(spread):
    return jnp.concatenate([spread[:, :1], spread[:, HD : HD + 1]], axis=0)


def norm_rope(raw, gain, cosine, sine):
    inverse = lax.rsqrt(head_sum(raw * raw) * (1.0 / HD) + EPS_NORM)
    scaled = raw * inverse * gain
    return scaled * cosine + swap_halves(scaled) * sine


def norm_rope_back(raw, gain, cosine, sine, d_out):
    inverse = lax.rsqrt(head_sum(raw * raw) * (1.0 / HD) + EPS_NORM)
    normed = raw * inverse
    d_scaled = d_out * cosine - swap_halves(d_out) * sine
    d_gain = jnp.sum(d_scaled * normed, axis=0, keepdims=True)
    d_normed = d_scaled * gain
    d_raw = inverse * (d_normed - normed * (head_sum(d_normed * normed) * (1.0 / HD)))
    return d_raw, d_gain


def split_three(values):
    high = values.astype(bf16)
    rest = values - high.astype(f32)
    middle = rest.astype(bf16)
    last = (rest - middle.astype(f32)).astype(bf16)
    return jnp.concatenate([high, middle, last], axis=1)


def joined(packed, rows):
    wide = packed.astype(f32)
    return wide[:, :rows] + wide[:, rows : 2 * rows] + wide[:, 2 * rows : 3 * rows]


def put_row(table, index, row):
    at = lax.broadcasted_iota(jnp.int32, table.shape, 0) == index
    return jnp.where(at, row, table)


def take_row(table, index):
    at = lax.broadcasted_iota(jnp.int32, table.shape, 0) == index
    return jnp.sum(jnp.where(at, table, 0.0), axis=0, keepdims=True)


def as_row(column):
    return jnp.broadcast_to(column, (column.shape[0], LANES)).T[:1]


def project_kernel(a_ref, wq_ref, wk_ref, wv_ref, gq_ref, gk_ref, cos_ref, sin_ref, q_ref, kv_ref, raw_ref):
    a = a_ref[...]
    cosine, sine = cos_ref[...], sin_ref[...]
    raw_q = mm(a, wq_ref[...], 1, 0)
    raw_k = mm(a, wk_ref[...], 1, 0)
    raw_ref[0] = raw_q
    raw_ref[1] = raw_k
    q_ref[...] = norm_rope(raw_q, gq_ref[...], cosine, sine).astype(bf16) * jnp.asarray(HD**-0.5, bf16)
    kv_ref[0] = norm_rope(raw_k, gk_ref[...], cosine, sine).astype(bf16)
    kv_ref[1] = mm(a, wv_ref[...], 1, 0).astype(bf16)


def piece_views(piece_refs, counts, per):
    views = []
    for ref, count in zip(piece_refs, counts):
        for at in range(count):
            views.append((ref, at * per))
    return views


def attend_kernel(counts, tok, flag_ref, q_ref, own_ids_ref, ids_ref, tk_ref, tv_ref, gate_ref, *rest):
    pieces = piece_views(rest[: len(counts)], counts, 2)
    mixed_ref, self_ref, cross_ref, lse_self_ref, lse_cross_ref, pack_ref = rest[len(counts) : len(counts) + 6]
    scores_ref, most_ref, total_ref, acc_ref, table_ref = rest[len(counts) + 6 :]
    step = pl.program_id(0)
    own_ids = own_ids_ref[...]
    q_pair = q_ref[...]
    q_two = two_heads(q_pair)
    own_two = jnp.concatenate([own_ids, own_ids], axis=0)
    most_ref[...] = jnp.full(most_ref.shape, MASKED, f32)
    total_ref[...] = jnp.zeros(total_ref.shape, f32)
    acc_ref[...] = jnp.zeros(acc_ref.shape, f32)
    for slot, (ref, at) in enumerate(pieces):
        rows = ref.shape[1]

        @pl.when(flag_ref[slot] > 0)
        def _(slot=slot, ref=ref, at=at, rows=rows):
            scores = mm(q_two, ref[at], 1, 1)
            scores = jnp.where(own_two == ids_ref[slot : slot + 1, :rows], scores, MASKED)
            scores_ref[slot, :, :rows] = scores
            most = most_ref[...]
            for part in range(rows // LANES):
                most = jnp.maximum(most, scores[:, part * LANES : (part + 1) * LANES])
            most_ref[...] = most

    row_most = jnp.max(most_ref[...], axis=1, keepdims=True)
    for slot, (ref, at) in enumerate(pieces):
        rows = ref.shape[1]

        @pl.when(flag_ref[slot] > 0)
        def _(slot=slot, ref=ref, at=at, rows=rows):
            weights = jnp.exp(scores_ref[slot, :, :rows] - row_most)
            total = total_ref[...]
            for part in range(rows // LANES):
                total = total + weights[:, part * LANES : (part + 1) * LANES]
            total_ref[...] = total
            acc_ref[...] += mm(weights.astype(bf16), ref[at + 1], 1, 0)

    row_total = jnp.sum(total_ref[...], axis=1, keepdims=True)
    self_out = one_pair(acc_ref[...] / row_total)
    lse_self = row_most + jnp.log(row_total)

    cross_scores = mm(q_two, tk_ref[...], 1, 1)
    cross_most = jnp.max(cross_scores, axis=1, keepdims=True)
    cross_weights = jnp.exp(cross_scores - cross_most)
    cross_total = jnp.sum(cross_weights, axis=1, keepdims=True)
    cross_out = one_pair(mm(cross_weights.astype(bf16), tv_ref[...], 1, 0) / cross_total)
    lse_cross = cross_most + jnp.log(cross_total)

    self_ref[...] = self_out
    cross_ref[...] = cross_out
    mixed_ref[...] = (self_out + gate_ref[...] * cross_out).astype(bf16)
    spread = (tok, LANES)
    low = lane_index(tok) < HD
    lse_self_ref[...] = jnp.where(
        low, jnp.broadcast_to(lse_self[:tok], spread), jnp.broadcast_to(lse_self[tok:], spread)
    )
    lse_cross_ref[...] = jnp.where(
        low, jnp.broadcast_to(lse_cross[:tok], spread), jnp.broadcast_to(lse_cross[tok:], spread)
    )

    @pl.when(step == 0)
    def _():
        table_ref[...] = jnp.zeros(table_ref.shape, f32)

    table = put_row(table_ref[...], 2 * step, as_row(lse_self[:tok]))
    table = put_row(table, 2 * step + 1, as_row(lse_self[tok:]))
    table_ref[...] = table
    pack_ref[0, :tok, pl.ds(pl.multiple_of(step * LANES, LANES), LANES)] = q_pair

    @pl.when(step == pl.num_programs(0) - 1)
    def _():
        pack_ref[0, tok:, :] = split_three(table_ref[...])


def mixed_back_kernel(tok, d_attn_ref, w_ref, self_ref, cross_ref, gate_ref, pack_ref, d_cross_ref, d_gate_ref, table_ref):
    step = pl.program_id(0)
    d_mixed = mm(d_attn_ref[...], w_ref[...], 1, 1)
    d_self = d_mixed.astype(bf16)
    d_cross_ref[...] = (gate_ref[...] * d_mixed).astype(bf16)
    d_gate_ref[...] = jnp.sum(d_mixed * cross_ref[...], axis=0, keepdims=True)
    delta = head_sum(d_self.astype(f32) * self_ref[...])

    @pl.when(step == 0)
    def _():
        table_ref[...] = jnp.zeros(table_ref.shape, f32)

    table = put_row(table_ref[...], 2 * step, as_row(delta[:, :1]))
    table = put_row(table, 2 * step + 1, as_row(delta[:, HD : HD + 1]))
    table_ref[...] = table
    pack_ref[0, :tok, pl.ds(pl.multiple_of(step * LANES, LANES), LANES)] = d_self

    @pl.when(step == pl.num_programs(0) - 1)
    def _():
        pack_ref[0, tok:, :] = split_three(table_ref[...])


def query_back_kernel(
    counts, tok, flag_ref, q_ref, own_ids_ref, ids_ref, tk_ref, tv_ref, d_self_ref, d_cross_ref,
    self_ref, cross_ref, lse_self_ref, lse_cross_ref, raw_ref, gain_ref, cos_ref, sin_ref, *rest
):
    pieces = piece_views(rest[: len(counts)], counts, 2)
    d_raw_ref, d_gain_ref, d_tk_ref, d_tv_ref, acc_ref = rest[len(counts) :]
    own_ids = own_ids_ref[...]
    own_two = jnp.concatenate([own_ids, own_ids], axis=0)
    q_two = two_heads(q_ref[...])
    d_self = d_self_ref[0]
    d_self_two = two_heads(d_self)
    delta = columns_of(head_sum(d_self.astype(f32) * self_ref[...]))
    lse = columns_of(lse_self_ref[...])

    d_cross = d_cross_ref[...]
    d_cross_two = two_heads(d_cross)
    delta_cross = columns_of(head_sum(d_cross.astype(f32) * cross_ref[...]))
    lse_cross = columns_of(lse_cross_ref[...])
    cross_p = jnp.exp(mm(q_two, tk_ref[...], 1, 1) - lse_cross)
    d_cross_p = mm(d_cross_two, tv_ref[...], 1, 1)
    d_cross_s = (cross_p * (d_cross_p - delta_cross)).astype(bf16)
    d_tv_ref[...] = mm(cross_p.astype(bf16), d_cross_two, 0, 0)
    d_tk_ref[...] = mm(d_cross_s, q_two, 0, 0)
    acc_ref[...] = mm(d_cross_s, tk_ref[...], 1, 0)
    for slot, (ref, at) in enumerate(pieces):
        rows = ref.shape[1]

        @pl.when(flag_ref[slot] > 0)
        def _(slot=slot, ref=ref, at=at, rows=rows):
            key = ref[at]
            scores = mm(q_two, key, 1, 1)
            scores = jnp.where(own_two == ids_ref[slot : slot + 1, :rows], scores, MASKED)
            weights = jnp.exp(scores - lse)
            d_weights = mm(d_self_two, ref[at + 1], 1, 1)
            d_scores = (weights * (d_weights - delta)).astype(bf16)
            acc_ref[...] += mm(d_scores, key, 1, 0)

    d_query = one_pair(acc_ref[...]) * (HD**-0.5)
    d_raw, d_gain = norm_rope_back(raw_ref[0], gain_ref[...], cos_ref[...], sin_ref[...], d_query)
    d_raw_ref[...] = d_raw.astype(bf16)
    d_gain_ref[...] = d_gain


def key_back_kernel(counts, tok, flag_ref, kv_ref, own_ids_ref, ids_ref, raw_ref, gain_ref, cos_ref, sin_ref, *rest):
    n = len(counts)
    q_views = piece_views(rest[:n], counts, 1)
    q_tables = piece_views(rest[n : 2 * n], counts, 1)
    g_views = piece_views(rest[2 * n : 3 * n], counts, 1)
    g_tables = piece_views(rest[3 * n : 4 * n], counts, 1)
    d_raw_ref, d_gain_ref, d_value_ref, acc_k_ref, acc_v_ref = rest[4 * n :]
    step = pl.program_id(0)
    own_ids = own_ids_ref[...]
    k_two = two_heads(kv_ref[0])
    v_two = two_heads(kv_ref[1])
    acc_k_ref[...] = jnp.zeros(acc_k_ref.shape, f32)
    acc_v_ref[...] = jnp.zeros(acc_v_ref.shape, f32)
    for slot in range(PIECES):
        q_ref, at = q_views[slot]
        rows = q_ref.shape[1]
        first = tok - EDGE if slot == PIECES - 2 else 0

        @pl.when(flag_ref[slot] > 0)
        def _(slot=slot, q_ref=q_ref, at=at, rows=rows, first=first):
            query = q_ref[at]
            d_self = g_views[slot][0][at]
            lse = joined(q_tables[slot][0][at], tok)[:, first : first + rows]
            delta = joined(g_tables[slot][0][at], tok)[:, first : first + rows]
            same = own_ids == ids_ref[slot : slot + 1, :rows]
            scores = mm(k_two, query, 1, 1)
            d_weights = mm(v_two, d_self, 1, 1)
            p_low, d_low = [], []
            for head in range(2):
                part = slice(head * tok, (head + 1) * tok)
                masked = jnp.where(same, scores[part], MASKED)
                weights = jnp.exp(masked - take_row(lse, 2 * step + head))
                p_low.append(weights.astype(bf16))
                d_low.append((weights * (d_weights[part] - take_row(delta, 2 * step + head))).astype(bf16))
            acc_v_ref[...] += mm(jnp.concatenate(p_low, axis=0), d_self, 1, 0)
            acc_k_ref[...] += mm(jnp.concatenate(d_low, axis=0), query, 1, 0)

    d_raw, d_gain = norm_rope_back(
        raw_ref[0], gain_ref[...], cos_ref[...], sin_ref[...], one_pair(acc_k_ref[...])
    )
    d_raw_ref[...] = d_raw.astype(bf16)
    d_gain_ref[...] = d_gain
    d_value_ref[...] = one_pair(acc_v_ref[...]).astype(bf16)


def update_kernel(clip_ref, g_ref, one_ref, two_ref, w_ref, avg_ref, one_out, two_out, w_out, avg_out, low_out):
    one, two, weight, moving = adam_update(
        g_ref[...] * clip_ref[0], one_ref[...], two_ref[...], w_ref[...], avg_ref[...], RATE_MATRIX, DECAY_WEIGHT
    )
    one_out[...] = one
    two_out[...] = two
    w_out[...] = weight
    avg_out[...] = moving
    low_out[...] = weight.astype(bf16)


def adam_update(gradient, first_moment, second_moment, weight, moving, rate, decay):
    first_new = BETA_ONE * first_moment + (1.0 - BETA_ONE) * gradient
    second_new = BETA_TWO * second_moment + (1.0 - BETA_TWO) * gradient * gradient
    corr_one = 1.0 - BETA_ONE**STEP
    corr_two = 1.0 - BETA_TWO**STEP
    step_dir = first_new / corr_one / (jnp.sqrt(second_new / corr_two) + ADAM_EPS)
    weight_new = weight - rate * (step_dir + decay * weight)
    moving_new = EMA_DECAY * moving + (1.0 - EMA_DECAY) * weight_new
    return (first_new, second_new, weight_new, moving_new)


def call(kernel, grid, in_specs, out_specs, out_shape, args, scratch=(), prefetch=0, flops=0, moved=0):
    return pl.pallas_call(
        kernel,
        grid_spec=pltpu.PrefetchScalarGridSpec(
            num_scalar_prefetch=prefetch, grid=grid, in_specs=in_specs, out_specs=out_specs, scratch_shapes=scratch
        ),
        out_shape=out_shape,
        compiler_params=pltpu.CompilerParams(dimension_semantics=("arbitrary",) * len(grid), vmem_limit_bytes=VMEM),
        cost_estimate=pl.CostEstimate(flops=flops, bytes_accessed=moved, transcendentals=0),
    )(*args)


def whole(shape):
    return pl.BlockSpec(shape, lambda *_: (0,) * len(shape))


def pair(rows, first=0):
    return pl.BlockSpec((rows, LANES), lambda j, *_: (0, first + j))


def pairs(count, rows, at=0):
    return pl.BlockSpec((count, rows, LANES), lambda j, *_: (at, 0, j))


def shape_of(shape, dtype):
    return jax.ShapeDtypeStruct(shape, dtype)


def shifted(x, by):
    count = lax.axis_size("img")
    return lax.ppermute(x, "img", [(i + by, i) for i in range(count) if 0 <= i + by < count])


def crossed(x, bit):
    count = lax.axis_size("img")
    return lax.ppermute(x, "img", [(i, i ^ bit) for i in range(count)])


def other_txt(x):
    return lax.ppermute(x, "txt", [(0, 1), (1, 0)])


def neighbourhood(x, low_edge, high_edge):
    beside = crossed(x, 1)
    across = crossed(x, 2)
    above, below = shifted(x, 4), shifted(x, -4)
    low, high = shifted(low_edge, -5), shifted(high_edge, 5)
    above_across, below_across = shifted(across, 4), shifted(across, -4)
    three = crossed(jnp.concatenate([across, above, below], axis=0), 1)
    two = crossed(jnp.concatenate([above_across, below_across], axis=0), 1)
    return [x, beside, across, above, below, three, above_across, below_across, two, low, high]


PIECE_COUNTS = (1, 1, 1, 1, 1, 3, 1, 1, 2, 1, 1)


def neighbour_indices(i):
    b = i ^ 1
    return [
        i, b, i ^ 2, i + 4, i - 4, b ^ 2, b + 4, b - 4, (i ^ 2) + 4, (i ^ 2) - 4, (b ^ 2) + 4, (b ^ 2) - 4, i - 5, i + 5
    ]


def token_places(row_index, image_sides):
    heights = image_sides[:, 0]
    widths = image_sides[:, 1]
    lengths = heights * (widths + 1)
    sample_ends = jnp.cumsum(lengths, dtype=jnp.int32)
    starts = sample_ends - lengths
    sample_ids = ids_of(row_index, sample_ends)
    matched = jnp.arange(image_sides.shape[0], dtype=jnp.int32)[None, :] == sample_ids[:, None]
    first_row = jnp.sum(jnp.where(matched, starts[None, :], 0), axis=1, dtype=jnp.int32)
    row_width = jnp.sum(jnp.where(matched, widths[None, :] + 1, 0), axis=1, dtype=jnp.int32)
    row_width = jnp.maximum(row_width, 1)
    offset = row_index - first_row
    return (sample_ids, offset // row_width, offset % row_width, sample_ends)


def ids_of(rows, sample_ends):
    return jnp.sum((sample_ends <= rows[..., None]).astype(jnp.int32), axis=-1, dtype=jnp.int32)


def turn_tables(row_pos, col_pos):
    quarter = HD // 4
    frequency = 10000.0 ** (-jnp.arange(quarter, dtype=f32) / quarter)
    angles = jnp.concatenate(
        [row_pos.astype(f32)[:, None] * frequency[None, :], col_pos.astype(f32)[:, None] * frequency[None, :]], axis=1
    )
    cosine, sine = jnp.cos(angles), jnp.sin(angles)
    return jnp.concatenate([cosine] * 4, axis=1), jnp.concatenate([-sine, sine, -sine, sine], axis=1)


def rms_norm(values):
    return values * lax.rsqrt(jnp.mean(values * values, axis=-1, keepdims=True) + EPS_NORM)


def rms_back(values, d_normed):
    inverse = lax.rsqrt(jnp.mean(values * values, axis=-1, keepdims=True) + EPS_NORM)
    normed = values * inverse
    return inverse * (d_normed - normed * jnp.mean(d_normed * normed, axis=-1, keepdims=True))


def on_device(
    tokens, cotangent, text_states, conditions, image_sides, master, moment_one, moment_two, average,
    small_master, small_one, small_two, small_average,
):
    n_img = lax.axis_size("img")
    n_txt = lax.axis_size("txt")
    img_index = lax.axis_index("img")
    txt_index = lax.axis_index("txt")
    tok = tokens.shape[0]
    samples = image_sides.shape[0]
    half_d = D // n_txt
    half_ff = FF // n_txt
    local_heads = half_d // HD
    n_pairs = half_d // LANES

    tables = [
        (D // n_img, 2 * half_ff),
        (half_ff // n_img, D),
        (D // n_img, 3 * half_d),
        (TXT_D // n_img, 2 * half_d),
        (half_d // n_img, D),
        (COND // n_img, 6 * half_d),
    ]
    flat = master.reshape(-1)
    own_rows = []
    offset = 0
    for rows, columns in tables:
        own_rows.append(flat[offset : offset + rows * columns].reshape(rows, columns).astype(bf16))
        offset += rows * columns
    own_updown, own_down, own_project, own_text, own_output, own_modulate = own_rows

    def gather(rows):
        return lax.all_gather(rows, "img", axis=0, tiled=True)

    def scatter(terms):
        return lax.psum_scatter(terms, "img", scatter_dimension=0, tiled=True)

    w_project = gather(own_project)

    gain_attn = small_master[:D]
    gain_ffn = small_master[D : 2 * D]
    gain_query = small_master[2 * D : 2 * D + HD]
    gain_key = small_master[2 * D + HD : 2 * D + 2 * HD]
    gain_text = small_master[2 * D + 2 * HD : 2 * D + 3 * HD]
    gate_heads = small_master[2 * D + 3 * HD :]
    gate_local = lax.dynamic_slice_in_dim(gate_heads, txt_index * local_heads, local_heads)
    tanh_gate = jnp.tanh(gate_local)
    gate_lanes = jnp.repeat(tanh_gate, HD)[None, :]
    gain_query_pair = jnp.tile(gain_query, 2)[None, :]
    gain_key_pair = jnp.tile(gain_key, 2)[None, :]

    cond_rows = COND // n_img
    cond_own = lax.dynamic_slice_in_dim(conditions, img_index * cond_rows, cond_rows, 1)
    silu_own = jax.nn.silu(cond_own.astype(f32)).astype(bf16)
    mod_half = lax.psum(jnp.dot(silu_own, own_modulate, preferred_element_type=f32), "img").astype(bf16)
    mods = lax.all_gather(mod_half.reshape(samples, 6, half_d), "txt", axis=2, tiled=True)

    row_index = img_index * tok + jnp.arange(tok, dtype=jnp.int32)
    sample_ids, row_pos, col_pos, sample_ends = token_places(row_index, image_sides)
    cosine, sine = turn_tables(row_pos, col_pos)
    one_hot = sample_ids[:, None] == jnp.arange(samples, dtype=jnp.int32)[None, :]
    per_token = jnp.dot(one_hot.astype(bf16), mods.reshape(samples, 6 * D), preferred_element_type=f32).astype(bf16)
    shift_one, scale_one, gate_one, shift_two, scale_two, gate_two = (
        per_token[:, c * D : (c + 1) * D].astype(f32) for c in range(6)
    )

    pieces = jnp.stack([jnp.asarray(p, jnp.int32) for p in neighbour_indices(img_index)])
    place = img_index % 4
    inside = (pieces >= 0) & (pieces < n_img)
    slots = jnp.arange(PIECES)
    inside &= (slots != PIECES - 2) | (place == 0)
    inside &= (slots != PIECES - 1) | (place == 3)
    column = jnp.arange(tok, dtype=jnp.int32)[None, :]
    piece_rows = pieces[:, None] * tok + column + jnp.where(slots == PIECES - 2, tok - EDGE, 0)[:, None]
    there = inside[:, None] & ((slots[:, None] < PIECES - 2) | (column < EDGE))
    piece_ids = jnp.where(there, ids_of(piece_rows, sample_ends), -1)
    flags = jnp.any((piece_ids >= sample_ids[0]) & (piece_ids <= sample_ids[-1]), axis=1).astype(jnp.int32)
    piece_ids = jnp.concatenate([piece_ids, jnp.full((16 - PIECES, tok), -1, jnp.int32)], axis=0)
    own_ids = sample_ids[:, None]

    text_rows = text_states.shape[0]
    text_len = text_rows * n_img
    text_columns = lax.all_to_all(text_states, "img", split_axis=1, concat_axis=0, tiled=True)
    text_proj = scatter(jnp.dot(text_columns, own_text, preferred_element_type=f32))
    text_shape = (text_rows, local_heads, HD)
    text_raw = text_proj[:, :half_d].reshape(text_shape)
    text_normed = rms_norm(text_raw)
    text_key_low = (text_normed * gain_text).reshape(text_rows, half_d).astype(bf16)
    text_low = jnp.concatenate([text_key_low, text_proj[:, half_d:].astype(bf16)], axis=1)
    all_text = gather(text_low)

    x_float = tokens.astype(f32)
    x_normed = rms_norm(x_float)
    normed_one = x_normed * gain_attn
    attn_in = (normed_one * (1.0 + scale_one) + shift_one).astype(bf16)
    queries, own_kv, raw_qk = call(
        project_kernel,
        (n_pairs,),
        [whole((tok, D)), pair(D), pair(D, n_pairs), pair(D, 2 * n_pairs)]
        + [whole((1, LANES))] * 2
        + [whole((tok, LANES))] * 2,
        [pair(tok), pairs(2, tok), pairs(2, tok)],
        [
            shape_of((tok, half_d), bf16),
            shape_of((2, tok, half_d), bf16),
            shape_of((2, tok, half_d), f32),
        ],
        (attn_in, w_project, w_project, w_project, gain_query_pair, gain_key_pair, cosine, sine),
        flops=2 * tok * D * 3 * half_d,
        moved=2 * D * 3 * half_d,
    )
    kv_pieces = neighbourhood(own_kv, own_kv[:, tok - EDGE :], own_kv[:, :EDGE])

    w_output = gather(own_output)
    w_updown = gather(own_updown)
    w_down = gather(own_down)
    w_output_other = other_txt(w_output)

    kv_specs = [pairs(2 * c, a.shape[1]) for c, a in zip(PIECE_COUNTS, kv_pieces)]
    id_specs = [whole((tok, 1)), whole((16, tok))]
    text_specs = [pair(text_len), pair(text_len, n_pairs)]
    attention_flops = 2 * 2 * tok * 12 * tok * half_d
    mixed_low, self_out, cross_out, lse_self, lse_cross, query_pack = call(
        functools.partial(attend_kernel, PIECE_COUNTS, tok),
        (n_pairs,),
        [pair(tok)] + id_specs + text_specs + [pair(1)] + kv_specs,
        [pair(tok)] * 5 + [whole((1, tok + PACK, half_d))],
        [shape_of((tok, half_d), bf16)]
        + [shape_of((tok, half_d), f32)] * 4
        + [shape_of((1, tok + PACK, half_d), bf16)],
        (flags, queries, own_ids, piece_ids, all_text, all_text, gate_lanes, *kv_pieces),
        scratch=[
            pltpu.VMEM((PIECES, 2 * tok, tok), f32),
            pltpu.VMEM((2 * tok, LANES), f32),
            pltpu.VMEM((2 * tok, LANES), f32),
            pltpu.VMEM((2 * tok, LANES), f32),
            pltpu.VMEM((PACK, tok), f32),
        ],
        prefetch=1,
        flops=attention_flops,
        moved=13 * 4 * tok * half_d,
    )

    def pack_edges(pack):
        table = pack[:, tok:]
        return (
            jnp.concatenate([pack[:, tok - EDGE : tok], table], axis=1),
            jnp.concatenate([pack[:, :EDGE], table], axis=1),
        )

    query_pieces = neighbourhood(query_pack, *pack_edges(query_pack))

    mixed_other = other_txt(mixed_low)
    attn_out = jnp.dot(mixed_low, w_output, preferred_element_type=f32) + jnp.dot(
        mixed_other, w_output_other, preferred_element_type=f32
    )
    hidden = x_float + gate_one * attn_out
    h_normed = rms_norm(hidden)
    normed_two = h_normed * gain_ffn
    ffn_in = (normed_two * (1.0 + scale_two) + shift_two).astype(bf16)
    gate_up = jnp.dot(ffn_in, w_updown, preferred_element_type=f32)
    gate, up = gate_up[:, :half_ff], gate_up[:, half_ff:]
    sigmoid = jax.nn.sigmoid(gate)
    activated = gate * sigmoid
    hidden_units = (activated * up).astype(bf16)
    branch_part = jnp.dot(hidden_units, w_down, preferred_element_type=f32)
    branch = branch_part + other_txt(branch_part)
    block_out = hidden + gate_two * branch

    d_out = cotangent.astype(f32)
    d_gate_two = d_out * branch
    d_branch = (d_out * gate_two).astype(bf16)
    d_units = mm(d_branch, w_down, 1, 1)
    d_gate = d_units * up * sigmoid * (1.0 + gate * (1.0 - sigmoid))
    d_up = d_units * activated
    d_gate_up = jnp.concatenate([d_gate.astype(bf16), d_up.astype(bf16)], axis=1)
    d_ffn_part = mm(d_gate_up, w_updown, 1, 1).astype(bf16)
    d_ffn_in = d_ffn_part.astype(f32) + other_txt(d_ffn_part).astype(f32)
    grad_down = scatter(mm(hidden_units, d_branch, 0, 0).astype(bf16)).astype(f32)
    grad_updown = scatter(mm(ffn_in, d_gate_up, 0, 0).astype(bf16)).astype(f32)

    d_scale_two = d_ffn_in * normed_two
    d_normed_two = d_ffn_in * (1.0 + scale_two)
    d_gain_ffn = jnp.sum(d_normed_two * h_normed, axis=0)
    d_hidden = d_out + rms_back(hidden, d_normed_two * gain_ffn)
    d_gate_one = d_hidden * attn_out
    d_attn = (d_hidden * gate_one).astype(bf16)
    grad_pack, d_cross_low, d_gate_lanes = call(
        functools.partial(mixed_back_kernel, tok),
        (n_pairs,),
        [whole((tok, D)), pl.BlockSpec((LANES, D), lambda j: (j, 0)), pair(tok), pair(tok), pair(1)],
        [whole((1, tok + PACK, half_d)), pair(tok), pair(1)],
        [
            shape_of((1, tok + PACK, half_d), bf16),
            shape_of((tok, half_d), bf16),
            shape_of((1, half_d), f32),
        ],
        (d_attn, w_output, self_out, cross_out, gate_lanes),
        scratch=[pltpu.VMEM((PACK, tok), f32)],
        flops=2 * tok * D * half_d,
        moved=4 * D * half_d,
    )
    grad_pieces = neighbourhood(grad_pack, *pack_edges(grad_pack))
    grad_output = scatter(mm(mixed_low, d_attn, 0, 0).astype(bf16)).astype(f32)

    turn_specs = [whole((1, LANES)), whole((tok, LANES)), whole((tok, LANES))]
    d_query_raw, d_gain_query, d_text_key, d_text_value = call(
        functools.partial(query_back_kernel, PIECE_COUNTS, tok),
        (n_pairs,),
        [pair(tok)]
        + id_specs
        + text_specs
        + [pairs(1, tok), pair(tok)]
        + [pair(tok)] * 4
        + [pairs(1, tok)]
        + turn_specs
        + kv_specs,
        [pair(tok), pair(1), pair(text_len), pair(text_len)],
        [
            shape_of((tok, half_d), bf16),
            shape_of((1, half_d), f32),
            shape_of((text_len, half_d), f32),
            shape_of((text_len, half_d), f32),
        ],
        (
            flags, queries, own_ids, piece_ids, all_text, all_text, grad_pack, d_cross_low,
            self_out, cross_out, lse_self, lse_cross, raw_qk, gain_query_pair, cosine, sine, *kv_pieces,
        ),
        scratch=[pltpu.VMEM((2 * tok, LANES), f32)],
        prefetch=1,
        flops=attention_flops * 3 // 2,
        moved=13 * 4 * tok * half_d,
    )

    def pack_specs(arrays):
        views = [pairs(c, a.shape[1] - PACK) for c, a in zip(PIECE_COUNTS, arrays)]
        rows = [
            pl.BlockSpec((c, PACK, half_d), lambda j, *_, at=(a.shape[1] - PACK) // PACK: (0, at, 0))
            for c, a in zip(PIECE_COUNTS, arrays)
        ]
        return views + rows

    d_key_raw, d_gain_key, d_value = call(
        functools.partial(key_back_kernel, PIECE_COUNTS, tok),
        (n_pairs,),
        [pairs(2, tok)]
        + id_specs
        + [pairs(1, tok, 1)]
        + turn_specs
        + pack_specs(query_pieces)
        + pack_specs(grad_pieces),
        [pair(tok), pair(1), pair(tok)],
        [
            shape_of((tok, half_d), bf16),
            shape_of((1, half_d), f32),
            shape_of((tok, half_d), bf16),
        ],
        (
            flags, own_kv, own_ids, piece_ids, raw_qk, gain_key_pair, cosine, sine,
            *query_pieces, *query_pieces, *grad_pieces, *grad_pieces,
        ),
        scratch=[pltpu.VMEM((2 * tok, LANES), f32)] * 2,
        prefetch=1,
        flops=attention_flops * 2,
        moved=13 * 4 * tok * half_d,
    )
    d_projected = jnp.concatenate([d_query_raw, d_key_raw, d_value], axis=1)
    grad_project = scatter(mm(attn_in, d_projected, 0, 0).astype(bf16)).astype(f32)
    d_attn_part = mm(d_projected, w_project, 1, 1)
    d_attn_in = d_attn_part + other_txt(d_attn_part)

    text_own = scatter(jnp.concatenate([d_text_key, d_text_value], axis=1))
    d_text_scaled = text_own[:, :half_d].reshape(text_shape)
    d_gain_text = jnp.sum(d_text_scaled * text_normed, axis=(0, 1))
    d_text_raw = rms_back(text_raw, d_text_scaled * gain_text).reshape(text_rows, half_d)
    d_text_proj = gather(jnp.concatenate([d_text_raw, text_own[:, half_d:]], axis=1).astype(bf16))
    grad_text = mm(text_columns, d_text_proj, 0, 0)

    d_scale_one = d_attn_in * normed_one
    d_normed_one = d_attn_in * (1.0 + scale_one)
    d_gain_attn = jnp.sum(d_normed_one * x_normed, axis=0)
    d_tokens = d_hidden + rms_back(x_float, d_normed_one * gain_attn)

    one_hot_wide = one_hot.astype(f32)

    def by_sample(values):
        summed = lax.dot_general(one_hot_wide, values, (((0,), (0,)), ((), ())), precision=HIGH)
        return lax.dynamic_slice_in_dim(summed, txt_index * half_d, half_d, 1)

    d_mod = lax.psum(
        jnp.concatenate(
            [by_sample(v) for v in (d_attn_in, d_scale_one, d_gate_one, d_ffn_in, d_scale_two, d_gate_two)], axis=1
        ),
        "img",
    )
    grad_modulate = lax.dot_general(silu_own.astype(f32), d_mod, (((0,), (0,)), ((), ())), precision=HIGH)

    grads = [grad_updown, grad_down, grad_project, grad_text, grad_output, grad_modulate]
    reduced = jnp.concatenate([g.reshape(-1, LANES) for g in grads], axis=0)

    replica = (txt_index == 0).astype(f32)
    d_gate_local = jnp.sum(d_gate_lanes.reshape(local_heads, HD), axis=1) * (1.0 - tanh_gate**2)
    gate_full = lax.dynamic_update_slice(jnp.zeros((HEADS,), f32), d_gate_local, (txt_index * local_heads,))
    small_terms = jnp.concatenate(
        [
            d_gain_attn * replica,
            d_gain_ffn * replica,
            jnp.sum(d_gain_query.reshape(local_heads, HD), axis=0),
            jnp.sum(d_gain_key.reshape(local_heads, HD), axis=0),
            d_gain_text,
            gate_full,
        ]
    )
    local_square = jnp.sum(reduced * reduced)
    small_grad, square_big = lax.psum((small_terms, local_square), ("img", "txt"))
    grad_square = square_big + jnp.sum(small_grad * small_grad)
    clip_factor = MAX_NORM / jnp.maximum(jnp.sqrt(grad_square), MAX_NORM)

    lines = reduced.shape[0]
    block = math.gcd(lines, 512)
    line_spec = pl.BlockSpec((block, LANES), lambda i: (i, 0))
    as_lines = (lines, LANES)
    updated = call(
        update_kernel,
        (lines // block,),
        [pl.BlockSpec(memory_space=pltpu.SMEM)] + [line_spec] * 5,
        [line_spec] * 5,
        [shape_of(as_lines, f32)] * 4 + [shape_of(as_lines, bf16)],
        (clip_factor.reshape(1), reduced, *(a.reshape(as_lines) for a in (moment_one, moment_two, master, average))),
        flops=20 * lines * LANES,
        moved=38 * lines * LANES,
    )
    one_new, two_new, master_new, average_new, master_low = (a.reshape(master.shape) for a in updated)
    small_one_new, small_two_new, small_new, small_average_new = adam_update(
        small_grad * clip_factor, small_one, small_two, small_master, small_average, RATE_SMALL, 0.0
    )
    return (
        block_out,
        d_tokens,
        grad_square,
        one_new,
        two_new,
        master_new,
        average_new,
        master_low,
        small_one_new,
        small_two_new,
        small_new,
        small_average_new,
    )


def solution(mesh):
    rows = P("img", None)
    shards = P("img", "txt", None)
    in_specs = (rows, rows, rows, P(), P(), shards, shards, shards, shards, P(), P(), P(), P())
    out_specs = (rows, rows, P(), shards, shards, shards, shards, shards, P(), P(), P(), P())
    return jax.shard_map(on_device, mesh=mesh, in_specs=in_specs, out_specs=out_specs, check_vma=False)
```

time: 4420 us -> 1230 us (0.28)
  waiting for transfers between devices: 2460 us -> 611 us
  local copies, waits for them, and re-layouts: 776 us -> 102 us
  blocking collectives: 501 us -> 185 us
  matrix products: 351 us -> 82.9 us
  other arithmetic: 216 us -> 40.7 us
  Pallas kernels: 0 us -> 110 us
    all_to_all x1, waiting for transfers between devices: 1760 us -> 0.01 us  [on_device(): lax.all_to_all(text_states, 'img', split_axis=1, concat_axis=0, tiled=True)]
    all_gather x1 -> x4, waiting for transfers between devices: 482 us -> 44.3 us  [gather(): return lax.all_gather(rows, 'img', axis=0, tiled=True)]
    psum x1, blocking collectives: 443 us -> 39.8 us  [on_device(): lax.psum((small_terms, local_square), ('img', 'txt'))]
    reduce_scatter x1 -> x6, waiting for transfers between devices: 0.02 us -> 378 us  [scatter(): return lax.psum_scatter(terms, 'img', scatter_dimension=0, tiled=True)]
    dot_general x185 -> x21, matrix products: 348 us -> 79.7 us  [the longest x8 46 us: mm(): lax.dot_general(a, b, (((on_a,), (on_b,)), ((), ())), preferred_element_t...]
    reshape x10 -> x13, local copies, waits for them, and re-layouts: 201 us -> 15.5 us  [the longest x6 11.2 us: on_device(): reduced = jnp.concatenate([g.reshape(-1, LANES) for g in grads], axis=0)]
    unnamed x232 -> x183, local copies, waits for them, and re-layouts: 190 us -> 25.9 us
    dot_general x4 -> x1, local copies, waits for them, and re-layouts: 117 us -> 1.62 us  [mm(): lax.dot_general(a, b, (((on_a,), (on_b,)), ((), ())), preferred_element_t...]
  transfers between devices with their start and end apart: 26 -> 47, of which waited for: 12 -> 20; matrix products, arithmetic and copies ran while one was open for 11% -> 13% of each run, Pallas kernels for 0% -> 5%
where the time goes in v1:
time: 1230 us; the launch traced here: 1220 us
  waiting for transfers between devices  611 us (50%)
  blocking collectives  185 us (15%)
  Pallas kernels  110 us (9%)
  local copies, waits for them, and re-layouts  102 us (8%)
  matrix products  82.9 us (7%)
  starting transfers between devices  71.7 us (6%)
  other arithmetic  40.7 us (3%)
  between operations  18.1 us (1%)
    reduce_scatter x6, waiting for transfers between devices, scatter(): return lax.psum_scatter(terms, 'img', scatter_dimension=0, tiled=True)  378 us
    pallas_call x6, Pallas kernels, call(): pl.pallas_call(kernel, grid_spec=pltpu.PrefetchScalarGridSpec(num_scalar_...  110 us
    all_gather x2, blocking collectives, gather(): return lax.all_gather(rows, 'img', axis=0, tiled=True)  72 us
    psum x1, blocking collectives, on_device(): lax.psum(jnp.dot(silu_own, own_modulate, preferred_element_type=f32), 'img')  67.2 us
    ppermute x5, waiting for transfers between devices, other_txt(): return lax.ppermute(x, 'txt', [(0, 1), (1, 0)])  64.5 us
    psum x1, waiting for transfers between devices, on_device(): lax.psum(jnp.concatenate([by_sample(v) for v in (d_attn_in, d_scale_one,...  64.3 us
    ppermute x18, starting transfers between devices, shifted(): lax.ppermute(x, 'img', [(i + by, i) for i in range(count) if 0 <= i + by...  52.6 us
    dot_general x8, matrix products, mm(): lax.dot_general(a, b, (((on_a,), (on_b,)), ((), ())), preferred_element_t...  46 us
  transfers between devices with their start and end apart: 47, of which 20 were waited for; matrix products, arithmetic and copies ran while one was open for 13% of the time, Pallas kernels for 5%

profile of v1, /device:TPU:0, one launch (start us, length us, event | category | flops | bytes accessed | tf_op | source)
XLA Modules:
  0.0 1221.6 jit_solution(15925344535651208077)
XLA Ops:
  35.2 18.0 %slice_reduce_fusion = (bf16[393216]{0:T(1024)(128)(2,1)S(1)}, bf16[393216]{0:T(1024)(128)(2,1)S(1)}) fusion(bf16[1,1,1572864]{2,1,0:T(2,128)(2,1)} %copy-done.32), kind=kLoop, calls=%fused_computation.44 | loop fusion | bytes 3145728 | tf_op jit(solution)/shard_map/slice | solution.py:479
  67.3 10.8 slice_reduce_fusion.2
  79.8 67.2 %all-reduce.6 = bf16[16,4608]{1,0:T(8,128)(2,1)S(1)} all-reduce(f32[16,4608]{1,0:T(8,128)S(1)} %fusion.61), channel_id=1, replica_groups=mesh['img'=16,'txt'=2] {'img'}, use_global_device_ids=true, to_apply=%region_2.3 | all-reduce | flops 73728 | bytes 442368 | tf_op jit(solution)/shard_map/psum | solution.py:506
  174.1 11.0 collective-permute-done.1.rest_2_
  200.7 8.5 collective-permute-done.5.rest_6_
  223.0 16.2 %collective-permute-done.8.rest_9_ = bf16[2,128,768]{2,1,0:T(8,128)(2,1)S(1)} collective-permute-done((bf16[2,128,768]{2,1,0:T(8,128)(2,1)S(1)}, bf16[2,128,768]{2,1,0:T(8,128)(2,1)S(1)}, u32[]{:S(2)}, u32[]{:S(2)}) %collective-permute-start.8) | collective-permute-done | bytes 393248 | tf_op jit(solution)/shard_map/ppermute | solution.py:380
  240.4 50.0 %all_gather.23.tk_ref.tv_ref = bf16[256,1536]{1,0:T(8,128)(2,1)S(1)} all-gather(bf16[16,1536]{1,0:T(8,128)(2,1)S(1)} %pad_maximum_fusion.14), channel_id=1, replica_groups=mesh['img'=16,'txt'=2] {'img'}, dimensions={0}, use_global_device_ids=true | all-gather | bytes 835584 | tf_op jit(solution)/shard_map/all_gather | solution.py:484
  293.4 22.9 %shard_map.221 = (bf16[256,768]{1,0:T(8,128)(2,1)S(1)}, f32[256,768]{1,0:T(8,128)S(1)}, f32[256,768]{1,0:T(8,128)S(1)}, f32[256,768]{1,0:T(8,128)S(1)}, f32[256,...) custom-call(s32[14]{0:T(128)S(1)} %convert_element_type.149.flag_ref, bf16[256,768]{1,0:T(8,128)(2,1)S(1)} %copy-done.11, ...), custom_call_target="tpu_custom_call" | custom-call | flops 2415919104 | bytes 10223616 | tf_op jit(solution)/shard_map/pallas_call | solution.py:351
  318.6 9.6 collective-permute-done.10
  337.7 10.5 fusion.70
  348.3 44.2 %all-gather.11.cloned.1.call-done = bf16[2048,1536]{1,0:T(8,128)(2,1)} async-done(((bf16[128,1536]{1,0:T(8,128)(2,1)}), bf16[2048,1536]{1,0:T(8,128)(2,1)}) %all-gather.11.cloned.1.call-update) | async-done | bytes 6291472 | tf_op jit(solution)/shard_map/all_gather | solution.py:484
  405.0 8.8 convolution_convert_fusion.5
  427.0 30.2 %collective-permute-done.13 = bf16[256,1536]{1,0:T(8,128)(2,1)S(1)} collective-permute-done((bf16[256,1536]{1,0:T(8,128)(2,1)S(1)}, bf16[256,1536]{1,0:T(8,128)(2,1)S(1)}, u32[]{:S(2)}, u32[]{:S(2)}) %collective-permute-start.13) | collective-permute-done | bytes 786464 | tf_op jit(solution)/shard_map/ppermute | solution.py:389
  514.2 28.4 %shard_map.223 = (bf16[256,768]{1,0:T(8,128)(2,1)S(1)}, f32[1,768]{1,0:T(1,128)S(1)}, f32[256,768]{1,0:T(8,128)S(1)}, f32[256,768]{1,0:T(8,128)S(1)}) custom-call(s32[14]{0:T(128)S(1)} %convert_element_type.149.flag_ref, bf16[256,768]{1,0:T(8,128)(2,1)S(1)} %copy-done.12, s32[256,1]{1,0:T(8,128)S(1)} %copy.63.own_ids_ref, ...), custom_call_target="tpu_custom_call" | custom-call | flops 3623878656 | bytes 10223616 | tf_op jit(solution)/shard_map/pallas_call | solution.py:351
  544.8 20.2 %shard_map.224 = (bf16[256,768]{1,0:T(8,128)(2,1)S(1)}, f32[1,768]{1,0:T(1,128)S(1)}, bf16[256,768]{1,0:T(8,128)(2,1)S(1)}) custom-call(s32[14]{0:T(128)S(1)} %convert_element_type.149.flag_ref, bf16[2,256,768]{2,1,0:T(8,128)(2,1)} %copy-done, s32[256,1]{1,0:T(8,128)S(1)} %copy.63.own_ids_ref, s32[16,256]{1,0:T(8,128)S(1)} %concatenate.81.ids_ref, ...), custom_call_target="tpu_custom_call" | custom-call | flops 4831838208 | bytes 10223616 | tf_op jit(solution)/shard_map/pallas_call | solution.py:351
  584.5 24.7 %collective-permute-done.34 = f32[256,1536]{1,0:T(8,128)} collective-permute-done((f32[256,1536]{1,0:T(8,128)}, f32[256,1536]{1,0:T(8,128)}, u32[]{:S(2)}, u32[]{:S(2)}) %collective-permute-start.34) | collective-permute-done | bytes 1572896 | tf_op jit(solution)/shard_map/ppermute | solution.py:389
  648.7 22.0 %all_gather.27 = bf16[256,1536]{1,0:T(8,128)(2,1)S(1)} all-gather(bf16[16,1536]{1,0:T(8,128)(2,1)S(1)} %pad_maximum_fusion.15), channel_id=1, replica_groups=mesh['img'=16,'txt'=2] {'img'}, dimensions={0}, use_global_device_ids=true | all-gather | bytes 835584 | tf_op jit(solution)/shard_map/all_gather | solution.py:484
  674.4 64.3 %all-reduce.5.cloned.1.call-done = f32[16,4608]{1,0:T(8,128)} async-done(((f32[16,4608]{1,0:T(8,128)}), f32[16,4608]{1,0:T(8,128)}) %all-reduce.5.cloned.1.call-update) | async-done | bytes 294928 | tf_op jit(solution)/shard_map/psum | solution.py:741
  743.8 61.2 %reduce-scatter.17.cloned.1.call-done = bf16[48,1536]{1,0:T(8,128)(2,1)} async-done(((bf16[768,1536]{1,0:T(8,128)(2,1)}), bf16[48,1536]{1,0:T(8,128)(2,1)}) %reduce-scatter.17.cloned.1.call-update) | async-done | bytes 147472 | tf_op jit(solution)/shard_map/reduce_scatter | solution.py:487
  806.1 88.2 %reduce-scatter.11.cloned.1.call-done = bf16[128,1536]{1,0:T(8,128)(2,1)} async-done(((bf16[2048,1536]{1,0:T(8,128)(2,1)}), bf16[128,1536]{1,0:T(8,128)(2,1)}) %reduce-scatter.11.cloned.1.call-update) | async-done | bytes 393232 | tf_op jit(solution)/shard_map/reduce_scatter | solution.py:487
  895.8 91.8 %reduce-scatter.13.cloned.1.call-done = bf16[96,2304]{1,0:T(8,128)(2,1)} async-done(((bf16[1536,2304]{1,0:T(8,128)(2,1)}), bf16[96,2304]{1,0:T(8,128)(2,1)}) %reduce-scatter.13.cloned.1.call-update) | async-done | bytes 442384 | tf_op jit(solution)/shard_map/reduce_scatter | solution.py:487
  990.0 136.5 %reduce-scatter.9.cloned.1.call-done = bf16[96,4096]{1,0:T(8,128)(2,1)} async-done(((bf16[1536,4096]{1,0:T(8,128)(2,1)}), bf16[96,4096]{1,0:T(8,128)(2,1)}) %reduce-scatter.9.cloned.1.call-update) | async-done | bytes 786448 | tf_op jit(solution)/shard_map/reduce_scatter | solution.py:487
  1140.8 39.8 %all-reduce.1 = (f32[]{:T(128)}, f32[3288]{0:T(1024)S(1)}) all-reduce(f32[]{:T(128)} %multiply_reduce_fusion, f32[3288]{0:T(1024)S(1)} %concatenate.99), channel_id=1, replica_groups=mesh['img'=16,'txt'=2] {'img','txt'}, use_global_device_ids=true, to_apply=%region_21.22 | all-reduce | flops 3289 | bytes 26312 | tf_op jit(solution)/shard_map/psum | solution.py:766
  1182.5 26.8 %shard_map.225 = (f32[12288,128]{1,0:T(8,128)}, f32[12288,128]{1,0:T(8,128)}, f32[12288,128]{1,0:T(8,128)}, f32[12288,128]{1,0:T(8,128)}, bf16[12288,128]{1,0:T(8,128)(2,1)S(1)}) custom-call(f32[1]{0:T(128)} %bitcast.23.clip_ref, f32[12288,128]{1,0:T(8,128)} %copy-done.28, f32[12288,128]{1,0:T(8,128)} %bitcast.74, f32[12288,128]{1,0:T(8,128)} %bitcast.75, ...), custom_call_target="tpu_custom_call" | custom-call | flops 31457280 | bytes 59768832 | tf_op jit(solution)/shard_map/pallas_call | solution.py:351
  (427 shorter events, 291.8 us)
Async XLA Ops:
  7.2 151.4 %all-gather.5.cloned.1.call-start = ((), (), s32[]{:S(2)}) async-start(), calls=%async_computation.7 | async-start | bytes 7520256 | tf_op jit(solution)/shard_map/all_gather | solution.py:484
  24.2 174.9 %all-gather.7.cloned.1.call-start = ((), (), s32[]{:S(2)}) async-start(), calls=%async_computation.9 | async-start | bytes 2506752 | tf_op jit(solution)/shard_map/all_gather | solution.py:484
  35.0 179.9 %reduce-scatter.7.cloned.1.call-start = ((), (), s32[]{:S(2)}) async-start(), calls=%async_computation.8 | async-start | bytes 1671168 | tf_op jit(solution)/shard_map/reduce_scatter | solution.py:487
  55.6 282.1 %all-gather.9.cloned.1.call-start = ((), (), s32[]{:S(2)}) async-start(), calls=%async_computation.10 | async-start | bytes 13369344 | tf_op jit(solution)/shard_map/all_gather | solution.py:484
  56.9 335.5 %all-gather.11.cloned.1.call-start = ((), (), s32[]{:S(2)}) async-start(), calls=%async_computation.11 | async-start | bytes 6684672 | tf_op jit(solution)/shard_map/all_gather | solution.py:484
  65.8 579.9 %reduce-scatter.15.cloned.1.call-start = ((), (), s32[]{:S(2)}) async-start(), calls=%async_computation.15 | async-start | bytes 1671168 | tf_op jit(solution)/shard_map/reduce_scatter | solution.py:487
  198.9 91.5 %collective-permute-start.4 = (bf16[6,256,768]{2,1,0:T(8,128)(2,1)}, bf16[6,256,768]{2,1,0:T(8,128)(2,1)}, u32[]{:S(2)}, u32[]{:S(2)}) collective-permute-start(bf16[6,256,768]{2,1,0:T(8,128)(2,1)} %pad_maximum_fusion), channel_id=1, source_target_pairs={{0,2},{2,0},{4,6},{6,4},{8,10},{10,8},{12,14},{14,12},{16,18},{18,... | collective-permute-start | bytes 7077896 | tf_op jit(solution)/shard_map/ppermute | solution.py:385
  199.1 119.5 %collective-permute-start.11 = (bf16[768,1536]{1,0:T(8,128)(2,1)}, bf16[768,1536]{1,0:T(8,128)(2,1)}, u32[]{:S(2)}, u32[]{:S(2)}) collective-permute-start(bf16[768,1536]{1,0:T(8,128)(2,1)} %all-gather.7.cloned.1.call-done.w_ref), channel_id=1, source_target_pairs={{0,1},{1,0},{2,3},{3,2},{4,5},{5,4},{6,7},{7,6},{8,9},{9,8},{10,11... | collective-permute-start | bytes 7077896 | tf_op jit(solution)/shard_map/ppermute | solution.py:389
  212.9 77.5 %collective-permute-start.7 = (bf16[4,256,768]{2,1,0:T(8,128)(2,1)}, bf16[4,256,768]{2,1,0:T(8,128)(2,1)}, u32[]{:S(2)}, u32[]{:S(2)}) collective-permute-start(bf16[4,256,768]{2,1,0:T(8,128)(2,1)} %pad_maximum_fusion.2), channel_id=1, source_target_pairs={{0,2},{2,0},{4,6},{6,4},{8,10},{10,8},{12,14},{14,12},{16,18},{18,... | collective-permute-start | bytes 4718600 | tf_op jit(solution)/shard_map/ppermute | solution.py:385
  221.7 68.7 %collective-permute-start = (bf16[2,256,768]{2,1,0:T(8,128)(2,1)S(1)}, bf16[2,256,768]{2,1,0:T(8,128)(2,1)S(1)}, u32[]{:S(2)}, u32[]{:S(2)}) collective-permute-start(bf16[2,256,768]{2,1,0:T(8,128)(2,1)S(1)} %get-tuple-element.37.rest_0_.kv_ref), channel_id=1, source_target_pairs={{0,2},{2,0},{4,6},{6,4},{8,10},{10,8},{12,14},{14,12},{16,18},{18,... | collective-permute-start | bytes 2359304 | tf_op jit(solution)/shard_map/ppermute | solution.py:385
  239.1 51.3 %collective-permute-start.9 = (bf16[2,128,768]{2,1,0:T(8,128)(2,1)}, bf16[2,128,768]{2,1,0:T(8,128)(2,1)S(1)}, u32[]{:S(2)}, u32[]{:S(2)}) collective-permute-start(bf16[2,128,768]{2,1,0:T(8,128)(2,1)} %get-tuple-element.85), channel_id=1, source_target_pairs={{10,0},{12,2},{14,4},{16,6},{18,8},{20,10},{22,12},{24,14},{26,16}... | collective-permute-start | bytes 1179656 | tf_op jit(solution)/shard_map/ppermute | solution.py:380
  403.6 58.6 %collective-permute-start.12 = (f32[256,1536]{1,0:T(8,128)}, f32[256,1536]{1,0:T(8,128)}, u32[]{:S(2)}, u32[]{:S(2)}) collective-permute-start(f32[256,1536]{1,0:T(8,128)} %fusion.71), channel_id=1, source_target_pairs={{0,1},{1,0},{2,3},{3,2},{4,5},{5,4},{6,7},{7,6},{8,9},{9,8},{10,11... | collective-permute-start | bytes 4718600 | tf_op jit(solution)/shard_map/ppermute | solution.py:389
  413.8 43.3 %collective-permute-start.13 = (bf16[256,1536]{1,0:T(8,128)(2,1)S(1)}, bf16[256,1536]{1,0:T(8,128)(2,1)S(1)}, u32[]{:S(2)}, u32[]{:S(2)}) collective-permute-start(bf16[256,1536]{1,0:T(8,128)(2,1)S(1)} %convolution_convert_fusion.5), channel_id=1, source_target_pairs={{0,1},{1,0},{2,3},{3,2},{4,5},{5,4},{6,7},{7,6},{8,9},{9,8},{10,11... | collective-permute-start | bytes 2359304 | tf_op jit(solution)/shard_map/ppermute | solution.py:389
  415.0 57.0 %collective-permute-start.16 = (bf16[1,272,768]{2,1,0:T(8,128)(2,1)S(1)}, bf16[1,272,768]{2,1,0:T(8,128)(2,1)S(1)}, u32[]{:S(2)}, u32[]{:S(2)}) collective-permute-start(bf16[1,272,768]{2,1,0:T(8,128)(2,1)S(1)} %get-tuple-element.47.rest_0_.rest_11_), channel_id=1, source_target_pairs={{8,0},{10,2},{12,4},{14,6},{16,8},{18,10},{20,12},{22,14},{24,16},... | collective-permute-start | bytes 1253384 | tf_op jit(solution)/shard_map/ppermute | solution.py:380
  416.4 56.9 %collective-permute-start.17 = (bf16[1,272,768]{2,1,0:T(8,128)(2,1)S(1)}, bf16[1,272,768]{2,1,0:T(8,128)(2,1)S(1)}, u32[]{:S(2)}, u32[]{:S(2)}) collective-permute-start(bf16[1,272,768]{2,1,0:T(8,128)(2,1)S(1)} %get-tuple-element.47.rest_0_.rest_11_), channel_id=1, source_target_pairs={{0,8},{2,10},{4,12},{6,14},{8,16},{10,18},{12,20},{14,22},{16,24},... | collective-permute-start | bytes 1253384 | tf_op jit(solution)/shard_map/ppermute | solution.py:380
  425.7 52.4 %collective-permute-start.19 = (bf16[1,272,768]{2,1,0:T(8,128)(2,1)S(1)}, bf16[1,272,768]{2,1,0:T(8,128)(2,1)S(1)}, u32[]{:S(2)}, u32[]{:S(2)}) collective-permute-start(bf16[1,272,768]{2,1,0:T(8,128)(2,1)S(1)} %collective-permute-done.15.rest_2_.rest_13_), channel_id=1, source_target_pairs={{8,0},{10,2},{12,4},{14,6},{16,8},{18,10},{20,12},{22,14},{24,16},... | collective-permute-start | bytes 1253384 | tf_op jit(solution)/shard_map/ppermute | solution.py:380
  491.2 51.5 %collective-permute-start.28 = (bf16[3,272,768]{2,1,0:T(8,128)(2,1)}, bf16[3,272,768]{2,1,0:T(8,128)(2,1)S(1)}, u32[]{:S(2)}, u32[]{:S(2)}) collective-permute-start(bf16[3,272,768]{2,1,0:T(8,128)(2,1)} %pad_maximum_fusion.7), channel_id=1, source_target_pairs={{0,2},{2,0},{4,6},{6,4},{8,10},{10,8},{12,14},{14,12},{16,18},{18,... | collective-permute-start | bytes 3760136 | tf_op jit(solution)/shard_map/ppermute | solution.py:385
  507.1 35.6 %collective-permute-start.31 = (bf16[2,272,768]{2,1,0:T(8,128)(2,1)}, bf16[2,272,768]{2,1,0:T(8,128)(2,1)S(1)}, u32[]{:S(2)}, u32[]{:S(2)}) collective-permute-start(bf16[2,272,768]{2,1,0:T(8,128)(2,1)} %pad_maximum_fusion.9), channel_id=1, source_target_pairs={{0,2},{2,0},{4,6},{6,4},{8,10},{10,8},{12,14},{14,12},{16,18},{18,... | collective-permute-start | bytes 2506760 | tf_op jit(solution)/shard_map/ppermute | solution.py:385
  571.8 37.4 %collective-permute-start.34 = (f32[256,1536]{1,0:T(8,128)}, f32[256,1536]{1,0:T(8,128)}, u32[]{:S(2)}, u32[]{:S(2)}) collective-permute-start(f32[256,1536]{1,0:T(8,128)} %fusion.72), channel_id=1, source_target_pairs={{0,1},{1,0},{2,3},{3,2},{4,5},{5,4},{6,7},{7,6},{8,9},{9,8},{10,11... | collective-permute-start | bytes 4718600 | tf_op jit(solution)/shard_map/ppermute | solution.py:389
  577.4 161.3 %all-reduce.5.cloned.1.call-start = ((), (), s32[]{:S(2)}) async-start(), calls=%async_computation.17 | async-start | bytes 589824 | tf_op jit(solution)/shard_map/psum | solution.py:741
  618.0 187.0 %reduce-scatter.17.cloned.1.call-start = ((), (), s32[]{:S(2)}) async-start(), calls=%async_computation.16 | async-start | bytes 2506752 | tf_op jit(solution)/shard_map/reduce_scatter | solution.py:487
  620.3 274.1 %reduce-scatter.11.cloned.1.call-start = ((), (), s32[]{:S(2)}) async-start(), calls=%async_computation.13 | async-start | bytes 6684672 | tf_op jit(solution)/shard_map/reduce_scatter | solution.py:487
  627.4 360.1 %reduce-scatter.13.cloned.1.call-start = ((), (), s32[]{:S(2)}) async-start(), calls=%async_computation.14 | async-start | bytes 7520256 | tf_op jit(solution)/shard_map/reduce_scatter | solution.py:487
  633.7 492.8 %reduce-scatter.9.cloned.1.call-start = ((), (), s32[]{:S(2)}) async-start(), calls=%async_computation.12 | async-start | bytes 13369344 | tf_op jit(solution)/shard_map/reduce_scatter | solution.py:487
  (108 other events, 1939.6 us)
Sparse Core Ops, SparseCore 0:
  24.3 72.9 all-gather.4
  100.2 41.4 all-gather.6
  145.9 63.3 reduce-scatter.6
  212.3 116.7 all-gather.8
  331.4 60.9 all-gather.10
  577.5 67.9 reduce-scatter.14
  648.8 89.8 all-reduce.4
  743.0 61.9 reduce-scatter.16
  810.0 84.2 reduce-scatter.10
  898.2 89.3 reduce-scatter.12
  992.1 134.2 reduce-scatter.8

commit v2 on v1

--- a/solution.py
+++ b/solution.py
@@ -325,6 +325,28 @@
     d_value_ref[...] = one_pair(acc_v_ref[...]).astype(bf16)
 
 
+def unflatten_kernel(tables, *refs):
+    for (rows, columns), lines_ref, out_ref in zip(tables, refs, refs[len(tables) :]):
+        per_row = columns // LANES
+        for at in range(per_row):
+            out_ref[:, at * LANES : (at + 1) * LANES] = lines_ref[pl.ds(at, rows, stride=per_row), :].astype(bf16)
+
+
+def flatten_kernel(*refs):
+    *grad_refs, lines_ref, square_ref = refs
+    offset = 0
+    square = jnp.zeros((1, LANES), f32)
+    for ref in grad_refs:
+        rows, columns = ref.shape
+        per_row = columns // LANES
+        for at in range(per_row):
+            part = ref[:, at * LANES : (at + 1) * LANES]
+            lines_ref[pl.ds(offset + at, rows, stride=per_row), :] = part
+            square = square + jnp.sum(part * part, axis=0, keepdims=True)
+        offset += rows * per_row
+    square_ref[...] = square
+
+
 def update_kernel(clip_ref, g_ref, one_ref, two_ref, w_ref, avg_ref, one_out, two_out, w_out, avg_out, low_out):
     one, two, weight, moving = adam_update(
         g_ref[...] * clip_ref[0], one_ref[...], two_ref[...], w_ref[...], avg_ref[...], RATE_MATRIX, DECAY_WEIGHT
@@ -398,6 +420,72 @@
     three = crossed(jnp.concatenate([across, above, below], axis=0), 1)
     two = crossed(jnp.concatenate([above_across, below_across], axis=0), 1)
     return [x, beside, across, above, below, three, above_across, below_across, two, low, high]
+
+
+def index_bits(count):
+    bits = count.bit_length() - 1
+    assert count == 1 << bits
+    return bits
+
+
+def sum_over_img(x):
+    for bit in range(index_bits(lax.axis_size("img"))):
+        x = x + crossed(x, 1 << bit)
+    return x
+
+
+def sum_over_all(x):
+    x = sum_over_img(x)
+    return x + other_txt(x)
+
+
+def own_and_other(x, bit):
+    mine = (lax.axis_index("img") >> bit) & 1
+    split = x.reshape(x.shape[0] // 2, 2, *x.shape[1:])
+    own = lax.dynamic_index_in_dim(split, mine, 1, keepdims=False)
+    other = lax.dynamic_index_in_dim(split, 1 - mine, 1, keepdims=False)
+    return own, other
+
+
+def halved(x, bit, sent_as):
+    own, other = own_and_other(x, bit)
+    return own + crossed(other.astype(sent_as), 1 << bit).astype(f32)
+
+
+def scatter_sum(x, sent_as):
+    count = lax.axis_size("img")
+    x = x.reshape(count, x.shape[0] // count, x.shape[1])
+    for bit in range(index_bits(count)):
+        x = halved(x, bit, sent_as)
+    return x[0]
+
+
+def gather_doubling(x):
+    for axis, bit in enumerate(reversed(range(index_bits(lax.axis_size("img"))))):
+        mine = (lax.axis_index("img") >> bit) & 1
+        got = crossed(x, 1 << bit)
+        x = jnp.where(mine == 0, jnp.stack([x, got], axis), jnp.stack([got, x], axis))
+    return x.reshape(-1, x.shape[-1])
+
+
+def weight_gradient(left, right):
+    count = lax.axis_size("img")
+    bits = index_bits(count)
+    tall = left.T.reshape(count, left.shape[1] // count, left.shape[0])
+    rows, width = tall.shape[1], right.shape[1]
+
+    def terms(chunks):
+        return mm(chunks.reshape(-1, chunks.shape[2]), right, 1, 0).reshape(chunks.shape[0], rows, width)
+
+    own, other = own_and_other(tall, 0)
+    got = crossed(terms(other).astype(bf16), 1)
+    own, other = own_and_other(own, 1)
+    got_own, got_other = own_and_other(got, 1)
+    got = crossed((terms(other) + got_other.astype(f32)).astype(bf16), 2)
+    total = terms(own) + got_own.astype(f32) + got.astype(f32)
+    for bit in range(2, bits):
+        total = halved(total, bit, bf16)
+    return total[0]
 
 
 PIECE_COUNTS = (1, 1, 1, 1, 1, 3, 1, 1, 2, 1, 1)
@@ -472,19 +560,26 @@
         (half_d // n_img, D),
         (COND // n_img, 6 * half_d),
     ]
-    flat = master.reshape(-1)
-    own_rows = []
-    offset = 0
+    master_lines = master.reshape(-1, LANES)
+    lines = master_lines.shape[0]
+    starts = [0]
     for rows, columns in tables:
-        own_rows.append(flat[offset : offset + rows * columns].reshape(rows, columns).astype(bf16))
-        offset += rows * columns
-    own_updown, own_down, own_project, own_text, own_output, own_modulate = own_rows
+        starts.append(starts[-1] + rows * columns // LANES)
+
+    def own_rows(*which):
+        shapes = [tables[w] for w in which]
+        return pl.pallas_call(
+            functools.partial(unflatten_kernel, shapes),
+            out_shape=[shape_of(s, bf16) for s in shapes],
+            compiler_params=pltpu.CompilerParams(vmem_limit_bytes=VMEM),
+        )(*(master_lines[starts[w] : starts[w + 1]] for w in which))
+
+    (own_project,) = own_rows(2)
+    own_modulate, own_text = own_rows(5, 3)
+    own_updown, own_down, own_output = own_rows(0, 1, 4)
 
     def gather(rows):
         return lax.all_gather(rows, "img", axis=0, tiled=True)
-
-    def scatter(terms):
-        return lax.psum_scatter(terms, "img", scatter_dimension=0, tiled=True)
 
     w_project = gather(own_project)
 
@@ -503,7 +598,7 @@
     cond_rows = COND // n_img
     cond_own = lax.dynamic_slice_in_dim(conditions, img_index * cond_rows, cond_rows, 1)
     silu_own = jax.nn.silu(cond_own.astype(f32)).astype(bf16)
-    mod_half = lax.psum(jnp.dot(silu_own, own_modulate, preferred_element_type=f32), "img").astype(bf16)
+    mod_half = sum_over_img(jnp.dot(silu_own, own_modulate, preferred_element_type=f32)).astype(bf16)
     mods = lax.all_gather(mod_half.reshape(samples, 6, half_d), "txt", axis=2, tiled=True)
 
     row_index = img_index * tok + jnp.arange(tok, dtype=jnp.int32)
@@ -532,13 +627,13 @@
     text_rows = text_states.shape[0]
     text_len = text_rows * n_img
     text_columns = lax.all_to_all(text_states, "img", split_axis=1, concat_axis=0, tiled=True)
-    text_proj = scatter(jnp.dot(text_columns, own_text, preferred_element_type=f32))
+    text_proj = scatter_sum(jnp.dot(text_columns, own_text, preferred_element_type=f32), f32)
     text_shape = (text_rows, local_heads, HD)
     text_raw = text_proj[:, :half_d].reshape(text_shape)
     text_normed = rms_norm(text_raw)
     text_key_low = (text_normed * gain_text).reshape(text_rows, half_d).astype(bf16)
     text_low = jnp.concatenate([text_key_low, text_proj[:, half_d:].astype(bf16)], axis=1)
-    all_text = gather(text_low)
+    all_text = gather_doubling(text_low)
 
     x_float = tokens.astype(f32)
     x_normed = rms_norm(x_float)
@@ -627,8 +722,8 @@
     d_gate_up = jnp.concatenate([d_gate.astype(bf16), d_up.astype(bf16)], axis=1)
     d_ffn_part = mm(d_gate_up, w_updown, 1, 1).astype(bf16)
     d_ffn_in = d_ffn_part.astype(f32) + other_txt(d_ffn_part).astype(f32)
-    grad_down = scatter(mm(hidden_units, d_branch, 0, 0).astype(bf16)).astype(f32)
-    grad_updown = scatter(mm(ffn_in, d_gate_up, 0, 0).astype(bf16)).astype(f32)
+    grad_down = weight_gradient(hidden_units, d_branch)
+    grad_updown = weight_gradient(ffn_in, d_gate_up)
 
     d_scale_two = d_ffn_in * normed_two
     d_normed_two = d_ffn_in * (1.0 + scale_two)
@@ -652,7 +747,7 @@
         moved=4 * D * half_d,
     )
     grad_pieces = neighbourhood(grad_pack, *pack_edges(grad_pack))
-    grad_output = scatter(mm(mixed_low, d_attn, 0, 0).astype(bf16)).astype(f32)
+    grad_output = weight_gradient(mixed_low, d_attn)
 
     turn_specs = [whole((1, LANES)), whole((tok, LANES)), whole((tok, LANES))]
     d_query_raw, d_gain_query, d_text_key, d_text_value = call(
@@ -716,15 +811,15 @@
         moved=13 * 4 * tok * half_d,
     )
     d_projected = jnp.concatenate([d_query_raw, d_key_raw, d_value], axis=1)
-    grad_project = scatter(mm(attn_in, d_projected, 0, 0).astype(bf16)).astype(f32)
+    grad_project = weight_gradient(attn_in, d_projected)
     d_attn_part = mm(d_projected, w_project, 1, 1)
     d_attn_in = d_attn_part + other_txt(d_attn_part)
 
-    text_own = scatter(jnp.concatenate([d_text_key, d_text_value], axis=1))
+    text_own = scatter_sum(jnp.concatenate([d_text_key, d_text_value], axis=1), f32)
     d_text_scaled = text_own[:, :half_d].reshape(text_shape)
     d_gain_text = jnp.sum(d_text_scaled * text_normed, axis=(0, 1))
     d_text_raw = rms_back(text_raw, d_text_scaled * gain_text).reshape(text_rows, half_d)
-    d_text_proj = gather(jnp.concatenate([d_text_raw, text_own[:, half_d:]], axis=1).astype(bf16))
+    d_text_proj = gather_doubling(jnp.concatenate([d_text_raw, text_own[:, half_d:]], axis=1).astype(bf16))
     grad_text = mm(text_columns, d_text_proj, 0, 0)
 
     d_scale_one = d_attn_in * normed_one
@@ -738,16 +833,19 @@
         summed = lax.dot_general(one_hot_wide, values, (((0,), (0,)), ((), ())), precision=HIGH)
         return lax.dynamic_slice_in_dim(summed, txt_index * half_d, half_d, 1)
 
-    d_mod = lax.psum(
-        jnp.concatenate(
-            [by_sample(v) for v in (d_attn_in, d_scale_one, d_gate_one, d_ffn_in, d_scale_two, d_gate_two)], axis=1
-        ),
-        "img",
-    )
+    d_mod_early = sum_over_img(
+        jnp.concatenate([by_sample(v) for v in (d_gate_one, d_ffn_in, d_scale_two, d_gate_two)], axis=1)
+    )
+    d_mod_late = sum_over_img(jnp.concatenate([by_sample(v) for v in (d_attn_in, d_scale_one)], axis=1))
+    d_mod = jnp.concatenate([d_mod_late, d_mod_early], axis=1)
     grad_modulate = lax.dot_general(silu_own.astype(f32), d_mod, (((0,), (0,)), ((), ())), precision=HIGH)
 
     grads = [grad_updown, grad_down, grad_project, grad_text, grad_output, grad_modulate]
-    reduced = jnp.concatenate([g.reshape(-1, LANES) for g in grads], axis=0)
+    reduced, squares = pl.pallas_call(
+        flatten_kernel,
+        out_shape=[shape_of((lines, LANES), f32), shape_of((1, LANES), f32)],
+        compiler_params=pltpu.CompilerParams(vmem_limit_bytes=VMEM),
+    )(*grads)
 
     replica = (txt_index == 0).astype(f32)
     d_gate_local = jnp.sum(d_gate_lanes.reshape(local_heads, HD), axis=1) * (1.0 - tanh_gate**2)
@@ -762,13 +860,12 @@
             gate_full,
         ]
     )
-    local_square = jnp.sum(reduced * reduced)
-    small_grad, square_big = lax.psum((small_terms, local_square), ("img", "txt"))
+    small_grad = sum_over_all(small_terms)
+    square_big = jnp.sum(sum_over_all(squares))
     grad_square = square_big + jnp.sum(small_grad * small_grad)
     clip_factor = MAX_NORM / jnp.maximum(jnp.sqrt(grad_square), MAX_NORM)
 
-    lines = reduced.shape[0]
-    block = math.gcd(lines, 512)
+    block = math.gcd(lines, 1024)
     line_spec = pl.BlockSpec((block, LANES), lambda i: (i, 0))
     as_lines = (lines, LANES)
     updated = call(

time: 1230 us -> 976 us (0.79)
  blocking collectives: 185 us -> 7.51 us
  waiting for transfers between devices: 611 us -> 482 us
  starting transfers between devices: 71.7 us -> 133 us
  local copies, waits for them, and re-layouts: 102 us -> 52.6 us
  other arithmetic: 40.7 us -> 62 us
    reduce_scatter x6 -> x0, waiting for transfers between devices: 378 us -> none  [scatter(): return lax.psum_scatter(terms, 'img', scatter_dimension=0, tiled=True)]
    ppermute x12 -> x64, waiting for transfers between devices: 18.4 us -> 363 us  [crossed(): return lax.ppermute(x, 'img', [(i, i ^ bit) for i in range(count)])]
    psum x2 -> x0, blocking collectives: 107 us -> none  [the longest x1 67.2 us: on_device(): lax.psum(jnp.dot(silu_own, own_modulate, preferred_element_type=f32), 'img')]
    all_gather x2 -> x0, blocking collectives: 72 us -> none  [gather(): return lax.all_gather(rows, 'img', axis=0, tiled=True)]
    psum x1 -> x0, waiting for transfers between devices: 64.3 us -> none  [on_device(): lax.psum(jnp.concatenate([by_sample(v) for v in (d_attn_in, d_scale_one,...]
    ppermute x12 -> x64, starting transfers between devices: 3.23 us -> 64.4 us  [crossed(): return lax.ppermute(x, 'img', [(i, i ^ bit) for i in range(count)])]
    ppermute x18, waiting for transfers between devices: 42 us -> 101 us  [shifted(): lax.ppermute(x, 'img', [(i + by, i) for i in range(count) if 0 <= i + by...]
    ppermute x5 -> x7, waiting for transfers between devices: 64.5 us -> 8.64 us  [other_txt(): return lax.ppermute(x, 'txt', [(0, 1), (1, 0)])]
  transfers between devices with their start and end apart: 47 -> 94, of which waited for: 20 -> 37; matrix products, arithmetic and copies ran while one was open for 13% -> 18% of each run, Pallas kernels for 5% -> 9%
where the time goes in v2:
time: 976 us; the launch traced here: 959 us
  waiting for transfers between devices  482 us (49%)
  starting transfers between devices  133 us (14%)
  Pallas kernels  115 us (12%)
  matrix products  88.8 us (9%)
  other arithmetic  62 us (6%)
  local copies, waits for them, and re-layouts  52.6 us (5%)
  between operations  19.2 us (2%)
    ppermute x64, waiting for transfers between devices, crossed(): return lax.ppermute(x, 'img', [(i, i ^ bit) for i in range(count)])  363 us
    pallas_call x6, Pallas kernels, call(): pl.pallas_call(kernel, grid_spec=pltpu.PrefetchScalarGridSpec(num_scalar_...  105 us
    ppermute x18, waiting for transfers between devices, shifted(): lax.ppermute(x, 'img', [(i + by, i) for i in range(count) if 0 <= i + by...  101 us
    ppermute x64, starting transfers between devices, crossed(): return lax.ppermute(x, 'img', [(i, i ^ bit) for i in range(count)])  64.4 us
    dot_general x16, matrix products, mm(): lax.dot_general(a, b, (((on_a,), (on_b,)), ((), ())), preferred_element_t...  55.5 us
    ppermute x18, starting transfers between devices, shifted(): lax.ppermute(x, 'img', [(i + by, i) for i in range(count) if 0 <= i + by...  54.5 us
  transfers between devices with their start and end apart: 94, of which 37 were waited for; matrix products, arithmetic and copies ran while one was open for 18% of the time, Pallas kernels for 9%

profile of v2, /device:TPU:0, one launch (start us, length us, event | category | flops | bytes accessed | tf_op | source)
XLA Modules:
  0.0 959.4 jit_solution(5559264552919388439)
XLA Ops:
  42.8 10.3 %collective-permute-done.1 = f32[16,4608]{1,0:T(8,128)S(1)} collective-permute-done((f32[16,4608]{1,0:T(8,128)S(1)}, f32[16,4608]{1,0:T(8,128)S(1)}, u32[]{:S(2)}, u32[]{:S(2)}) %collective-permute-start.1) | collective-permute-done | bytes 294944 | tf_op jit(solution)/shard_map/ppermute | solution.py:407
  54.8 22.4 %collective-permute-done.2 = f32[16,4608]{1,0:T(8,128)S(1)} collective-permute-done((f32[16,4608]{1,0:T(8,128)S(1)}, f32[16,4608]{1,0:T(8,128)S(1)}, u32[]{:S(2)}, u32[]{:S(2)}) %collective-permute-start.2) | collective-permute-done | bytes 294944 | tf_op jit(solution)/shard_map/ppermute | solution.py:407
  78.7 17.7 %collective-permute-done.3 = f32[16,4608]{1,0:T(8,128)S(1)} collective-permute-done((f32[16,4608]{1,0:T(8,128)S(1)}, f32[16,4608]{1,0:T(8,128)S(1)}, u32[]{:S(2)}, u32[]{:S(2)}) %collective-permute-start.3) | collective-permute-done | bytes 294944 | tf_op jit(solution)/shard_map/ppermute | solution.py:407
  105.8 8.1 collective-permute-done.6
  137.8 17.7 %collective-permute-done.8 = bf16[16,1536]{1,0:T(8,128)(2,1)S(1)} collective-permute-done((bf16[16,1536]{1,0:T(8,128)(2,1)S(1)}, bf16[16,1536]{1,0:T(8,128)(2,1)S(1)}, u32[]{:S(2)}, u32[]{:S(2)}) %collective-permute-start.8) | collective-permute-done | bytes 49184 | tf_op jit(solution)/shard_map/ppermute | solution.py:407
  168.6 31.5 %collective-permute-done.17.rest_6_ = bf16[2,256,768]{2,1,0:T(8,128)(2,1)} collective-permute-done((bf16[2,256,768]{2,1,0:T(8,128)(2,1)S(1)}, bf16[2,256,768]{2,1,0:T(8,128)(2,1)}, u32[]{:S(2)}, u32[]{:S(2)}) %collective-permute-start.17) | collective-permute-done | bytes 786464 | tf_op jit(solution)/shard_map/ppermute | solution.py:402
  209.3 15.3 %collective-permute-done.20.rest_9_ = bf16[2,128,768]{2,1,0:T(8,128)(2,1)S(1)} collective-permute-done((bf16[2,128,768]{2,1,0:T(8,128)(2,1)}, bf16[2,128,768]{2,1,0:T(8,128)(2,1)S(1)}, u32[]{:S(2)}, u32[]{:S(2)}) %collective-permute-start.20) | collective-permute-done | bytes 393248 | tf_op jit(solution)/shard_map/ppermute | solution.py:402
  226.6 25.0 %collective-permute-done.21.rest_10_ = bf16[2,128,768]{2,1,0:T(8,128)(2,1)S(1)} collective-permute-done((bf16[2,128,768]{2,1,0:T(8,128)(2,1)}, bf16[2,128,768]{2,1,0:T(8,128)(2,1)S(1)}, u32[]{:S(2)}, u32[]{:S(2)}) %collective-permute-start.21) | collective-permute-done | bytes 393248 | tf_op jit(solution)/shard_map/ppermute | solution.py:402
  252.7 23.2 %shard_map.223 = (bf16[256,768]{1,0:T(8,128)(2,1)}, f32[256,768]{1,0:T(8,128)S(1)}, f32[256,768]{1,0:T(8,128)S(1)}, f32[256,768]{1,0:T(8,128)S(1)}, f32[256,768]...) custom-call(s32[14]{0:T(128)S(1)} %convert_element_type.276.flag_ref, bf16[256,768]{1,0:T(8,128)(2,1)S(1)} %copy-done.17, ...), custom_call_target="tpu_custom_call" | custom-call | flops 2415919104 | bytes 10223616 | tf_op jit(solution)/shard_map/pallas_call | solution.py:373
  282.0 19.2 %collective-permute-start.27 = (bf16[1,272,768]{2,1,0:T(8,128)(2,1)S(1)}, bf16[1,272,768]{2,1,0:T(8,128)(2,1)S(1)}, u32[]{:S(2)}, u32[]{:S(2)}) collective-permute-start(bf16[1,272,768]{2,1,0:T(8,128)(2,1)S(1)} %get-tuple-element.59.rest_0_.rest_11_), channel_id=1, source_target_pairs={{0,4},{2,6},{4,0},{6,2},{8,12},{10,14},{12,8},{14,10},{16,20},{18,... | collective-permute-start | bytes 1253384 | tf_op jit(solution)/shard_map/ppermute | solution.py:407
  330.9 15.6 %collective-permute-done.31.rest_6_.rest_17_ = bf16[1,272,768]{2,1,0:T(8,128)(2,1)} collective-permute-done((bf16[1,272,768]{2,1,0:T(8,128)(2,1)S(1)}, bf16[1,272,768]{2,1,0:T(8,128)(2,1)}, u32[]{:S(2)}, u32[]{:S(2)}) %collective-permute-start.31) | collective-permute-done | bytes 417824 | tf_op jit(solution)/shard_map/ppermute | solution.py:402
  348.7 10.4 %fusion.145 = f32[256,4096]{1,0:T(8,128)} fusion(bf16[256,1536]{1,0:T(8,128)(2,1)} %get-tuple-element.99, bf16[1536,4096]{1,0:T(8,128)(2,1)} %all-gather.9.cloned.1.call-done), kind=kOutput, calls=%fused_computation.301 | convolution fusion | flops 3221225472 | bytes 17563648 | tf_op jit(solution)/shard_map/dot_general | solution.py:707
  373.3 8.2 convolution_convert_fusion.5
  432.7 28.3 %shard_map.226 = (bf16[256,768]{1,0:T(8,128)(2,1)S(1)}, f32[1,768]{1,0:T(1,128)S(1)}, f32[256,768]{1,0:T(8,128)S(1)}, f32[256,768]{1,0:T(8,128)S(1)}) custom-call(s32[14]{0:T(128)S(1)} %convert_element_type.276.flag_ref, bf16[256,768]{1,0:T(8,128)(2,1)S(1)} %copy-done.18, s32[256,1]{1,0:T(8,128)S(1)} %copy-done.13, s32[16,256]{1,0:T(8,128)S(1)} %concatenate.263.ids_ref, ...), custom_call_target="tpu_custom_call" | custom-call | flops 3623878656 | bytes 10223616 | tf_op jit(solution)/shard_map/pallas_call | solution.py:373
  467.6 8.2 collective-permute-start.39
  501.4 10.0 %collective-permute-done.78 = f32[16,3072]{1,0:T(8,128)S(1)} collective-permute-done((f32[16,3072]{1,0:T(8,128)S(1)}, f32[16,3072]{1,0:T(8,128)S(1)}, u32[]{:S(2)}, u32[]{:S(2)}) %collective-permute-start.78) | collective-permute-done | bytes 196640 | tf_op jit(solution)/shard_map/ppermute | solution.py:407
  519.8 9.4 collective-permute-done.62
  576.4 20.1 %shard_map.227 = (bf16[256,768]{1,0:T(8,128)(2,1)S(1)}, f32[1,768]{1,0:T(1,128)S(1)}, bf16[256,768]{1,0:T(8,128)(2,1)S(1)}) custom-call(s32[14]{0:T(128)S(1)} %convert_element_type.276.flag_ref, bf16[2,256,768]{2,1,0:T(8,128)(2,1)} %copy-done, s32[256,1]{1,0:T(8,128)S(1)} %copy-done.13, s32[16,256]{1,0:T(8,128)S(1)} %concatenate.263.ids_ref, ...), custom_call_target="tpu_custom_call" | custom-call | flops 4831838208 | bytes 10223616 | tf_op jit(solution)/shard_map/pallas_call | solution.py:373
  603.5 23.0 %collective-permute-done.65 = bf16[2,2,16,1536]{3,2,0,1:T(8,128)(2,1)} collective-permute-done((bf16[2,2,16,1536]{3,2,0,1:T(8,128)(2,1)}, bf16[2,2,16,1536]{3,2,0,1:T(8,128)(2,1)}, u32[]{:S(2)}, u32[]{:S(2)}) %collective-permute-start.65) | collective-permute-done | bytes 196640 | tf_op jit(solution)/shard_map/ppermute | solution.py:407
  662.9 103.8 %collective-permute-done.72 = f32[16,1536]{1,0:T(8,128)S(1)} collective-permute-done((f32[16,1536]{1,0:T(8,128)S(1)}, f32[16,1536]{1,0:T(8,128)S(1)}, u32[]{:S(2)}, u32[]{:S(2)}) %collective-permute-start.72) | collective-permute-done | bytes 98336 | tf_op jit(solution)/shard_map/ppermute | solution.py:407
  799.3 23.0 %collective-permute-done.57 = bf16[2,96,2304]{2,1,0:T(8,128)(2,1)S(1)} collective-permute-done((bf16[2,96,2304]{2,1,0:T(8,128)(2,1)S(1)}, bf16[2,96,2304]{2,1,0:T(8,128)(2,1)S(1)}, u32[]{:S(2)}, u32[]{:S(2)}) %collective-permute-start.57) | collective-permute-done | bytes 884768 | tf_op jit(solution)/shard_map/ppermute | solution.py:407
  823.2 40.6 %collective-permute-done.49 = bf16[2,96,4096]{2,1,0:T(8,128)(2,1)S(1)} collective-permute-done((bf16[2,96,4096]{2,1,0:T(8,128)(2,1)S(1)}, bf16[2,96,4096]{2,1,0:T(8,128)(2,1)S(1)}, u32[]{:S(2)}, u32[]{:S(2)}) %collective-permute-start.49) | collective-permute-done | bytes 1572896 | tf_op jit(solution)/shard_map/ppermute | solution.py:407
  865.7 34.4 %collective-permute-done.50 = bf16[1,96,4096]{2,1,0:T(8,128)(2,1)S(1)} collective-permute-done((bf16[1,96,4096]{2,1,0:T(8,128)(2,1)S(1)}, bf16[1,96,4096]{2,1,0:T(8,128)(2,1)S(1)}, u32[]{:S(2)}, u32[]{:S(2)}) %collective-permute-start.50) | collective-permute-done | bytes 786464 | tf_op jit(solution)/shard_map/ppermute | solution.py:407
  924.9 21.9 %shard_map.229 = (f32[12288,128]{1,0:T(8,128)}, f32[12288,128]{1,0:T(8,128)}, f32[12288,128]{1,0:T(8,128)}, f32[12288,128]{1,0:T(8,128)}, bf16[12288,128]{1,0:T(8,128)(2,1)S(1)}) custom-call(f32[1]{0:T(128)} %bitcast.131.clip_ref, f32[12288,128]{1,0:T(8,128)} %get-tuple-element.68.g_ref, f32[12288,128]{1,0:T(8,128)} %bitcast.345, f32[12288,128]{1,0:T(8,128)} %bitcast.346, ...), custom_call_target="tpu_custom_call" | custom-call | flops 31457280 | bytes 59768832 | tf_op jit(solution)/shard_map/pallas_call | solution.py:373
  (662 shorter events, 393.0 us)
Async XLA Ops:
  7.2 114.1 %all-gather.5.cloned.1.call-start = ((), (), s32[]{:S(2)}) async-start(), calls=%async_computation.1 | async-start | bytes 7520256 | tf_op jit(solution)/shard_map/all_gather | solution.py:582
  9.3 157.9 %all-gather.7.cloned.1.call-start = ((), (), s32[]{:S(2)}) async-start(), calls=%async_computation.2 | async-start | bytes 2506752 | tf_op jit(solution)/shard_map/all_gather | solution.py:582
  16.4 332.2 %all-gather.9.cloned.1.call-start = ((), (), s32[]{:S(2)}) async-start(), calls=%async_computation.3 | async-start | bytes 13369344 | tf_op jit(solution)/shard_map/all_gather | solution.py:582
  29.9 329.2 %all-gather.11.cloned.1.call-start = ((), (), s32[]{:S(2)}) async-start(), calls=%async_computation.4 | async-start | bytes 6684672 | tf_op jit(solution)/shard_map/all_gather | solution.py:582
  156.0 44.1 %collective-permute-start.17 = (bf16[2,256,768]{2,1,0:T(8,128)(2,1)S(1)}, bf16[2,256,768]{2,1,0:T(8,128)(2,1)}, u32[]{:S(2)}, u32[]{:S(2)}) collective-permute-start(bf16[2,256,768]{2,1,0:T(8,128)(2,1)S(1)} %collective-permute-done.13.rest_2_), channel_id=1, source_target_pairs={{8,0},{10,2},{12,4},{14,6},{16,8},{18,10},{20,12},{22,14},{24,16},... | collective-permute-start | bytes 2359304 | tf_op jit(solution)/shard_map/ppermute | solution.py:402
  165.8 85.8 %collective-permute-start.16 = (bf16[6,256,768]{2,1,0:T(8,128)(2,1)}, bf16[6,256,768]{2,1,0:T(8,128)(2,1)}, u32[]{:S(2)}, u32[]{:S(2)}) collective-permute-start(bf16[6,256,768]{2,1,0:T(8,128)(2,1)} %pad_maximum_fusion), channel_id=1, source_target_pairs={{0,2},{2,0},{4,6},{6,4},{8,10},{10,8},{12,14},{14,12},{16,18},{18,... | collective-permute-start | bytes 7077896 | tf_op jit(solution)/shard_map/ppermute | solution.py:407
  167.2 143.2 %collective-permute-start.23 = (bf16[768,1536]{1,0:T(8,128)(2,1)}, bf16[768,1536]{1,0:T(8,128)(2,1)}, u32[]{:S(2)}, u32[]{:S(2)}) collective-permute-start(bf16[768,1536]{1,0:T(8,128)(2,1)} %all-gather.7.cloned.1.call-done.w_ref), channel_id=1, source_target_pairs={{0,1},{1,0},{2,3},{3,2},{4,5},{5,4},{6,7},{7,6},{8,9},{9,8},{10,11... | collective-permute-start | bytes 7077896 | tf_op jit(solution)/shard_map/ppermute | solution.py:411
  202.7 48.8 %collective-permute-start.19 = (bf16[4,256,768]{2,1,0:T(8,128)(2,1)}, bf16[4,256,768]{2,1,0:T(8,128)(2,1)}, u32[]{:S(2)}, u32[]{:S(2)}) collective-permute-start(bf16[4,256,768]{2,1,0:T(8,128)(2,1)} %pad_maximum_fusion.2), channel_id=1, source_target_pairs={{0,2},{2,0},{4,6},{6,4},{8,10},{10,8},{12,14},{14,12},{16,18},{18,... | collective-permute-start | bytes 4718600 | tf_op jit(solution)/shard_map/ppermute | solution.py:407
  208.2 43.4 %collective-permute-start.12 = (bf16[2,256,768]{2,1,0:T(8,128)(2,1)S(1)}, bf16[2,256,768]{2,1,0:T(8,128)(2,1)}, u32[]{:S(2)}, u32[]{:S(2)}) collective-permute-start(bf16[2,256,768]{2,1,0:T(8,128)(2,1)S(1)} %get-tuple-element.46.rest_0_.kv_ref), channel_id=1, source_target_pairs={{0,2},{2,0},{4,6},{6,4},{8,10},{10,8},{12,14},{14,12},{16,18},{18,... | collective-permute-start | bytes 2359304 | tf_op jit(solution)/shard_map/ppermute | solution.py:407
  368.7 52.7 %collective-permute-start.24 = (f32[256,1536]{1,0:T(8,128)}, f32[256,1536]{1,0:T(8,128)}, u32[]{:S(2)}, u32[]{:S(2)}) collective-permute-start(f32[256,1536]{1,0:T(8,128)} %fusion.146), channel_id=1, source_target_pairs={{0,1},{1,0},{2,3},{3,2},{4,5},{5,4},{6,7},{7,6},{8,9},{9,8},{10,11... | collective-permute-start | bytes 4718600 | tf_op jit(solution)/shard_map/ppermute | solution.py:411
  430.6 55.7 %collective-permute-start.37 = (bf16[1,272,768]{2,1,0:T(8,128)(2,1)S(1)}, bf16[1,272,768]{2,1,0:T(8,128)(2,1)}, u32[]{:S(2)}, u32[]{:S(2)}) collective-permute-start(bf16[1,272,768]{2,1,0:T(8,128)(2,1)S(1)} %get-tuple-element.53.d_self_ref.rest_22_.rest_33_), channel_id=1, source_target_pairs={{0,4},{2,6},{4,0},{6,2},{8,12},{10,14},{12,8},{14,10},{16,20},{18,... | collective-permute-start | bytes 1253384 | tf_op jit(solution)/shard_map/ppermute | solution.py:407
  431.0 65.8 %collective-permute-start.38 = (bf16[1,272,768]{2,1,0:T(8,128)(2,1)S(1)}, bf16[1,272,768]{2,1,0:T(8,128)(2,1)}, u32[]{:S(2)}, u32[]{:S(2)}) collective-permute-start(bf16[1,272,768]{2,1,0:T(8,128)(2,1)S(1)} %get-tuple-element.53.d_self_ref.rest_22_.rest_33_), channel_id=1, source_target_pairs={{8,0},{10,2},{12,4},{14,6},{16,8},{18,10},{20,12},{22,14},{24,16},... | collective-permute-start | bytes 1253384 | tf_op jit(solution)/shard_map/ppermute | solution.py:402
  545.4 105.5 %collective-permute-start.47 = (bf16[8,96,4096]{2,1,0:T(8,128)(2,1)}, bf16[8,96,4096]{2,1,0:T(8,128)(2,1)}, u32[]{:S(2)}, u32[]{:S(2)}) collective-permute-start(bf16[8,96,4096]{2,1,0:T(8,128)(2,1)} %convolution_convert_fusion.1), channel_id=1, source_target_pairs={{0,2},{2,0},{4,6},{6,4},{8,10},{10,8},{12,14},{14,12},{16,18},{18,... | collective-permute-start | bytes 18874376 | tf_op jit(solution)/shard_map/ppermute | solution.py:407
  574.3 192.4 %collective-permute-start.52 = (bf16[4,128,1536]{2,1,0:T(8,128)(2,1)}, bf16[4,128,1536]{2,1,0:T(8,128)(2,1)}, u32[]{:S(2)}, u32[]{:S(2)}) collective-permute-start(bf16[4,128,1536]{2,1,0:T(8,128)(2,1)} %fusion.4), channel_id=1, source_target_pairs={{0,4},{2,6},{4,0},{6,2},{8,12},{10,14},{12,8},{14,10},{16,20},{18,... | collective-permute-start | bytes 4718600 | tf_op jit(solution)/shard_map/ppermute | solution.py:407
  574.3 52.2 %collective-permute-start.65 = (bf16[2,2,16,1536]{3,2,0,1:T(8,128)(2,1)}, bf16[2,2,16,1536]{3,2,0,1:T(8,128)(2,1)}, u32[]{:S(2)}, u32[]{:S(2)}) collective-permute-start(bf16[2,2,16,1536]{3,2,0,1:T(8,128)(2,1)} %maximum_select_fusion.9), channel_id=1, source_target_pairs={{0,4},{2,6},{4,0},{6,2},{8,12},{10,14},{12,8},{14,10},{16,20},{18,... | collective-permute-start | bytes 589832 | tf_op jit(solution)/shard_map/ppermute | solution.py:407
  598.7 48.1 %collective-permute-start.46 = (f32[256,1536]{1,0:T(8,128)S(1)}, f32[256,1536]{1,0:T(8,128)}, u32[]{:S(2)}, u32[]{:S(2)}) collective-permute-start(f32[256,1536]{1,0:T(8,128)S(1)} %fusion.147), channel_id=1, source_target_pairs={{0,1},{1,0},{2,3},{3,2},{4,5},{5,4},{6,7},{7,6},{8,9},{9,8},{10,11... | collective-permute-start | bytes 4718600 | tf_op jit(solution)/shard_map/ppermute | solution.py:411
  601.9 56.3 %collective-permute-start.55 = (bf16[8,96,2304]{2,1,0:T(8,128)(2,1)S(1)}, bf16[8,96,2304]{2,1,0:T(8,128)(2,1)S(1)}, u32[]{:S(2)}, u32[]{:S(2)}) collective-permute-start(bf16[8,96,2304]{2,1,0:T(8,128)(2,1)S(1)} %convolution_convert_fusion.2), channel_id=1, source_target_pairs={{0,2},{2,0},{4,6},{6,4},{8,10},{10,8},{12,14},{14,12},{16,18},{18,... | collective-permute-start | bytes 10616840 | tf_op jit(solution)/shard_map/ppermute | solution.py:407
  656.3 128.6 %collective-permute-start.48 = (bf16[4,96,4096]{2,1,0:T(8,128)(2,1)}, bf16[4,96,4096]{2,1,0:T(8,128)(2,1)}, u32[]{:S(2)}, u32[]{:S(2)}) collective-permute-start(bf16[4,96,4096]{2,1,0:T(8,128)(2,1)} %fusion), channel_id=1, source_target_pairs={{0,4},{2,6},{4,0},{6,2},{8,12},{10,14},{12,8},{14,10},{16,20},{18,... | collective-permute-start | bytes 9437192 | tf_op jit(solution)/shard_map/ppermute | solution.py:407
  660.6 118.8 %collective-permute-start.56 = (bf16[4,96,2304]{2,1,0:T(8,128)(2,1)}, bf16[4,96,2304]{2,1,0:T(8,128)(2,1)}, u32[]{:S(2)}, u32[]{:S(2)}) collective-permute-start(bf16[4,96,2304]{2,1,0:T(8,128)(2,1)} %fusion.3), channel_id=1, source_target_pairs={{0,4},{2,6},{4,0},{6,2},{8,12},{10,14},{12,8},{14,10},{16,20},{18,... | collective-permute-start | bytes 5308424 | tf_op jit(solution)/shard_map/ppermute | solution.py:407
  660.9 105.7 %collective-permute-start.72 = (f32[16,1536]{1,0:T(8,128)S(1)}, f32[16,1536]{1,0:T(8,128)S(1)}, u32[]{:S(2)}, u32[]{:S(2)}) collective-permute-start(f32[16,1536]{1,0:T(8,128)S(1)} %fusion.134), channel_id=1, source_target_pairs={{0,4},{2,6},{4,0},{6,2},{8,12},{10,14},{12,8},{14,10},{16,20},{18,... | collective-permute-start | bytes 294920 | tf_op jit(solution)/shard_map/ppermute | solution.py:407
  662.8 107.6 %collective-permute-start.84 = (f32[3288]{0:T(1024)S(1)}, f32[3288]{0:T(1024)S(1)}, u32[]{:S(2)}, u32[]{:S(2)}) collective-permute-start(f32[3288]{0:T(1024)S(1)} %concatenate.285), channel_id=1, source_target_pairs={{0,2},{2,0},{4,6},{6,4},{8,10},{10,8},{12,14},{14,12},{16,18},{18,... | collective-permute-start | bytes 39464 | tf_op jit(solution)/shard_map/ppermute | solution.py:407
  774.3 134.1 %collective-permute-start.86 = (f32[3288]{0:T(1024)S(1)}, f32[3288]{0:T(1024)S(1)}, u32[]{:S(2)}, u32[]{:S(2)}) collective-permute-start(f32[3288]{0:T(1024)S(1)} %add.550), channel_id=1, source_target_pairs={{0,8},{2,10},{4,12},{6,14},{8,0},{10,2},{12,4},{14,6},{16,24},{18,... | collective-permute-start | bytes 39464 | tf_op jit(solution)/shard_map/ppermute | solution.py:407
  794.6 69.2 %collective-permute-start.49 = (bf16[2,96,4096]{2,1,0:T(8,128)(2,1)S(1)}, bf16[2,96,4096]{2,1,0:T(8,128)(2,1)S(1)}, u32[]{:S(2)}, u32[]{:S(2)}) collective-permute-start(bf16[2,96,4096]{2,1,0:T(8,128)(2,1)S(1)} %fusion.34), channel_id=1, source_target_pairs={{0,8},{2,10},{4,12},{6,14},{8,0},{10,2},{12,4},{14,6},{16,24},{18,... | collective-permute-start | bytes 4718600 | tf_op jit(solution)/shard_map/ppermute | solution.py:407
  796.6 68.9 %collective-permute-start.54 = (bf16[1,128,1536]{2,1,0:T(8,128)(2,1)S(1)}, bf16[1,128,1536]{2,1,0:T(8,128)(2,1)S(1)}, u32[]{:S(2)}, u32[]{:S(2)}) collective-permute-start(bf16[1,128,1536]{2,1,0:T(8,128)(2,1)S(1)} %dynamic-slice_convert_fusion.2), channel_id=1, source_target_pairs={{0,16},{2,18},{4,20},{6,22},{8,24},{10,26},{12,28},{14,30},{16,0},... | collective-permute-start | bytes 1179656 | tf_op jit(solution)/shard_map/ppermute | solution.py:407
  (189 other events, 2854.2 us)
Sparse Core Ops, SparseCore 0:
  10.9 82.0 all-gather.4
  95.8 45.3 all-gather.6
  144.0 130.4 all-gather.8
  276.6 74.6 all-gather.10

commit v3 on v2

--- a/solution.py
+++ b/solution.py
@@ -31,9 +31,10 @@
 LANES = 128
 EDGE = 128
 PACK = 16
-PIECES = 14
+WIDE = 256
+PIECES = 13
 MASKED = -1e30
-VMEM = 48 * 1024 * 1024
+MIB = 1024 * 1024
 
 bf16 = jnp.bfloat16
 f32 = jnp.float32
@@ -296,14 +297,12 @@
     for slot in range(PIECES):
         q_ref, at = q_views[slot]
         rows = q_ref.shape[1]
-        first = tok - EDGE if slot == PIECES - 2 else 0
-
         @pl.when(flag_ref[slot] > 0)
-        def _(slot=slot, q_ref=q_ref, at=at, rows=rows, first=first):
+        def _(slot=slot, q_ref=q_ref, at=at, rows=rows):
             query = q_ref[at]
             d_self = g_views[slot][0][at]
-            lse = joined(q_tables[slot][0][at], tok)[:, first : first + rows]
-            delta = joined(g_tables[slot][0][at], tok)[:, first : first + rows]
+            lse = joined(q_tables[slot][0][at], tok)[:, :rows]
+            delta = joined(g_tables[slot][0][at], tok)[:, :rows]
             same = own_ids == ids_ref[slot : slot + 1, :rows]
             scores = mm(k_two, query, 1, 1)
             d_weights = mm(v_two, d_self, 1, 1)
@@ -332,18 +331,34 @@
             out_ref[:, at * LANES : (at + 1) * LANES] = lines_ref[pl.ds(at, rows, stride=per_row), :].astype(bf16)
 
 
-def flatten_kernel(*refs):
-    *grad_refs, lines_ref, square_ref = refs
-    offset = 0
-    square = jnp.zeros((1, LANES), f32)
-    for ref in grad_refs:
-        rows, columns = ref.shape
+def pack_kernel(tables, *refs):
+    *lines_refs, out_ref = refs
+    top = 0
+    for (rows, columns), lines_ref in zip(tables, lines_refs):
         per_row = columns // LANES
         for at in range(per_row):
+            row = top + at // (WIDE // LANES) * rows
+            lane = at % (WIDE // LANES) * LANES
+            out_ref[row : row + rows, lane : lane + LANES] = lines_ref[pl.ds(at, rows, stride=per_row), :].astype(bf16)
+        top += columns // WIDE * rows
+
+
+def unpack_kernel(tables, block_ref, *out_refs):
+    top = 0
+    for (rows, columns), out_ref in zip(tables, out_refs):
+        for at in range(columns // WIDE):
+            out_ref[:, at * WIDE : (at + 1) * WIDE] = block_ref[0, top : top + rows, :]
+            top += rows
+
+
+def flatten_kernel(places, *refs):
+    *grad_refs, lines_ref, square_ref = refs
+    square = jnp.zeros((1, LANES), f32)
+    for (start, column, columns), ref in zip(places, grad_refs):
+        for at in range(ref.shape[1] // LANES):
             part = ref[:, at * LANES : (at + 1) * LANES]
-            lines_ref[pl.ds(offset + at, rows, stride=per_row), :] = part
+            lines_ref[pl.ds(start + column // LANES + at, ref.shape[0], stride=columns // LANES), :] = part
             square = square + jnp.sum(part * part, axis=0, keepdims=True)
-        offset += rows * per_row
     square_ref[...] = square
 
 
@@ -369,14 +384,14 @@
     return (first_new, second_new, weight_new, moving_new)
 
 
-def call(kernel, grid, in_specs, out_specs, out_shape, args, scratch=(), prefetch=0, flops=0, moved=0):
+def call(kernel, grid, in_specs, out_specs, out_shape, args, scratch=(), prefetch=0, flops=0, moved=0, vmem=16):
     return pl.pallas_call(
         kernel,
         grid_spec=pltpu.PrefetchScalarGridSpec(
             num_scalar_prefetch=prefetch, grid=grid, in_specs=in_specs, out_specs=out_specs, scratch_shapes=scratch
         ),
         out_shape=out_shape,
-        compiler_params=pltpu.CompilerParams(dimension_semantics=("arbitrary",) * len(grid), vmem_limit_bytes=VMEM),
+        compiler_params=pltpu.CompilerParams(dimension_semantics=("arbitrary",) * len(grid), vmem_limit_bytes=vmem * MIB),
         cost_estimate=pl.CostEstimate(flops=flops, bytes_accessed=moved, transcendentals=0),
     )(*args)
 
@@ -409,17 +424,6 @@
 
 def other_txt(x):
     return lax.ppermute(x, "txt", [(0, 1), (1, 0)])
-
-
-def neighbourhood(x, low_edge, high_edge):
-    beside = crossed(x, 1)
-    across = crossed(x, 2)
-    above, below = shifted(x, 4), shifted(x, -4)
-    low, high = shifted(low_edge, -5), shifted(high_edge, 5)
-    above_across, below_across = shifted(across, 4), shifted(across, -4)
-    three = crossed(jnp.concatenate([across, above, below], axis=0), 1)
-    two = crossed(jnp.concatenate([above_across, below_across], axis=0), 1)
-    return [x, beside, across, above, below, three, above_across, below_across, two, low, high]
 
 
 def index_bits(count):
@@ -439,63 +443,157 @@
     return x + other_txt(x)
 
 
-def own_and_other(x, bit):
+def own_and_other(x, bit, below=1):
     mine = (lax.axis_index("img") >> bit) & 1
-    split = x.reshape(x.shape[0] // 2, 2, *x.shape[1:])
+    split = x.reshape(x.shape[0] // (2 * below), 2, below, *x.shape[1:])
     own = lax.dynamic_index_in_dim(split, mine, 1, keepdims=False)
     other = lax.dynamic_index_in_dim(split, 1 - mine, 1, keepdims=False)
-    return own, other
-
-
-def halved(x, bit, sent_as):
-    own, other = own_and_other(x, bit)
-    return own + crossed(other.astype(sent_as), 1 << bit).astype(f32)
-
-
-def scatter_sum(x, sent_as):
+    return own.reshape(-1, *x.shape[1:]), other.reshape(-1, *x.shape[1:])
+
+
+class TermSum:
+    def __init__(self, clock, terms, order):
+        count = lax.axis_size("img")
+        self.clock, self.order, self.level = clock, order, 0
+        self.keep = clock.stage(terms).reshape(count, terms.shape[0] // count, terms.shape[1])
+        self.send()
+
+    def send(self):
+        bit = self.order[self.level]
+        below = 1 << sum(other < bit for other in self.order[self.level :])
+        self.keep, self.sent = own_and_other(self.keep, bit, below)
+        self.clock.mark(self.sent)
+
+    def advance(self):
+        got = self.clock.stage(crossed(self.sent, 1 << self.order[self.level]))
+        self.keep = self.keep + got
+        self.level += 1
+        if self.level == len(self.order):
+            self.clock.mark(self.keep)
+            return self.keep[0]
+        self.send()
+
+    def finish(self):
+        while True:
+            result = self.advance()
+            if result is not None:
+                return result
+
+
+def gather_doubling(x):
+    x = x[None]
+    for bit in reversed(range(index_bits(lax.axis_size("img")))):
+        x = doubled(x, bit)
+    return x.reshape(-1, x.shape[-1])
+
+
+def doubled(x, bit):
+    mine = (lax.axis_index("img") >> bit) & 1
+    got = crossed(x, 1 << bit)
+    both = jnp.where(mine == 0, jnp.stack([x, got], 1), jnp.stack([got, x], 1))
+    return both.reshape(-1, *x.shape[1:])
+
+
+def tie(x, *others):
+    return lax.optimization_barrier((x, others))[0]
+
+
+def tall(left):
     count = lax.axis_size("img")
-    x = x.reshape(count, x.shape[0] // count, x.shape[1])
-    for bit in range(index_bits(count)):
-        x = halved(x, bit, sent_as)
-    return x[0]
-
-
-def gather_doubling(x):
-    for axis, bit in enumerate(reversed(range(index_bits(lax.axis_size("img"))))):
-        mine = (lax.axis_index("img") >> bit) & 1
-        got = crossed(x, 1 << bit)
-        x = jnp.where(mine == 0, jnp.stack([x, got], axis), jnp.stack([got, x], axis))
-    return x.reshape(-1, x.shape[-1])
-
-
-def weight_gradient(left, right):
-    count = lax.axis_size("img")
-    bits = index_bits(count)
-    tall = left.T.reshape(count, left.shape[1] // count, left.shape[0])
-    rows, width = tall.shape[1], right.shape[1]
-
-    def terms(chunks):
-        return mm(chunks.reshape(-1, chunks.shape[2]), right, 1, 0).reshape(chunks.shape[0], rows, width)
-
-    own, other = own_and_other(tall, 0)
-    got = crossed(terms(other).astype(bf16), 1)
-    own, other = own_and_other(own, 1)
-    got_own, got_other = own_and_other(got, 1)
-    got = crossed((terms(other) + got_other.astype(f32)).astype(bf16), 2)
-    total = terms(own) + got_own.astype(f32) + got.astype(f32)
-    for bit in range(2, bits):
-        total = halved(total, bit, bf16)
-    return total[0]
-
-
-PIECE_COUNTS = (1, 1, 1, 1, 1, 3, 1, 1, 2, 1, 1)
+    return left.T.reshape(count, left.shape[1] // count, left.shape[0])
+
+
+class Clock:
+    def __init__(self):
+        self.token = ()
+
+    def stage(self, *arrays):
+        arrays, _ = lax.optimization_barrier((arrays, self.token))
+        return arrays if len(arrays) > 1 else arrays[0]
+
+    def mark(self, *arrays):
+        self.token = arrays
+
+
+class GradientSum:
+    def __init__(self, clock, left, right):
+        bits = index_bits(left.shape[0])
+        self.order = list(range(bits))
+        self.level = 0
+        self.clock = clock
+        left, self.right = clock.stage(left, right)
+        self.own, other = own_and_other(left, 0)
+        self.sent = self.terms(other).astype(bf16)
+        clock.mark(self.sent)
+
+    def terms(self, chunks):
+        product = mm(chunks.reshape(-1, chunks.shape[2]), self.right, 1, 0)
+        return product.reshape(chunks.shape[0], chunks.shape[1], self.right.shape[1])
+
+    def receive(self):
+        self.got = self.clock.stage(crossed(self.sent, 1 << self.order[self.level]))
+        self.clock.mark(self.got)
+        self.level += 1
+
+    def advance(self, received=False):
+        if not received:
+            self.receive()
+        got = self.clock.stage(self.got)
+        if self.level == len(self.order):
+            return (self.keep + got.astype(f32))[0]
+        bit = self.order[self.level]
+        if self.level == 1:
+            own, other = own_and_other(self.own, bit)
+            got_own, got_other = own_and_other(got, bit)
+            self.sent = (self.terms(other) + got_other.astype(f32)).astype(bf16)
+            self.keep = self.terms(own) + got_own.astype(f32)
+        else:
+            own, other = own_and_other(self.keep + got.astype(f32), bit)
+            self.sent, self.keep = other.astype(bf16), own
+        self.clock.mark(self.sent)
+        return self.sent
+
+
+class Neighbourhood:
+    def __init__(self, clock, x, end, beginning):
+        count = lax.axis_size("img")
+        self.clock = clock
+        self.x = x
+        self.across = crossed(x, 2)
+        self.above, self.below = shifted(x, 4), shifted(x, -4)
+        edge = jnp.where(lax.axis_index("img") % 4 == 3, end, beginning)
+        pairs_low = [(i - 5, i) for i in range(0, count, 4) if i >= 5]
+        pairs_high = [(i + 5, i) for i in range(3, count, 4) if i + 5 < count]
+        self.edge = lax.ppermute(edge, "img", pairs_low + pairs_high)
+
+    def second(self):
+        across, above, below = self.clock.stage(self.across, self.above, self.below)
+        self.across, self.above, self.below = across, above, below
+        self.four_sent = jnp.concatenate([self.x, across, above, below], axis=0)
+        self.above_across, self.below_across = shifted(across, 4), shifted(across, -4)
+        self.clock.mark(self.four_sent)
+
+    def third(self):
+        four = crossed(self.four_sent, 1)
+        self.above_across, self.below_across, self.four, self.edge = self.clock.stage(
+            self.above_across, self.below_across, four, self.edge
+        )
+        self.two_sent = jnp.concatenate([self.above_across, self.below_across], axis=0)
+        self.clock.mark(self.two_sent)
+
+    def collect(self):
+        two = self.clock.stage(crossed(self.two_sent, 1))
+        self.clock.mark(two)
+        return [self.x, self.across, self.above, self.below, self.four, self.above_across, self.below_across, two, self.edge]
+
+
+PIECE_COUNTS = (1, 1, 1, 1, 4, 1, 1, 2, 1)
 
 
 def neighbour_indices(i):
     b = i ^ 1
-    return [
-        i, b, i ^ 2, i + 4, i - 4, b ^ 2, b + 4, b - 4, (i ^ 2) + 4, (i ^ 2) - 4, (b ^ 2) + 4, (b ^ 2) - 4, i - 5, i + 5
-    ]
+    edge = jnp.where(i % 4 == 0, i - 5, i + 5)
+    return [i, i ^ 2, i + 4, i - 4, b, b ^ 2, b + 4, b - 4, (i ^ 2) + 4, (i ^ 2) - 4, (b ^ 2) + 4, (b ^ 2) - 4, edge]
 
 
 def token_places(row_index, image_sides):
@@ -571,17 +669,39 @@
         return pl.pallas_call(
             functools.partial(unflatten_kernel, shapes),
             out_shape=[shape_of(s, bf16) for s in shapes],
-            compiler_params=pltpu.CompilerParams(vmem_limit_bytes=VMEM),
+            compiler_params=pltpu.CompilerParams(vmem_limit_bytes=32 * MIB),
         )(*(master_lines[starts[w] : starts[w + 1]] for w in which))
-
-    (own_project,) = own_rows(2)
-    own_modulate, own_text = own_rows(5, 3)
-    own_updown, own_down, own_output = own_rows(0, 1, 4)
 
     def gather(rows):
         return lax.all_gather(rows, "img", axis=0, tiled=True)
 
-    w_project = gather(own_project)
+    together = [0, 1, 4, 2]
+    shapes = [tables[w] for w in together]
+    heights = [rows * columns // WIDE for rows, columns in shapes]
+    if all(rows % 16 == 0 for rows, _ in shapes) and sum(heights[:3]) % heights[3] == 0:
+        block = pl.pallas_call(
+            functools.partial(pack_kernel, shapes),
+            out_shape=shape_of((sum(heights), WIDE), bf16),
+            compiler_params=pltpu.CompilerParams(vmem_limit_bytes=32 * MIB),
+        )(*(master_lines[starts[w] : starts[w + 1]] for w in together))
+        blocks = gather(block[None])
+
+        def unpack(which, height, at, gathered):
+            return call(
+                functools.partial(unpack_kernel, which),
+                (n_img,),
+                [pl.BlockSpec((1, height, WIDE), lambda i: (i, at, 0))],
+                [pl.BlockSpec(shape, lambda i: (i, 0)) for shape in which],
+                [shape_of((n_img * rows, columns), bf16) for rows, columns in which],
+                (gathered,),
+                vmem=52,
+            )
+
+    else:
+        blocks = None
+        w_project = gather(own_rows(2)[0])
+    (own_modulate,) = own_rows(5)
+    (own_text,) = own_rows(3)
 
     gain_attn = small_master[:D]
     gain_ffn = small_master[D : 2 * D]
@@ -598,8 +718,12 @@
     cond_rows = COND // n_img
     cond_own = lax.dynamic_slice_in_dim(conditions, img_index * cond_rows, cond_rows, 1)
     silu_own = jax.nn.silu(cond_own.astype(f32)).astype(bf16)
-    mod_half = sum_over_img(jnp.dot(silu_own, own_modulate, preferred_element_type=f32)).astype(bf16)
-    mods = lax.all_gather(mod_half.reshape(samples, 6, half_d), "txt", axis=2, tiled=True)
+    mod_sum = sum_over_img(jnp.dot(silu_own, own_modulate, preferred_element_type=f32))
+    mod_half = mod_sum.astype(bf16)
+    mod_other = other_txt(mod_half)
+    mods = jnp.where(
+        txt_index == 0, jnp.stack([mod_half, mod_other], 0), jnp.stack([mod_other, mod_half], 0)
+    ).reshape(n_txt, samples, 6, half_d).transpose(1, 2, 0, 3)
 
     row_index = img_index * tok + jnp.arange(tok, dtype=jnp.int32)
     sample_ids, row_pos, col_pos, sample_ends = token_places(row_index, image_sides)
@@ -614,11 +738,11 @@
     place = img_index % 4
     inside = (pieces >= 0) & (pieces < n_img)
     slots = jnp.arange(PIECES)
-    inside &= (slots != PIECES - 2) | (place == 0)
-    inside &= (slots != PIECES - 1) | (place == 3)
+    inside &= (slots != PIECES - 1) | (place == 0) | (place == 3)
     column = jnp.arange(tok, dtype=jnp.int32)[None, :]
-    piece_rows = pieces[:, None] * tok + column + jnp.where(slots == PIECES - 2, tok - EDGE, 0)[:, None]
-    there = inside[:, None] & ((slots[:, None] < PIECES - 2) | (column < EDGE))
+    edge_start = jnp.where((slots == PIECES - 1) & (place == 0), tok - EDGE, 0)
+    piece_rows = pieces[:, None] * tok + column + edge_start[:, None]
+    there = inside[:, None] & ((slots[:, None] < PIECES - 1) | (column < EDGE))
     piece_ids = jnp.where(there, ids_of(piece_rows, sample_ends), -1)
     flags = jnp.any((piece_ids >= sample_ids[0]) & (piece_ids <= sample_ids[-1]), axis=1).astype(jnp.int32)
     piece_ids = jnp.concatenate([piece_ids, jnp.full((16 - PIECES, tok), -1, jnp.int32)], axis=0)
@@ -627,7 +751,8 @@
     text_rows = text_states.shape[0]
     text_len = text_rows * n_img
     text_columns = lax.all_to_all(text_states, "img", split_axis=1, concat_axis=0, tiled=True)
-    text_proj = scatter_sum(jnp.dot(text_columns, own_text, preferred_element_type=f32), f32)
+    z_first = [0] + list(range(2, index_bits(n_img))) + [1]
+    text_proj = TermSum(Clock(), jnp.dot(text_columns, own_text, preferred_element_type=f32), z_first).finish()
     text_shape = (text_rows, local_heads, HD)
     text_raw = text_proj[:, :half_d].reshape(text_shape)
     text_normed = rms_norm(text_raw)
@@ -635,6 +760,9 @@
     text_low = jnp.concatenate([text_key_low, text_proj[:, half_d:].astype(bf16)], axis=1)
     all_text = gather_doubling(text_low)
 
+    if blocks is not None:
+        blocks = tie(blocks, all_text, per_token, cosine, sine, flags, piece_ids)
+        (w_project,) = unpack(shapes[3:], heights[3], sum(heights[:3]) // heights[3], blocks)
     x_float = tokens.astype(f32)
     x_normed = rms_norm(x_float)
     normed_one = x_normed * gain_attn
@@ -655,17 +783,22 @@
         flops=2 * tok * D * 3 * half_d,
         moved=2 * D * 3 * half_d,
     )
-    kv_pieces = neighbourhood(own_kv, own_kv[:, tok - EDGE :], own_kv[:, :EDGE])
-
-    w_output = gather(own_output)
-    w_updown = gather(own_updown)
-    w_down = gather(own_down)
+    clock = Clock()
+    clock.mark(own_kv)
+    kv_near = Neighbourhood(clock, own_kv, own_kv[:, tok - EDGE :], own_kv[:, :EDGE])
+    if blocks is None:
+        w_updown, w_down, w_output = (gather(tie(rows, own_kv)) for rows in own_rows(0, 1, 4))
+    else:
+        w_updown, w_down, w_output = unpack(shapes[:3], sum(heights[:3]), 0, clock.stage(blocks))
     w_output_other = other_txt(w_output)
+    clock.mark(w_updown)
+    kv_near.second()
+    kv_near.third()
+    kv_pieces = kv_near.collect()
 
     kv_specs = [pairs(2 * c, a.shape[1]) for c, a in zip(PIECE_COUNTS, kv_pieces)]
     id_specs = [whole((tok, 1)), whole((16, tok))]
     text_specs = [pair(text_len), pair(text_len, n_pairs)]
-    attention_flops = 2 * 2 * tok * 12 * tok * half_d
     mixed_low, self_out, cross_out, lse_self, lse_cross, query_pack = call(
         functools.partial(attend_kernel, PIECE_COUNTS, tok),
         (n_pairs,),
@@ -674,7 +807,7 @@
         [shape_of((tok, half_d), bf16)]
         + [shape_of((tok, half_d), f32)] * 4
         + [shape_of((1, tok + PACK, half_d), bf16)],
-        (flags, queries, own_ids, piece_ids, all_text, all_text, gate_lanes, *kv_pieces),
+        (flags, clock.stage(queries), own_ids, piece_ids, all_text, all_text, gate_lanes, *kv_pieces),
         scratch=[
             pltpu.VMEM((PIECES, 2 * tok, tok), f32),
             pltpu.VMEM((2 * tok, LANES), f32),
@@ -683,20 +816,24 @@
             pltpu.VMEM((PACK, tok), f32),
         ],
         prefetch=1,
-        flops=attention_flops,
-        moved=13 * 4 * tok * half_d,
+        vmem=32,
     )
 
     def pack_edges(pack):
         table = pack[:, tok:]
+        ending = jnp.concatenate(
+            [table[:, :, part * tok + tok - EDGE : (part + 1) * tok] for part in range(3) for _ in range(tok // EDGE)],
+            axis=2,
+        )
         return (
-            jnp.concatenate([pack[:, tok - EDGE : tok], table], axis=1),
+            jnp.concatenate([pack[:, tok - EDGE : tok], ending], axis=1),
             jnp.concatenate([pack[:, :EDGE], table], axis=1),
         )
 
-    query_pieces = neighbourhood(query_pack, *pack_edges(query_pack))
-
+    clock.mark(mixed_low)
     mixed_other = other_txt(mixed_low)
+    query_near = Neighbourhood(clock, query_pack, *pack_edges(query_pack))
+    mixed_other, mixed_low = clock.stage(mixed_other, mixed_low)
     attn_out = jnp.dot(mixed_low, w_output, preferred_element_type=f32) + jnp.dot(
         mixed_other, w_output_other, preferred_element_type=f32
     )
@@ -704,33 +841,44 @@
     h_normed = rms_norm(hidden)
     normed_two = h_normed * gain_ffn
     ffn_in = (normed_two * (1.0 + scale_two) + shift_two).astype(bf16)
+    clock.mark(ffn_in)
+    query_near.second()
+    ffn_in = clock.stage(ffn_in)
     gate_up = jnp.dot(ffn_in, w_updown, preferred_element_type=f32)
     gate, up = gate_up[:, :half_ff], gate_up[:, half_ff:]
     sigmoid = jax.nn.sigmoid(gate)
     activated = gate * sigmoid
     hidden_units = (activated * up).astype(bf16)
-    branch_part = jnp.dot(hidden_units, w_down, preferred_element_type=f32)
-    branch = branch_part + other_txt(branch_part)
-    block_out = hidden + gate_two * branch
+    clock.mark(hidden_units)
+    query_near.third()
 
     d_out = cotangent.astype(f32)
-    d_gate_two = d_out * branch
     d_branch = (d_out * gate_two).astype(bf16)
-    d_units = mm(d_branch, w_down, 1, 1)
-    d_gate = d_units * up * sigmoid * (1.0 + gate * (1.0 - sigmoid))
-    d_up = d_units * activated
-    d_gate_up = jnp.concatenate([d_gate.astype(bf16), d_up.astype(bf16)], axis=1)
+    down_sum = GradientSum(clock, tall(hidden_units), d_branch)
+    query_pieces = query_near.collect()
+    d_units = mm(clock.stage(d_branch), w_down, 1, 1)
+    d_gate = (d_units * up * sigmoid * (1.0 + gate * (1.0 - sigmoid))).astype(bf16)
+    d_up = (d_units * activated).astype(bf16)
+    d_gate_up = jnp.concatenate([d_gate, d_up], axis=1)
+    clock.mark(d_gate_up)
+    down_sum.advance()
+    d_gate_up = clock.stage(d_gate_up)
     d_ffn_part = mm(d_gate_up, w_updown, 1, 1).astype(bf16)
-    d_ffn_in = d_ffn_part.astype(f32) + other_txt(d_ffn_part).astype(f32)
-    grad_down = weight_gradient(hidden_units, d_branch)
-    grad_updown = weight_gradient(ffn_in, d_gate_up)
-
+    clock.mark(d_ffn_part)
+    d_ffn_other = other_txt(d_ffn_part)
+    ffn_tall = tall(ffn_in)
+    gate_sum = GradientSum(clock, ffn_tall, d_gate)
+    up_sum = GradientSum(clock, ffn_tall, d_up)
+    gate_sum.receive()
+    up_sum.receive()
+    d_ffn_part, d_ffn_other = clock.stage(d_ffn_part, d_ffn_other)
+    d_ffn_in = d_ffn_part.astype(f32) + d_ffn_other.astype(f32)
     d_scale_two = d_ffn_in * normed_two
     d_normed_two = d_ffn_in * (1.0 + scale_two)
     d_gain_ffn = jnp.sum(d_normed_two * h_normed, axis=0)
     d_hidden = d_out + rms_back(hidden, d_normed_two * gain_ffn)
-    d_gate_one = d_hidden * attn_out
     d_attn = (d_hidden * gate_one).astype(bf16)
+    clock.mark(d_attn)
     grad_pack, d_cross_low, d_gate_lanes = call(
         functools.partial(mixed_back_kernel, tok),
         (n_pairs,),
@@ -741,42 +889,69 @@
             shape_of((tok, half_d), bf16),
             shape_of((1, half_d), f32),
         ],
-        (d_attn, w_output, self_out, cross_out, gate_lanes),
+        (clock.stage(d_attn), w_output, self_out, cross_out, gate_lanes),
         scratch=[pltpu.VMEM((PACK, tok), f32)],
         flops=2 * tok * D * half_d,
         moved=4 * D * half_d,
     )
-    grad_pieces = neighbourhood(grad_pack, *pack_edges(grad_pack))
-    grad_output = weight_gradient(mixed_low, d_attn)
-
+    clock.mark(grad_pack)
+    grad_near = Neighbourhood(clock, grad_pack, *pack_edges(grad_pack))
+    down_sum.receive()
+    gate_sum.advance(received=True)
+    grad_near.second()
+    down_sum.advance(received=True)
     turn_specs = [whole((1, LANES)), whole((tok, LANES)), whole((tok, LANES))]
-    d_query_raw, d_gain_query, d_text_key, d_text_value = call(
-        functools.partial(query_back_kernel, PIECE_COUNTS, tok),
-        (n_pairs,),
-        [pair(tok)]
-        + id_specs
-        + text_specs
-        + [pairs(1, tok), pair(tok)]
-        + [pair(tok)] * 4
-        + [pairs(1, tok)]
-        + turn_specs
-        + kv_specs,
-        [pair(tok), pair(1), pair(text_len), pair(text_len)],
-        [
-            shape_of((tok, half_d), bf16),
-            shape_of((1, half_d), f32),
-            shape_of((text_len, half_d), f32),
-            shape_of((text_len, half_d), f32),
-        ],
-        (
-            flags, queries, own_ids, piece_ids, all_text, all_text, grad_pack, d_cross_low,
-            self_out, cross_out, lse_self, lse_cross, raw_qk, gain_query_pair, cosine, sine, *kv_pieces,
-        ),
-        scratch=[pltpu.VMEM((2 * tok, LANES), f32)],
-        prefetch=1,
-        flops=attention_flops * 3 // 2,
-        moved=13 * 4 * tok * half_d,
-    )
+
+    def query_back(first, count, d_cross):
+        def at(rows, also=0):
+            return pair(rows, first + also)
+
+        def some(arrays, rows, index=0):
+            return pl.BlockSpec((arrays, rows, LANES), lambda j, *_: (index, 0, first + j))
+
+        return call(
+            functools.partial(query_back_kernel, PIECE_COUNTS, tok),
+            (count,),
+            [at(tok)]
+            + id_specs
+            + [at(text_len), at(text_len, n_pairs)]
+            + [some(1, tok), at(tok)]
+            + [at(tok)] * 4
+            + [some(1, tok)]
+            + turn_specs
+            + [some(2 * c, a.shape[1]) for c, a in zip(PIECE_COUNTS, kv_pieces)],
+            [pair(tok), pair(1), pair(text_len), pair(text_len)],
+            [
+                shape_of((tok, count * LANES), bf16),
+                shape_of((1, count * LANES), f32),
+                shape_of((text_len, count * LANES), f32),
+                shape_of((text_len, count * LANES), f32),
+            ],
+            (
+                flags, queries, own_ids, piece_ids, all_text, all_text, grad_pack, d_cross,
+                self_out, cross_out, lse_self, lse_cross, raw_qk, gain_query_pair, cosine, sine, *kv_pieces,
+            ),
+            scratch=[pltpu.VMEM((2 * tok, LANES), f32)],
+            prefetch=1,
+        )
+
+    head_half = n_pairs // 2
+    first_half = query_back(0, head_half, clock.stage(d_cross_low))
+    clock.mark(first_half[0])
+    grad_near.third()
+    up_sum.advance(received=True)
+    output_sum = GradientSum(clock, tall(mixed_low), d_attn)
+    grad_pieces = grad_near.collect()
+    second_half = query_back(head_half, n_pairs - head_half, clock.stage(d_cross_low))
+    clock.mark(second_half[0])
+    d_query_raw, d_gain_query, d_text_key, d_text_value = (
+        jnp.concatenate(halves, axis=1) for halves in zip(first_half, second_half)
+    )
+    gate_sum.advance()
+    text_sum = TermSum(clock, jnp.concatenate([d_text_key, d_text_value], axis=1), z_first)
+    down_sum.advance()
+    text_sum.advance()
+    attn_tall = tall(attn_in)
 
     def pack_specs(arrays):
         views = [pairs(c, a.shape[1] - PACK) for c, a in zip(PIECE_COUNTS, arrays)]
@@ -802,20 +977,36 @@
             shape_of((tok, half_d), bf16),
         ],
         (
-            flags, own_kv, own_ids, piece_ids, raw_qk, gain_key_pair, cosine, sine,
-            *query_pieces, *query_pieces, *grad_pieces, *grad_pieces,
+            flags, clock.stage(own_kv), own_ids, piece_ids, raw_qk, gain_key_pair,
+            cosine, sine, *query_pieces, *query_pieces, *grad_pieces, *grad_pieces,
         ),
         scratch=[pltpu.VMEM((2 * tok, LANES), f32)] * 2,
         prefetch=1,
-        flops=attention_flops * 2,
-        moved=13 * 4 * tok * half_d,
-    )
+    )
+    clock.mark(d_value)
+    query_sum = GradientSum(clock, attn_tall, d_query_raw)
+    key_value_sum = GradientSum(clock, attn_tall, jnp.concatenate([d_key_raw, d_value], axis=1))
+    d_query_raw, d_key_raw, d_value = clock.stage(d_query_raw, d_key_raw, d_value)
     d_projected = jnp.concatenate([d_query_raw, d_key_raw, d_value], axis=1)
-    grad_project = weight_gradient(attn_in, d_projected)
-    d_attn_part = mm(d_projected, w_project, 1, 1)
-    d_attn_in = d_attn_part + other_txt(d_attn_part)
-
-    text_own = scatter_sum(jnp.concatenate([d_text_key, d_text_value], axis=1), f32)
+    d_attn_part = mm(d_projected, w_project, 1, 1).astype(bf16)
+    clock.mark(d_attn_part)
+    d_attn_other = other_txt(d_attn_part)
+    output_sum.advance()
+    query_sum.advance()
+    text_sum.advance()
+    up_sum.advance()
+    key_value_sum.advance()
+    gate_sum.advance()
+    branch_part = jnp.dot(clock.stage(hidden_units), w_down, preferred_element_type=f32)
+    clock.mark(branch_part)
+    d_attn_other = clock.stage(d_attn_other)
+    d_attn_in = d_attn_part.astype(f32) + d_attn_other.astype(f32)
+    branch = branch_part + other_txt(branch_part)
+    block_out = hidden + gate_two * branch
+    d_gate_two = d_out * branch
+    d_gate_one = d_hidden * attn_out
+
+    text_own = text_sum.finish()
     d_text_scaled = text_own[:, :half_d].reshape(text_shape)
     d_gain_text = jnp.sum(d_text_scaled * text_normed, axis=(0, 1))
     d_text_raw = rms_back(text_raw, d_text_scaled * gain_text).reshape(text_rows, half_d)
@@ -833,19 +1024,9 @@
         summed = lax.dot_general(one_hot_wide, values, (((0,), (0,)), ((), ())), precision=HIGH)
         return lax.dynamic_slice_in_dim(summed, txt_index * half_d, half_d, 1)
 
-    d_mod_early = sum_over_img(
-        jnp.concatenate([by_sample(v) for v in (d_gate_one, d_ffn_in, d_scale_two, d_gate_two)], axis=1)
-    )
-    d_mod_late = sum_over_img(jnp.concatenate([by_sample(v) for v in (d_attn_in, d_scale_one)], axis=1))
-    d_mod = jnp.concatenate([d_mod_late, d_mod_early], axis=1)
-    grad_modulate = lax.dot_general(silu_own.astype(f32), d_mod, (((0,), (0,)), ((), ())), precision=HIGH)
-
-    grads = [grad_updown, grad_down, grad_project, grad_text, grad_output, grad_modulate]
-    reduced, squares = pl.pallas_call(
-        flatten_kernel,
-        out_shape=[shape_of((lines, LANES), f32), shape_of((1, LANES), f32)],
-        compiler_params=pltpu.CompilerParams(vmem_limit_bytes=VMEM),
-    )(*grads)
+    d_mod = jnp.concatenate(
+        [by_sample(v) for v in (d_attn_in, d_scale_one, d_gate_one, d_ffn_in, d_scale_two, d_gate_two)], axis=1
+    )
 
     replica = (txt_index == 0).astype(f32)
     d_gate_local = jnp.sum(d_gate_lanes.reshape(local_heads, HD), axis=1) * (1.0 - tanh_gate**2)
@@ -856,16 +1037,50 @@
             d_gain_ffn * replica,
             jnp.sum(d_gain_query.reshape(local_heads, HD), axis=0),
             jnp.sum(d_gain_key.reshape(local_heads, HD), axis=0),
-            d_gain_text,
+            jnp.zeros((HD,), f32),
             gate_full,
         ]
     )
-    small_grad = sum_over_all(small_terms)
-    square_big = jnp.sum(sum_over_all(squares))
-    grad_square = square_big + jnp.sum(small_grad * small_grad)
+    small_count = small_terms.shape[0]
+    small_row = jnp.pad(small_terms, (0, d_mod.shape[1] - small_count))[None]
+    sums = sum_over_img(jnp.concatenate([d_mod, small_row], axis=0))
+    d_mod = sums[:samples]
+    small_row = sums[samples:, :]
+    small_grad = (small_row + other_txt(small_row))[0, :small_count]
+    grad_modulate = lax.dot_general(silu_own.astype(f32), d_mod, (((0,), (0,)), ((), ())), precision=HIGH)
+
+    pending = [down_sum, gate_sum, output_sum, query_sum, up_sum, key_value_sum]
+    while pending:
+        for one in list(pending):
+            one.result = one.advance()
+            if one.level == len(one.order):
+                pending.remove(one)
+    grad_down, grad_gate, grad_output, grad_query, grad_up, grad_key_value = (
+        one.result for one in (down_sum, gate_sum, output_sum, query_sum, up_sum, key_value_sum)
+    )
+    grads = [grad_gate, grad_up, grad_down, grad_query, grad_key_value, grad_text, grad_output, grad_modulate]
+    places = [
+        (starts[0], 0, 2 * half_ff),
+        (starts[0], half_ff, 2 * half_ff),
+        (starts[1], 0, D),
+        (starts[2], 0, 3 * half_d),
+        (starts[2], half_d, 3 * half_d),
+        (starts[3], 0, 2 * half_d),
+        (starts[4], 0, D),
+        (starts[5], 0, 6 * half_d),
+    ]
+    reduced, squares = pl.pallas_call(
+        functools.partial(flatten_kernel, places),
+        out_shape=[shape_of((lines, LANES), f32), shape_of((1, LANES), f32)],
+        compiler_params=pltpu.CompilerParams(vmem_limit_bytes=32 * MIB),
+    )(*grads)
+
+    last = sum_over_all(jnp.concatenate([squares, jnp.pad(d_gain_text, (0, LANES - HD))[None]], axis=0))
+    small_grad = lax.dynamic_update_slice(small_grad, last[1, :HD], (2 * D + 2 * HD,))
+    grad_square = jnp.sum(last[0]) + jnp.sum(small_grad * small_grad)
     clip_factor = MAX_NORM / jnp.maximum(jnp.sqrt(grad_square), MAX_NORM)
 
-    block = math.gcd(lines, 1024)
+    block = math.gcd(lines, 512)
     line_spec = pl.BlockSpec((block, LANES), lambda i: (i, 0))
     as_lines = (lines, LANES)
     updated = call(
@@ -875,6 +1090,7 @@
         [line_spec] * 5,
         [shape_of(as_lines, f32)] * 4 + [shape_of(as_lines, bf16)],
         (clip_factor.reshape(1), reduced, *(a.reshape(as_lines) for a in (moment_one, moment_two, master, average))),
+        vmem=52,
         flops=20 * lines * LANES,
         moved=38 * lines * LANES,
     )

time: 976 us -> 860 us (0.88)
  waiting for transfers between devices: 482 us -> 294 us
  local copies, waits for them, and re-layouts: 52.6 us -> 97.3 us
  Pallas kernels: 115 us -> 150 us
    ppermute x64 -> x61, waiting for transfers between devices: 363 us -> 206 us  [crossed(): return lax.ppermute(x, 'img', [(i, i ^ bit) for i in range(count)])]
    ppermute x18 -> x12, waiting for transfers between devices: 101 us -> 16.2 us  [shifted(): lax.ppermute(x, 'img', [(i + by, i) for i in range(count) if 0 <= i + by...]
    all_gather x4 -> x1, waiting for transfers between devices: 0.03 us -> 55 us  [gather(): return lax.all_gather(rows, 'img', axis=0, tiled=True)]
    pallas_call x6 -> x9, Pallas kernels: 105 us -> 145 us  [call(): pl.pallas_call(kernel, grid_spec=pltpu.PrefetchScalarGridSpec(num_scalar_...]
    unnamed x242 -> x397, local copies, waits for them, and re-layouts: 15.1 us -> 50.3 us
    ppermute x18 -> x12, starting transfers between devices: 54.5 us -> 36.1 us  [shifted(): lax.ppermute(x, 'img', [(i + by, i) for i in range(count) if 0 <= i + by...]
    ppermute x64 -> x61, starting transfers between devices: 64.4 us -> 79.4 us  [crossed(): return lax.ppermute(x, 'img', [(i, i ^ bit) for i in range(count)])]
    concatenate x10 -> x6, other arithmetic: 14 us -> 0.49 us  [the longest x1 0.21 us: on_device(): d_gate_up = jnp.concatenate([d_gate, d_up], axis=1)]
  transfers between devices with their start and end apart: 94 -> 86, of which waited for: 37 -> 35; matrix products, arithmetic and copies ran while one was open for 18% -> 19% of each run, Pallas kernels for 9% -> 12%
where the time goes in v3:
time: 860 us; the launch traced here: 845 us
  waiting for transfers between devices  294 us (34%)
  Pallas kernels  150 us (17%)
  starting transfers between devices  134 us (16%)
  local copies, waits for them, and re-layouts  97.3 us (11%)
  matrix products  96.2 us (11%)
  other arithmetic  52.9 us (6%)
  between operations  20.1 us (2%)
    ppermute x61, waiting for transfers between devices, crossed(): return lax.ppermute(x, 'img', [(i, i ^ bit) for i in range(count)])  206 us
    pallas_call x9, Pallas kernels, call(): pl.pallas_call(kernel, grid_spec=pltpu.PrefetchScalarGridSpec(num_scalar_...  145 us
    ppermute x61, starting transfers between devices, crossed(): return lax.ppermute(x, 'img', [(i, i ^ bit) for i in range(count)])  79.4 us
    dot_general x22, matrix products, mm(): lax.dot_general(a, b, (((on_a,), (on_b,)), ((), ())), preferred_element_t...  64.1 us
    all_gather x1, waiting for transfers between devices, gather(): return lax.all_gather(rows, 'img', axis=0, tiled=True)  55 us
    unnamed x397, local copies, waits for them, and re-layouts  50.3 us
    ppermute x12, starting transfers between devices, shifted(): lax.ppermute(x, 'img', [(i + by, i) for i in range(count) if 0 <= i + by...  36.1 us
  transfers between devices with their start and end apart: 86, of which 35 were waited for; matrix products, arithmetic and copies ran while one was open for 19% of the time, Pallas kernels for 12%

profile of v3, /device:TPU:0, one launch (start us, length us, event | category | flops | bytes accessed | tf_op | source)
XLA Modules:
  0.0 845.1 jit_solution(11181062105134924523)
XLA Ops:
  39.5 13.5 %collective-permute-done.1 = f32[16,4608]{1,0:T(8,128)S(1)} collective-permute-done((f32[16,4608]{1,0:T(8,128)S(1)}, f32[16,4608]{1,0:T(8,128)S(1)}, u32[]{:S(2)}, u32[]{:S(2)}) %collective-permute-start.1) | collective-permute-done | bytes 294944 | tf_op jit(solution)/shard_map/ppermute | solution.py:422
  54.0 16.6 %collective-permute-done.2 = f32[16,4608]{1,0:T(8,128)S(1)} collective-permute-done((f32[16,4608]{1,0:T(8,128)S(1)}, f32[16,4608]{1,0:T(8,128)S(1)}, u32[]{:S(2)}, u32[]{:S(2)}) %collective-permute-start.2) | collective-permute-done | bytes 294944 | tf_op jit(solution)/shard_map/ppermute | solution.py:422
  73.8 23.6 %collective-permute-done.3 = f32[16,4608]{1,0:T(8,128)S(1)} collective-permute-done((f32[16,4608]{1,0:T(8,128)S(1)}, f32[16,4608]{1,0:T(8,128)S(1)}, u32[]{:S(2)}, u32[]{:S(2)}) %collective-permute-start.3) | collective-permute-done | bytes 294944 | tf_op jit(solution)/shard_map/ppermute | solution.py:422
  137.6 55.0 %all-gather.3.cloned.1.call-done = bf16[55296,256]{1,0:T(8,128)(2,1)} async-done(((bf16[3456,256]{1,0:T(8,128)(2,1)}), bf16[55296,256]{1,0:T(8,128)(2,1)}) %all-gather.3.cloned.1.call-update) | async-done | bytes 28311568 | tf_op jit(solution)/shard_map/all_gather | solution.py:676
  192.6 11.3 %shard_map.223.wq_ref.wk_ref.wv_ref = bf16[1536,2304]{1,0:T(8,128)(2,1)} custom-call(bf16[16,3456,256]{2,1,0:T(8,128)(2,1)} %bitcast.429), custom_call_target="tpu_custom_call" | custom-call | tf_op jit(solution)/shard_map/pallas_call | solution.py:388
  221.3 20.1 %shard_map.225 = (bf16[1536,4096]{1,0:T(8,128)(2,1)}, bf16[2048,1536]{1,0:T(8,128)(2,1)}, bf16[768,1536]{1,0:T(8,128)(2,1)}) custom-call(bf16[16,3456,256]{2,1,0:T(8,128)(2,1)} %bitcast.430), custom_call_target="tpu_custom_call" | custom-call | tf_op jit(solution)/shard_map/pallas_call | solution.py:388
  250.8 13.9 %collective-permute-done.16.rest_5_ = bf16[2,256,768]{2,1,0:T(8,128)(2,1)S(1)} collective-permute-done((bf16[2,256,768]{2,1,0:T(8,128)(2,1)S(1)}, bf16[2,256,768]{2,1,0:T(8,128)(2,1)S(1)}, u32[]{:S(2)}, u32[]{:S(2)}) %collective-permute-start.16) | collective-permute-done | bytes 786464 | tf_op jit(solution)/shard_map/ppermute | solution.py:417
  289.5 22.8 %shard_map.226 = (bf16[256,768]{1,0:T(8,128)(2,1)S(1)}, f32[256,768]{1,0:T(8,128)S(1)}, f32[256,768]{1,0:T(8,128)S(1)}, f32[256,768]{1,0:T(8,128)S(1)}, f32[256,...) custom-call(s32[13]{0:T(128)S(1)} %copy-done.79, bf16[256,768]{1,0:T(8,128)(2,1)S(1)} %get-tuple-element.156.q_ref, ...), custom_call_target="tpu_custom_call" | custom-call | tf_op jit(solution)/shard_map/pallas_call | solution.py:388
  312.4 9.9 %collective-permute-start.23 = (bf16[1,272,768]{2,1,0:T(8,128)(2,1)S(1)}, bf16[1,272,768]{2,1,0:T(8,128)(2,1)S(1)}, u32[]{:S(2)}, u32[]{:S(2)}) collective-permute-start(bf16[1,272,768]{2,1,0:T(8,128)(2,1)S(1)} %get-tuple-element.163.rest_0_.rest_9_), channel_id=1, source_target_pairs={{0,4},{2,6},{4,0},{6,2},{8,12},{10,14},{12,8},{14,10},{16,20},{18,... | collective-permute-start | bytes 1253384 | tf_op jit(solution)/shard_map/ppermute | solution.py:422
  329.0 9.2 %collective-permute-done.21 = bf16[256,768]{1,0:T(8,128)(2,1)S(1)} collective-permute-done((bf16[256,768]{1,0:T(8,128)(2,1)S(1)}, bf16[256,768]{1,0:T(8,128)(2,1)S(1)}, u32[]{:S(2)}, u32[]{:S(2)}) %collective-permute-start.21) | collective-permute-done | bytes 393248 | tf_op jit(solution)/shard_map/ppermute | solution.py:426
  393.4 7.7 convolution_convert_fusion.7
  409.6 11.2 %collective-permute-start.33 = (bf16[4,128,1536]{2,1,0:T(8,128)(2,1)}, bf16[4,128,1536]{2,1,0:T(8,128)(2,1)S(1)}, u32[]{:S(2)}, u32[]{:S(2)}) collective-permute-start(bf16[4,128,1536]{2,1,0:T(8,128)(2,1)} %fusion.5), channel_id=1, source_target_pairs={{0,4},{2,6},{4,0},{6,2},{8,12},{10,14},{12,8},{14,10},{16,20},{18,... | collective-permute-start | bytes 4718600 | tf_op jit(solution)/shard_map/ppermute | solution.py:422
  441.3 10.2 %collective-permute-start.37 = (bf16[1,272,768]{2,1,0:T(8,128)(2,1)S(1)}, bf16[1,272,768]{2,1,0:T(8,128)(2,1)}, u32[]{:S(2)}, u32[]{:S(2)}) collective-permute-start(bf16[1,272,768]{2,1,0:T(8,128)(2,1)S(1)} %get-tuple-element.188.d_self_ref.rest_18_.rest_27_), channel_id=1, source_target_pairs={{0,4},{2,6},{4,0},{6,2},{8,12},{10,14},{12,8},{14,10},{16,20},{18,... | collective-permute-start | bytes 1253384 | tf_op jit(solution)/shard_map/ppermute | solution.py:422
  489.6 15.0 %shard_map.228 = (bf16[256,384]{1,0:T(8,128)(2,1)S(1)}, f32[1,384]{1,0:T(1,128)S(1)}, f32[256,384]{1,0:T(8,128)S(1)}, f32[256,384]{1,0:T(8,128)S(1)}) custom-call(s32[13]{0:T(128)S(1)} %copy-done.80, bf16[256,768]{1,0:T(8,128)(2,1)S(1)} %copy-done.52, s32[256,1]{1,0:T(8,128)S(1)} %copy-done.65, s32[16,256]{1,0:T(8,128)S(1)} %concatenate.197.ids_ref, ...), custom_call_target="tpu_custom_call" | custom-call | tf_op jit(solution)/shard_map/pallas_call | solution.py:388
  518.7 14.8 %shard_map.229 = (bf16[256,384]{1,0:T(8,128)(2,1)S(1)}, f32[1,384]{1,0:T(1,128)S(1)}, f32[256,384]{1,0:T(8,128)S(1)}, f32[256,384]{1,0:T(8,128)S(1)}) custom-call(s32[13]{0:T(128)S(1)} %copy-done.80, bf16[256,768]{1,0:T(8,128)(2,1)S(1)} %copy-done.52, s32[256,1]{1,0:T(8,128)S(1)} %copy-done.65, s32[16,256]{1,0:T(8,128)S(1)} %concatenate.197.ids_ref, ...), custom_call_target="tpu_custom_call" | custom-call | tf_op jit(solution)/shard_map/pallas_call | solution.py:388
  554.5 20.0 %shard_map.230 = (bf16[256,768]{1,0:T(8,128)(2,1)S(1)}, f32[1,768]{1,0:T(1,128)S(1)}, bf16[256,768]{1,0:T(8,128)(2,1)S(1)}) custom-call(s32[13]{0:T(128)S(1)} %copy-done.80, bf16[2,256,768]{2,1,0:T(8,128)(2,1)S(1)} %get-tuple-element.217.rest_0_.kv_ref, s32[256,1]{1,0:T(8,128)S(1)} %copy-done.66, s32[16,256]{1,0:T(8,128)S(1)} %concatenate.197.ids_ref, ...), custom_call_target="tpu_custom_call" | custom-call | tf_op jit(solution)/shard_map/pallas_call | solution.py:388
  646.5 10.8 %collective-permute-done.70 = bf16[1,16,1536]{2,1,0:T(8,128)(2,1)} collective-permute-done((bf16[1,16,1536]{2,1,0:T(8,128)(2,1)}, bf16[1,16,1536]{2,1,0:T(8,128)(2,1)}, u32[]{:S(2)}, u32[]{:S(2)}) %collective-permute-start.70) | collective-permute-done | bytes 49184 | tf_op jit(solution)/shard_map/ppermute | solution.py:422
  671.7 22.4 %collective-permute-done.72 = bf16[4,16,1536]{2,1,0:T(8,128)(2,1)S(1)} collective-permute-done((bf16[4,16,1536]{2,1,0:T(8,128)(2,1)S(1)}, bf16[4,16,1536]{2,1,0:T(8,128)(2,1)S(1)}, u32[]{:S(2)}, u32[]{:S(2)}) %collective-permute-start.72) | collective-permute-done | bytes 196640 | tf_op jit(solution)/shard_map/ppermute | solution.py:422
  702.2 14.4 %collective-permute-done.62 = bf16[1,96,2048]{2,1,0:T(8,128)(2,1)S(1)} collective-permute-done((bf16[1,96,2048]{2,1,0:T(8,128)(2,1)S(1)}, bf16[1,96,2048]{2,1,0:T(8,128)(2,1)S(1)}, u32[]{:S(2)}, u32[]{:S(2)}) %collective-permute-start.62) | collective-permute-done | bytes 393248 | tf_op jit(solution)/shard_map/ppermute | solution.py:422
  717.6 9.0 %collective-permute-done.68 = bf16[2,96,1536]{2,1,0:T(8,128)(2,1)S(1)} collective-permute-done((bf16[2,96,1536]{2,1,0:T(8,128)(2,1)S(1)}, bf16[2,96,1536]{2,1,0:T(8,128)(2,1)S(1)}, u32[]{:S(2)}, u32[]{:S(2)}) %collective-permute-start.68) | collective-permute-done | bytes 589856 | tf_op jit(solution)/shard_map/ppermute | solution.py:422
  728.7 9.4 %collective-permute-done.75 = f32[17,4608]{1,0:T(8,128)S(1)} collective-permute-done((f32[17,4608]{1,0:T(8,128)S(1)}, f32[17,4608]{1,0:T(8,128)S(1)}, u32[]{:S(2)}, u32[]{:S(2)}) %collective-permute-start.75) | collective-permute-done | bytes 313376 | tf_op jit(solution)/shard_map/ppermute | solution.py:422
  742.0 9.4 %collective-permute-done.76 = f32[17,4608]{1,0:T(8,128)S(1)} collective-permute-done((f32[17,4608]{1,0:T(8,128)S(1)}, f32[17,4608]{1,0:T(8,128)S(1)}, u32[]{:S(2)}, u32[]{:S(2)}) %collective-permute-start.76) | collective-permute-done | bytes 313376 | tf_op jit(solution)/shard_map/ppermute | solution.py:422
  751.6 21.5 %collective-permute-done.77 = f32[17,4608]{1,0:T(8,128)S(1)} collective-permute-done((f32[17,4608]{1,0:T(8,128)S(1)}, f32[17,4608]{1,0:T(8,128)S(1)}, u32[]{:S(2)}, u32[]{:S(2)}) %collective-permute-start.77) | collective-permute-done | bytes 313376 | tf_op jit(solution)/shard_map/ppermute | solution.py:422
  801.5 28.7 %shard_map.232 = (f32[12288,128]{1,0:T(8,128)}, f32[12288,128]{1,0:T(8,128)}, f32[12288,128]{1,0:T(8,128)}, f32[12288,128]{1,0:T(8,128)}, bf16[12288,128]{1,0:T(8,128)(2,1)}) custom-call(f32[1]{0:T(128)} %bitcast.162.clip_ref, f32[12288,128]{1,0:T(8,128)} %copy-done.38, f32[12288,128]{1,0:T(8,128)} %bitcast.454, f32[12288,128]{1,0:T(8,128)} %bitcast.455, ...), custom_call_target="tpu_custom_call" | custom-call | flops 31457280 | bytes 59768832 | tf_op jit(solution)/shard_map/pallas_call | solution.py:388
  (813 shorter events, 424.4 us)
Async XLA Ops:
  7.2 185.4 %all-gather.3.cloned.1.call-start = ((), (), s32[]{:S(2)}) async-start(), calls=%async_computation.1 | async-start | bytes 30081024 | tf_op jit(solution)/shard_map/all_gather | solution.py:676
  37.8 34.2 %collective-permute-start.6 = (f32[4,16,1536]{2,1,0:T(8,128)S(1)}, f32[4,16,1536]{2,1,0:T(8,128)S(1)}, u32[]{:S(2)}, u32[]{:S(2)}) collective-permute-start(f32[4,16,1536]{2,1,0:T(8,128)S(1)} %bitcast.499), channel_id=1, source_target_pairs={{0,8},{2,10},{4,12},{6,14},{8,0},{10,2},{12,4},{14,6},{16,24},{18,... | collective-permute-start | bytes 1179656 | tf_op jit(solution)/shard_map/ppermute | solution.py:422
  72.1 33.3 %collective-permute-start.7 = (f32[2,16,1536]{2,1,0:T(8,128)S(1)}, f32[2,16,1536]{2,1,0:T(8,128)S(1)}, u32[]{:S(2)}, u32[]{:S(2)}) collective-permute-start(f32[2,16,1536]{2,1,0:T(8,128)S(1)} %dynamic-slice_bitcast_fusion.3), channel_id=1, source_target_pairs={{0,16},{2,18},{4,20},{6,22},{8,24},{10,26},{12,28},{14,30},{16,0},... | collective-permute-start | bytes 589832 | tf_op jit(solution)/shard_map/ppermute | solution.py:422
  271.3 67.6 %collective-permute-start.22 = (bf16[768,1536]{1,0:T(8,128)(2,1)}, bf16[768,1536]{1,0:T(8,128)(2,1)}, u32[]{:S(2)}, u32[]{:S(2)}) collective-permute-start(bf16[768,1536]{1,0:T(8,128)(2,1)} %get-tuple-element.161.w_ref), channel_id=1, source_target_pairs={{0,1},{1,0},{2,3},{3,2},{4,5},{5,4},{6,7},{7,6},{8,9},{9,8},{10,11... | collective-permute-start | bytes 7077896 | tf_op jit(solution)/shard_map/ppermute | solution.py:426
  312.4 34.9 %collective-permute-start.23 = (bf16[1,272,768]{2,1,0:T(8,128)(2,1)S(1)}, bf16[1,272,768]{2,1,0:T(8,128)(2,1)S(1)}, u32[]{:S(2)}, u32[]{:S(2)}) collective-permute-start(bf16[1,272,768]{2,1,0:T(8,128)(2,1)S(1)} %get-tuple-element.163.rest_0_.rest_9_), channel_id=1, source_target_pairs={{0,4},{2,6},{4,0},{6,2},{8,12},{10,14},{12,8},{14,10},{16,20},{18,... | collective-permute-start | bytes 1253384 | tf_op jit(solution)/shard_map/ppermute | solution.py:422
  409.6 50.7 %collective-permute-start.33 = (bf16[4,128,1536]{2,1,0:T(8,128)(2,1)}, bf16[4,128,1536]{2,1,0:T(8,128)(2,1)S(1)}, u32[]{:S(2)}, u32[]{:S(2)}) collective-permute-start(bf16[4,128,1536]{2,1,0:T(8,128)(2,1)} %fusion.5), channel_id=1, source_target_pairs={{0,4},{2,6},{4,0},{6,2},{8,12},{10,14},{12,8},{14,10},{16,20},{18,... | collective-permute-start | bytes 4718600 | tf_op jit(solution)/shard_map/ppermute | solution.py:422
  459.0 45.7 %collective-permute-start.43 = (bf16[1,144,768]{2,1,0:T(8,128)(2,1)}, bf16[1,144,768]{2,1,0:T(8,128)(2,1)}, u32[]{:S(2)}, u32[]{:S(2)}) collective-permute-start(bf16[1,144,768]{2,1,0:T(8,128)(2,1)} %maximum_select_fusion.6), channel_id=1, source_target_pairs={{6,16},{14,24},{16,6},{24,14},{7,17},{15,25},{17,7},{25,15}} | collective-permute-start | bytes 663560 | tf_op jit(solution)/shard_map/ppermute | solution.py:567
  464.1 69.5 %collective-permute-start.36 = (bf16[4,96,2048]{2,1,0:T(8,128)(2,1)}, bf16[4,96,2048]{2,1,0:T(8,128)(2,1)}, u32[]{:S(2)}, u32[]{:S(2)}) collective-permute-start(bf16[4,96,2048]{2,1,0:T(8,128)(2,1)} %fusion.3), channel_id=1, source_target_pairs={{0,4},{2,6},{4,0},{6,2},{8,12},{10,14},{12,8},{14,10},{16,20},{18,... | collective-permute-start | bytes 4718600 | tf_op jit(solution)/shard_map/ppermute | solution.py:422
  469.0 35.7 %collective-permute-start.42 = (bf16[4,272,768]{2,1,0:T(8,128)(2,1)S(1)}, bf16[4,272,768]{2,1,0:T(8,128)(2,1)S(1)}, u32[]{:S(2)}, u32[]{:S(2)}) collective-permute-start(bf16[4,272,768]{2,1,0:T(8,128)(2,1)S(1)} %constant_dynamic-update-slice_fusion.18), channel_id=1, source_target_pairs={{0,2},{2,0},{4,6},{6,4},{8,10},{10,8},{12,14},{14,12},{16,18},{18,... | collective-permute-start | bytes 5013512 | tf_op jit(solution)/shard_map/ppermute | solution.py:422
  507.7 34.5 %collective-permute-start.47 = (bf16[2,128,1536]{2,1,0:T(8,128)(2,1)S(1)}, bf16[2,128,1536]{2,1,0:T(8,128)(2,1)S(1)}, u32[]{:S(2)}, u32[]{:S(2)}) collective-permute-start(bf16[2,128,1536]{2,1,0:T(8,128)(2,1)S(1)} %fusion.53), channel_id=1, source_target_pairs={{0,8},{2,10},{4,12},{6,14},{8,0},{10,2},{12,4},{14,6},{16,24},{18,... | collective-permute-start | bytes 2359304 | tf_op jit(solution)/shard_map/ppermute | solution.py:422
  514.9 80.2 %collective-permute-start.49 = (bf16[4,96,2048]{2,1,0:T(8,128)(2,1)}, bf16[4,96,2048]{2,1,0:T(8,128)(2,1)}, u32[]{:S(2)}, u32[]{:S(2)}) collective-permute-start(bf16[4,96,2048]{2,1,0:T(8,128)(2,1)} %fusion.2), channel_id=1, source_target_pairs={{0,4},{2,6},{4,0},{6,2},{8,12},{10,14},{12,8},{14,10},{16,20},{18,... | collective-permute-start | bytes 4718600 | tf_op jit(solution)/shard_map/ppermute | solution.py:422
  517.1 63.2 %collective-permute-start.52 = (bf16[8,48,1536]{2,1,0:T(8,128)(2,1)}, bf16[8,48,1536]{2,1,0:T(8,128)(2,1)}, u32[]{:S(2)}, u32[]{:S(2)}) collective-permute-start(bf16[8,48,1536]{2,1,0:T(8,128)(2,1)} %convolution_convert_fusion.5), channel_id=1, source_target_pairs={{0,2},{2,0},{4,6},{6,4},{8,10},{10,8},{12,14},{14,12},{16,18},{18,... | collective-permute-start | bytes 3538952 | tf_op jit(solution)/shard_map/ppermute | solution.py:422
  537.4 69.6 %collective-permute-start.45 = (bf16[2,96,2048]{2,1,0:T(8,128)(2,1)}, bf16[2,96,2048]{2,1,0:T(8,128)(2,1)}, u32[]{:S(2)}, u32[]{:S(2)}) collective-permute-start(bf16[2,96,2048]{2,1,0:T(8,128)(2,1)} %fusion.54), channel_id=1, source_target_pairs={{0,8},{2,10},{4,12},{6,14},{8,0},{10,2},{12,4},{14,6},{16,24},{18,... | collective-permute-start | bytes 2359304 | tf_op jit(solution)/shard_map/ppermute | solution.py:422
  550.9 41.0 %collective-permute-start.50 = (f32[4,16,1536]{2,1,0:T(8,128)}, f32[4,16,1536]{2,1,0:T(8,128)}, u32[]{:S(2)}, u32[]{:S(2)}) collective-permute-start(f32[4,16,1536]{2,1,0:T(8,128)} %bitcast.96), channel_id=1, source_target_pairs={{0,8},{2,10},{4,12},{6,14},{8,0},{10,2},{12,4},{14,6},{16,24},{18,... | collective-permute-start | bytes 1179656 | tf_op jit(solution)/shard_map/ppermute | solution.py:422
  586.3 51.2 %collective-permute-start.56 = (bf16[1,128,1536]{2,1,0:T(8,128)(2,1)}, bf16[1,128,1536]{2,1,0:T(8,128)(2,1)}, u32[]{:S(2)}, u32[]{:S(2)}) collective-permute-start(bf16[1,128,1536]{2,1,0:T(8,128)(2,1)} %dynamic-slice_convert_fusion.2), channel_id=1, source_target_pairs={{0,16},{2,18},{4,20},{6,22},{8,24},{10,26},{12,28},{14,30},{16,0},... | collective-permute-start | bytes 1179656 | tf_op jit(solution)/shard_map/ppermute | solution.py:422
  595.1 68.8 %collective-permute-start.61 = (bf16[4,48,1536]{2,1,0:T(8,128)(2,1)}, bf16[4,48,1536]{2,1,0:T(8,128)(2,1)}, u32[]{:S(2)}, u32[]{:S(2)}) collective-permute-start(bf16[4,48,1536]{2,1,0:T(8,128)(2,1)} %fusion.7), channel_id=1, source_target_pairs={{0,4},{2,6},{4,0},{6,2},{8,12},{10,14},{12,8},{14,10},{16,20},{18,... | collective-permute-start | bytes 1769480 | tf_op jit(solution)/shard_map/ppermute | solution.py:422
  607.0 59.9 %collective-permute-start.60 = (bf16[4,96,768]{2,1,0:T(8,128)(2,1)}, bf16[4,96,768]{2,1,0:T(8,128)(2,1)}, u32[]{:S(2)}, u32[]{:S(2)}) collective-permute-start(bf16[4,96,768]{2,1,0:T(8,128)(2,1)} %fusion.38), channel_id=1, source_target_pairs={{0,4},{2,6},{4,0},{6,2},{8,12},{10,14},{12,8},{14,10},{16,20},{18,... | collective-permute-start | bytes 1769480 | tf_op jit(solution)/shard_map/ppermute | solution.py:422
  616.2 52.1 %collective-permute-start.59 = (bf16[2,96,2048]{2,1,0:T(8,128)(2,1)}, bf16[2,96,2048]{2,1,0:T(8,128)(2,1)}, u32[]{:S(2)}, u32[]{:S(2)}) collective-permute-start(bf16[2,96,2048]{2,1,0:T(8,128)(2,1)} %fusion.55), channel_id=1, source_target_pairs={{0,8},{2,10},{4,12},{6,14},{8,0},{10,2},{12,4},{14,6},{16,24},{18,... | collective-permute-start | bytes 2359304 | tf_op jit(solution)/shard_map/ppermute | solution.py:422
  662.9 53.7 %collective-permute-start.53 = (f32[256,1536]{1,0:T(8,128)}, f32[256,1536]{1,0:T(8,128)S(1)}, u32[]{:S(2)}, u32[]{:S(2)}) collective-permute-start(f32[256,1536]{1,0:T(8,128)} %fusion.174), channel_id=1, source_target_pairs={{0,1},{1,0},{2,3},{3,2},{4,5},{5,4},{6,7},{7,6},{8,9},{9,8},{10,11... | collective-permute-start | bytes 4718600 | tf_op jit(solution)/shard_map/ppermute | solution.py:426
  663.5 34.0 %collective-permute-start.65 = (bf16[4,96,1536]{2,1,0:T(8,128)(2,1)}, bf16[4,96,1536]{2,1,0:T(8,128)(2,1)S(1)}, u32[]{:S(2)}, u32[]{:S(2)}) collective-permute-start(bf16[4,96,1536]{2,1,0:T(8,128)(2,1)} %fusion.6), channel_id=1, source_target_pairs={{0,4},{2,6},{4,0},{6,2},{8,12},{10,14},{12,8},{14,10},{16,20},{18,... | collective-permute-start | bytes 3538952 | tf_op jit(solution)/shard_map/ppermute | solution.py:422
  664.0 30.1 %collective-permute-start.72 = (bf16[4,16,1536]{2,1,0:T(8,128)(2,1)S(1)}, bf16[4,16,1536]{2,1,0:T(8,128)(2,1)S(1)}, u32[]{:S(2)}, u32[]{:S(2)}) collective-permute-start(bf16[4,16,1536]{2,1,0:T(8,128)(2,1)S(1)} %bitcast.492), channel_id=1, source_target_pairs={{0,4},{2,6},{4,0},{6,2},{8,12},{10,14},{12,8},{14,10},{16,20},{18,... | collective-permute-start | bytes 589832 | tf_op jit(solution)/shard_map/ppermute | solution.py:422
  666.9 32.0 %collective-permute-start.64 = (bf16[2,48,1536]{2,1,0:T(8,128)(2,1)S(1)}, bf16[2,48,1536]{2,1,0:T(8,128)(2,1)S(1)}, u32[]{:S(2)}, u32[]{:S(2)}) collective-permute-start(bf16[2,48,1536]{2,1,0:T(8,128)(2,1)S(1)} %fusion.85), channel_id=1, source_target_pairs={{0,8},{2,10},{4,12},{6,14},{8,0},{10,2},{12,4},{14,6},{16,24},{18,... | collective-permute-start | bytes 884744 | tf_op jit(solution)/shard_map/ppermute | solution.py:422
  668.4 33.6 %collective-permute-start.63 = (bf16[2,96,768]{2,1,0:T(8,128)(2,1)S(1)}, bf16[2,96,768]{2,1,0:T(8,128)(2,1)S(1)}, u32[]{:S(2)}, u32[]{:S(2)}) collective-permute-start(bf16[2,96,768]{2,1,0:T(8,128)(2,1)S(1)} %fusion.86), channel_id=1, source_target_pairs={{0,8},{2,10},{4,12},{6,14},{8,0},{10,2},{12,4},{14,6},{16,24},{18,... | collective-permute-start | bytes 884744 | tf_op jit(solution)/shard_map/ppermute | solution.py:422
  702.1 36.2 %collective-permute-start.66 = (bf16[1,96,768]{2,1,0:T(8,128)(2,1)S(1)}, bf16[1,96,768]{2,1,0:T(8,128)(2,1)S(1)}, u32[]{:S(2)}, u32[]{:S(2)}) collective-permute-start(bf16[1,96,768]{2,1,0:T(8,128)(2,1)S(1)} %dynamic-slice_convert_fusion.4), channel_id=1, source_target_pairs={{0,16},{2,18},{4,20},{6,22},{8,24},{10,26},{12,28},{14,30},{16,0},... | collective-permute-start | bytes 442376 | tf_op jit(solution)/shard_map/ppermute | solution.py:422
  (246 other events, 3169.7 us)
Sparse Core Ops, SparseCore 0:
  15.9 176.6 all-gather.2

commit v4 on v3

--- a/solution.py
+++ b/solution.py
@@ -30,7 +30,8 @@
 
 LANES = 128
 EDGE = 128
-PACK = 16
+TABLE = 16
+PACK = 2 * TABLE
 WIDE = 256
 PIECES = 13
 MASKED = -1e30
@@ -121,16 +122,93 @@
     return jnp.broadcast_to(column, (column.shape[0], LANES)).T[:1]
 
 
+def tile(ref):
+    return ref[...].reshape(-1, WIDE)
+
+
+def tiles(ref, count):
+    if len(ref.shape) == 2:
+        return [ref[:, at * WIDE : (at + 1) * WIDE] for at in range(count)]
+    rows = ref.shape[1] // count
+    return [ref[:, at * rows : (at + 1) * rows, :].reshape(-1, WIDE) for at in range(count)]
+
+
+def add_transposed(acc_ref, a_ref, w_ref):
+    count = a_ref.shape[1] // WIDE
+    blocks = tiles(w_ref, count)
+    for row in range(0, acc_ref.shape[1], WIDE):
+        part = slice(row, row + WIDE)
+        total = mm(a_ref[:, :WIDE], blocks[0][part], 1, 1)
+        for at in range(1, count):
+            total = total + mm(a_ref[:, at * WIDE : (at + 1) * WIDE], blocks[at][part], 1, 1)
+        acc_ref[:, part] += total
+
+
 def project_kernel(a_ref, wq_ref, wk_ref, wv_ref, gq_ref, gk_ref, cos_ref, sin_ref, q_ref, kv_ref, raw_ref):
     a = a_ref[...]
     cosine, sine = cos_ref[...], sin_ref[...]
-    raw_q = mm(a, wq_ref[...], 1, 0)
-    raw_k = mm(a, wk_ref[...], 1, 0)
+    raw_q = mm(a, tile(wq_ref), 1, 0)
+    raw_k = mm(a, tile(wk_ref), 1, 0)
     raw_ref[0] = raw_q
     raw_ref[1] = raw_k
-    q_ref[...] = norm_rope(raw_q, gq_ref[...], cosine, sine).astype(bf16) * jnp.asarray(HD**-0.5, bf16)
-    kv_ref[0] = norm_rope(raw_k, gk_ref[...], cosine, sine).astype(bf16)
-    kv_ref[1] = mm(a, wv_ref[...], 1, 0).astype(bf16)
+    for at in range(0, WIDE, LANES):
+        part = slice(at, at + LANES)
+        query = norm_rope(raw_q[:, part], gq_ref[...], cosine, sine).astype(bf16)
+        q_ref[:, part] = query * jnp.asarray(HD**-0.5, bf16)
+        kv_ref[0, :, part] = norm_rope(raw_k[:, part], gk_ref[...], cosine, sine).astype(bf16)
+    kv_ref[1] = mm(a, tile(wv_ref), 1, 0).astype(bf16)
+
+
+def times_kernel(a_ref, w_ref, out_ref):
+    out_ref[...] = mm(a_ref[...], tile(w_ref), 1, 0)
+
+
+def two_times_kernel(a_ref, w_ref, other_a_ref, other_w_ref, out_ref):
+    out_ref[...] = mm(a_ref[...], tile(w_ref), 1, 0) + mm(other_a_ref[...], tile(other_w_ref), 1, 0)
+
+
+def times_transposed_kernel(a_ref, w_ref, out_ref, acc_ref):
+    step = pl.program_id(0)
+
+    @pl.when(step == 0)
+    def _():
+        acc_ref[...] = jnp.zeros(acc_ref.shape, f32)
+
+    add_transposed(acc_ref, a_ref, w_ref)
+
+    @pl.when(step == pl.num_programs(0) - 1)
+    def _():
+        out_ref[...] = acc_ref[...].astype(out_ref.dtype)
+
+
+def hidden_kernel(b_ref, w_gate_ref, w_up_ref, gate_ref, up_ref, hidden_ref, turned_ref):
+    gate = mm(b_ref[...], tile(w_gate_ref), 1, 0)
+    up = mm(b_ref[...], tile(w_up_ref), 1, 0)
+    hidden = (gate * jax.nn.sigmoid(gate) * up).astype(bf16)
+    gate_ref[...] = gate
+    up_ref[...] = up
+    hidden_ref[...] = hidden
+    turned_ref[...] = hidden.T
+
+
+def hidden_back_kernel(d_branch_ref, w_ref, gate_ref, up_ref, d_gate_ref, d_up_ref, acc_ref):
+    step = pl.program_id(0)
+
+    @pl.when(step == 0)
+    def _():
+        acc_ref[...] = jnp.zeros(acc_ref.shape, f32)
+
+    add_transposed(acc_ref, d_branch_ref, w_ref)
+
+    @pl.when(step == pl.num_programs(0) - 1)
+    def _():
+        for at in range(0, acc_ref.shape[1], WIDE):
+            part = slice(at, at + WIDE)
+            d_units, gate = acc_ref[:, part], gate_ref[:, part]
+            sigmoid = jax.nn.sigmoid(gate)
+            d_gate = d_units * up_ref[:, part] * sigmoid * (1.0 + gate * (1.0 - sigmoid))
+            d_gate_ref[:, part] = d_gate.astype(bf16)
+            d_up_ref[:, part] = (d_units * (gate * sigmoid)).astype(bf16)
 
 
 def piece_views(piece_refs, counts, per):
@@ -143,7 +221,7 @@
 
 def attend_kernel(counts, tok, flag_ref, q_ref, own_ids_ref, ids_ref, tk_ref, tv_ref, gate_ref, *rest):
     pieces = piece_views(rest[: len(counts)], counts, 2)
-    mixed_ref, self_ref, cross_ref, lse_self_ref, lse_cross_ref, pack_ref = rest[len(counts) : len(counts) + 6]
+    mixed_ref, self_ref, cross_ref, lse_self_ref, lse_cross_ref, split_ref = rest[len(counts) : len(counts) + 6]
     scores_ref, most_ref, total_ref, acc_ref, table_ref = rest[len(counts) + 6 :]
     step = pl.program_id(0)
     own_ids = own_ids_ref[...]
@@ -209,33 +287,36 @@
     table = put_row(table_ref[...], 2 * step, as_row(lse_self[:tok]))
     table = put_row(table, 2 * step + 1, as_row(lse_self[tok:]))
     table_ref[...] = table
-    pack_ref[0, :tok, pl.ds(pl.multiple_of(step * LANES, LANES), LANES)] = q_pair
 
     @pl.when(step == pl.num_programs(0) - 1)
     def _():
-        pack_ref[0, tok:, :] = split_three(table_ref[...])
-
-
-def mixed_back_kernel(tok, d_attn_ref, w_ref, self_ref, cross_ref, gate_ref, pack_ref, d_cross_ref, d_gate_ref, table_ref):
+        split_ref[...] = split_three(table_ref[...])
+
+
+def mixed_back_kernel(tok, d_attn_ref, w_ref, self_ref, cross_ref, gate_ref, lse_ref, pack_ref, d_cross_ref, d_gate_ref, acc_ref):
     step = pl.program_id(0)
-    d_mixed = mm(d_attn_ref[...], w_ref[...], 1, 1)
-    d_self = d_mixed.astype(bf16)
-    d_cross_ref[...] = (gate_ref[...] * d_mixed).astype(bf16)
-    d_gate_ref[...] = jnp.sum(d_mixed * cross_ref[...], axis=0, keepdims=True)
-    delta = head_sum(d_self.astype(f32) * self_ref[...])
 
     @pl.when(step == 0)
     def _():
-        table_ref[...] = jnp.zeros(table_ref.shape, f32)
-
-    table = put_row(table_ref[...], 2 * step, as_row(delta[:, :1]))
-    table = put_row(table, 2 * step + 1, as_row(delta[:, HD : HD + 1]))
-    table_ref[...] = table
-    pack_ref[0, :tok, pl.ds(pl.multiple_of(step * LANES, LANES), LANES)] = d_self
+        acc_ref[...] = jnp.zeros(acc_ref.shape, f32)
+
+    add_transposed(acc_ref, d_attn_ref, w_ref)
 
     @pl.when(step == pl.num_programs(0) - 1)
     def _():
-        pack_ref[0, tok:, :] = split_three(table_ref[...])
+        rows = []
+        for at in range(0, acc_ref.shape[1], LANES):
+            part = slice(at, at + LANES)
+            d_mixed = acc_ref[:, part]
+            d_self = d_mixed.astype(bf16)
+            d_cross_ref[:, part] = (gate_ref[:, part] * d_mixed).astype(bf16)
+            d_gate_ref[:, part] = jnp.sum(d_mixed * cross_ref[:, part], axis=0, keepdims=True)
+            delta = head_sum(d_self.astype(f32) * self_ref[:, part])
+            rows += [as_row(delta[:, :1]), as_row(delta[:, HD : HD + 1])]
+            pack_ref[0, :tok, part] = d_self
+        rows += [jnp.zeros_like(rows[0])] * (TABLE - len(rows))
+        pack_ref[0, tok : tok + TABLE, :] = split_three(jnp.concatenate(rows, axis=0))
+        pack_ref[0, tok + TABLE :, :] = lse_ref[...]
 
 
 def query_back_kernel(
@@ -284,10 +365,9 @@
 def key_back_kernel(counts, tok, flag_ref, kv_ref, own_ids_ref, ids_ref, raw_ref, gain_ref, cos_ref, sin_ref, *rest):
     n = len(counts)
     q_views = piece_views(rest[:n], counts, 1)
-    q_tables = piece_views(rest[n : 2 * n], counts, 1)
-    g_views = piece_views(rest[2 * n : 3 * n], counts, 1)
-    g_tables = piece_views(rest[3 * n : 4 * n], counts, 1)
-    d_raw_ref, d_gain_ref, d_value_ref, acc_k_ref, acc_v_ref = rest[4 * n :]
+    g_views = piece_views(rest[n : 2 * n], counts, 1)
+    g_tables = piece_views(rest[2 * n : 3 * n], counts, 1)
+    d_raw_ref, d_gain_ref, d_value_ref, acc_k_ref, acc_v_ref = rest[3 * n :]
     step = pl.program_id(0)
     own_ids = own_ids_ref[...]
     k_two = two_heads(kv_ref[0])
@@ -301,8 +381,8 @@
         def _(slot=slot, q_ref=q_ref, at=at, rows=rows):
             query = q_ref[at]
             d_self = g_views[slot][0][at]
-            lse = joined(q_tables[slot][0][at], tok)[:, :rows]
-            delta = joined(g_tables[slot][0][at], tok)[:, :rows]
+            tables = joined(g_tables[slot][0][at], tok)[:, :rows]
+            delta, lse = tables[:TABLE], tables[TABLE:]
             same = own_ids == ids_ref[slot : slot + 1, :rows]
             scores = mm(k_two, query, 1, 1)
             d_weights = mm(v_two, d_self, 1, 1)
@@ -343,20 +423,12 @@
         top += columns // WIDE * rows
 
 
-def unpack_kernel(tables, block_ref, *out_refs):
-    top = 0
-    for (rows, columns), out_ref in zip(tables, out_refs):
-        for at in range(columns // WIDE):
-            out_ref[:, at * WIDE : (at + 1) * WIDE] = block_ref[0, top : top + rows, :]
-            top += rows
-
-
 def flatten_kernel(places, *refs):
     *grad_refs, lines_ref, square_ref = refs
     square = jnp.zeros((1, LANES), f32)
     for (start, column, columns), ref in zip(places, grad_refs):
         for at in range(ref.shape[1] // LANES):
-            part = ref[:, at * LANES : (at + 1) * LANES]
+            part = ref[:, at * LANES : (at + 1) * LANES].astype(f32)
             lines_ref[pl.ds(start + column // LANES + at, ref.shape[0], stride=columns // LANES), :] = part
             square = square + jnp.sum(part * part, axis=0, keepdims=True)
     square_ref[...] = square
@@ -384,7 +456,7 @@
     return (first_new, second_new, weight_new, moving_new)
 
 
-def call(kernel, grid, in_specs, out_specs, out_shape, args, scratch=(), prefetch=0, flops=0, moved=0, vmem=16):
+def call(kernel, grid, in_specs, out_specs, out_shape, args, scratch=(), prefetch=0, flops=0, moved=0, vmem=58):
     return pl.pallas_call(
         kernel,
         grid_spec=pltpu.PrefetchScalarGridSpec(
@@ -515,6 +587,24 @@
         self.token = arrays
 
 
+class SmallSum:
+    def __init__(self, clock, x):
+        self.clock, self.x, self.level = clock, x, 0
+        self.levels = index_bits(lax.axis_size("img"))
+        clock.mark(x)
+
+    def advance(self):
+        got = self.clock.stage(crossed(self.x, 1 << self.level))
+        self.x = self.x + got
+        self.clock.mark(self.x)
+        self.level += 1
+
+    def finish(self):
+        while self.level < self.levels:
+            self.advance()
+        return self.x
+
+
 class GradientSum:
     def __init__(self, clock, left, right):
         bits = index_bits(left.shape[0])
@@ -524,6 +614,7 @@
         left, self.right = clock.stage(left, right)
         self.own, other = own_and_other(left, 0)
         self.sent = self.terms(other).astype(bf16)
+        self.result = None
         clock.mark(self.sent)
 
     def terms(self, chunks):
@@ -540,7 +631,8 @@
             self.receive()
         got = self.clock.stage(self.got)
         if self.level == len(self.order):
-            return (self.keep + got.astype(f32))[0]
+            self.result = (self.keep + got.astype(f32))[0]
+            return self.result
         bit = self.order[self.level]
         if self.level == 1:
             own, other = own_and_other(self.own, bit)
@@ -551,7 +643,6 @@
             own, other = own_and_other(self.keep + got.astype(f32), bit)
             self.sent, self.keep = other.astype(bf16), own
         self.clock.mark(self.sent)
-        return self.sent
 
 
 class Neighbourhood:
@@ -669,8 +760,11 @@
         return pl.pallas_call(
             functools.partial(unflatten_kernel, shapes),
             out_shape=[shape_of(s, bf16) for s in shapes],
-            compiler_params=pltpu.CompilerParams(vmem_limit_bytes=32 * MIB),
+            compiler_params=pltpu.CompilerParams(vmem_limit_bytes=58 * MIB),
         )(*(master_lines[starts[w] : starts[w + 1]] for w in which))
+
+    def scatter(terms):
+        return lax.psum_scatter(terms, "img", scatter_dimension=0, tiled=True)
 
     def gather(rows):
         return lax.all_gather(rows, "img", axis=0, tiled=True)
@@ -678,28 +772,32 @@
     together = [0, 1, 4, 2]
     shapes = [tables[w] for w in together]
     heights = [rows * columns // WIDE for rows, columns in shapes]
-    if all(rows % 16 == 0 for rows, _ in shapes) and sum(heights[:3]) % heights[3] == 0:
+    if all(rows % 16 == 0 for rows, _ in shapes):
         block = pl.pallas_call(
             functools.partial(pack_kernel, shapes),
             out_shape=shape_of((sum(heights), WIDE), bf16),
-            compiler_params=pltpu.CompilerParams(vmem_limit_bytes=32 * MIB),
+            compiler_params=pltpu.CompilerParams(vmem_limit_bytes=58 * MIB),
         )(*(master_lines[starts[w] : starts[w + 1]] for w in together))
         blocks = gather(block[None])
-
-        def unpack(which, height, at, gathered):
-            return call(
-                functools.partial(unpack_kernel, which),
-                (n_img,),
-                [pl.BlockSpec((1, height, WIDE), lambda i: (i, at, 0))],
-                [pl.BlockSpec(shape, lambda i: (i, 0)) for shape in which],
-                [shape_of((n_img * rows, columns), bf16) for rows, columns in which],
-                (gathered,),
-                vmem=52,
-            )
-
     else:
         blocks = None
-        w_project = gather(own_rows(2)[0])
+        natural = dict(zip(together, (gather(rows) for rows in own_rows(*together))))
+
+    def weight(which):
+        if blocks is None:
+            array = natural[which]
+            return array, lambda at, group=1: pl.BlockSpec((array.shape[0], group * WIDE), lambda j, *_: (0, at(j)))
+        place = together.index(which)
+        rows = shapes[place][0]
+        first = sum(heights[:place]) // rows
+        assert first * rows == sum(heights[:place])
+
+        def spec(at, group=1):
+            assert first % group == 0
+            return pl.BlockSpec((n_img, group * rows, WIDE), lambda j, *_: (0, first // group + at(j), 0))
+
+        return blocks, spec
+
     (own_modulate,) = own_rows(5)
     (own_text,) = own_rows(3)
 
@@ -762,18 +860,23 @@
 
     if blocks is not None:
         blocks = tie(blocks, all_text, per_token, cosine, sine, flags, piece_ids)
-        (w_project,) = unpack(shapes[3:], heights[3], sum(heights[:3]) // heights[3], blocks)
     x_float = tokens.astype(f32)
     x_normed = rms_norm(x_float)
     normed_one = x_normed * gain_attn
     attn_in = (normed_one * (1.0 + scale_one) + shift_one).astype(bf16)
+    def wide(rows, group=1):
+        return pl.BlockSpec((rows, group * WIDE), lambda j, *_: (0, j))
+
+    thirds = half_d // WIDE
+    w_project, project_spec = weight(2)
     queries, own_kv, raw_qk = call(
         project_kernel,
-        (n_pairs,),
-        [whole((tok, D)), pair(D), pair(D, n_pairs), pair(D, 2 * n_pairs)]
+        (thirds,),
+        [whole((tok, D))]
+        + [project_spec(lambda j, c=c: c * thirds + j) for c in range(3)]
         + [whole((1, LANES))] * 2
         + [whole((tok, LANES))] * 2,
-        [pair(tok), pairs(2, tok), pairs(2, tok)],
+        [wide(tok)] + [pl.BlockSpec((2, tok, WIDE), lambda j: (0, 0, j))] * 2,
         [
             shape_of((tok, half_d), bf16),
             shape_of((2, tok, half_d), bf16),
@@ -786,12 +889,20 @@
     clock = Clock()
     clock.mark(own_kv)
     kv_near = Neighbourhood(clock, own_kv, own_kv[:, tok - EDGE :], own_kv[:, :EDGE])
+    w_updown, updown_spec = weight(0)
+    w_down, down_spec = weight(1)
+    w_output, output_spec = weight(4)
     if blocks is None:
-        w_updown, w_down, w_output = (gather(tie(rows, own_kv)) for rows in own_rows(0, 1, 4))
+        w_output_other = other_txt(w_output)
+        other_spec = output_spec
     else:
-        w_updown, w_down, w_output = unpack(shapes[:3], sum(heights[:3]), 0, clock.stage(blocks))
-    w_output_other = other_txt(w_output)
-    clock.mark(w_updown)
+        top = sum(heights[:2])
+        w_output_other = other_txt(clock.stage(blocks)[:, top : top + heights[2]])
+        other_spec = lambda at: pl.BlockSpec((n_img, shapes[2][0], WIDE), lambda j, *_: (0, at(j), 0))
+
+    def step(j):
+        return j
+
     kv_near.second()
     kv_near.third()
     kv_pieces = kv_near.collect()
@@ -799,24 +910,25 @@
     kv_specs = [pairs(2 * c, a.shape[1]) for c, a in zip(PIECE_COUNTS, kv_pieces)]
     id_specs = [whole((tok, 1)), whole((16, tok))]
     text_specs = [pair(text_len), pair(text_len, n_pairs)]
-    mixed_low, self_out, cross_out, lse_self, lse_cross, query_pack = call(
+    own_queries = queries[None]
+    query_near = Neighbourhood(clock, own_queries, own_queries[:, tok - EDGE :], own_queries[:, :EDGE])
+    mixed_low, self_out, cross_out, lse_self, lse_cross, lse_split = call(
         functools.partial(attend_kernel, PIECE_COUNTS, tok),
         (n_pairs,),
         [pair(tok)] + id_specs + text_specs + [pair(1)] + kv_specs,
-        [pair(tok)] * 5 + [whole((1, tok + PACK, half_d))],
+        [pair(tok)] * 5 + [whole((TABLE, 3 * tok))],
         [shape_of((tok, half_d), bf16)]
         + [shape_of((tok, half_d), f32)] * 4
-        + [shape_of((1, tok + PACK, half_d), bf16)],
+        + [shape_of((TABLE, 3 * tok), bf16)],
         (flags, clock.stage(queries), own_ids, piece_ids, all_text, all_text, gate_lanes, *kv_pieces),
         scratch=[
             pltpu.VMEM((PIECES, 2 * tok, tok), f32),
             pltpu.VMEM((2 * tok, LANES), f32),
             pltpu.VMEM((2 * tok, LANES), f32),
             pltpu.VMEM((2 * tok, LANES), f32),
-            pltpu.VMEM((PACK, tok), f32),
+            pltpu.VMEM((TABLE, tok), f32),
         ],
         prefetch=1,
-        vmem=32,
     )
 
     def pack_edges(pack):
@@ -832,45 +944,71 @@
 
     clock.mark(mixed_low)
     mixed_other = other_txt(mixed_low)
-    query_near = Neighbourhood(clock, query_pack, *pack_edges(query_pack))
+    query_near.second()
     mixed_other, mixed_low = clock.stage(mixed_other, mixed_low)
-    attn_out = jnp.dot(mixed_low, w_output, preferred_element_type=f32) + jnp.dot(
-        mixed_other, w_output_other, preferred_element_type=f32
-    )
+    attn_out = call(
+        two_times_kernel,
+        (D // WIDE,),
+        [whole((tok, half_d)), output_spec(step), whole((tok, half_d)), other_spec(step)],
+        [wide(tok)],
+        [shape_of((tok, D), f32)],
+        (mixed_low, w_output, mixed_other, w_output_other),
+        flops=4 * tok * half_d * D,
+        moved=4 * half_d * D,
+    )[0]
+    clock.mark(attn_out)
     hidden = x_float + gate_one * attn_out
     h_normed = rms_norm(hidden)
     normed_two = h_normed * gain_ffn
     ffn_in = (normed_two * (1.0 + scale_two) + shift_two).astype(bf16)
     clock.mark(ffn_in)
-    query_near.second()
-    ffn_in = clock.stage(ffn_in)
-    gate_up = jnp.dot(ffn_in, w_updown, preferred_element_type=f32)
-    gate, up = gate_up[:, :half_ff], gate_up[:, half_ff:]
-    sigmoid = jax.nn.sigmoid(gate)
-    activated = gate * sigmoid
-    hidden_units = (activated * up).astype(bf16)
-    clock.mark(hidden_units)
     query_near.third()
-
+    gate, up, hidden_units, hidden_turned = call(
+        hidden_kernel,
+        (half_ff // WIDE,),
+        [whole((tok, D)), updown_spec(step), updown_spec(lambda j: half_ff // WIDE + j)],
+        [wide(tok)] * 3 + [pl.BlockSpec((WIDE, tok), lambda j: (j, 0))],
+        [shape_of((tok, half_ff), f32)] * 2 + [shape_of((tok, half_ff), bf16), shape_of((half_ff, tok), bf16)],
+        (clock.stage(ffn_in), w_updown, w_updown),
+        flops=4 * tok * D * half_ff,
+        moved=4 * D * half_ff,
+    )
+    clock.mark(hidden_turned)
+    query_pieces = query_near.collect()
     d_out = cotangent.astype(f32)
     d_branch = (d_out * gate_two).astype(bf16)
-    down_sum = GradientSum(clock, tall(hidden_units), d_branch)
-    query_pieces = query_near.collect()
-    d_units = mm(clock.stage(d_branch), w_down, 1, 1)
-    d_gate = (d_units * up * sigmoid * (1.0 + gate * (1.0 - sigmoid))).astype(bf16)
-    d_up = (d_units * activated).astype(bf16)
-    d_gate_up = jnp.concatenate([d_gate, d_up], axis=1)
-    clock.mark(d_gate_up)
-    down_sum.advance()
-    d_gate_up = clock.stage(d_gate_up)
-    d_ffn_part = mm(d_gate_up, w_updown, 1, 1).astype(bf16)
+    down_terms = mm(clock.stage(hidden_turned), d_branch, 1, 0).astype(bf16)
+    clock.mark(down_terms)
+    grad_down = scatter(down_terms)
+    d_gate, d_up = call(
+        hidden_back_kernel,
+        (D // WIDE // 3,),
+        [wide(tok, 3), down_spec(step, 3), whole((tok, half_ff)), whole((tok, half_ff))],
+        [whole((tok, half_ff))] * 2,
+        [shape_of((tok, half_ff), bf16)] * 2,
+        (clock.stage(d_branch), w_down, gate, up),
+        scratch=[pltpu.VMEM((tok, half_ff), f32)],
+        flops=2 * tok * D * half_ff,
+        moved=2 * D * half_ff,
+    )
+    clock.mark(d_gate, d_up)
+    d_gate_up = clock.stage(jnp.concatenate([d_gate, d_up], axis=1))
+    d_ffn_part = call(
+        times_transposed_kernel,
+        (2 * half_ff // WIDE // 4,),
+        [wide(tok, 4), updown_spec(step, 4)],
+        [whole((tok, D))],
+        [shape_of((tok, D), bf16)],
+        (d_gate_up, w_updown),
+        scratch=[pltpu.VMEM((tok, D), f32)],
+        flops=4 * tok * D * half_ff,
+        moved=4 * D * half_ff,
+    )[0]
     clock.mark(d_ffn_part)
     d_ffn_other = other_txt(d_ffn_part)
-    ffn_tall = tall(ffn_in)
-    gate_sum = GradientSum(clock, ffn_tall, d_gate)
-    up_sum = GradientSum(clock, ffn_tall, d_up)
-    gate_sum.receive()
-    up_sum.receive()
+    updown_terms = mm(clock.stage(ffn_in), d_gate_up, 0, 0).astype(bf16)
+    clock.mark(updown_terms)
+    grad_updown = scatter(updown_terms)
     d_ffn_part, d_ffn_other = clock.stage(d_ffn_part, d_ffn_other)
     d_ffn_in = d_ffn_part.astype(f32) + d_ffn_other.astype(f32)
     d_scale_two = d_ffn_in * normed_two
@@ -881,25 +1019,35 @@
     clock.mark(d_attn)
     grad_pack, d_cross_low, d_gate_lanes = call(
         functools.partial(mixed_back_kernel, tok),
-        (n_pairs,),
-        [whole((tok, D)), pl.BlockSpec((LANES, D), lambda j: (j, 0)), pair(tok), pair(tok), pair(1)],
-        [whole((1, tok + PACK, half_d)), pair(tok), pair(1)],
+        (D // WIDE // 3,),
+        [wide(tok, 3), output_spec(step, 3), whole((tok, half_d)), whole((tok, half_d)), whole((1, half_d)), whole((TABLE, 3 * tok))],
+        [whole((1, tok + PACK, half_d)), whole((tok, half_d)), whole((1, half_d))],
         [
             shape_of((1, tok + PACK, half_d), bf16),
             shape_of((tok, half_d), bf16),
             shape_of((1, half_d), f32),
         ],
-        (clock.stage(d_attn), w_output, self_out, cross_out, gate_lanes),
-        scratch=[pltpu.VMEM((PACK, tok), f32)],
+        (clock.stage(d_attn), w_output, self_out, cross_out, gate_lanes, lse_split),
+        scratch=[pltpu.VMEM((tok, half_d), f32)],
         flops=2 * tok * D * half_d,
-        moved=4 * D * half_d,
+        moved=2 * D * half_d,
     )
     clock.mark(grad_pack)
     grad_near = Neighbourhood(clock, grad_pack, *pack_edges(grad_pack))
-    down_sum.receive()
-    gate_sum.advance(received=True)
+    branch_part = call(
+        times_kernel,
+        (D // WIDE,),
+        [whole((tok, half_ff)), down_spec(step)],
+        [wide(tok)],
+        [shape_of((tok, D), f32)],
+        (clock.stage(hidden_units), w_down),
+        flops=2 * tok * D * half_ff,
+        moved=2 * D * half_ff,
+    )[0]
+    clock.mark(branch_part)
+    branch_other = other_txt(branch_part)
+    output_sum = GradientSum(clock, tall(mixed_low), d_attn)
     grad_near.second()
-    down_sum.advance(received=True)
     turn_specs = [whole((1, LANES)), whole((tok, LANES)), whole((tok, LANES))]
 
     def query_back(first, count, d_cross):
@@ -939,27 +1087,25 @@
     first_half = query_back(0, head_half, clock.stage(d_cross_low))
     clock.mark(first_half[0])
     grad_near.third()
-    up_sum.advance(received=True)
-    output_sum = GradientSum(clock, tall(mixed_low), d_attn)
+    output_sum.advance()
     grad_pieces = grad_near.collect()
     second_half = query_back(head_half, n_pairs - head_half, clock.stage(d_cross_low))
     clock.mark(second_half[0])
     d_query_raw, d_gain_query, d_text_key, d_text_value = (
         jnp.concatenate(halves, axis=1) for halves in zip(first_half, second_half)
     )
-    gate_sum.advance()
+    attn_tall = tall(attn_in)
     text_sum = TermSum(clock, jnp.concatenate([d_text_key, d_text_value], axis=1), z_first)
-    down_sum.advance()
+    query_sum = GradientSum(clock, attn_tall, d_query_raw)
+    output_sum.advance()
     text_sum.advance()
-    attn_tall = tall(attn_in)
-
-    def pack_specs(arrays):
-        views = [pairs(c, a.shape[1] - PACK) for c, a in zip(PIECE_COUNTS, arrays)]
-        rows = [
-            pl.BlockSpec((c, PACK, half_d), lambda j, *_, at=(a.shape[1] - PACK) // PACK: (0, at, 0))
-            for c, a in zip(PIECE_COUNTS, arrays)
-        ]
-        return views + rows
+    branch_other = clock.stage(branch_other)
+
+    query_specs = [pairs(c, a.shape[1]) for c, a in zip(PIECE_COUNTS, query_pieces)]
+    pack_specs = [pairs(c, a.shape[1] - PACK) for c, a in zip(PIECE_COUNTS, grad_pieces)] + [
+        pl.BlockSpec((c, PACK, half_d), lambda j, *_, at=(a.shape[1] - PACK) // PACK: (0, at, 0))
+        for c, a in zip(PIECE_COUNTS, grad_pieces)
+    ]
 
     d_key_raw, d_gain_key, d_value = call(
         functools.partial(key_back_kernel, PIECE_COUNTS, tok),
@@ -968,8 +1114,8 @@
         + id_specs
         + [pairs(1, tok, 1)]
         + turn_specs
-        + pack_specs(query_pieces)
-        + pack_specs(grad_pieces),
+        + query_specs
+        + pack_specs,
         [pair(tok), pair(1), pair(tok)],
         [
             shape_of((tok, half_d), bf16),
@@ -978,41 +1124,37 @@
         ],
         (
             flags, clock.stage(own_kv), own_ids, piece_ids, raw_qk, gain_key_pair,
-            cosine, sine, *query_pieces, *query_pieces, *grad_pieces, *grad_pieces,
+            cosine, sine, *query_pieces, *grad_pieces, *grad_pieces,
         ),
         scratch=[pltpu.VMEM((2 * tok, LANES), f32)] * 2,
         prefetch=1,
     )
     clock.mark(d_value)
-    query_sum = GradientSum(clock, attn_tall, d_query_raw)
     key_value_sum = GradientSum(clock, attn_tall, jnp.concatenate([d_key_raw, d_value], axis=1))
-    d_query_raw, d_key_raw, d_value = clock.stage(d_query_raw, d_key_raw, d_value)
-    d_projected = jnp.concatenate([d_query_raw, d_key_raw, d_value], axis=1)
-    d_attn_part = mm(d_projected, w_project, 1, 1).astype(bf16)
+    d_projected = clock.stage(jnp.concatenate([d_query_raw, d_key_raw, d_value], axis=1))
+    d_attn_part = call(
+        times_transposed_kernel,
+        (thirds,),
+        [wide(tok, 3), project_spec(step, 3)],
+        [whole((tok, D))],
+        [shape_of((tok, D), bf16)],
+        (d_projected, w_project),
+        scratch=[pltpu.VMEM((tok, D), f32)],
+        flops=6 * tok * D * half_d,
+        moved=6 * D * half_d,
+    )[0]
     clock.mark(d_attn_part)
     d_attn_other = other_txt(d_attn_part)
+    query_sum.advance()
+    key_value_sum.advance()
+    text_sum.advance()
     output_sum.advance()
-    query_sum.advance()
-    text_sum.advance()
-    up_sum.advance()
-    key_value_sum.advance()
-    gate_sum.advance()
-    branch_part = jnp.dot(clock.stage(hidden_units), w_down, preferred_element_type=f32)
-    clock.mark(branch_part)
     d_attn_other = clock.stage(d_attn_other)
     d_attn_in = d_attn_part.astype(f32) + d_attn_other.astype(f32)
-    branch = branch_part + other_txt(branch_part)
+    branch = branch_part + branch_other
     block_out = hidden + gate_two * branch
     d_gate_two = d_out * branch
     d_gate_one = d_hidden * attn_out
-
-    text_own = text_sum.finish()
-    d_text_scaled = text_own[:, :half_d].reshape(text_shape)
-    d_gain_text = jnp.sum(d_text_scaled * text_normed, axis=(0, 1))
-    d_text_raw = rms_back(text_raw, d_text_scaled * gain_text).reshape(text_rows, half_d)
-    d_text_proj = gather_doubling(jnp.concatenate([d_text_raw, text_own[:, half_d:]], axis=1).astype(bf16))
-    grad_text = mm(text_columns, d_text_proj, 0, 0)
-
     d_scale_one = d_attn_in * normed_one
     d_normed_one = d_attn_in * (1.0 + scale_one)
     d_gain_attn = jnp.sum(d_normed_one * x_normed, axis=0)
@@ -1043,36 +1185,42 @@
     )
     small_count = small_terms.shape[0]
     small_row = jnp.pad(small_terms, (0, d_mod.shape[1] - small_count))[None]
-    sums = sum_over_img(jnp.concatenate([d_mod, small_row], axis=0))
+    small_sum = SmallSum(clock, jnp.concatenate([d_mod, small_row], axis=0))
+    query_sum.advance()
+    text_sum.advance()
+    small_sum.advance()
+    key_value_sum.advance()
+
+    text_own = text_sum.finish()
+    d_text_scaled = text_own[:, :half_d].reshape(text_shape)
+    d_gain_text = jnp.sum(d_text_scaled * text_normed, axis=(0, 1))
+    d_text_raw = rms_back(text_raw, d_text_scaled * gain_text).reshape(text_rows, half_d)
+    d_text_proj = gather_doubling(jnp.concatenate([d_text_raw, text_own[:, half_d:]], axis=1).astype(bf16))
+    grad_text = mm(text_columns, d_text_proj, 0, 0)
+
+    small_sum.advance()
+    query_sum.advance()
+    key_value_sum.advance()
+    sums = small_sum.finish()
     d_mod = sums[:samples]
     small_row = sums[samples:, :]
     small_grad = (small_row + other_txt(small_row))[0, :small_count]
     grad_modulate = lax.dot_general(silu_own.astype(f32), d_mod, (((0,), (0,)), ((), ())), precision=HIGH)
 
-    pending = [down_sum, gate_sum, output_sum, query_sum, up_sum, key_value_sum]
+    pending = [output_sum, query_sum, key_value_sum]
     while pending:
         for one in list(pending):
-            one.result = one.advance()
-            if one.level == len(one.order):
+            if one.result is None:
+                one.result = one.advance()
+            if one.result is not None:
                 pending.remove(one)
-    grad_down, grad_gate, grad_output, grad_query, grad_up, grad_key_value = (
-        one.result for one in (down_sum, gate_sum, output_sum, query_sum, up_sum, key_value_sum)
-    )
-    grads = [grad_gate, grad_up, grad_down, grad_query, grad_key_value, grad_text, grad_output, grad_modulate]
-    places = [
-        (starts[0], 0, 2 * half_ff),
-        (starts[0], half_ff, 2 * half_ff),
-        (starts[1], 0, D),
-        (starts[2], 0, 3 * half_d),
-        (starts[2], half_d, 3 * half_d),
-        (starts[3], 0, 2 * half_d),
-        (starts[4], 0, D),
-        (starts[5], 0, 6 * half_d),
-    ]
+    grads = [grad_updown, grad_down, query_sum.result, grad_text, output_sum.result, grad_modulate, key_value_sum.result]
+    places = [(start, 0, columns) for start, (_, columns) in zip(starts, tables)]
+    places.append((starts[2], half_d, 3 * half_d))
     reduced, squares = pl.pallas_call(
         functools.partial(flatten_kernel, places),
         out_shape=[shape_of((lines, LANES), f32), shape_of((1, LANES), f32)],
-        compiler_params=pltpu.CompilerParams(vmem_limit_bytes=32 * MIB),
+        compiler_params=pltpu.CompilerParams(vmem_limit_bytes=58 * MIB),
     )(*grads)
 
     last = sum_over_all(jnp.concatenate([squares, jnp.pad(d_gain_text, (0, LANES - HD))[None]], axis=0))
@@ -1080,7 +1228,7 @@
     grad_square = jnp.sum(last[0]) + jnp.sum(small_grad * small_grad)
     clip_factor = MAX_NORM / jnp.maximum(jnp.sqrt(grad_square), MAX_NORM)
 
-    block = math.gcd(lines, 512)
+    block = math.gcd(lines, 1024)
     line_spec = pl.BlockSpec((block, LANES), lambda i: (i, 0))
     as_lines = (lines, LANES)
     updated = call(
@@ -1090,7 +1238,6 @@
         [line_spec] * 5,
         [shape_of(as_lines, f32)] * 4 + [shape_of(as_lines, bf16)],
         (clip_factor.reshape(1), reduced, *(a.reshape(as_lines) for a in (moment_one, moment_two, master, average))),
-        vmem=52,
         flops=20 * lines * LANES,
         moved=38 * lines * LANES,
     )

time: 860 us -> 758 us (0.88)
  waiting for transfers between devices: 294 us -> 247 us
  matrix products: 96.2 us -> 53.2 us
  Pallas kernels: 150 us -> 178 us
  local copies, waits for them, and re-layouts: 97.3 us -> 73 us
  starting transfers between devices: 134 us -> 111 us
  other arithmetic: 52.9 us -> 68.6 us
    ppermute x61 -> x49, waiting for transfers between devices: 206 us -> 146 us  [crossed(): return lax.ppermute(x, 'img', [(i, i ^ bit) for i in range(count)])]
    unnamed x397 -> x223, local copies, waits for them, and re-layouts: 50.3 us -> 19 us
    dot_general x22 -> x12, matrix products: 64.1 us -> 33 us  [mm(): lax.dot_general(a, b, (((on_a,), (on_b,)), ((), ())), preferred_element_t...]
    ppermute x61 -> x49, starting transfers between devices: 79.4 us -> 51.9 us  [crossed(): return lax.ppermute(x, 'img', [(i, i ^ bit) for i in range(count)])]
    ppermute x12, waiting for transfers between devices: 16.2 us -> 35.5 us  [shifted(): lax.ppermute(x, 'img', [(i + by, i) for i in range(count) if 0 <= i + by...]
    dot_general x4 -> x0, matrix products: 18.8 us -> none  [the longest x1 6.43 us: on_device(): gate_up = jnp.dot(ffn_in, w_updown, preferred_element_type=f32)]
    pallas_call x9 -> x13, Pallas kernels: 145 us -> 161 us  [call(): pl.pallas_call(kernel, grid_spec=pltpu.PrefetchScalarGridSpec(num_scalar_...]
  transfers between devices with their start and end apart: 86 -> 76, of which waited for: 35 -> 28; matrix products, arithmetic and copies ran while one was open for 19% -> 21% of each run, Pallas kernels for 12% -> 18%
where the time goes in v4:
time: 758 us; the launch traced here: 749 us
  waiting for transfers between devices  247 us (33%)
  Pallas kernels  178 us (23%)
  starting transfers between devices  111 us (15%)
  local copies, waits for them, and re-layouts  73 us (10%)
  other arithmetic  68.6 us (9%)
  matrix products  53.2 us (7%)
  between operations  18.3 us (2%)
    pallas_call x13, Pallas kernels, call(): pl.pallas_call(kernel, grid_spec=pltpu.PrefetchScalarGridSpec(num_scalar_...  161 us
    ppermute x49, waiting for transfers between devices, crossed(): return lax.ppermute(x, 'img', [(i, i ^ bit) for i in range(count)])  146 us
    ppermute x49, starting transfers between devices, crossed(): return lax.ppermute(x, 'img', [(i, i ^ bit) for i in range(count)])  51.9 us
    all_gather x1, waiting for transfers between devices, gather(): return lax.all_gather(rows, 'img', axis=0, tiled=True)  51 us
    ppermute x12, starting transfers between devices, shifted(): lax.ppermute(x, 'img', [(i + by, i) for i in range(count) if 0 <= i + by...  39.6 us
    ppermute x12, waiting for transfers between devices, shifted(): lax.ppermute(x, 'img', [(i + by, i) for i in range(count) if 0 <= i + by...  35.5 us
    dot_general x12, matrix products, mm(): lax.dot_general(a, b, (((on_a,), (on_b,)), ((), ())), preferred_element_t...  33 us
    unnamed x223, local copies, waits for them, and re-layouts  19 us
  transfers between devices with their start and end apart: 76, of which 28 were waited for; matrix products, arithmetic and copies ran while one was open for 21% of the time, Pallas kernels for 18%

profile of v4, /device:TPU:0, one launch (start us, length us, event | category | flops | bytes accessed | tf_op | source)
XLA Modules:
  0.0 748.7 jit_solution(5198654791366169068)
XLA Ops:
  23.1 7.4 all-to-all-start
  51.2 10.5 %collective-permute-done.1 = f32[16,4608]{1,0:T(8,128)S(1)} collective-permute-done((f32[16,4608]{1,0:T(8,128)S(1)}, f32[16,4608]{1,0:T(8,128)S(1)}, u32[]{:S(2)}, u32[]{:S(2)}) %collective-permute-start.1) | collective-permute-done | bytes 294944 | tf_op jit(solution)/shard_map/ppermute | solution.py:494
  62.8 17.8 %collective-permute-done.2 = f32[16,4608]{1,0:T(8,128)S(1)} collective-permute-done((f32[16,4608]{1,0:T(8,128)S(1)}, f32[16,4608]{1,0:T(8,128)S(1)}, u32[]{:S(2)}, u32[]{:S(2)}) %collective-permute-start.2) | collective-permute-done | bytes 294944 | tf_op jit(solution)/shard_map/ppermute | solution.py:494
  83.7 24.0 %collective-permute-done.3 = f32[16,4608]{1,0:T(8,128)S(1)} collective-permute-done((f32[16,4608]{1,0:T(8,128)S(1)}, f32[16,4608]{1,0:T(8,128)S(1)}, u32[]{:S(2)}, u32[]{:S(2)}) %collective-permute-start.3) | collective-permute-done | bytes 294944 | tf_op jit(solution)/shard_map/ppermute | solution.py:494
  137.3 7.1 collective-permute-done.11
  147.4 51.0 %all-gather.3.cloned.1.call-done = bf16[55296,256]{1,0:T(8,128)(2,1)} async-done(((bf16[3456,256]{1,0:T(8,128)(2,1)}), bf16[55296,256]{1,0:T(8,128)(2,1)}) %all-gather.3.cloned.1.call-update) | async-done | bytes 28311568 | tf_op jit(solution)/shard_map/all_gather | solution.py:770
  211.9 12.9 %collective-permute-done.15.rest_3_ = bf16[2,256,768]{2,1,0:T(8,128)(2,1)S(1)} collective-permute-done((bf16[2,256,768]{2,1,0:T(8,128)(2,1)}, bf16[2,256,768]{2,1,0:T(8,128)(2,1)S(1)}, u32[]{:S(2)}, u32[]{:S(2)}) %collective-permute-start.15) | collective-permute-done | bytes 786464 | tf_op jit(solution)/shard_map/ppermute | solution.py:489
  241.5 10.6 %collective-permute-done.17.rest_6_ = bf16[2,256,768]{2,1,0:T(8,128)(2,1)S(1)} collective-permute-done((bf16[2,256,768]{2,1,0:T(8,128)(2,1)S(1)}, bf16[2,256,768]{2,1,0:T(8,128)(2,1)S(1)}, u32[]{:S(2)}, u32[]{:S(2)}) %collective-permute-start.17) | collective-permute-done | bytes 786464 | tf_op jit(solution)/shard_map/ppermute | solution.py:489
  258.3 7.2 collective-permute-start.24
  276.6 23.2 %shard_map.224 = (bf16[256,768]{1,0:T(8,128)(2,1)}, f32[256,768]{1,0:T(8,128)}, f32[256,768]{1,0:T(8,128)}, f32[256,768]{1,0:T(8,128)}, f32[256,768]{1,0:T(8,128)}, /*index=5*/bf16[16,768]{1,0:T(8,128)(2,1)}) custom-call(s32[13]{0:T(128)} %convert_element_type.245.flag_ref, bf16[256,768]{1,0:T(8,128)(2,1)} %get-tuple-element.138.q_ref, ...), custom_call_target="tpu_custom_call" | custom-call | tf_op jit(solution)/shard_map/pallas_call | solution.py:460
  305.4 9.8 %collective-permute-start.27 = (bf16[1,256,768]{2,1,0:T(8,128)(2,1)S(1)}, bf16[1,256,768]{2,1,0:T(8,128)(2,1)S(1)}, u32[]{:S(2)}, u32[]{:S(2)}) collective-permute-start(bf16[1,256,768]{2,1,0:T(8,128)(2,1)S(1)} %collective-permute-done.22.rest_1_), channel_id=1, source_target_pairs={{0,8},{2,10},{4,12},{6,14},{8,16},{10,18},{12,20},{14,22},{16,24},... | collective-permute-start | bytes 1179656 | tf_op jit(solution)/shard_map/ppermute | solution.py:489
  328.6 11.2 %shard_map.226 = (f32[256,2048]{1,0:T(8,128)}, f32[256,2048]{1,0:T(8,128)}, bf16[256,2048]{1,0:T(8,128)(2,1)}, bf16[2048,256]{1,0:T(8,128)(2,1)}) custom-call(bf16[256,1536]{1,0:T(8,128)(2,1)} %get-tuple-element.161.b_ref, bf16[16,3456,256]{2,1,0:T(8,128)(2,1)} %bitcast.274, bf16[16,3456,256]{2,1,0:T(8,128)(2,1)} %bitcast.275), custom_call_target="tpu_custom_call" | custom-call | flops 3221225472 | bytes 12582912 | tf_op jit(solution)/shard_map/pallas_call | solution.py:460
  349.7 8.2 %shard_map.227 = (bf16[256,2048]{1,0:T(8,128)(2,1)}, bf16[256,2048]{1,0:T(8,128)(2,1)}) custom-call(bf16[256,1536]{1,0:T(8,128)(2,1)} %copy-done.29, bf16[16,3456,256]{2,1,0:T(8,128)(2,1)} %bitcast.276, f32[256,2048]{1,0:T(8,128)} %get-tuple-element.156.gate_ref, f32[256,2048]{1,0:T(8,128)} %get-tuple-element.157.up_ref), custom_call_target="tpu_custom_call" | custom-call | flops 1610612736 | bytes 6291456 | tf_op jit(solution)/shard_map/pallas_call | solution.py:460
  361.1 9.4 %shard_map.228 = bf16[256,1536]{1,0:T(8,128)(2,1)} custom-call(bf16[256,4096]{1,0:T(8,128)(2,1)} %pad_maximum_fusion.a_ref, bf16[16,3456,256]{2,1,0:T(8,128)(2,1)} %bitcast.277), custom_call_target="tpu_custom_call" | custom-call | flops 3221225472 | bytes 12582912 | tf_op jit(solution)/shard_map/pallas_call | solution.py:460
  377.7 12.8 %collective-permute-done.31 = bf16[256,1536]{1,0:T(8,128)(2,1)} collective-permute-done((bf16[256,1536]{1,0:T(8,128)(2,1)}, bf16[256,1536]{1,0:T(8,128)(2,1)}, u32[]{:S(2)}, u32[]{:S(2)}) %collective-permute-start.31) | collective-permute-done | bytes 786464 | tf_op jit(solution)/shard_map/ppermute | solution.py:498
  408.3 7.2 shard_map.230
  432.5 16.1 %shard_map.231 = (bf16[256,384]{1,0:T(8,128)(2,1)}, f32[1,384]{1,0:T(1,128)}, f32[256,384]{1,0:T(8,128)}, f32[256,384]{1,0:T(8,128)}) custom-call(s32[13]{0:T(128)} %convert_element_type.245.flag_ref, bf16[256,768]{1,0:T(8,128)(2,1)} %get-tuple-element.138.q_ref, s32[256,1]{1,0:T(8,128)} %copy.265.own_ids_ref, s32[16,256]{1,0:T(8,128)} %concatenate.173.ids_ref, ...), custom_call_target="tpu_custom_call" | custom-call | tf_op jit(solution)/shard_map/pallas_call | solution.py:460
  467.0 16.6 %shard_map.232 = (bf16[256,384]{1,0:T(8,128)(2,1)}, f32[1,384]{1,0:T(1,128)}, f32[256,384]{1,0:T(8,128)}, f32[256,384]{1,0:T(8,128)}) custom-call(s32[13]{0:T(128)} %convert_element_type.245.flag_ref, bf16[256,768]{1,0:T(8,128)(2,1)} %get-tuple-element.138.q_ref, s32[256,1]{1,0:T(8,128)} %copy.265.own_ids_ref, s32[16,256]{1,0:T(8,128)} %concatenate.173.ids_ref, ...), custom_call_target="tpu_custom_call" | custom-call | tf_op jit(solution)/shard_map/pallas_call | solution.py:460
  490.9 20.7 %shard_map.233 = (bf16[256,768]{1,0:T(8,128)(2,1)}, f32[1,768]{1,0:T(1,128)}, bf16[256,768]{1,0:T(8,128)(2,1)}) custom-call(s32[13]{0:T(128)} %convert_element_type.245.flag_ref, bf16[2,256,768]{2,1,0:T(8,128)(2,1)} %get-tuple-element.197.rest_0_.kv_ref, s32[256,1]{1,0:T(8,128)} %copy.265.own_ids_ref, s32[16,256]{1,0:T(8,128)} %concatenate.173.ids_ref, ...), custom_call_target="tpu_custom_call" | custom-call | tf_op jit(solution)/shard_map/pallas_call | solution.py:460
  519.0 7.8 %collective-permute-start.45 = (bf16[2,48,1536]{2,1,0:T(8,128)(2,1)}, bf16[2,48,1536]{2,1,0:T(8,128)(2,1)}, u32[]{:S(2)}, u32[]{:S(2)}) collective-permute-start(bf16[2,48,1536]{2,1,0:T(8,128)(2,1)} %fusion.53), channel_id=1, source_target_pairs={{0,8},{2,10},{4,12},{6,14},{8,0},{10,2},{12,4},{14,6},{16,24},{18,... | collective-permute-start | bytes 884744 | tf_op jit(solution)/shard_map/ppermute | solution.py:494
  586.8 13.5 %collective-permute-done.55 = bf16[4,96,1536]{2,1,0:T(8,128)(2,1)} collective-permute-done((bf16[4,96,1536]{2,1,0:T(8,128)(2,1)}, bf16[4,96,1536]{2,1,0:T(8,128)(2,1)}, u32[]{:S(2)}, u32[]{:S(2)}) %collective-permute-start.55) | collective-permute-done | bytes 1179680 | tf_op jit(solution)/shard_map/ppermute | solution.py:494
  647.0 28.6 %collective-permute-done.60 = f32[17,4608]{1,0:T(8,128)S(1)} collective-permute-done((f32[17,4608]{1,0:T(8,128)S(1)}, f32[17,4608]{1,0:T(8,128)S(1)}, u32[]{:S(2)}, u32[]{:S(2)}) %collective-permute-start.60) | collective-permute-done | bytes 313376 | tf_op jit(solution)/shard_map/ppermute | solution.py:494
  681.7 7.5 %shard_map.235 = (f32[12288,128]{1,0:T(8,128)}, f32[1,128]{1,0:T(1,128)}) custom-call(bf16[96,4096]{1,0:T(8,128)(2,1)} %reduce-scatter.3.cloned.1.call-done.refs_0_, bf16[128,1536]{1,0:T(8,128)(2,1)} %reduce-scatter.5.cloned.1.call-done.refs_1_, f32[96,768]{1,0:T(8,128)} %add_bitcast_fusion.2.refs_2_, f32[256,1536]{1,0:T(8,128)} %convolution_bitcast_fusion.refs_3_, ...), custom_call_target="tpu_custom_call" | custom-call | tf_op jit(solution)/shard_map/pallas_call | solution.py:1220
  711.2 23.2 %shard_map.236 = (f32[12288,128]{1,0:T(8,128)}, f32[12288,128]{1,0:T(8,128)}, f32[12288,128]{1,0:T(8,128)}, f32[12288,128]{1,0:T(8,128)}, bf16[12288,128]{1,0:T(8,128)(2,1)}) custom-call(f32[1]{0:T(128)} %bitcast.121.clip_ref, f32[12288,128]{1,0:T(8,128)} %get-tuple-element.232.g_ref, f32[12288,128]{1,0:T(8,128)} %bitcast.300, f32[12288,128]{1,0:T(8,128)} %bitcast.301, ...), custom_call_target="tpu_custom_call" | custom-call | flops 31457280 | bytes 59768832 | tf_op jit(solution)/shard_map/pallas_call | solution.py:460
  (588 shorter events, 366.3 us)
Async XLA Ops:
  7.2 191.2 %all-gather.3.cloned.1.call-start = ((), (), s32[]{:S(2)}) async-start(), calls=%async_computation.5 | async-start | bytes 30081024 | tf_op jit(solution)/shard_map/all_gather | solution.py:770
  30.5 651.1 %reduce-scatter.5.cloned.1.call-start = ((), (), s32[]{:S(2)}) async-start(), calls=%async_computation.4 | async-start | bytes 6684672 | tf_op jit(solution)/shard_map/reduce_scatter | solution.py:767
  47.8 35.2 %collective-permute-start.6 = (f32[4,16,1536]{2,1,0:T(8,128)S(1)}, f32[4,16,1536]{2,1,0:T(8,128)S(1)}, u32[]{:S(2)}, u32[]{:S(2)}) collective-permute-start(f32[4,16,1536]{2,1,0:T(8,128)S(1)} %bitcast.342), channel_id=1, source_target_pairs={{0,8},{2,10},{4,12},{6,14},{8,0},{10,2},{12,4},{14,6},{16,24},{18,... | collective-permute-start | bytes 1179656 | tf_op jit(solution)/shard_map/ppermute | solution.py:494
  80.6 27.1 %collective-permute-start.3 = (f32[16,4608]{1,0:T(8,128)S(1)}, f32[16,4608]{1,0:T(8,128)S(1)}, u32[]{:S(2)}, u32[]{:S(2)}) collective-permute-start(f32[16,4608]{1,0:T(8,128)S(1)} %add.415), channel_id=1, source_target_pairs={{0,16},{2,18},{4,20},{6,22},{8,24},{10,26},{12,28},{14,30},{16,0},... | collective-permute-start | bytes 884744 | tf_op jit(solution)/shard_map/ppermute | solution.py:494
  83.1 32.2 %collective-permute-start.7 = (f32[2,16,1536]{2,1,0:T(8,128)S(1)}, f32[2,16,1536]{2,1,0:T(8,128)S(1)}, u32[]{:S(2)}, u32[]{:S(2)}) collective-permute-start(f32[2,16,1536]{2,1,0:T(8,128)S(1)} %dynamic-slice_bitcast_fusion.3), channel_id=1, source_target_pairs={{0,16},{2,18},{4,20},{6,22},{8,24},{10,26},{12,28},{14,30},{16,0},... | collective-permute-start | bytes 589832 | tf_op jit(solution)/shard_map/ppermute | solution.py:494
  240.0 76.5 %collective-permute-start.25 = (bf16[16,288,256]{2,1,0:T(8,128)(2,1)}, bf16[16,288,256]{2,1,0:T(8,128)(2,1)}, u32[]{:S(2)}, u32[]{:S(2)}) collective-permute-start(bf16[16,288,256]{2,1,0:T(8,128)(2,1)} %slice.180), channel_id=1, source_target_pairs={{0,1},{1,0},{2,3},{3,2},{4,5},{5,4},{6,7},{7,6},{8,9},{9,8},{10,11... | collective-permute-start | bytes 7077896 | tf_op jit(solution)/shard_map/ppermute | solution.py:498
  258.3 43.1 %collective-permute-start.24 = (bf16[1,256,768]{2,1,0:T(8,128)(2,1)}, bf16[1,256,768]{2,1,0:T(8,128)(2,1)S(1)}, u32[]{:S(2)}, u32[]{:S(2)}) collective-permute-start(bf16[1,256,768]{2,1,0:T(8,128)(2,1)} %bitcast.51.rest_0_), channel_id=1, source_target_pairs={{0,8},{2,10},{4,12},{6,14},{8,16},{10,18},{12,20},{14,22},{16,24},... | collective-permute-start | bytes 1179656 | tf_op jit(solution)/shard_map/ppermute | solution.py:489
  265.5 35.9 %collective-permute-start.23 = (bf16[1,256,768]{2,1,0:T(8,128)(2,1)}, bf16[1,256,768]{2,1,0:T(8,128)(2,1)S(1)}, u32[]{:S(2)}, u32[]{:S(2)}) collective-permute-start(bf16[1,256,768]{2,1,0:T(8,128)(2,1)} %bitcast.51.rest_0_), channel_id=1, source_target_pairs={{8,0},{10,2},{12,4},{14,6},{16,8},{18,10},{20,12},{22,14},{24,16},... | collective-permute-start | bytes 1179656 | tf_op jit(solution)/shard_map/ppermute | solution.py:489
  267.3 34.1 %collective-permute-start.22 = (bf16[1,256,768]{2,1,0:T(8,128)(2,1)}, bf16[1,256,768]{2,1,0:T(8,128)(2,1)S(1)}, u32[]{:S(2)}, u32[]{:S(2)}) collective-permute-start(bf16[1,256,768]{2,1,0:T(8,128)(2,1)} %bitcast.51.rest_0_), channel_id=1, source_target_pairs={{0,4},{2,6},{4,0},{6,2},{8,12},{10,14},{12,8},{14,10},{16,20},{18,... | collective-permute-start | bytes 1179656 | tf_op jit(solution)/shard_map/ppermute | solution.py:494
  346.5 335.2 %reduce-scatter.3.cloned.1.call-start = ((), (), s32[]{:S(2)}) async-start(), calls=%async_computation.3 | async-start | bytes 13369344 | tf_op jit(solution)/shard_map/reduce_scatter | solution.py:767
  422.7 33.2 %collective-permute-start.41 = (bf16[8,48,1536]{2,1,0:T(8,128)(2,1)}, bf16[8,48,1536]{2,1,0:T(8,128)(2,1)}, u32[]{:S(2)}, u32[]{:S(2)}) collective-permute-start(bf16[8,48,1536]{2,1,0:T(8,128)(2,1)} %convolution_convert_fusion.4), channel_id=1, source_target_pairs={{0,2},{2,0},{4,6},{6,4},{8,10},{10,8},{12,14},{14,12},{16,18},{18,... | collective-permute-start | bytes 3538952 | tf_op jit(solution)/shard_map/ppermute | solution.py:494
  451.1 78.7 %collective-permute-start.32 = (f32[256,1536]{1,0:T(8,128)}, f32[256,1536]{1,0:T(8,128)}, u32[]{:S(2)}, u32[]{:S(2)}) collective-permute-start(f32[256,1536]{1,0:T(8,128)} %shard_map.230), channel_id=1, source_target_pairs={{0,1},{1,0},{2,3},{3,2},{4,5},{5,4},{6,7},{7,6},{8,9},{9,8},{10,11... | collective-permute-start | bytes 4718600 | tf_op jit(solution)/shard_map/ppermute | solution.py:498
  458.1 29.7 %collective-permute-start.43 = (bf16[4,48,1536]{2,1,0:T(8,128)(2,1)}, bf16[4,48,1536]{2,1,0:T(8,128)(2,1)}, u32[]{:S(2)}, u32[]{:S(2)}) collective-permute-start(bf16[4,48,1536]{2,1,0:T(8,128)(2,1)} %fusion.1), channel_id=1, source_target_pairs={{0,4},{2,6},{4,0},{6,2},{8,12},{10,14},{12,8},{14,10},{16,20},{18,... | collective-permute-start | bytes 1769480 | tf_op jit(solution)/shard_map/ppermute | solution.py:494
  515.0 35.0 %collective-permute-start.47 = (bf16[8,96,1536]{2,1,0:T(8,128)(2,1)}, bf16[8,96,1536]{2,1,0:T(8,128)(2,1)}, u32[]{:S(2)}, u32[]{:S(2)}) collective-permute-start(bf16[8,96,1536]{2,1,0:T(8,128)(2,1)} %convolution_convert_fusion.3), channel_id=1, source_target_pairs={{0,2},{2,0},{4,6},{6,4},{8,10},{10,8},{12,14},{14,12},{16,18},{18,... | collective-permute-start | bytes 7077896 | tf_op jit(solution)/shard_map/ppermute | solution.py:494
  518.3 27.0 %collective-permute-start.48 = (bf16[8,96,768]{2,1,0:T(8,128)(2,1)}, bf16[8,96,768]{2,1,0:T(8,128)(2,1)}, u32[]{:S(2)}, u32[]{:S(2)}) collective-permute-start(bf16[8,96,768]{2,1,0:T(8,128)(2,1)} %convolution_convert_fusion.5), channel_id=1, source_target_pairs={{0,2},{2,0},{4,6},{6,4},{8,10},{10,8},{12,14},{14,12},{16,18},{18,... | collective-permute-start | bytes 3538952 | tf_op jit(solution)/shard_map/ppermute | solution.py:494
  519.0 37.7 %collective-permute-start.45 = (bf16[2,48,1536]{2,1,0:T(8,128)(2,1)}, bf16[2,48,1536]{2,1,0:T(8,128)(2,1)}, u32[]{:S(2)}, u32[]{:S(2)}) collective-permute-start(bf16[2,48,1536]{2,1,0:T(8,128)(2,1)} %fusion.53), channel_id=1, source_target_pairs={{0,8},{2,10},{4,12},{6,14},{8,0},{10,2},{12,4},{14,6},{16,24},{18,... | collective-permute-start | bytes 884744 | tf_op jit(solution)/shard_map/ppermute | solution.py:494
  552.8 47.4 %collective-permute-start.55 = (bf16[4,96,1536]{2,1,0:T(8,128)(2,1)}, bf16[4,96,1536]{2,1,0:T(8,128)(2,1)}, u32[]{:S(2)}, u32[]{:S(2)}) collective-permute-start(bf16[4,96,1536]{2,1,0:T(8,128)(2,1)} %fusion), channel_id=1, source_target_pairs={{0,4},{2,6},{4,0},{6,2},{8,12},{10,14},{12,8},{14,10},{16,20},{18,... | collective-permute-start | bytes 3538952 | tf_op jit(solution)/shard_map/ppermute | solution.py:494
  558.6 117.1 %collective-permute-start.57 = (bf16[1,48,1536]{2,1,0:T(8,128)(2,1)}, bf16[1,48,1536]{2,1,0:T(8,128)(2,1)}, u32[]{:S(2)}, u32[]{:S(2)}) collective-permute-start(bf16[1,48,1536]{2,1,0:T(8,128)(2,1)} %dynamic-slice_convert_fusion.2), channel_id=1, source_target_pairs={{0,16},{2,18},{4,20},{6,22},{8,24},{10,26},{12,28},{14,30},{16,0},... | collective-permute-start | bytes 442376 | tf_op jit(solution)/shard_map/ppermute | solution.py:494
  575.6 36.6 %collective-permute-start.50 = (bf16[2,96,768]{2,1,0:T(8,128)(2,1)S(1)}, bf16[2,96,768]{2,1,0:T(8,128)(2,1)S(1)}, u32[]{:S(2)}, u32[]{:S(2)}) collective-permute-start(bf16[2,96,768]{2,1,0:T(8,128)(2,1)S(1)} %fusion.54), channel_id=1, source_target_pairs={{0,8},{2,10},{4,12},{6,14},{8,0},{10,2},{12,4},{14,6},{16,24},{18,... | collective-permute-start | bytes 884744 | tf_op jit(solution)/shard_map/ppermute | solution.py:494
  604.2 34.8 %collective-permute-start.59 = (bf16[2,96,1536]{2,1,0:T(8,128)(2,1)}, bf16[2,96,1536]{2,1,0:T(8,128)(2,1)}, u32[]{:S(2)}, u32[]{:S(2)}) collective-permute-start(bf16[2,96,1536]{2,1,0:T(8,128)(2,1)} %fusion.44), channel_id=1, source_target_pairs={{0,8},{2,10},{4,12},{6,14},{8,0},{10,2},{12,4},{14,6},{16,24},{18,... | collective-permute-start | bytes 1769480 | tf_op jit(solution)/shard_map/ppermute | solution.py:494
  610.9 31.8 %collective-permute-start.58 = (f32[17,4608]{1,0:T(8,128)}, f32[17,4608]{1,0:T(8,128)}, u32[]{:S(2)}, u32[]{:S(2)}) collective-permute-start(f32[17,4608]{1,0:T(8,128)} %add.473), channel_id=1, source_target_pairs={{0,8},{2,10},{4,12},{6,14},{8,0},{10,2},{12,4},{14,6},{16,24},{18,... | collective-permute-start | bytes 940040 | tf_op jit(solution)/shard_map/ppermute | solution.py:494
  634.5 41.3 %collective-permute-start.56 = (bf16[1,96,768]{2,1,0:T(8,128)(2,1)S(1)}, bf16[1,96,768]{2,1,0:T(8,128)(2,1)S(1)}, u32[]{:S(2)}, u32[]{:S(2)}) collective-permute-start(bf16[1,96,768]{2,1,0:T(8,128)(2,1)S(1)} %dynamic-slice_convert_fusion.1), channel_id=1, source_target_pairs={{0,16},{2,18},{4,20},{6,22},{8,24},{10,26},{12,28},{14,30},{16,0},... | collective-permute-start | bytes 442376 | tf_op jit(solution)/shard_map/ppermute | solution.py:494
  640.3 35.4 %collective-permute-start.65 = (bf16[1,96,1536]{2,1,0:T(8,128)(2,1)S(1)}, bf16[1,96,1536]{2,1,0:T(8,128)(2,1)S(1)}, u32[]{:S(2)}, u32[]{:S(2)}) collective-permute-start(bf16[1,96,1536]{2,1,0:T(8,128)(2,1)S(1)} %dynamic-slice_convert_fusion), channel_id=1, source_target_pairs={{0,16},{2,18},{4,20},{6,22},{8,24},{10,26},{12,28},{14,30},{16,0},... | collective-permute-start | bytes 884744 | tf_op jit(solution)/shard_map/ppermute | solution.py:494
  643.9 31.8 %collective-permute-start.60 = (f32[17,4608]{1,0:T(8,128)S(1)}, f32[17,4608]{1,0:T(8,128)S(1)}, u32[]{:S(2)}, u32[]{:S(2)}) collective-permute-start(f32[17,4608]{1,0:T(8,128)S(1)} %add.476), channel_id=1, source_target_pairs={{0,16},{2,18},{4,20},{6,22},{8,24},{10,26},{12,28},{14,30},{16,0},... | collective-permute-start | bytes 940040 | tf_op jit(solution)/shard_map/ppermute | solution.py:494
  (154 other events, 1697.4 us)
Sparse Core Ops, SparseCore 0:
  21.7 176.6 all-gather.2
  346.6 89.8 reduce-scatter.4
  441.1 164.4 reduce-scatter.2

commit v5 on v4

--- a/solution.py
+++ b/solution.py
@@ -144,7 +144,7 @@
         acc_ref[:, part] += total
 
 
-def project_kernel(a_ref, wq_ref, wk_ref, wv_ref, gq_ref, gk_ref, cos_ref, sin_ref, q_ref, kv_ref, raw_ref):
+def project_kernel(a_ref, wq_ref, wk_ref, wv_ref, gq_ref, gk_ref, cos_ref, sin_ref, qkv_ref, raw_ref):
     a = a_ref[...]
     cosine, sine = cos_ref[...], sin_ref[...]
     raw_q = mm(a, tile(wq_ref), 1, 0)
@@ -154,17 +154,13 @@
     for at in range(0, WIDE, LANES):
         part = slice(at, at + LANES)
         query = norm_rope(raw_q[:, part], gq_ref[...], cosine, sine).astype(bf16)
-        q_ref[:, part] = query * jnp.asarray(HD**-0.5, bf16)
-        kv_ref[0, :, part] = norm_rope(raw_k[:, part], gk_ref[...], cosine, sine).astype(bf16)
-    kv_ref[1] = mm(a, tile(wv_ref), 1, 0).astype(bf16)
+        qkv_ref[0, :, part] = query * jnp.asarray(HD**-0.5, bf16)
+        qkv_ref[1, :, part] = norm_rope(raw_k[:, part], gk_ref[...], cosine, sine).astype(bf16)
+    qkv_ref[2] = mm(a, tile(wv_ref), 1, 0).astype(bf16)
 
 
 def times_kernel(a_ref, w_ref, out_ref):
-    out_ref[...] = mm(a_ref[...], tile(w_ref), 1, 0)
-
-
-def two_times_kernel(a_ref, w_ref, other_a_ref, other_w_ref, out_ref):
-    out_ref[...] = mm(a_ref[...], tile(w_ref), 1, 0) + mm(other_a_ref[...], tile(other_w_ref), 1, 0)
+    out_ref[...] = mm(a_ref[...], tile(w_ref), 1, 0).astype(out_ref.dtype)
 
 
 def times_transposed_kernel(a_ref, w_ref, out_ref, acc_ref):
@@ -177,6 +173,26 @@
     add_transposed(acc_ref, a_ref, w_ref)
 
     @pl.when(step == pl.num_programs(0) - 1)
+    def _():
+        out_ref[...] = acc_ref[...].astype(out_ref.dtype)
+
+
+def input_back_kernel(d_query_ref, d_key_value_ref, w_ref, out_ref, acc_ref):
+    step = pl.program_id(0)
+    half = d_query_ref.shape[1]
+
+    @pl.when(step == 0)
+    def _():
+        acc_ref[...] = jnp.zeros(acc_ref.shape, f32)
+        add_transposed(acc_ref, d_query_ref, w_ref)
+
+    for at in range(2):
+
+        @pl.when(step == at + 1)
+        def _(at=at):
+            add_transposed(acc_ref, d_key_value_ref.at[:, at * half : (at + 1) * half], w_ref)
+
+    @pl.when(step == 2)
     def _():
         out_ref[...] = acc_ref[...].astype(out_ref.dtype)
 
@@ -191,7 +207,7 @@
     turned_ref[...] = hidden.T
 
 
-def hidden_back_kernel(d_branch_ref, w_ref, gate_ref, up_ref, d_gate_ref, d_up_ref, acc_ref):
+def hidden_back_kernel(d_branch_ref, w_ref, gate_ref, up_ref, d_ref, acc_ref):
     step = pl.program_id(0)
 
     @pl.when(step == 0)
@@ -207,8 +223,8 @@
             d_units, gate = acc_ref[:, part], gate_ref[:, part]
             sigmoid = jax.nn.sigmoid(gate)
             d_gate = d_units * up_ref[:, part] * sigmoid * (1.0 + gate * (1.0 - sigmoid))
-            d_gate_ref[:, part] = d_gate.astype(bf16)
-            d_up_ref[:, part] = (d_units * (gate * sigmoid)).astype(bf16)
+            d_ref[:, part] = d_gate.astype(bf16)
+            d_ref[:, acc_ref.shape[1] + at : acc_ref.shape[1] + at + WIDE] = (d_units * (gate * sigmoid)).astype(bf16)
 
 
 def piece_views(piece_refs, counts, per):
@@ -220,13 +236,12 @@
 
 
 def attend_kernel(counts, tok, flag_ref, q_ref, own_ids_ref, ids_ref, tk_ref, tv_ref, gate_ref, *rest):
-    pieces = piece_views(rest[: len(counts)], counts, 2)
+    pieces = piece_views(rest[: len(counts)], counts, 3)
     mixed_ref, self_ref, cross_ref, lse_self_ref, lse_cross_ref, split_ref = rest[len(counts) : len(counts) + 6]
     scores_ref, most_ref, total_ref, acc_ref, table_ref = rest[len(counts) + 6 :]
     step = pl.program_id(0)
     own_ids = own_ids_ref[...]
-    q_pair = q_ref[...]
-    q_two = two_heads(q_pair)
+    q_two = two_heads(q_ref[0])
     own_two = jnp.concatenate([own_ids, own_ids], axis=0)
     most_ref[...] = jnp.full(most_ref.shape, MASKED, f32)
     total_ref[...] = jnp.zeros(total_ref.shape, f32)
@@ -236,7 +251,7 @@
 
         @pl.when(flag_ref[slot] > 0)
         def _(slot=slot, ref=ref, at=at, rows=rows):
-            scores = mm(q_two, ref[at], 1, 1)
+            scores = mm(q_two, ref[at + 1], 1, 1)
             scores = jnp.where(own_two == ids_ref[slot : slot + 1, :rows], scores, MASKED)
             scores_ref[slot, :, :rows] = scores
             most = most_ref[...]
@@ -255,7 +270,7 @@
             for part in range(rows // LANES):
                 total = total + weights[:, part * LANES : (part + 1) * LANES]
             total_ref[...] = total
-            acc_ref[...] += mm(weights.astype(bf16), ref[at + 1], 1, 0)
+            acc_ref[...] += mm(weights.astype(bf16), ref[at + 2], 1, 0)
 
     row_total = jnp.sum(total_ref[...], axis=1, keepdims=True)
     self_out = one_pair(acc_ref[...] / row_total)
@@ -323,11 +338,11 @@
     counts, tok, flag_ref, q_ref, own_ids_ref, ids_ref, tk_ref, tv_ref, d_self_ref, d_cross_ref,
     self_ref, cross_ref, lse_self_ref, lse_cross_ref, raw_ref, gain_ref, cos_ref, sin_ref, *rest
 ):
-    pieces = piece_views(rest[: len(counts)], counts, 2)
+    pieces = piece_views(rest[: len(counts)], counts, 3)
     d_raw_ref, d_gain_ref, d_tk_ref, d_tv_ref, acc_ref = rest[len(counts) :]
     own_ids = own_ids_ref[...]
     own_two = jnp.concatenate([own_ids, own_ids], axis=0)
-    q_two = two_heads(q_ref[...])
+    q_two = two_heads(q_ref[0])
     d_self = d_self_ref[0]
     d_self_two = two_heads(d_self)
     delta = columns_of(head_sum(d_self.astype(f32) * self_ref[...]))
@@ -348,11 +363,11 @@
 
         @pl.when(flag_ref[slot] > 0)
         def _(slot=slot, ref=ref, at=at, rows=rows):
-            key = ref[at]
+            key = ref[at + 1]
             scores = mm(q_two, key, 1, 1)
             scores = jnp.where(own_two == ids_ref[slot : slot + 1, :rows], scores, MASKED)
             weights = jnp.exp(scores - lse)
-            d_weights = mm(d_self_two, ref[at + 1], 1, 1)
+            d_weights = mm(d_self_two, ref[at + 2], 1, 1)
             d_scores = (weights * (d_weights - delta)).astype(bf16)
             acc_ref[...] += mm(d_scores, key, 1, 0)
 
@@ -362,25 +377,26 @@
     d_gain_ref[...] = d_gain
 
 
-def key_back_kernel(counts, tok, flag_ref, kv_ref, own_ids_ref, ids_ref, raw_ref, gain_ref, cos_ref, sin_ref, *rest):
+def key_back_kernel(counts, tok, flag_ref, k_ref, v_ref, own_ids_ref, ids_ref, raw_ref, gain_ref, cos_ref, sin_ref, *rest):
     n = len(counts)
-    q_views = piece_views(rest[:n], counts, 1)
+    q_views = piece_views(rest[:n], counts, 3)
     g_views = piece_views(rest[n : 2 * n], counts, 1)
     g_tables = piece_views(rest[2 * n : 3 * n], counts, 1)
-    d_raw_ref, d_gain_ref, d_value_ref, acc_k_ref, acc_v_ref = rest[3 * n :]
+    d_both_ref, d_gain_ref, acc_k_ref, acc_v_ref = rest[3 * n :]
     step = pl.program_id(0)
     own_ids = own_ids_ref[...]
-    k_two = two_heads(kv_ref[0])
-    v_two = two_heads(kv_ref[1])
+    k_two = two_heads(k_ref[0])
+    v_two = two_heads(v_ref[0])
     acc_k_ref[...] = jnp.zeros(acc_k_ref.shape, f32)
     acc_v_ref[...] = jnp.zeros(acc_v_ref.shape, f32)
     for slot in range(PIECES):
-        q_ref, at = q_views[slot]
+        q_ref, q_at = q_views[slot]
+        g_ref, at = g_views[slot]
         rows = q_ref.shape[1]
         @pl.when(flag_ref[slot] > 0)
-        def _(slot=slot, q_ref=q_ref, at=at, rows=rows):
-            query = q_ref[at]
-            d_self = g_views[slot][0][at]
+        def _(slot=slot, q_ref=q_ref, q_at=q_at, g_ref=g_ref, at=at, rows=rows):
+            query = q_ref[q_at]
+            d_self = g_ref[at]
             tables = joined(g_tables[slot][0][at], tok)[:, :rows]
             delta, lse = tables[:TABLE], tables[TABLE:]
             same = own_ids == ids_ref[slot : slot + 1, :rows]
@@ -399,32 +415,38 @@
     d_raw, d_gain = norm_rope_back(
         raw_ref[0], gain_ref[...], cos_ref[...], sin_ref[...], one_pair(acc_k_ref[...])
     )
-    d_raw_ref[...] = d_raw.astype(bf16)
     d_gain_ref[...] = d_gain
-    d_value_ref[...] = one_pair(acc_v_ref[...]).astype(bf16)
-
-
-def unflatten_kernel(tables, *refs):
-    for (rows, columns), lines_ref, out_ref in zip(tables, refs, refs[len(tables) :]):
-        per_row = columns // LANES
-        for at in range(per_row):
-            out_ref[:, at * LANES : (at + 1) * LANES] = lines_ref[pl.ds(at, rows, stride=per_row), :].astype(bf16)
-
-
-def pack_kernel(tables, *refs):
-    *lines_refs, out_ref = refs
+    place = pl.multiple_of(step * LANES, LANES)
+    d_both_ref[:, pl.ds(place, LANES)] = d_raw.astype(bf16)
+    half = pl.num_programs(0) * LANES
+    d_both_ref[:, pl.ds(pl.multiple_of(half + place, LANES), LANES)] = one_pair(acc_v_ref[...]).astype(bf16)
+
+
+def place_rows(lines_ref, start, table, out_ref, top=None):
+    rows, columns = table
+    per_row = columns // LANES
+    for at in range(per_row):
+        part = lines_ref[pl.ds(start + at, rows, stride=per_row), :].astype(bf16)
+        if top is None:
+            out_ref[:, at * LANES : (at + 1) * LANES] = part
+        else:
+            row, lane = top + at // (WIDE // LANES) * rows, at % (WIDE // LANES) * LANES
+            out_ref[row : row + rows, lane : lane + LANES] = part
+
+
+def own_rows_kernel(tables, starts, packed, apart, lines_ref, *out_refs):
     top = 0
-    for (rows, columns), lines_ref in zip(tables, lines_refs):
-        per_row = columns // LANES
-        for at in range(per_row):
-            row = top + at // (WIDE // LANES) * rows
-            lane = at % (WIDE // LANES) * LANES
-            out_ref[row : row + rows, lane : lane + LANES] = lines_ref[pl.ds(at, rows, stride=per_row), :].astype(bf16)
+    for which in packed:
+        rows, columns = tables[which]
+        place_rows(lines_ref, starts[which], tables[which], out_refs[0], top)
         top += columns // WIDE * rows
+    for which, ref in zip(apart, out_refs[bool(packed) :]):
+        place_rows(lines_ref, starts[which], tables[which], ref)
 
 
 def flatten_kernel(places, *refs):
-    *grad_refs, lines_ref, square_ref = refs
+    *in_refs, lines_ref, square_ref = refs
+    grad_refs = in_refs[: len(places)]
     square = jnp.zeros((1, LANES), f32)
     for (start, column, columns), ref in zip(places, grad_refs):
         for at in range(ref.shape[1] // LANES):
@@ -511,7 +533,12 @@
 
 
 def sum_over_all(x):
-    x = sum_over_img(x)
+    bits = index_bits(lax.axis_size("img"))
+    for bit in range(0, bits - 1, 2):
+        low, high = 1 << bit, 2 << bit
+        x = (x + crossed(x, low)) + (crossed(x, high) + crossed(x, low | high))
+    if bits % 2:
+        x = x + crossed(x, 1 << (bits - 1))
     return x + other_txt(x)
 
 
@@ -524,8 +551,9 @@
 
 
 class TermSum:
-    def __init__(self, clock, terms, order):
+    def __init__(self, clock, terms, order, sent_as):
         count = lax.axis_size("img")
+        self.sent_as = sent_as
         self.clock, self.order, self.level = clock, order, 0
         self.keep = clock.stage(terms).reshape(count, terms.shape[0] // count, terms.shape[1])
         self.send()
@@ -533,12 +561,18 @@
     def send(self):
         bit = self.order[self.level]
         below = 1 << sum(other < bit for other in self.order[self.level :])
-        self.keep, self.sent = own_and_other(self.keep, bit, below)
+        self.keep, sent = own_and_other(self.keep, bit, below)
+        self.sent = sent.astype(self.sent_as)
         self.clock.mark(self.sent)
 
-    def advance(self):
-        got = self.clock.stage(crossed(self.sent, 1 << self.order[self.level]))
-        self.keep = self.keep + got
+    def receive(self):
+        self.got = self.clock.stage(crossed(self.sent, 1 << self.order[self.level]))
+        self.clock.mark(self.got)
+
+    def advance(self, received=False):
+        if not received:
+            self.receive()
+        self.keep = self.keep + self.clock.stage(self.got).astype(f32)
         self.level += 1
         if self.level == len(self.order):
             self.clock.mark(self.keep)
@@ -578,9 +612,11 @@
 class Clock:
     def __init__(self):
         self.token = ()
+        self.kept = []
 
     def stage(self, *arrays):
-        arrays, _ = lax.optimization_barrier((arrays, self.token))
+        arrays, passed = lax.optimization_barrier((arrays, self.token))
+        self.kept += passed
         return arrays if len(arrays) > 1 else arrays[0]
 
     def mark(self, *arrays):
@@ -588,21 +624,47 @@
 
 
 class SmallSum:
+    def __init__(self, clock, x, row):
+        self.x, self.row = clock.stage(x, row)
+        self.clock, self.level = clock, 0
+        self.levels = index_bits(lax.axis_size("img"))
+        self.send()
+
+    def send(self):
+        high = lax.reduce_precision(self.row, 8, 7)
+        low = lax.reduce_precision(self.row - high, 8, 7)
+        self.row = high + low
+        self.sent = jnp.concatenate([self.x, high, low], axis=0).astype(bf16)
+        self.clock.mark(self.sent)
+
+    def advance(self):
+        got = self.clock.stage(crossed(self.sent, 1 << self.level)).astype(f32)
+        count = self.x.shape[0]
+        self.x = self.x + got[:count]
+        self.row = self.row + (got[count : count + 1] + got[count + 1 :])
+        self.level += 1
+        if self.level < self.levels:
+            self.send()
+        else:
+            self.clock.mark(self.x)
+
+
+class SmallGather:
     def __init__(self, clock, x):
-        self.clock, self.x, self.level = clock, x, 0
-        self.levels = index_bits(lax.axis_size("img"))
+        x = clock.stage(x)
+        self.clock, self.x, self.bit = clock, x[None], index_bits(lax.axis_size("img"))
         clock.mark(x)
 
     def advance(self):
-        got = self.clock.stage(crossed(self.x, 1 << self.level))
-        self.x = self.x + got
+        self.bit -= 1
+        mine = (lax.axis_index("img") >> self.bit) & 1
+        got = self.clock.stage(crossed(self.x, 1 << self.bit))
+        both = jnp.where(mine == 0, jnp.stack([self.x, got], 1), jnp.stack([got, self.x], 1))
+        self.x = both.reshape(-1, *got.shape[1:])
         self.clock.mark(self.x)
-        self.level += 1
-
-    def finish(self):
-        while self.level < self.levels:
-            self.advance()
-        return self.x
+
+    def result(self):
+        return self.x.reshape(-1, self.x.shape[-1])
 
 
 class GradientSum:
@@ -626,8 +688,12 @@
         self.clock.mark(self.got)
         self.level += 1
 
-    def advance(self, received=False):
-        if not received:
+    def advance(self, received=False, beside=None):
+        if beside is not None:
+            self.got, *beside = self.clock.stage(crossed(self.sent, 1 << self.order[self.level]), *beside)
+            self.clock.mark(self.got)
+            self.level += 1
+        elif not received:
             self.receive()
         got = self.clock.stage(self.got)
         if self.level == len(self.order):
@@ -643,6 +709,7 @@
             own, other = own_and_other(self.keep + got.astype(f32), bit)
             self.sent, self.keep = other.astype(bf16), own
         self.clock.mark(self.sent)
+        return beside
 
 
 class Neighbourhood:
@@ -658,7 +725,7 @@
         self.edge = lax.ppermute(edge, "img", pairs_low + pairs_high)
 
     def second(self):
-        across, above, below = self.clock.stage(self.across, self.above, self.below)
+        across, above, below, self.edge = self.clock.stage(self.across, self.above, self.below, self.edge)
         self.across, self.above, self.below = across, above, below
         self.four_sent = jnp.concatenate([self.x, across, above, below], axis=0)
         self.above_across, self.below_across = shifted(across, 4), shifted(across, -4)
@@ -666,9 +733,7 @@
 
     def third(self):
         four = crossed(self.four_sent, 1)
-        self.above_across, self.below_across, self.four, self.edge = self.clock.stage(
-            self.above_across, self.below_across, four, self.edge
-        )
+        self.above_across, self.below_across, self.four = self.clock.stage(self.above_across, self.below_across, four)
         self.two_sent = jnp.concatenate([self.above_across, self.below_across], axis=0)
         self.clock.mark(self.two_sent)
 
@@ -755,14 +820,6 @@
     for rows, columns in tables:
         starts.append(starts[-1] + rows * columns // LANES)
 
-    def own_rows(*which):
-        shapes = [tables[w] for w in which]
-        return pl.pallas_call(
-            functools.partial(unflatten_kernel, shapes),
-            out_shape=[shape_of(s, bf16) for s in shapes],
-            compiler_params=pltpu.CompilerParams(vmem_limit_bytes=58 * MIB),
-        )(*(master_lines[starts[w] : starts[w + 1]] for w in which))
-
     def scatter(terms):
         return lax.psum_scatter(terms, "img", scatter_dimension=0, tiled=True)
 
@@ -772,16 +829,20 @@
     together = [0, 1, 4, 2]
     shapes = [tables[w] for w in together]
     heights = [rows * columns // WIDE for rows, columns in shapes]
-    if all(rows % 16 == 0 for rows, _ in shapes):
-        block = pl.pallas_call(
-            functools.partial(pack_kernel, shapes),
-            out_shape=shape_of((sum(heights), WIDE), bf16),
-            compiler_params=pltpu.CompilerParams(vmem_limit_bytes=58 * MIB),
-        )(*(master_lines[starts[w] : starts[w + 1]] for w in together))
-        blocks = gather(block[None])
+    in_blocks = all(rows % 16 == 0 for rows, _ in shapes)
+    packed = together if in_blocks else []
+    apart = [5, 3] if in_blocks else [5, 3] + together
+    own = pl.pallas_call(
+        functools.partial(own_rows_kernel, tables, starts, packed, apart),
+        out_shape=[shape_of((sum(heights), WIDE), bf16)] * in_blocks + [shape_of(tables[w], bf16) for w in apart],
+        compiler_params=pltpu.CompilerParams(vmem_limit_bytes=58 * MIB),
+    )(master_lines)
+    own_modulate, own_text = own[in_blocks : in_blocks + 2]
+    if in_blocks:
+        blocks = gather(own[0][None])
     else:
         blocks = None
-        natural = dict(zip(together, (gather(rows) for rows in own_rows(*together))))
+        natural = dict(zip(together, (gather(rows) for rows in own[2:])))
 
     def weight(which):
         if blocks is None:
@@ -798,8 +859,6 @@
 
         return blocks, spec
 
-    (own_modulate,) = own_rows(5)
-    (own_text,) = own_rows(3)
 
     gain_attn = small_master[:D]
     gain_ffn = small_master[D : 2 * D]
@@ -850,7 +909,7 @@
     text_len = text_rows * n_img
     text_columns = lax.all_to_all(text_states, "img", split_axis=1, concat_axis=0, tiled=True)
     z_first = [0] + list(range(2, index_bits(n_img))) + [1]
-    text_proj = TermSum(Clock(), jnp.dot(text_columns, own_text, preferred_element_type=f32), z_first).finish()
+    text_proj = TermSum(Clock(), jnp.dot(text_columns, own_text, preferred_element_type=f32), z_first, bf16).finish()
     text_shape = (text_rows, local_heads, HD)
     text_raw = text_proj[:, :half_d].reshape(text_shape)
     text_normed = rms_norm(text_raw)
@@ -869,58 +928,44 @@
 
     thirds = half_d // WIDE
     w_project, project_spec = weight(2)
-    queries, own_kv, raw_qk = call(
+    own_qkv, raw_qk = call(
         project_kernel,
         (thirds,),
         [whole((tok, D))]
         + [project_spec(lambda j, c=c: c * thirds + j) for c in range(3)]
         + [whole((1, LANES))] * 2
         + [whole((tok, LANES))] * 2,
-        [wide(tok)] + [pl.BlockSpec((2, tok, WIDE), lambda j: (0, 0, j))] * 2,
-        [
-            shape_of((tok, half_d), bf16),
-            shape_of((2, tok, half_d), bf16),
-            shape_of((2, tok, half_d), f32),
-        ],
+        [pl.BlockSpec((n, tok, WIDE), lambda j: (0, 0, j)) for n in (3, 2)],
+        [shape_of((3, tok, half_d), bf16), shape_of((2, tok, half_d), f32)],
         (attn_in, w_project, w_project, w_project, gain_query_pair, gain_key_pair, cosine, sine),
         flops=2 * tok * D * 3 * half_d,
         moved=2 * D * 3 * half_d,
     )
     clock = Clock()
-    clock.mark(own_kv)
-    kv_near = Neighbourhood(clock, own_kv, own_kv[:, tok - EDGE :], own_kv[:, :EDGE])
+    clock.mark(own_qkv)
+    qkv_near = Neighbourhood(clock, own_qkv, own_qkv[:, tok - EDGE :], own_qkv[:, :EDGE])
     w_updown, updown_spec = weight(0)
     w_down, down_spec = weight(1)
     w_output, output_spec = weight(4)
-    if blocks is None:
-        w_output_other = other_txt(w_output)
-        other_spec = output_spec
-    else:
-        top = sum(heights[:2])
-        w_output_other = other_txt(clock.stage(blocks)[:, top : top + heights[2]])
-        other_spec = lambda at: pl.BlockSpec((n_img, shapes[2][0], WIDE), lambda j, *_: (0, at(j), 0))
-
     def step(j):
         return j
 
-    kv_near.second()
-    kv_near.third()
-    kv_pieces = kv_near.collect()
-
-    kv_specs = [pairs(2 * c, a.shape[1]) for c, a in zip(PIECE_COUNTS, kv_pieces)]
+    qkv_near.second()
+    qkv_near.third()
+    qkv_pieces = qkv_near.collect()
+
+    qkv_specs = [pairs(3 * c, a.shape[1]) for c, a in zip(PIECE_COUNTS, qkv_pieces)]
     id_specs = [whole((tok, 1)), whole((16, tok))]
     text_specs = [pair(text_len), pair(text_len, n_pairs)]
-    own_queries = queries[None]
-    query_near = Neighbourhood(clock, own_queries, own_queries[:, tok - EDGE :], own_queries[:, :EDGE])
     mixed_low, self_out, cross_out, lse_self, lse_cross, lse_split = call(
         functools.partial(attend_kernel, PIECE_COUNTS, tok),
         (n_pairs,),
-        [pair(tok)] + id_specs + text_specs + [pair(1)] + kv_specs,
+        [pairs(1, tok)] + id_specs + text_specs + [pair(1)] + qkv_specs,
         [pair(tok)] * 5 + [whole((TABLE, 3 * tok))],
         [shape_of((tok, half_d), bf16)]
         + [shape_of((tok, half_d), f32)] * 4
         + [shape_of((TABLE, 3 * tok), bf16)],
-        (flags, clock.stage(queries), own_ids, piece_ids, all_text, all_text, gate_lanes, *kv_pieces),
+        (flags, clock.stage(own_qkv), own_ids, piece_ids, all_text, all_text, gate_lanes, *qkv_pieces),
         scratch=[
             pltpu.VMEM((PIECES, 2 * tok, tok), f32),
             pltpu.VMEM((2 * tok, LANES), f32),
@@ -943,26 +988,24 @@
         )
 
     clock.mark(mixed_low)
-    mixed_other = other_txt(mixed_low)
-    query_near.second()
-    mixed_other, mixed_low = clock.stage(mixed_other, mixed_low)
-    attn_out = call(
-        two_times_kernel,
+    attn_part = call(
+        times_kernel,
         (D // WIDE,),
-        [whole((tok, half_d)), output_spec(step), whole((tok, half_d)), other_spec(step)],
+        [whole((tok, half_d)), output_spec(step)],
         [wide(tok)],
-        [shape_of((tok, D), f32)],
-        (mixed_low, w_output, mixed_other, w_output_other),
-        flops=4 * tok * half_d * D,
-        moved=4 * half_d * D,
+        [shape_of((tok, D), bf16)],
+        (clock.stage(mixed_low), w_output),
+        flops=2 * tok * half_d * D,
+        moved=2 * half_d * D,
     )[0]
-    clock.mark(attn_out)
+    clock.mark(attn_part)
+    attn_other = clock.stage(other_txt(attn_part))
+    attn_out = attn_part.astype(f32) + attn_other.astype(f32)
     hidden = x_float + gate_one * attn_out
     h_normed = rms_norm(hidden)
     normed_two = h_normed * gain_ffn
     ffn_in = (normed_two * (1.0 + scale_two) + shift_two).astype(bf16)
     clock.mark(ffn_in)
-    query_near.third()
     gate, up, hidden_units, hidden_turned = call(
         hidden_kernel,
         (half_ff // WIDE,),
@@ -974,25 +1017,24 @@
         moved=4 * D * half_ff,
     )
     clock.mark(hidden_turned)
-    query_pieces = query_near.collect()
     d_out = cotangent.astype(f32)
     d_branch = (d_out * gate_two).astype(bf16)
     down_terms = mm(clock.stage(hidden_turned), d_branch, 1, 0).astype(bf16)
     clock.mark(down_terms)
     grad_down = scatter(down_terms)
-    d_gate, d_up = call(
+    d_gate_up = call(
         hidden_back_kernel,
         (D // WIDE // 3,),
         [wide(tok, 3), down_spec(step, 3), whole((tok, half_ff)), whole((tok, half_ff))],
-        [whole((tok, half_ff))] * 2,
-        [shape_of((tok, half_ff), bf16)] * 2,
+        [whole((tok, 2 * half_ff))],
+        [shape_of((tok, 2 * half_ff), bf16)],
         (clock.stage(d_branch), w_down, gate, up),
         scratch=[pltpu.VMEM((tok, half_ff), f32)],
         flops=2 * tok * D * half_ff,
         moved=2 * D * half_ff,
-    )
-    clock.mark(d_gate, d_up)
-    d_gate_up = clock.stage(jnp.concatenate([d_gate, d_up], axis=1))
+    )[0]
+    clock.mark(d_gate_up)
+    d_gate_up = clock.stage(d_gate_up)
     d_ffn_part = call(
         times_transposed_kernel,
         (2 * half_ff // WIDE // 4,),
@@ -1046,7 +1088,6 @@
     )[0]
     clock.mark(branch_part)
     branch_other = other_txt(branch_part)
-    output_sum = GradientSum(clock, tall(mixed_low), d_attn)
     grad_near.second()
     turn_specs = [whole((1, LANES)), whole((tok, LANES)), whole((tok, LANES))]
 
@@ -1060,14 +1101,14 @@
         return call(
             functools.partial(query_back_kernel, PIECE_COUNTS, tok),
             (count,),
-            [at(tok)]
+            [some(1, tok)]
             + id_specs
             + [at(text_len), at(text_len, n_pairs)]
             + [some(1, tok), at(tok)]
             + [at(tok)] * 4
             + [some(1, tok)]
             + turn_specs
-            + [some(2 * c, a.shape[1]) for c, a in zip(PIECE_COUNTS, kv_pieces)],
+            + [some(3 * c, a.shape[1]) for c, a in zip(PIECE_COUNTS, qkv_pieces)],
             [pair(tok), pair(1), pair(text_len), pair(text_len)],
             [
                 shape_of((tok, count * LANES), bf16),
@@ -1076,8 +1117,8 @@
                 shape_of((text_len, count * LANES), f32),
             ],
             (
-                flags, queries, own_ids, piece_ids, all_text, all_text, grad_pack, d_cross,
-                self_out, cross_out, lse_self, lse_cross, raw_qk, gain_query_pair, cosine, sine, *kv_pieces,
+                flags, own_qkv, own_ids, piece_ids, all_text, all_text, grad_pack, d_cross,
+                self_out, cross_out, lse_self, lse_cross, raw_qk, gain_query_pair, cosine, sine, *qkv_pieces,
             ),
             scratch=[pltpu.VMEM((2 * tok, LANES), f32)],
             prefetch=1,
@@ -1087,88 +1128,95 @@
     first_half = query_back(0, head_half, clock.stage(d_cross_low))
     clock.mark(first_half[0])
     grad_near.third()
+    output_sum = GradientSum(clock, tall(mixed_low), d_attn)
+    grad_pieces = grad_near.collect()
     output_sum.advance()
-    grad_pieces = grad_near.collect()
     second_half = query_back(head_half, n_pairs - head_half, clock.stage(d_cross_low))
     clock.mark(second_half[0])
+    grad_down, branch_other = clock.stage(grad_down, branch_other)
+    clock.mark(grad_down, branch_other)
     d_query_raw, d_gain_query, d_text_key, d_text_value = (
         jnp.concatenate(halves, axis=1) for halves in zip(first_half, second_half)
     )
     attn_tall = tall(attn_in)
-    text_sum = TermSum(clock, jnp.concatenate([d_text_key, d_text_value], axis=1), z_first)
+    text_sum = TermSum(clock, jnp.concatenate([d_text_key, d_text_value], axis=1), z_first, bf16)
     query_sum = GradientSum(clock, attn_tall, d_query_raw)
-    output_sum.advance()
     text_sum.advance()
-    branch_other = clock.stage(branch_other)
-
-    query_specs = [pairs(c, a.shape[1]) for c, a in zip(PIECE_COUNTS, query_pieces)]
+    query_sum.advance()
+
     pack_specs = [pairs(c, a.shape[1] - PACK) for c, a in zip(PIECE_COUNTS, grad_pieces)] + [
         pl.BlockSpec((c, PACK, half_d), lambda j, *_, at=(a.shape[1] - PACK) // PACK: (0, at, 0))
         for c, a in zip(PIECE_COUNTS, grad_pieces)
     ]
 
-    d_key_raw, d_gain_key, d_value = call(
+    d_key_value, d_gain_key = call(
         functools.partial(key_back_kernel, PIECE_COUNTS, tok),
         (n_pairs,),
-        [pairs(2, tok)]
+        [pairs(1, tok, 1), pairs(1, tok, 2)]
         + id_specs
         + [pairs(1, tok, 1)]
         + turn_specs
-        + query_specs
+        + qkv_specs
         + pack_specs,
-        [pair(tok), pair(1), pair(tok)],
-        [
-            shape_of((tok, half_d), bf16),
-            shape_of((1, half_d), f32),
-            shape_of((tok, half_d), bf16),
-        ],
+        [whole((tok, 2 * half_d)), pair(1)],
+        [shape_of((tok, 2 * half_d), bf16), shape_of((1, half_d), f32)],
         (
-            flags, clock.stage(own_kv), own_ids, piece_ids, raw_qk, gain_key_pair,
-            cosine, sine, *query_pieces, *grad_pieces, *grad_pieces,
+            flags, clock.stage(own_qkv), own_qkv, own_ids, piece_ids, raw_qk, gain_key_pair,
+            cosine, sine, *qkv_pieces, *grad_pieces, *grad_pieces,
         ),
         scratch=[pltpu.VMEM((2 * tok, LANES), f32)] * 2,
         prefetch=1,
     )
-    clock.mark(d_value)
-    key_value_sum = GradientSum(clock, attn_tall, jnp.concatenate([d_key_raw, d_value], axis=1))
-    d_projected = clock.stage(jnp.concatenate([d_query_raw, d_key_raw, d_value], axis=1))
+    clock.mark(d_key_value)
+    key_value_sum = GradientSum(clock, attn_tall, d_key_value)
+    d_key_value = clock.stage(d_key_value)
     d_attn_part = call(
-        times_transposed_kernel,
-        (thirds,),
-        [wide(tok, 3), project_spec(step, 3)],
+        input_back_kernel,
+        (3,),
+        [whole((tok, half_d)), whole((tok, 2 * half_d)), project_spec(step, thirds)],
         [whole((tok, D))],
         [shape_of((tok, D), bf16)],
-        (d_projected, w_project),
+        (d_query_raw, d_key_value, w_project),
         scratch=[pltpu.VMEM((tok, D), f32)],
         flops=6 * tok * D * half_d,
         moved=6 * D * half_d,
     )[0]
     clock.mark(d_attn_part)
     d_attn_other = other_txt(d_attn_part)
-    query_sum.advance()
     key_value_sum.advance()
     text_sum.advance()
     output_sum.advance()
+
+    one_hot_wide = one_hot.astype(f32)
+
+    def by_sample(values):
+        summed = lax.dot_general(one_hot_wide, values, (((0,), (0,)), ((), ())), precision=HIGH)
+        return lax.dynamic_slice_in_dim(summed, txt_index * half_d, half_d, 1)
+
+    d_hidden_late, d_ffn_late = clock.stage(d_hidden, d_ffn_in)
+    branch = branch_part + branch_other
+    block_out = hidden + gate_two * branch
+    d_mod_early = jnp.concatenate(
+        [
+            by_sample(v)
+            for v in (d_hidden_late * attn_out, d_ffn_late, d_ffn_late * normed_two, d_out * branch)
+        ],
+        axis=1,
+    )
+    clock.mark(d_mod_early)
+    text_own = text_sum.finish()
+    d_text_scaled = text_own[:, :half_d].reshape(text_shape)
+    d_gain_text = jnp.sum(d_text_scaled * text_normed, axis=(0, 1))
+    d_text_raw = rms_back(text_raw, d_text_scaled * gain_text).reshape(text_rows, half_d)
+    text_gather = SmallGather(clock, jnp.concatenate([d_text_raw, text_own[:, half_d:]], axis=1).astype(bf16))
+    query_sum.advance()
     d_attn_other = clock.stage(d_attn_other)
     d_attn_in = d_attn_part.astype(f32) + d_attn_other.astype(f32)
-    branch = branch_part + branch_other
-    block_out = hidden + gate_two * branch
-    d_gate_two = d_out * branch
-    d_gate_one = d_hidden * attn_out
     d_scale_one = d_attn_in * normed_one
     d_normed_one = d_attn_in * (1.0 + scale_one)
     d_gain_attn = jnp.sum(d_normed_one * x_normed, axis=0)
     d_tokens = d_hidden + rms_back(x_float, d_normed_one * gain_attn)
-
-    one_hot_wide = one_hot.astype(f32)
-
-    def by_sample(values):
-        summed = lax.dot_general(one_hot_wide, values, (((0,), (0,)), ((), ())), precision=HIGH)
-        return lax.dynamic_slice_in_dim(summed, txt_index * half_d, half_d, 1)
-
-    d_mod = jnp.concatenate(
-        [by_sample(v) for v in (d_attn_in, d_scale_one, d_gate_one, d_ffn_in, d_scale_two, d_gate_two)], axis=1
-    )
+    d_mod = jnp.concatenate([by_sample(d_attn_in), by_sample(d_scale_one), d_mod_early], axis=1)
 
     replica = (txt_index == 0).astype(f32)
     d_gate_local = jnp.sum(d_gate_lanes.reshape(local_heads, HD), axis=1) * (1.0 - tanh_gate**2)
@@ -1185,50 +1233,54 @@
     )
     small_count = small_terms.shape[0]
     small_row = jnp.pad(small_terms, (0, d_mod.shape[1] - small_count))[None]
-    small_sum = SmallSum(clock, jnp.concatenate([d_mod, small_row], axis=0))
-    query_sum.advance()
-    text_sum.advance()
+    small_sum = SmallSum(clock, d_mod, small_row)
+    text_gather.advance()
+    (grad_updown,) = key_value_sum.advance(beside=(grad_updown,))
+    small_sum.advance()
     small_sum.advance()
     key_value_sum.advance()
-
-    text_own = text_sum.finish()
-    d_text_scaled = text_own[:, :half_d].reshape(text_shape)
-    d_gain_text = jnp.sum(d_text_scaled * text_normed, axis=(0, 1))
-    d_text_raw = rms_back(text_raw, d_text_scaled * gain_text).reshape(text_rows, half_d)
-    d_text_proj = gather_doubling(jnp.concatenate([d_text_raw, text_own[:, half_d:]], axis=1).astype(bf16))
-    grad_text = mm(text_columns, d_text_proj, 0, 0)
-
     small_sum.advance()
+    text_gather.advance()
+    output_sum.advance()
     query_sum.advance()
+    text_gather.advance()
+    small_sum.advance()
     key_value_sum.advance()
-    sums = small_sum.finish()
-    d_mod = sums[:samples]
-    small_row = sums[samples:, :]
+    output_sum.advance()
+    query_sum.advance()
+    while text_gather.bit:
+        text_gather.advance()
+    grad_text = mm(text_columns, text_gather.result(), 0, 0)
+    pending = [one for one in (output_sum, query_sum, key_value_sum) if one.result is None]
+    while pending or small_sum.level < small_sum.levels:
+        if small_sum.level < small_sum.levels:
+            small_sum.advance()
+        for one in list(pending):
+            if one.result is None:
+                one.advance()
+            if one.result is not None:
+                pending.remove(one)
+    d_mod, small_row = small_sum.x, small_sum.row
     small_grad = (small_row + other_txt(small_row))[0, :small_count]
     grad_modulate = lax.dot_general(silu_own.astype(f32), d_mod, (((0,), (0,)), ((), ())), precision=HIGH)
 
-    pending = [output_sum, query_sum, key_value_sum]
-    while pending:
-        for one in list(pending):
-            if one.result is None:
-                one.result = one.advance()
-            if one.result is not None:
-                pending.remove(one)
     grads = [grad_updown, grad_down, query_sum.result, grad_text, output_sum.result, grad_modulate, key_value_sum.result]
     places = [(start, 0, columns) for start, (_, columns) in zip(starts, tables)]
     places.append((starts[2], half_d, 3 * half_d))
     reduced, squares = pl.pallas_call(
         functools.partial(flatten_kernel, places),
         out_shape=[shape_of((lines, LANES), f32), shape_of((1, LANES), f32)],
+        in_specs=[pl.BlockSpec(memory_space=pltpu.VMEM)] * len(grads)
+        + [pl.BlockSpec(memory_space=pl.ANY)] * len(clock.kept),
         compiler_params=pltpu.CompilerParams(vmem_limit_bytes=58 * MIB),
-    )(*grads)
+    )(*grads, *clock.kept)
 
     last = sum_over_all(jnp.concatenate([squares, jnp.pad(d_gain_text, (0, LANES - HD))[None]], axis=0))
     small_grad = lax.dynamic_update_slice(small_grad, last[1, :HD], (2 * D + 2 * HD,))
     grad_square = jnp.sum(last[0]) + jnp.sum(small_grad * small_grad)
     clip_factor = MAX_NORM / jnp.maximum(jnp.sqrt(grad_square), MAX_NORM)
 
-    block = math.gcd(lines, 1024)
+    block = math.gcd(lines, 2048)
     line_spec = pl.BlockSpec((block, LANES), lambda i: (i, 0))
     as_lines = (lines, LANES)
     updated = call(

time: 758 us -> 755 us (level)
  waiting for transfers between devices: 247 us -> 293 us
  local copies, waits for them, and re-layouts: 73 us -> 52.1 us
  other arithmetic: 68.6 us -> 50.7 us
    ppermute x8 -> x7, waiting for transfers between devices: 14.8 us -> 42.6 us  [other_txt(): return lax.ppermute(x, 'txt', [(0, 1), (1, 0)])]
    slice x7 -> x1, local copies, waits for them, and re-layouts: 17.2 us -> 0.01 us  [on_device(): text_own[:, half_d:]]
    ppermute x12 -> x8, starting transfers between devices: 39.6 us -> 25 us  [shifted(): lax.ppermute(x, 'img', [(i + by, i) for i in range(count) if 0 <= i + by...]
    all_gather x1, waiting for transfers between devices: 51 us -> 65.3 us  [gather(): return lax.all_gather(rows, 'img', axis=0, tiled=True)]
    ppermute x49 -> x48, starting transfers between devices: 51.9 us -> 63.8 us  [crossed(): return lax.ppermute(x, 'img', [(i, i ^ bit) for i in range(count)])]
    concatenate x5, other arithmetic: 9.21 us -> 1.6 us  [the longest x4 0.91 us: send(): self.sent = jnp.concatenate([self.x, high, low], axis=0).astype(bf16)]
    ppermute x12 -> x8, waiting for transfers between devices: 35.5 us -> 36.8 us  [shifted(): lax.ppermute(x, 'img', [(i + by, i) for i in range(count) if 0 <= i + by...]
    unnamed x223 -> x303, local copies, waits for them, and re-layouts: 19 us -> 17.8 us
  transfers between devices with their start and end apart: 76 -> 69, of which waited for: 28 -> 32; matrix products, arithmetic and copies ran while one was open for 21% -> 16% of each run, Pallas kernels for 18% -> 12%
where the time goes in v5:
time: 755 us; the launch traced here: 744 us
  waiting for transfers between devices  293 us (39%)
  Pallas kernels  172 us (23%)
  starting transfers between devices  109 us (14%)
  local copies, waits for them, and re-layouts  52.1 us (7%)
  other arithmetic  50.7 us (7%)
  matrix products  48.6 us (6%)
  between operations  18.9 us (3%)
    pallas_call x13, Pallas kernels, call(): pl.pallas_call(kernel, grid_spec=pltpu.PrefetchScalarGridSpec(num_scalar_...  159 us
    ppermute x48, waiting for transfers between devices, crossed(): return lax.ppermute(x, 'img', [(i, i ^ bit) for i in range(count)])  145 us
    all_gather x1, waiting for transfers between devices, gather(): return lax.all_gather(rows, 'img', axis=0, tiled=True)  65.3 us
    ppermute x48, starting transfers between devices, crossed(): return lax.ppermute(x, 'img', [(i, i ^ bit) for i in range(count)])  63.8 us
    ppermute x7, waiting for transfers between devices, other_txt(): return lax.ppermute(x, 'txt', [(0, 1), (1, 0)])  42.6 us
    ppermute x8, waiting for transfers between devices, shifted(): lax.ppermute(x, 'img', [(i + by, i) for i in range(count) if 0 <= i + by...  36.8 us
    dot_general x12, matrix products, mm(): lax.dot_general(a, b, (((on_a,), (on_b,)), ((), ())), preferred_element_t...  32.8 us
    ppermute x8, starting transfers between devices, shifted(): lax.ppermute(x, 'img', [(i + by, i) for i in range(count) if 0 <= i + by...  25 us
  transfers between devices with their start and end apart: 69, of which 32 were waited for; matrix products, arithmetic and copies ran while one was open for 16% of the time, Pallas kernels for 12%

profile of v5, /device:TPU:0, one launch (start us, length us, event | category | flops | bytes accessed | tf_op | source)
XLA Modules:
  0.0 744.0 jit_solution(4610594777263361230)
XLA Ops:
  36.7 11.6 %collective-permute-done.6 = bf16[4,16,1536]{2,1,0:T(8,128)(2,1)S(1)} collective-permute-done((bf16[4,16,1536]{2,1,0:T(8,128)(2,1)S(1)}, bf16[4,16,1536]{2,1,0:T(8,128)(2,1)S(1)}, u32[]{:S(2)}, u32[]{:S(2)}) %collective-permute-start.6) | collective-permute-done | bytes 196640 | tf_op jit(solution)/shard_map/ppermute | solution.py:516
  49.3 8.8 %collective-permute-done.7 = bf16[2,16,1536]{2,1,0:T(8,128)(2,1)S(1)} collective-permute-done((bf16[2,16,1536]{2,1,0:T(8,128)(2,1)S(1)}, bf16[2,16,1536]{2,1,0:T(8,128)(2,1)S(1)}, u32[]{:S(2)}, u32[]{:S(2)}) %collective-permute-start.7) | collective-permute-done | bytes 98336 | tf_op jit(solution)/shard_map/ppermute | solution.py:516
  72.1 9.0 %collective-permute-done.2 = f32[16,4608]{1,0:T(8,128)S(1)} collective-permute-done((f32[16,4608]{1,0:T(8,128)S(1)}, f32[16,4608]{1,0:T(8,128)S(1)}, u32[]{:S(2)}, u32[]{:S(2)}) %collective-permute-start.2) | collective-permute-done | bytes 294944 | tf_op jit(solution)/shard_map/ppermute | solution.py:516
  84.3 18.3 %collective-permute-done.3 = f32[16,4608]{1,0:T(8,128)S(1)} collective-permute-done((f32[16,4608]{1,0:T(8,128)S(1)}, f32[16,4608]{1,0:T(8,128)S(1)}, u32[]{:S(2)}, u32[]{:S(2)}) %collective-permute-start.3) | collective-permute-done | bytes 294944 | tf_op jit(solution)/shard_map/ppermute | solution.py:516
  118.2 65.3 %all-gather.3.cloned.1.call-done = bf16[55296,256]{1,0:T(8,128)(2,1)} async-done(((bf16[3456,256]{1,0:T(8,128)(2,1)}), bf16[55296,256]{1,0:T(8,128)(2,1)}) %all-gather.3.cloned.1.call-update) | async-done | bytes 28311568 | tf_op jit(solution)/shard_map/all_gather | solution.py:827
  199.5 19.1 %collective-permute-done.13.rest_1_ = bf16[3,256,768]{2,1,0:T(8,128)(2,1)S(1)} collective-permute-done((bf16[3,256,768]{2,1,0:T(8,128)(2,1)}, bf16[3,256,768]{2,1,0:T(8,128)(2,1)S(1)}, u32[]{:S(2)}, u32[]{:S(2)}) %collective-permute-start.13) | collective-permute-done | bytes 1179680 | tf_op jit(solution)/shard_map/ppermute | solution.py:516
  230.4 29.4 %collective-permute-done.17.rest_5_ = bf16[3,256,768]{2,1,0:T(8,128)(2,1)S(1)} collective-permute-done((bf16[3,256,768]{2,1,0:T(8,128)(2,1)S(1)}, bf16[3,256,768]{2,1,0:T(8,128)(2,1)S(1)}, u32[]{:S(2)}, u32[]{:S(2)}) %collective-permute-start.17) | collective-permute-done | bytes 1179680 | tf_op jit(solution)/shard_map/ppermute | solution.py:511
  268.2 23.5 %shard_map.222 = (bf16[256,768]{1,0:T(8,128)(2,1)}, f32[256,768]{1,0:T(8,128)}, f32[256,768]{1,0:T(8,128)}, f32[256,768]{1,0:T(8,128)}, f32[256,768]{1,0:T(8,128)}, /*index=5*/bf16[16,768]{1,0:T(8,128)(2,1)}) custom-call(s32[13]{0:T(128)} %convert_element_type.318.flag_ref, bf16[3,256,768]{2,1,0:T(8,128)(2,1)} %get-tuple-element.332.q_ref.rest_0_.k_ref.v_ref.refs_7_, ...), custom_call_target="tpu_custom_call" | custom-call | tf_op jit(solution)/shard_map/pallas_call | solution.py:482
  298.7 18.3 %collective-permute-done.21 = bf16[256,1536]{1,0:T(8,128)(2,1)S(1)} collective-permute-done((bf16[256,1536]{1,0:T(8,128)(2,1)}, bf16[256,1536]{1,0:T(8,128)(2,1)S(1)}, u32[]{:S(2)}, u32[]{:S(2)}) %collective-permute-start.21) | collective-permute-done | bytes 786464 | tf_op jit(solution)/shard_map/ppermute | solution.py:520
  322.4 11.3 %shard_map.224 = (f32[256,2048]{1,0:T(8,128)}, f32[256,2048]{1,0:T(8,128)}, bf16[256,2048]{1,0:T(8,128)(2,1)}, bf16[2048,256]{1,0:T(8,128)(2,1)}) custom-call(bf16[256,1536]{1,0:T(8,128)(2,1)} %get-tuple-element.338.b_ref.refs_13_, bf16[16,3456,256]{2,1,0:T(8,128)(2,1)} %bitcast.268, bf16[16,3456,256]{2,1,0:T(8,128)(2,1)} %bitcast.269), custom_call_target="tpu_custom_call" | custom-call | flops 3221225472 | bytes 12582912 | tf_op jit(solution)/shard_map/pallas_call | solution.py:482
  339.9 7.8 %shard_map.225.a_ref.refs_16_ = bf16[256,4096]{1,0:T(8,128)(2,1)} custom-call(bf16[256,1536]{1,0:T(8,128)(2,1)} %copy-done.35, bf16[16,3456,256]{2,1,0:T(8,128)(2,1)} %bitcast.270, f32[256,2048]{1,0:T(8,128)} %get-tuple-element.237.gate_ref, f32[256,2048]{1,0:T(8,128)} %get-tuple-element.238.up_ref), custom_call_target="tpu_custom_call" | custom-call | flops 1610612736 | bytes 6291456 | tf_op jit(solution)/shard_map/pallas_call | solution.py:482
  347.7 9.2 %shard_map.226.refs_17_ = bf16[256,1536]{1,0:T(8,128)(2,1)} custom-call(bf16[256,4096]{1,0:T(8,128)(2,1)} %shard_map.225.a_ref.refs_16_, bf16[16,3456,256]{2,1,0:T(8,128)(2,1)} %bitcast.271), custom_call_target="tpu_custom_call" | custom-call | flops 3221225472 | bytes 12582912 | tf_op jit(solution)/shard_map/pallas_call | solution.py:482
  365.2 10.7 %collective-permute-done.22 = bf16[256,1536]{1,0:T(8,128)(2,1)} collective-permute-done((bf16[256,1536]{1,0:T(8,128)(2,1)}, bf16[256,1536]{1,0:T(8,128)(2,1)}, u32[]{:S(2)}, u32[]{:S(2)}) %collective-permute-start.22) | collective-permute-done | bytes 786464 | tf_op jit(solution)/shard_map/ppermute | solution.py:520
  390.1 9.5 %collective-permute-start.24 = (bf16[1,288,768]{2,1,0:T(8,128)(2,1)}, bf16[1,288,768]{2,1,0:T(8,128)(2,1)S(1)}, u32[]{:S(2)}, u32[]{:S(2)}) collective-permute-start(bf16[1,288,768]{2,1,0:T(8,128)(2,1)} %get-tuple-element.345.d_self_ref.rest_9_.rest_18_.refs_20_), channel_id=1, source_target_pairs={{0,4},{2,6},{4,0},{6,2},{8,12},{10,14},{12,8},{14,10},{16,20},{18,... | collective-permute-start | bytes 1327112 | tf_op jit(solution)/shard_map/ppermute | solution.py:516
  433.2 16.4 %shard_map.229 = (bf16[256,384]{1,0:T(8,128)(2,1)}, f32[1,384]{1,0:T(1,128)}, f32[256,384]{1,0:T(8,128)}, f32[256,384]{1,0:T(8,128)}) custom-call(s32[13]{0:T(128)} %convert_element_type.318.flag_ref, bf16[3,256,768]{2,1,0:T(8,128)(2,1)} %get-tuple-element.332.q_ref.rest_0_.k_ref.v_ref.refs_7_, s32[256,1]{1,0:T(8,128)} %copy.222.own_ids_ref, ...), custom_call_target="tpu_custom_call" | custom-call | tf_op jit(solution)/shard_map/pallas_call | solution.py:482
  461.4 17.3 %shard_map.230 = (bf16[256,384]{1,0:T(8,128)(2,1)}, f32[1,384]{1,0:T(1,128)}, f32[256,384]{1,0:T(8,128)}, f32[256,384]{1,0:T(8,128)}) custom-call(s32[13]{0:T(128)} %convert_element_type.318.flag_ref, bf16[3,256,768]{2,1,0:T(8,128)(2,1)} %get-tuple-element.332.q_ref.rest_0_.k_ref.v_ref.refs_7_, s32[256,1]{1,0:T(8,128)} %copy.222.own_ids_ref, ...), custom_call_target="tpu_custom_call" | custom-call | tf_op jit(solution)/shard_map/pallas_call | solution.py:482
  482.3 8.6 %collective-permute-done.23.refs_31_ = f32[256,1536]{1,0:T(8,128)} collective-permute-done((f32[256,1536]{1,0:T(8,128)}, f32[256,1536]{1,0:T(8,128)}, u32[]{:S(2)}, u32[]{:S(2)}) %collective-permute-start.23) | collective-permute-done | bytes 1572896 | tf_op jit(solution)/shard_map/ppermute | solution.py:520
  500.3 21.7 %shard_map.231 = (bf16[256,1536]{1,0:T(8,128)(2,1)}, f32[1,768]{1,0:T(1,128)}) custom-call(s32[13]{0:T(128)} %convert_element_type.318.flag_ref, bf16[3,256,768]{2,1,0:T(8,128)(2,1)} %get-tuple-element.332.q_ref.rest_0_.k_ref.v_ref.refs_7_, bf16[3,256,768]{2,1,0:T(8,128)(2,1)} %get-tuple-element.332.q_ref.rest_0_.k_ref.v_ref.refs_7_, ...), custom_call_target="tpu_custom_call" | custom-call | tf_op jit(solution)/shard_map/pallas_call | solution.py:482
  547.9 8.1 %collective-permute-done.40.refs_45_ = bf16[4,48,1536]{2,1,0:T(8,128)(2,1)S(1)} collective-permute-done((bf16[4,48,1536]{2,1,0:T(8,128)(2,1)}, bf16[4,48,1536]{2,1,0:T(8,128)(2,1)S(1)}, u32[]{:S(2)}, u32[]{:S(2)}) %collective-permute-start.40) | collective-permute-done | bytes 589856 | tf_op jit(solution)/shard_map/ppermute | solution.py:516
  577.1 15.1 %collective-permute-done.36.refs_53_ = bf16[4,96,768]{2,1,0:T(8,128)(2,1)} collective-permute-done((bf16[4,96,768]{2,1,0:T(8,128)(2,1)}, bf16[4,96,768]{2,1,0:T(8,128)(2,1)}, u32[]{:S(2)}, u32[]{:S(2)}) %collective-permute-start.36) | collective-permute-done | bytes 589856 | tf_op jit(solution)/shard_map/ppermute | solution.py:516
  631.1 8.6 %collective-permute-done.50.refs_62_ = bf16[2,96,1536]{2,1,0:T(8,128)(2,1)S(1)} collective-permute-done((bf16[2,96,1536]{2,1,0:T(8,128)(2,1)S(1)}, bf16[2,96,1536]{2,1,0:T(8,128)(2,1)S(1)}, u32[]{:S(2)}, u32[]{:S(2)}) %collective-permute-start.50) | collective-permute-done | bytes 589856 | tf_op jit(solution)/shard_map/ppermute | solution.py:516
  652.4 18.8 %collective-permute-done.54 = bf16[18,4608]{1,0:T(8,128)(2,1)S(1)} collective-permute-done((bf16[18,4608]{1,0:T(8,128)(2,1)S(1)}, bf16[18,4608]{1,0:T(8,128)(2,1)S(1)}, u32[]{:S(2)}, u32[]{:S(2)}) %collective-permute-start.54) | collective-permute-done | bytes 165920 | tf_op jit(solution)/shard_map/ppermute | solution.py:516
  680.5 7.4 shard_map.233
  709.5 20.2 %shard_map.234 = (f32[12288,128]{1,0:T(8,128)}, f32[12288,128]{1,0:T(8,128)}, f32[12288,128]{1,0:T(8,128)}, f32[12288,128]{1,0:T(8,128)}, bf16[12288,128]{1,0:T(8,128)(2,1)}) custom-call(f32[1]{0:T(128)} %bitcast.112.clip_ref, f32[12288,128]{1,0:T(8,128)} %get-tuple-element.404.g_ref, f32[12288,128]{1,0:T(8,128)} %bitcast.290, f32[12288,128]{1,0:T(8,128)} %bitcast.291, ...), custom_call_target="tpu_custom_call" | custom-call | flops 31457280 | bytes 59768832 | tf_op jit(solution)/shard_map/pallas_call | solution.py:482
  (657 shorter events, 331.1 us)
Async XLA Ops:
  7.2 176.3 %all-gather.3.cloned.1.call-start = ((), (), s32[]{:S(2)}) async-start(), calls=%async_computation.5 | async-start | bytes 30081024 | tf_op jit(solution)/shard_map/all_gather | solution.py:827
  22.0 468.9 %reduce-scatter.3.cloned.1.call-start = ((), (), s32[]{:S(2)}) async-start(), calls=%async_computation.3 | async-start | bytes 6684672 | tf_op jit(solution)/shard_map/reduce_scatter | solution.py:824
  23.0 25.5 %collective-permute-start = (f32[16,4608]{1,0:T(8,128)S(1)}, f32[16,4608]{1,0:T(8,128)S(1)}, u32[]{:S(2)}, u32[]{:S(2)}) collective-permute-start(f32[16,4608]{1,0:T(8,128)S(1)} %fusion.118), channel_id=1, source_target_pairs={{0,2},{2,0},{4,6},{6,4},{8,10},{10,8},{12,14},{14,12},{16,18},{18,... | collective-permute-start | bytes 884744 | tf_op jit(solution)/shard_map/ppermute | solution.py:516
  190.2 28.4 %collective-permute-start.13 = (bf16[3,256,768]{2,1,0:T(8,128)(2,1)}, bf16[3,256,768]{2,1,0:T(8,128)(2,1)S(1)}, u32[]{:S(2)}, u32[]{:S(2)}) collective-permute-start(bf16[3,256,768]{2,1,0:T(8,128)(2,1)} %get-tuple-element.332.q_ref.rest_0_.k_ref.v_ref.refs_7_), channel_id=1, source_target_pairs={{0,4},{2,6},{4,0},{6,2},{8,12},{10,14},{12,8},{14,10},{16,20},{18,... | collective-permute-start | bytes 3538952 | tf_op jit(solution)/shard_map/ppermute | solution.py:516
  191.4 29.9 %collective-permute-start.14 = (bf16[3,256,768]{2,1,0:T(8,128)(2,1)}, bf16[3,256,768]{2,1,0:T(8,128)(2,1)S(1)}, u32[]{:S(2)}, u32[]{:S(2)}) collective-permute-start(bf16[3,256,768]{2,1,0:T(8,128)(2,1)} %get-tuple-element.332.q_ref.rest_0_.k_ref.v_ref.refs_7_), channel_id=1, source_target_pairs={{8,0},{10,2},{12,4},{14,6},{16,8},{18,10},{20,12},{22,14},{24,16},... | collective-permute-start | bytes 3538952 | tf_op jit(solution)/shard_map/ppermute | solution.py:511
  192.7 29.9 %collective-permute-start.15 = (bf16[3,256,768]{2,1,0:T(8,128)(2,1)}, bf16[3,256,768]{2,1,0:T(8,128)(2,1)S(1)}, u32[]{:S(2)}, u32[]{:S(2)}) collective-permute-start(bf16[3,256,768]{2,1,0:T(8,128)(2,1)} %get-tuple-element.332.q_ref.rest_0_.k_ref.v_ref.refs_7_), channel_id=1, source_target_pairs={{0,8},{2,10},{4,12},{6,14},{8,16},{10,18},{12,20},{14,22},{16,24},... | collective-permute-start | bytes 3538952 | tf_op jit(solution)/shard_map/ppermute | solution.py:511
  223.8 36.0 %collective-permute-start.19 = (bf16[12,256,768]{2,1,0:T(8,128)(2,1)S(1)}, bf16[12,256,768]{2,1,0:T(8,128)(2,1)}, u32[]{:S(2)}, u32[]{:S(2)}) collective-permute-start(bf16[12,256,768]{2,1,0:T(8,128)(2,1)S(1)} %constant_dynamic-update-slice_fusion.refs_8_), channel_id=1, source_target_pairs={{0,2},{2,0},{4,6},{6,4},{8,10},{10,8},{12,14},{14,12},{16,18},{18,... | collective-permute-start | bytes 14155784 | tf_op jit(solution)/shard_map/ppermute | solution.py:516
  223.9 35.9 %collective-permute-start.17 = (bf16[3,256,768]{2,1,0:T(8,128)(2,1)S(1)}, bf16[3,256,768]{2,1,0:T(8,128)(2,1)S(1)}, u32[]{:S(2)}, u32[]{:S(2)}) collective-permute-start(bf16[3,256,768]{2,1,0:T(8,128)(2,1)S(1)} %collective-permute-done.13.rest_1_), channel_id=1, source_target_pairs={{8,0},{10,2},{12,4},{14,6},{16,8},{18,10},{20,12},{22,14},{24,16},... | collective-permute-start | bytes 3538952 | tf_op jit(solution)/shard_map/ppermute | solution.py:511
  225.2 34.6 %collective-permute-start.18 = (bf16[3,256,768]{2,1,0:T(8,128)(2,1)S(1)}, bf16[3,256,768]{2,1,0:T(8,128)(2,1)S(1)}, u32[]{:S(2)}, u32[]{:S(2)}) collective-permute-start(bf16[3,256,768]{2,1,0:T(8,128)(2,1)S(1)} %collective-permute-done.13.rest_1_), channel_id=1, source_target_pairs={{0,8},{2,10},{4,12},{6,14},{8,16},{10,18},{12,20},{14,22},{16,24},... | collective-permute-start | bytes 3538952 | tf_op jit(solution)/shard_map/ppermute | solution.py:511
  339.5 276.2 %reduce-scatter.5.cloned.1.call-start = ((), (), s32[]{:S(2)}) async-start(), calls=%async_computation.4 | async-start | bytes 13369344 | tf_op jit(solution)/shard_map/reduce_scatter | solution.py:824
  390.1 28.5 %collective-permute-start.24 = (bf16[1,288,768]{2,1,0:T(8,128)(2,1)}, bf16[1,288,768]{2,1,0:T(8,128)(2,1)S(1)}, u32[]{:S(2)}, u32[]{:S(2)}) collective-permute-start(bf16[1,288,768]{2,1,0:T(8,128)(2,1)} %get-tuple-element.345.d_self_ref.rest_9_.rest_18_.refs_20_), channel_id=1, source_target_pairs={{0,4},{2,6},{4,0},{6,2},{8,12},{10,14},{12,8},{14,10},{16,20},{18,... | collective-permute-start | bytes 1327112 | tf_op jit(solution)/shard_map/ppermute | solution.py:516
  424.4 25.2 %collective-permute-start.30 = (bf16[4,288,768]{2,1,0:T(8,128)(2,1)}, bf16[4,288,768]{2,1,0:T(8,128)(2,1)}, u32[]{:S(2)}, u32[]{:S(2)}) collective-permute-start(bf16[4,288,768]{2,1,0:T(8,128)(2,1)} %constant_dynamic-update-slice_fusion.12.refs_22_), channel_id=1, source_target_pairs={{0,2},{2,0},{4,6},{6,4},{8,10},{10,8},{12,14},{14,12},{16,18},{18,... | collective-permute-start | bytes 5308424 | tf_op jit(solution)/shard_map/ppermute | solution.py:516
  424.4 25.1 %collective-permute-start.28 = (bf16[1,288,768]{2,1,0:T(8,128)(2,1)S(1)}, bf16[1,288,768]{2,1,0:T(8,128)(2,1)S(1)}, u32[]{:S(2)}, u32[]{:S(2)}) collective-permute-start(bf16[1,288,768]{2,1,0:T(8,128)(2,1)S(1)} %collective-permute-done.24.rest_10_.rest_19_), channel_id=1, source_target_pairs={{8,0},{10,2},{12,4},{14,6},{16,8},{18,10},{20,12},{22,14},{24,16},... | collective-permute-start | bytes 1327112 | tf_op jit(solution)/shard_map/ppermute | solution.py:511
  453.7 37.1 %collective-permute-start.23 = (f32[256,1536]{1,0:T(8,128)}, f32[256,1536]{1,0:T(8,128)}, u32[]{:S(2)}, u32[]{:S(2)}) collective-permute-start(f32[256,1536]{1,0:T(8,128)} %shard_map.228.refs_21_), channel_id=1, source_target_pairs={{0,1},{1,0},{2,3},{3,2},{4,5},{5,4},{6,7},{7,6},{8,9},{9,8},{10,11... | collective-permute-start | bytes 4718600 | tf_op jit(solution)/shard_map/ppermute | solution.py:520
  526.9 29.1 %collective-permute-start.40 = (bf16[4,48,1536]{2,1,0:T(8,128)(2,1)}, bf16[4,48,1536]{2,1,0:T(8,128)(2,1)S(1)}, u32[]{:S(2)}, u32[]{:S(2)}) collective-permute-start(bf16[4,48,1536]{2,1,0:T(8,128)(2,1)} %fusion.3.refs_28_), channel_id=1, source_target_pairs={{0,4},{2,6},{4,0},{6,2},{8,12},{10,14},{12,8},{14,10},{16,20},{18,... | collective-permute-start | bytes 1769480 | tf_op jit(solution)/shard_map/ppermute | solution.py:516
  567.3 32.1 %collective-permute-start.35 = (bf16[256,1536]{1,0:T(8,128)(2,1)S(1)}, bf16[256,1536]{1,0:T(8,128)(2,1)}, u32[]{:S(2)}, u32[]{:S(2)}) collective-permute-start(bf16[256,1536]{1,0:T(8,128)(2,1)S(1)} %copy-done.14), channel_id=1, source_target_pairs={{0,1},{1,0},{2,3},{3,2},{4,5},{5,4},{6,7},{7,6},{8,9},{9,8},{10,11... | collective-permute-start | bytes 2359304 | tf_op jit(solution)/shard_map/ppermute | solution.py:520
  569.5 46.2 %collective-permute-start.42 = (bf16[4,96,1536]{2,1,0:T(8,128)(2,1)}, bf16[4,96,1536]{2,1,0:T(8,128)(2,1)}, u32[]{:S(2)}, u32[]{:S(2)}) collective-permute-start(bf16[4,96,1536]{2,1,0:T(8,128)(2,1)} %fusion.1.refs_42_), channel_id=1, source_target_pairs={{0,4},{2,6},{4,0},{6,2},{8,12},{10,14},{12,8},{14,10},{16,20},{18,... | collective-permute-start | bytes 3538952 | tf_op jit(solution)/shard_map/ppermute | solution.py:516
  571.5 75.5 %collective-permute-start.45 = (bf16[2,48,1536]{2,1,0:T(8,128)(2,1)}, bf16[2,48,1536]{2,1,0:T(8,128)(2,1)}, u32[]{:S(2)}, u32[]{:S(2)}) collective-permute-start(bf16[2,48,1536]{2,1,0:T(8,128)(2,1)} %fusion.57.refs_46_), channel_id=1, source_target_pairs={{0,8},{2,10},{4,12},{6,14},{8,0},{10,2},{12,4},{14,6},{16,24},{18,... | collective-permute-start | bytes 884744 | tf_op jit(solution)/shard_map/ppermute | solution.py:516
  595.7 55.1 %collective-permute-start.44 = (bf16[2,96,768]{2,1,0:T(8,128)(2,1)}, bf16[2,96,768]{2,1,0:T(8,128)(2,1)}, u32[]{:S(2)}, u32[]{:S(2)}) collective-permute-start(bf16[2,96,768]{2,1,0:T(8,128)(2,1)} %fusion.58.refs_54_.refs_55_), channel_id=1, source_target_pairs={{0,8},{2,10},{4,12},{6,14},{8,0},{10,2},{12,4},{14,6},{16,24},{18,... | collective-permute-start | bytes 884744 | tf_op jit(solution)/shard_map/ppermute | solution.py:516
  612.6 31.8 %collective-permute-start.46 = (bf16[2,16,1536]{2,1,0:T(8,128)(2,1)}, bf16[2,16,1536]{2,1,0:T(8,128)(2,1)}, u32[]{:S(2)}, u32[]{:S(2)}) collective-permute-start(bf16[2,16,1536]{2,1,0:T(8,128)(2,1)} %maximum_select_fusion.10.refs_57_), channel_id=1, source_target_pairs={{0,8},{2,10},{4,12},{6,14},{8,0},{10,2},{12,4},{14,6},{16,24},{18,... | collective-permute-start | bytes 294920 | tf_op jit(solution)/shard_map/ppermute | solution.py:516
  640.5 33.3 %collective-permute-start.53 = (bf16[1,96,1536]{2,1,0:T(8,128)(2,1)S(1)}, bf16[1,96,1536]{2,1,0:T(8,128)(2,1)S(1)}, u32[]{:S(2)}, u32[]{:S(2)}) collective-permute-start(bf16[1,96,1536]{2,1,0:T(8,128)(2,1)S(1)} %dynamic-slice_convert_fusion.1.refs_63_), channel_id=1, source_target_pairs={{0,16},{2,18},{4,20},{6,22},{8,24},{10,26},{12,28},{14,30},{16,0},... | collective-permute-start | bytes 884744 | tf_op jit(solution)/shard_map/ppermute | solution.py:516
  644.4 26.8 %collective-permute-start.54 = (bf16[18,4608]{1,0:T(8,128)(2,1)S(1)}, bf16[18,4608]{1,0:T(8,128)(2,1)S(1)}, u32[]{:S(2)}, u32[]{:S(2)}) collective-permute-start(bf16[18,4608]{1,0:T(8,128)(2,1)S(1)} %pad_maximum_fusion.4.refs_64_), channel_id=1, source_target_pairs={{0,16},{2,18},{4,20},{6,22},{8,24},{10,26},{12,28},{14,30},{16,0},... | collective-permute-start | bytes 497672 | tf_op jit(solution)/shard_map/ppermute | solution.py:516
  648.0 26.7 %collective-permute-start.52 = (bf16[1,48,1536]{2,1,0:T(8,128)(2,1)S(1)}, bf16[1,48,1536]{2,1,0:T(8,128)(2,1)S(1)}, u32[]{:S(2)}, u32[]{:S(2)}) collective-permute-start(bf16[1,48,1536]{2,1,0:T(8,128)(2,1)S(1)} %dynamic-slice_convert_fusion.3.refs_67_), channel_id=1, source_target_pairs={{0,16},{2,18},{4,20},{6,22},{8,24},{10,26},{12,28},{14,30},{16,0},... | collective-permute-start | bytes 442376 | tf_op jit(solution)/shard_map/ppermute | solution.py:516
  652.3 25.7 %collective-permute-start.56 = (bf16[8,16,1536]{2,1,0:T(8,128)(2,1)S(1)}, bf16[8,16,1536]{2,1,0:T(8,128)(2,1)S(1)}, u32[]{:S(2)}, u32[]{:S(2)}) collective-permute-start(bf16[8,16,1536]{2,1,0:T(8,128)(2,1)S(1)} %bitcast.304), channel_id=1, source_target_pairs={{0,2},{2,0},{4,6},{6,4},{8,10},{10,8},{12,14},{14,12},{16,18},{18,... | collective-permute-start | bytes 1179656 | tf_op jit(solution)/shard_map/ppermute | solution.py:516
  (187 other events, 1976.1 us)
Sparse Core Ops, SparseCore 0:
  13.2 170.3 all-gather.2
  339.6 105.9 reduce-scatter.2
  450.2 158.7 reduce-scatter.4

commit v6 on v5

--- a/solution.py
+++ b/solution.py
@@ -445,15 +445,11 @@
 
 
 def flatten_kernel(places, *refs):
-    *in_refs, lines_ref, square_ref = refs
-    grad_refs = in_refs[: len(places)]
-    square = jnp.zeros((1, LANES), f32)
-    for (start, column, columns), ref in zip(places, grad_refs):
+    *in_refs, lines_ref = refs
+    for (start, column, columns), ref in zip(places, in_refs):
         for at in range(ref.shape[1] // LANES):
             part = ref[:, at * LANES : (at + 1) * LANES].astype(f32)
             lines_ref[pl.ds(start + column // LANES + at, ref.shape[0], stride=columns // LANES), :] = part
-            square = square + jnp.sum(part * part, axis=0, keepdims=True)
-    square_ref[...] = square
 
 
 def update_kernel(clip_ref, g_ref, one_ref, two_ref, w_ref, avg_ref, one_out, two_out, w_out, avg_out, low_out):
@@ -532,14 +528,14 @@
     return x
 
 
-def sum_over_all(x):
+def few_over_img(x):
     bits = index_bits(lax.axis_size("img"))
     for bit in range(0, bits - 1, 2):
         low, high = 1 << bit, 2 << bit
         x = (x + crossed(x, low)) + (crossed(x, high) + crossed(x, low | high))
     if bits % 2:
         x = x + crossed(x, 1 << (bits - 1))
-    return x + other_txt(x)
+    return x
 
 
 def own_and_other(x, bit, below=1):
@@ -1209,7 +1205,6 @@
     d_gain_text = jnp.sum(d_text_scaled * text_normed, axis=(0, 1))
     d_text_raw = rms_back(text_raw, d_text_scaled * gain_text).reshape(text_rows, half_d)
     text_gather = SmallGather(clock, jnp.concatenate([d_text_raw, text_own[:, half_d:]], axis=1).astype(bf16))
-    query_sum.advance()
     d_attn_other = clock.stage(d_attn_other)
     d_attn_in = d_attn_part.astype(f32) + d_attn_other.astype(f32)
     d_scale_one = d_attn_in * normed_one
@@ -1234,20 +1229,21 @@
     small_count = small_terms.shape[0]
     small_row = jnp.pad(small_terms, (0, d_mod.shape[1] - small_count))[None]
     small_sum = SmallSum(clock, d_mod, small_row)
+    output_sum.advance()
+    query_sum.advance()
     text_gather.advance()
     (grad_updown,) = key_value_sum.advance(beside=(grad_updown,))
     small_sum.advance()
     small_sum.advance()
+    query_sum.advance()
     key_value_sum.advance()
     small_sum.advance()
     text_gather.advance()
     output_sum.advance()
+    text_gather.advance()
     query_sum.advance()
-    text_gather.advance()
     small_sum.advance()
     key_value_sum.advance()
-    output_sum.advance()
-    query_sum.advance()
     while text_gather.bit:
         text_gather.advance()
     grad_text = mm(text_columns, text_gather.result(), 0, 0)
@@ -1267,15 +1263,19 @@
     grads = [grad_updown, grad_down, query_sum.result, grad_text, output_sum.result, grad_modulate, key_value_sum.result]
     places = [(start, 0, columns) for start, (_, columns) in zip(starts, tables)]
     places.append((starts[2], half_d, 3 * half_d))
-    reduced, squares = pl.pallas_call(
+    square = sum(jnp.sum(jnp.square(g.astype(f32))) for g in grads)
+    squares = jnp.pad(square.reshape(1, 1), ((0, 0), (0, LANES - 1)))
+    reduced = pl.pallas_call(
         functools.partial(flatten_kernel, places),
-        out_shape=[shape_of((lines, LANES), f32), shape_of((1, LANES), f32)],
+        out_shape=shape_of((lines, LANES), f32),
         in_specs=[pl.BlockSpec(memory_space=pltpu.VMEM)] * len(grads)
         + [pl.BlockSpec(memory_space=pl.ANY)] * len(clock.kept),
         compiler_params=pltpu.CompilerParams(vmem_limit_bytes=58 * MIB),
     )(*grads, *clock.kept)
 
-    last = sum_over_all(jnp.concatenate([squares, jnp.pad(d_gain_text, (0, LANES - HD))[None]], axis=0))
+    last = few_over_img(jnp.concatenate([squares, jnp.pad(d_gain_text, (0, LANES - HD))[None]], axis=0))
+    last, reduced = lax.optimization_barrier((last, reduced))
+    last = last + other_txt(last)
     small_grad = lax.dynamic_update_slice(small_grad, last[1, :HD], (2 * D + 2 * HD,))
     grad_square = jnp.sum(last[0]) + jnp.sum(small_grad * small_grad)
     clip_factor = MAX_NORM / jnp.maximum(jnp.sqrt(grad_square), MAX_NORM)

time: 755 us -> 755 us (level)
  Pallas kernels: 172 us -> 154 us
  other arithmetic: 50.7 us -> 59 us
    ppermute x48, waiting for transfers between devices: 145 us -> 125 us  [crossed(): return lax.ppermute(x, 'img', [(i, i ^ bit) for i in range(count)])]
    pallas_call x13, Pallas kernels: 159 us -> 141 us  [call(): pl.pallas_call(kernel, grid_spec=pltpu.PrefetchScalarGridSpec(num_scalar_...]
    ppermute x7, waiting for transfers between devices: 42.6 us -> 56.8 us  [other_txt(): return lax.ppermute(x, 'txt', [(0, 1), (1, 0)])]
    unnamed x303 -> x287, local copies, waits for them, and re-layouts: 17.8 us -> 16 us
  transfers between devices with their start and end apart: 69 -> 69, of which waited for: 32 -> 32; matrix products, arithmetic and copies ran while one was open for 16% -> 17% of each run, Pallas kernels for 12% -> 12%
where the time goes in v6:
time: 755 us; the launch traced here: 747 us
  waiting for transfers between devices  294 us (39%)
  Pallas kernels  154 us (20%)
  starting transfers between devices  116 us (15%)
  other arithmetic  59 us (8%)
  local copies, waits for them, and re-layouts  51.3 us (7%)
  matrix products  49.6 us (7%)
  between operations  23.6 us (3%)
    pallas_call x13, Pallas kernels, call(): pl.pallas_call(kernel, grid_spec=pltpu.PrefetchScalarGridSpec(num_scalar_...  141 us
    ppermute x48, waiting for transfers between devices, crossed(): return lax.ppermute(x, 'img', [(i, i ^ bit) for i in range(count)])  125 us
    all_gather x1, waiting for transfers between devices, gather(): return lax.all_gather(rows, 'img', axis=0, tiled=True)  65.3 us
    ppermute x48, starting transfers between devices, crossed(): return lax.ppermute(x, 'img', [(i, i ^ bit) for i in range(count)])  64 us
    ppermute x7, waiting for transfers between devices, other_txt(): return lax.ppermute(x, 'txt', [(0, 1), (1, 0)])  56.8 us
    ppermute x8, waiting for transfers between devices, shifted(): lax.ppermute(x, 'img', [(i + by, i) for i in range(count) if 0 <= i + by...  43.1 us
    dot_general x12, matrix products, mm(): lax.dot_general(a, b, (((on_a,), (on_b,)), ((), ())), preferred_element_t...  33.1 us
    ppermute x8, starting transfers between devices, shifted(): lax.ppermute(x, 'img', [(i + by, i) for i in range(count) if 0 <= i + by...  31.1 us
  transfers between devices with their start and end apart: 69, of which 32 were waited for; matrix products, arithmetic and copies ran while one was open for 17% of the time, Pallas kernels for 12%

profile of v6, /device:TPU:0, one launch (start us, length us, event | category | flops | bytes accessed | tf_op | source)
XLA Modules:
  0.0 747.0 jit_solution(13493178869519678209)
XLA Ops:
  36.7 11.6 %collective-permute-done.6 = bf16[4,16,1536]{2,1,0:T(8,128)(2,1)S(1)} collective-permute-done((bf16[4,16,1536]{2,1,0:T(8,128)(2,1)S(1)}, bf16[4,16,1536]{2,1,0:T(8,128)(2,1)S(1)}, u32[]{:S(2)}, u32[]{:S(2)}) %collective-permute-start.6) | collective-permute-done | bytes 196640 | tf_op jit(solution)/shard_map/ppermute | solution.py:512
  49.3 8.8 %collective-permute-done.7 = bf16[2,16,1536]{2,1,0:T(8,128)(2,1)S(1)} collective-permute-done((bf16[2,16,1536]{2,1,0:T(8,128)(2,1)S(1)}, bf16[2,16,1536]{2,1,0:T(8,128)(2,1)S(1)}, u32[]{:S(2)}, u32[]{:S(2)}) %collective-permute-start.7) | collective-permute-done | bytes 98336 | tf_op jit(solution)/shard_map/ppermute | solution.py:512
  72.1 9.0 %collective-permute-done.2 = f32[16,4608]{1,0:T(8,128)S(1)} collective-permute-done((f32[16,4608]{1,0:T(8,128)S(1)}, f32[16,4608]{1,0:T(8,128)S(1)}, u32[]{:S(2)}, u32[]{:S(2)}) %collective-permute-start.2) | collective-permute-done | bytes 294944 | tf_op jit(solution)/shard_map/ppermute | solution.py:512
  84.3 18.3 %collective-permute-done.3 = f32[16,4608]{1,0:T(8,128)S(1)} collective-permute-done((f32[16,4608]{1,0:T(8,128)S(1)}, f32[16,4608]{1,0:T(8,128)S(1)}, u32[]{:S(2)}, u32[]{:S(2)}) %collective-permute-start.3) | collective-permute-done | bytes 294944 | tf_op jit(solution)/shard_map/ppermute | solution.py:512
  118.2 65.3 %all-gather.3.cloned.1.call-done = bf16[55296,256]{1,0:T(8,128)(2,1)} async-done(((bf16[3456,256]{1,0:T(8,128)(2,1)}), bf16[55296,256]{1,0:T(8,128)(2,1)}) %all-gather.3.cloned.1.call-update) | async-done | bytes 28311568 | tf_op jit(solution)/shard_map/all_gather | solution.py:823
  199.4 19.1 %collective-permute-done.13.rest_1_ = bf16[3,256,768]{2,1,0:T(8,128)(2,1)S(1)} collective-permute-done((bf16[3,256,768]{2,1,0:T(8,128)(2,1)}, bf16[3,256,768]{2,1,0:T(8,128)(2,1)S(1)}, u32[]{:S(2)}, u32[]{:S(2)}) %collective-permute-start.13) | collective-permute-done | bytes 1179680 | tf_op jit(solution)/shard_map/ppermute | solution.py:512
  230.3 29.4 %collective-permute-done.17.rest_5_ = bf16[3,256,768]{2,1,0:T(8,128)(2,1)S(1)} collective-permute-done((bf16[3,256,768]{2,1,0:T(8,128)(2,1)S(1)}, bf16[3,256,768]{2,1,0:T(8,128)(2,1)S(1)}, u32[]{:S(2)}, u32[]{:S(2)}) %collective-permute-start.17) | collective-permute-done | bytes 1179680 | tf_op jit(solution)/shard_map/ppermute | solution.py:507
  268.2 18.0 %shard_map.222 = (bf16[256,768]{1,0:T(8,128)(2,1)}, f32[256,768]{1,0:T(8,128)}, f32[256,768]{1,0:T(8,128)}, f32[256,768]{1,0:T(8,128)}, f32[256,768]{1,0:T(8,128)}, /*index=5*/bf16[16,768]{1,0:T(8,128)(2,1)}) custom-call(s32[13]{0:T(128)} %convert_element_type.326.flag_ref, bf16[3,256,768]{2,1,0:T(8,128)(2,1)} %get-tuple-element.332.q_ref.rest_0_.k_ref.v_ref.refs_7_, ...), custom_call_target="tpu_custom_call" | custom-call | tf_op jit(solution)/shard_map/pallas_call | solution.py:478
  293.2 18.3 %collective-permute-done.21 = bf16[256,1536]{1,0:T(8,128)(2,1)S(1)} collective-permute-done((bf16[256,1536]{1,0:T(8,128)(2,1)}, bf16[256,1536]{1,0:T(8,128)(2,1)S(1)}, u32[]{:S(2)}, u32[]{:S(2)}) %collective-permute-start.21) | collective-permute-done | bytes 786464 | tf_op jit(solution)/shard_map/ppermute | solution.py:516
  316.8 11.3 %shard_map.224 = (f32[256,2048]{1,0:T(8,128)}, f32[256,2048]{1,0:T(8,128)}, bf16[256,2048]{1,0:T(8,128)(2,1)}, bf16[2048,256]{1,0:T(8,128)(2,1)}) custom-call(bf16[256,1536]{1,0:T(8,128)(2,1)} %get-tuple-element.338.b_ref.refs_13_, bf16[16,3456,256]{2,1,0:T(8,128)(2,1)} %bitcast.272, bf16[16,3456,256]{2,1,0:T(8,128)(2,1)} %bitcast.273), custom_call_target="tpu_custom_call" | custom-call | flops 3221225472 | bytes 12582912 | tf_op jit(solution)/shard_map/pallas_call | solution.py:478
  334.3 7.8 %shard_map.225.a_ref.refs_16_ = bf16[256,4096]{1,0:T(8,128)(2,1)} custom-call(bf16[256,1536]{1,0:T(8,128)(2,1)} %copy-done.35, bf16[16,3456,256]{2,1,0:T(8,128)(2,1)} %bitcast.274, f32[256,2048]{1,0:T(8,128)} %get-tuple-element.237.gate_ref, f32[256,2048]{1,0:T(8,128)} %get-tuple-element.238.up_ref), custom_call_target="tpu_custom_call" | custom-call | flops 1610612736 | bytes 6291456 | tf_op jit(solution)/shard_map/pallas_call | solution.py:478
  342.1 8.7 %shard_map.226.refs_17_ = bf16[256,1536]{1,0:T(8,128)(2,1)} custom-call(bf16[256,4096]{1,0:T(8,128)(2,1)} %shard_map.225.a_ref.refs_16_, bf16[16,3456,256]{2,1,0:T(8,128)(2,1)} %bitcast.275), custom_call_target="tpu_custom_call" | custom-call | flops 3221225472 | bytes 12582912 | tf_op jit(solution)/shard_map/pallas_call | solution.py:478
  359.0 10.9 %collective-permute-done.22 = bf16[256,1536]{1,0:T(8,128)(2,1)} collective-permute-done((bf16[256,1536]{1,0:T(8,128)(2,1)}, bf16[256,1536]{1,0:T(8,128)(2,1)}, u32[]{:S(2)}, u32[]{:S(2)}) %collective-permute-start.22) | collective-permute-done | bytes 786464 | tf_op jit(solution)/shard_map/ppermute | solution.py:516
  382.2 9.3 %collective-permute-start.24 = (bf16[1,288,768]{2,1,0:T(8,128)(2,1)}, bf16[1,288,768]{2,1,0:T(8,128)(2,1)S(1)}, u32[]{:S(2)}, u32[]{:S(2)}) collective-permute-start(bf16[1,288,768]{2,1,0:T(8,128)(2,1)} %get-tuple-element.345.d_self_ref.rest_9_.rest_18_.refs_20_), channel_id=1, source_target_pairs={{0,4},{2,6},{4,0},{6,2},{8,12},{10,14},{12,8},{14,10},{16,20},{18,... | collective-permute-start | bytes 1327112 | tf_op jit(solution)/shard_map/ppermute | solution.py:512
  421.5 10.4 %collective-permute-start.29 = (bf16[1,288,768]{2,1,0:T(8,128)(2,1)S(1)}, bf16[1,288,768]{2,1,0:T(8,128)(2,1)}, u32[]{:S(2)}, u32[]{:S(2)}) collective-permute-start(bf16[1,288,768]{2,1,0:T(8,128)(2,1)S(1)} %collective-permute-done.24.rest_10_.rest_19_), channel_id=1, source_target_pairs={{0,8},{2,10},{4,12},{6,14},{8,16},{10,18},{12,20},{14,22},{16,24},... | collective-permute-start | bytes 1327112 | tf_op jit(solution)/shard_map/ppermute | solution.py:507
  433.8 13.3 %shard_map.229 = (bf16[256,384]{1,0:T(8,128)(2,1)}, f32[1,384]{1,0:T(1,128)}, f32[256,384]{1,0:T(8,128)}, f32[256,384]{1,0:T(8,128)}) custom-call(s32[13]{0:T(128)} %convert_element_type.326.flag_ref, bf16[3,256,768]{2,1,0:T(8,128)(2,1)} %get-tuple-element.332.q_ref.rest_0_.k_ref.v_ref.refs_7_, s32[256,1]{1,0:T(8,128)} %copy.222.own_ids_ref, ...), custom_call_target="tpu_custom_call" | custom-call | tf_op jit(solution)/shard_map/pallas_call | solution.py:478
  463.8 14.2 %shard_map.230 = (bf16[256,384]{1,0:T(8,128)(2,1)}, f32[1,384]{1,0:T(1,128)}, f32[256,384]{1,0:T(8,128)}, f32[256,384]{1,0:T(8,128)}) custom-call(s32[13]{0:T(128)} %convert_element_type.326.flag_ref, bf16[3,256,768]{2,1,0:T(8,128)(2,1)} %get-tuple-element.332.q_ref.rest_0_.k_ref.v_ref.refs_7_, s32[256,1]{1,0:T(8,128)} %copy.222.own_ids_ref, ...), custom_call_target="tpu_custom_call" | custom-call | tf_op jit(solution)/shard_map/pallas_call | solution.py:478
  481.7 12.0 %collective-permute-done.23.refs_31_ = f32[256,1536]{1,0:T(8,128)} collective-permute-done((f32[256,1536]{1,0:T(8,128)}, f32[256,1536]{1,0:T(8,128)}, u32[]{:S(2)}, u32[]{:S(2)}) %collective-permute-start.23) | collective-permute-done | bytes 1572896 | tf_op jit(solution)/shard_map/ppermute | solution.py:516
  503.4 16.3 %shard_map.231 = (bf16[256,1536]{1,0:T(8,128)(2,1)}, f32[1,768]{1,0:T(1,128)}) custom-call(s32[13]{0:T(128)} %convert_element_type.326.flag_ref, bf16[3,256,768]{2,1,0:T(8,128)(2,1)} %get-tuple-element.332.q_ref.rest_0_.k_ref.v_ref.refs_7_, bf16[3,256,768]{2,1,0:T(8,128)(2,1)} %get-tuple-element.332.q_ref.rest_0_.k_ref.v_ref.refs_7_, ...), custom_call_target="tpu_custom_call" | custom-call | tf_op jit(solution)/shard_map/pallas_call | solution.py:478
  524.4 16.5 %collective-permute-start.39 = (bf16[4,48,1536]{2,1,0:T(8,128)(2,1)}, bf16[4,48,1536]{2,1,0:T(8,128)(2,1)}, u32[]{:S(2)}, u32[]{:S(2)}) collective-permute-start(bf16[4,48,1536]{2,1,0:T(8,128)(2,1)} %fusion.3.refs_28_), channel_id=1, source_target_pairs={{0,4},{2,6},{4,0},{6,2},{8,12},{10,14},{12,8},{14,10},{16,20},{18,... | collective-permute-start | bytes 1769480 | tf_op jit(solution)/shard_map/ppermute | solution.py:512
  585.8 10.9 %collective-permute-done.35 = bf16[256,1536]{1,0:T(8,128)(2,1)} collective-permute-done((bf16[256,1536]{1,0:T(8,128)(2,1)S(1)}, bf16[256,1536]{1,0:T(8,128)(2,1)}, u32[]{:S(2)}, u32[]{:S(2)}) %collective-permute-start.35) | collective-permute-done | bytes 786464 | tf_op jit(solution)/shard_map/ppermute | solution.py:516
  644.3 8.0 %collective-permute-done.51.refs_66_ = bf16[2,96,1536]{2,1,0:T(8,128)(2,1)} collective-permute-done((bf16[2,96,1536]{2,1,0:T(8,128)(2,1)}, bf16[2,96,1536]{2,1,0:T(8,128)(2,1)}, u32[]{:S(2)}, u32[]{:S(2)}) %collective-permute-start.51) | collective-permute-done | bytes 589856 | tf_op jit(solution)/shard_map/ppermute | solution.py:512
  665.3 11.8 %collective-permute-done.56 = bf16[18,4608]{1,0:T(8,128)(2,1)S(1)} collective-permute-done((bf16[18,4608]{1,0:T(8,128)(2,1)S(1)}, bf16[18,4608]{1,0:T(8,128)(2,1)S(1)}, u32[]{:S(2)}, u32[]{:S(2)}) %collective-permute-start.56) | collective-permute-done | bytes 165920 | tf_op jit(solution)/shard_map/ppermute | solution.py:512
  712.8 20.0 %shard_map.234 = (f32[12288,128]{1,0:T(8,128)}, f32[12288,128]{1,0:T(8,128)}, f32[12288,128]{1,0:T(8,128)}, f32[12288,128]{1,0:T(8,128)}, bf16[12288,128]{1,0:T(8,128)(2,1)}) custom-call(f32[1]{0:T(128)} %bitcast.113.clip_ref, f32[12288,128]{1,0:T(8,128)} %shard_map.233.g_ref, f32[12288,128]{1,0:T(8,128)} %bitcast.294, f32[12288,128]{1,0:T(8,128)} %bitcast.295, ...), custom_call_target="tpu_custom_call" | custom-call | flops 31457280 | bytes 59768832 | tf_op jit(solution)/shard_map/pallas_call | solution.py:478
  (643 shorter events, 344.2 us)
Async XLA Ops:
  7.2 176.3 %all-gather.3.cloned.1.call-start = ((), (), s32[]{:S(2)}) async-start(), calls=%async_computation.5 | async-start | bytes 30081024 | tf_op jit(solution)/shard_map/all_gather | solution.py:823
  22.0 471.8 %reduce-scatter.3.cloned.1.call-start = ((), (), s32[]{:S(2)}) async-start(), calls=%async_computation.3 | async-start | bytes 6684672 | tf_op jit(solution)/shard_map/reduce_scatter | solution.py:820
  23.0 25.5 %collective-permute-start = (f32[16,4608]{1,0:T(8,128)S(1)}, f32[16,4608]{1,0:T(8,128)S(1)}, u32[]{:S(2)}, u32[]{:S(2)}) collective-permute-start(f32[16,4608]{1,0:T(8,128)S(1)} %fusion.119), channel_id=1, source_target_pairs={{0,2},{2,0},{4,6},{6,4},{8,10},{10,8},{12,14},{14,12},{16,18},{18,... | collective-permute-start | bytes 884744 | tf_op jit(solution)/shard_map/ppermute | solution.py:512
  190.1 28.4 %collective-permute-start.13 = (bf16[3,256,768]{2,1,0:T(8,128)(2,1)}, bf16[3,256,768]{2,1,0:T(8,128)(2,1)S(1)}, u32[]{:S(2)}, u32[]{:S(2)}) collective-permute-start(bf16[3,256,768]{2,1,0:T(8,128)(2,1)} %get-tuple-element.332.q_ref.rest_0_.k_ref.v_ref.refs_7_), channel_id=1, source_target_pairs={{0,4},{2,6},{4,0},{6,2},{8,12},{10,14},{12,8},{14,10},{16,20},{18,... | collective-permute-start | bytes 3538952 | tf_op jit(solution)/shard_map/ppermute | solution.py:512
  191.3 29.9 %collective-permute-start.14 = (bf16[3,256,768]{2,1,0:T(8,128)(2,1)}, bf16[3,256,768]{2,1,0:T(8,128)(2,1)S(1)}, u32[]{:S(2)}, u32[]{:S(2)}) collective-permute-start(bf16[3,256,768]{2,1,0:T(8,128)(2,1)} %get-tuple-element.332.q_ref.rest_0_.k_ref.v_ref.refs_7_), channel_id=1, source_target_pairs={{8,0},{10,2},{12,4},{14,6},{16,8},{18,10},{20,12},{22,14},{24,16},... | collective-permute-start | bytes 3538952 | tf_op jit(solution)/shard_map/ppermute | solution.py:507
  192.6 29.9 %collective-permute-start.15 = (bf16[3,256,768]{2,1,0:T(8,128)(2,1)}, bf16[3,256,768]{2,1,0:T(8,128)(2,1)S(1)}, u32[]{:S(2)}, u32[]{:S(2)}) collective-permute-start(bf16[3,256,768]{2,1,0:T(8,128)(2,1)} %get-tuple-element.332.q_ref.rest_0_.k_ref.v_ref.refs_7_), channel_id=1, source_target_pairs={{0,8},{2,10},{4,12},{6,14},{8,16},{10,18},{12,20},{14,22},{16,24},... | collective-permute-start | bytes 3538952 | tf_op jit(solution)/shard_map/ppermute | solution.py:507
  223.7 36.0 %collective-permute-start.19 = (bf16[12,256,768]{2,1,0:T(8,128)(2,1)S(1)}, bf16[12,256,768]{2,1,0:T(8,128)(2,1)}, u32[]{:S(2)}, u32[]{:S(2)}) collective-permute-start(bf16[12,256,768]{2,1,0:T(8,128)(2,1)S(1)} %constant_dynamic-update-slice_fusion.refs_8_), channel_id=1, source_target_pairs={{0,2},{2,0},{4,6},{6,4},{8,10},{10,8},{12,14},{14,12},{16,18},{18,... | collective-permute-start | bytes 14155784 | tf_op jit(solution)/shard_map/ppermute | solution.py:512
  223.8 35.9 %collective-permute-start.17 = (bf16[3,256,768]{2,1,0:T(8,128)(2,1)S(1)}, bf16[3,256,768]{2,1,0:T(8,128)(2,1)S(1)}, u32[]{:S(2)}, u32[]{:S(2)}) collective-permute-start(bf16[3,256,768]{2,1,0:T(8,128)(2,1)S(1)} %collective-permute-done.13.rest_1_), channel_id=1, source_target_pairs={{8,0},{10,2},{12,4},{14,6},{16,8},{18,10},{20,12},{22,14},{24,16},... | collective-permute-start | bytes 3538952 | tf_op jit(solution)/shard_map/ppermute | solution.py:507
  225.1 34.6 %collective-permute-start.18 = (bf16[3,256,768]{2,1,0:T(8,128)(2,1)S(1)}, bf16[3,256,768]{2,1,0:T(8,128)(2,1)S(1)}, u32[]{:S(2)}, u32[]{:S(2)}) collective-permute-start(bf16[3,256,768]{2,1,0:T(8,128)(2,1)S(1)} %collective-permute-done.13.rest_1_), channel_id=1, source_target_pairs={{0,8},{2,10},{4,12},{6,14},{8,16},{10,18},{12,20},{14,22},{16,24},... | collective-permute-start | bytes 3538952 | tf_op jit(solution)/shard_map/ppermute | solution.py:507
  333.9 293.0 %reduce-scatter.5.cloned.1.call-start = ((), (), s32[]{:S(2)}) async-start(), calls=%async_computation.4 | async-start | bytes 13369344 | tf_op jit(solution)/shard_map/reduce_scatter | solution.py:820
  382.2 31.1 %collective-permute-start.24 = (bf16[1,288,768]{2,1,0:T(8,128)(2,1)}, bf16[1,288,768]{2,1,0:T(8,128)(2,1)S(1)}, u32[]{:S(2)}, u32[]{:S(2)}) collective-permute-start(bf16[1,288,768]{2,1,0:T(8,128)(2,1)} %get-tuple-element.345.d_self_ref.rest_9_.rest_18_.refs_20_), channel_id=1, source_target_pairs={{0,4},{2,6},{4,0},{6,2},{8,12},{10,14},{12,8},{14,10},{16,20},{18,... | collective-permute-start | bytes 1327112 | tf_op jit(solution)/shard_map/ppermute | solution.py:512
  391.5 26.2 %collective-permute-start.25 = (bf16[1,288,768]{2,1,0:T(8,128)(2,1)}, bf16[1,288,768]{2,1,0:T(8,128)(2,1)S(1)}, u32[]{:S(2)}, u32[]{:S(2)}) collective-permute-start(bf16[1,288,768]{2,1,0:T(8,128)(2,1)} %get-tuple-element.345.d_self_ref.rest_9_.rest_18_.refs_20_), channel_id=1, source_target_pairs={{8,0},{10,2},{12,4},{14,6},{16,8},{18,10},{20,12},{22,14},{24,16},... | collective-permute-start | bytes 1327112 | tf_op jit(solution)/shard_map/ppermute | solution.py:507
  420.1 32.3 %collective-permute-start.30 = (bf16[4,288,768]{2,1,0:T(8,128)(2,1)}, bf16[4,288,768]{2,1,0:T(8,128)(2,1)}, u32[]{:S(2)}, u32[]{:S(2)}) collective-permute-start(bf16[4,288,768]{2,1,0:T(8,128)(2,1)} %constant_dynamic-update-slice_fusion.12.refs_22_), channel_id=1, source_target_pairs={{0,2},{2,0},{4,6},{6,4},{8,10},{10,8},{12,14},{14,12},{16,18},{18,... | collective-permute-start | bytes 5308424 | tf_op jit(solution)/shard_map/ppermute | solution.py:512
  420.2 32.3 %collective-permute-start.28 = (bf16[1,288,768]{2,1,0:T(8,128)(2,1)S(1)}, bf16[1,288,768]{2,1,0:T(8,128)(2,1)S(1)}, u32[]{:S(2)}, u32[]{:S(2)}) collective-permute-start(bf16[1,288,768]{2,1,0:T(8,128)(2,1)S(1)} %collective-permute-done.24.rest_10_.rest_19_), channel_id=1, source_target_pairs={{8,0},{10,2},{12,4},{14,6},{16,8},{18,10},{20,12},{22,14},{24,16},... | collective-permute-start | bytes 1327112 | tf_op jit(solution)/shard_map/ppermute | solution.py:507
  421.5 30.9 %collective-permute-start.29 = (bf16[1,288,768]{2,1,0:T(8,128)(2,1)S(1)}, bf16[1,288,768]{2,1,0:T(8,128)(2,1)}, u32[]{:S(2)}, u32[]{:S(2)}) collective-permute-start(bf16[1,288,768]{2,1,0:T(8,128)(2,1)S(1)} %collective-permute-done.24.rest_10_.rest_19_), channel_id=1, source_target_pairs={{0,8},{2,10},{4,12},{6,14},{8,16},{10,18},{12,20},{14,22},{16,24},... | collective-permute-start | bytes 1327112 | tf_op jit(solution)/shard_map/ppermute | solution.py:507
  456.6 37.1 %collective-permute-start.23 = (f32[256,1536]{1,0:T(8,128)}, f32[256,1536]{1,0:T(8,128)}, u32[]{:S(2)}, u32[]{:S(2)}) collective-permute-start(f32[256,1536]{1,0:T(8,128)} %shard_map.228.refs_21_), channel_id=1, source_target_pairs={{0,1},{1,0},{2,3},{3,2},{4,5},{5,4},{6,7},{7,6},{8,9},{9,8},{10,11... | collective-permute-start | bytes 4718600 | tf_op jit(solution)/shard_map/ppermute | solution.py:516
  523.3 34.0 %collective-permute-start.37 = (bf16[8,96,1536]{2,1,0:T(8,128)(2,1)}, bf16[8,96,1536]{2,1,0:T(8,128)(2,1)}, u32[]{:S(2)}, u32[]{:S(2)}) collective-permute-start(bf16[8,96,1536]{2,1,0:T(8,128)(2,1)} %convolution_convert_fusion.3.refs_39_), channel_id=1, source_target_pairs={{0,2},{2,0},{4,6},{6,4},{8,10},{10,8},{12,14},{14,12},{16,18},{18,... | collective-permute-start | bytes 7077896 | tf_op jit(solution)/shard_map/ppermute | solution.py:512
  524.4 43.3 %collective-permute-start.39 = (bf16[4,48,1536]{2,1,0:T(8,128)(2,1)}, bf16[4,48,1536]{2,1,0:T(8,128)(2,1)}, u32[]{:S(2)}, u32[]{:S(2)}) collective-permute-start(bf16[4,48,1536]{2,1,0:T(8,128)(2,1)} %fusion.3.refs_28_), channel_id=1, source_target_pairs={{0,4},{2,6},{4,0},{6,2},{8,12},{10,14},{12,8},{14,10},{16,20},{18,... | collective-permute-start | bytes 1769480 | tf_op jit(solution)/shard_map/ppermute | solution.py:512
  579.0 36.5 %collective-permute-start.43 = (bf16[4,96,768]{2,1,0:T(8,128)(2,1)}, bf16[4,96,768]{2,1,0:T(8,128)(2,1)}, u32[]{:S(2)}, u32[]{:S(2)}) collective-permute-start(bf16[4,96,768]{2,1,0:T(8,128)(2,1)} %fusion.33.refs_37_), channel_id=1, source_target_pairs={{0,4},{2,6},{4,0},{6,2},{8,12},{10,14},{12,8},{14,10},{16,20},{18,... | collective-permute-start | bytes 1769480 | tf_op jit(solution)/shard_map/ppermute | solution.py:512
  580.1 31.9 %collective-permute-start.44 = (bf16[2,48,1536]{2,1,0:T(8,128)(2,1)}, bf16[2,48,1536]{2,1,0:T(8,128)(2,1)}, u32[]{:S(2)}, u32[]{:S(2)}) collective-permute-start(bf16[2,48,1536]{2,1,0:T(8,128)(2,1)} %fusion.57.refs_46_), channel_id=1, source_target_pairs={{0,8},{2,10},{4,12},{6,14},{8,0},{10,2},{12,4},{14,6},{16,24},{18,... | collective-permute-start | bytes 884744 | tf_op jit(solution)/shard_map/ppermute | solution.py:512
  581.0 45.8 %collective-permute-start.41 = (bf16[4,96,1536]{2,1,0:T(8,128)(2,1)}, bf16[4,96,1536]{2,1,0:T(8,128)(2,1)}, u32[]{:S(2)}, u32[]{:S(2)}) collective-permute-start(bf16[4,96,1536]{2,1,0:T(8,128)(2,1)} %fusion.1.refs_42_), channel_id=1, source_target_pairs={{0,4},{2,6},{4,0},{6,2},{8,12},{10,14},{12,8},{14,10},{16,20},{18,... | collective-permute-start | bytes 3538952 | tf_op jit(solution)/shard_map/ppermute | solution.py:512
  614.1 45.6 %collective-permute-start.53 = (bf16[1,48,1536]{2,1,0:T(8,128)(2,1)}, bf16[1,48,1536]{2,1,0:T(8,128)(2,1)}, u32[]{:S(2)}, u32[]{:S(2)}) collective-permute-start(bf16[1,48,1536]{2,1,0:T(8,128)(2,1)} %dynamic-slice_convert_fusion.3.refs_56_), channel_id=1, source_target_pairs={{0,16},{2,18},{4,20},{6,22},{8,24},{10,26},{12,28},{14,30},{16,0},... | collective-permute-start | bytes 442376 | tf_op jit(solution)/shard_map/ppermute | solution.py:512
  619.4 38.9 %collective-permute-start.49 = (bf16[2,16,1536]{2,1,0:T(8,128)(2,1)}, bf16[2,16,1536]{2,1,0:T(8,128)(2,1)}, u32[]{:S(2)}, u32[]{:S(2)}) collective-permute-start(bf16[2,16,1536]{2,1,0:T(8,128)(2,1)} %maximum_select_fusion.10.refs_59_), channel_id=1, source_target_pairs={{0,8},{2,10},{4,12},{6,14},{8,0},{10,2},{12,4},{14,6},{16,24},{18,... | collective-permute-start | bytes 294920 | tf_op jit(solution)/shard_map/ppermute | solution.py:512
  653.5 28.9 %collective-permute-start.55 = (bf16[1,96,1536]{2,1,0:T(8,128)(2,1)S(1)}, bf16[1,96,1536]{2,1,0:T(8,128)(2,1)S(1)}, u32[]{:S(2)}, u32[]{:S(2)}) collective-permute-start(bf16[1,96,1536]{2,1,0:T(8,128)(2,1)S(1)} %dynamic-slice_convert_fusion.1.refs_67_), channel_id=1, source_target_pairs={{0,16},{2,18},{4,20},{6,22},{8,24},{10,26},{12,28},{14,30},{16,0},... | collective-permute-start | bytes 884744 | tf_op jit(solution)/shard_map/ppermute | solution.py:512
  (179 other events, 1980.9 us)
Sparse Core Ops, SparseCore 0:
  13.2 170.3 all-gather.2
  334.0 119.8 reduce-scatter.2
  458.5 156.9 reduce-scatter.4

commit v7 on v6

--- a/solution.py
+++ b/solution.py
@@ -871,8 +871,13 @@
     cond_rows = COND // n_img
     cond_own = lax.dynamic_slice_in_dim(conditions, img_index * cond_rows, cond_rows, 1)
     silu_own = jax.nn.silu(cond_own.astype(f32)).astype(bf16)
-    mod_sum = sum_over_img(jnp.dot(silu_own, own_modulate, preferred_element_type=f32))
-    mod_half = mod_sum.astype(bf16)
+    z_first = [0] + list(range(2, index_bits(n_img))) + [1]
+    mod_width = 6 * half_d // n_img
+    mod_terms = jnp.dot(silu_own, own_modulate, preferred_element_type=f32)
+    mod_terms = mod_terms.reshape(samples, n_img, mod_width).transpose(1, 0, 2).reshape(-1, mod_width)
+    mod_own = TermSum(Clock(), mod_terms, z_first, f32).finish().astype(bf16)
+    mod_half = gather_doubling(mod_own).reshape(n_img, samples, mod_width).transpose(1, 0, 2)
+    mod_half = mod_half.reshape(samples, 6 * half_d)
     mod_other = other_txt(mod_half)
     mods = jnp.where(
         txt_index == 0, jnp.stack([mod_half, mod_other], 0), jnp.stack([mod_other, mod_half], 0)
@@ -904,7 +909,6 @@
     text_rows = text_states.shape[0]
     text_len = text_rows * n_img
     text_columns = lax.all_to_all(text_states, "img", split_axis=1, concat_axis=0, tiled=True)
-    z_first = [0] + list(range(2, index_bits(n_img))) + [1]
     text_proj = TermSum(Clock(), jnp.dot(text_columns, own_text, preferred_element_type=f32), z_first, bf16).finish()
     text_shape = (text_rows, local_heads, HD)
     text_raw = text_proj[:, :half_d].reshape(text_shape)

time: 755 us -> 743 us (0.984)
  waiting for transfers between devices: 294 us -> 248 us
  Pallas kernels: 154 us -> 171 us
  starting transfers between devices: 116 us -> 124 us
    pallas_call x13, Pallas kernels: 141 us -> 158 us  [call(): pl.pallas_call(kernel, grid_spec=pltpu.PrefetchScalarGridSpec(num_scalar_...]
    ppermute x48 -> x52, starting transfers between devices: 64 us -> 80.8 us  [crossed(): return lax.ppermute(x, 'img', [(i, i ^ bit) for i in range(count)])]
    ppermute x48 -> x52, waiting for transfers between devices: 125 us -> 111 us  [crossed(): return lax.ppermute(x, 'img', [(i, i ^ bit) for i in range(count)])]
    all_gather x1, waiting for transfers between devices: 65.3 us -> 53.1 us  [gather(): return lax.all_gather(rows, 'img', axis=0, tiled=True)]
    ppermute x7, waiting for transfers between devices: 56.8 us -> 47.9 us  [other_txt(): return lax.ppermute(x, 'txt', [(0, 1), (1, 0)])]
    unnamed x287 -> x297, local copies, waits for them, and re-layouts: 16 us -> 16.4 us
  transfers between devices with their start and end apart: 69 -> 73, of which waited for: 32 -> 34; matrix products, arithmetic and copies ran while one was open for 17% -> 18% of each run, Pallas kernels for 12% -> 13%
where the time goes in v7:
time: 743 us; the launch traced here: 730 us
  waiting for transfers between devices  248 us (33%)
  Pallas kernels  171 us (23%)
  starting transfers between devices  124 us (17%)
  other arithmetic  62 us (8%)
  local copies, waits for them, and re-layouts  52.6 us (7%)
  matrix products  48.4 us (7%)
  between operations  23.7 us (3%)
    pallas_call x13, Pallas kernels, call(): pl.pallas_call(kernel, grid_spec=pltpu.PrefetchScalarGridSpec(num_scalar_...  158 us
    ppermute x52, waiting for transfers between devices, crossed(): return lax.ppermute(x, 'img', [(i, i ^ bit) for i in range(count)])  111 us
    ppermute x52, starting transfers between devices, crossed(): return lax.ppermute(x, 'img', [(i, i ^ bit) for i in range(count)])  80.8 us
    all_gather x1, waiting for transfers between devices, gather(): return lax.all_gather(rows, 'img', axis=0, tiled=True)  53.1 us
    ppermute x7, waiting for transfers between devices, other_txt(): return lax.ppermute(x, 'txt', [(0, 1), (1, 0)])  47.9 us
    ppermute x8, waiting for transfers between devices, shifted(): lax.ppermute(x, 'img', [(i + by, i) for i in range(count) if 0 <= i + by...  36.1 us
    dot_general x12, matrix products, mm(): lax.dot_general(a, b, (((on_a,), (on_b,)), ((), ())), preferred_element_t...  33.3 us
    ppermute x8, starting transfers between devices, shifted(): lax.ppermute(x, 'img', [(i + by, i) for i in range(count) if 0 <= i + by...  24.8 us
  transfers between devices with their start and end apart: 73, of which 34 were waited for; matrix products, arithmetic and copies ran while one was open for 18% of the time, Pallas kernels for 13%

profile of v7, /device:TPU:0, one launch (start us, length us, event | category | flops | bytes accessed | tf_op | source)
XLA Modules:
  0.0 730.0 jit_solution(7663829883382896315)
XLA Ops:
  14.6 7.5 %all-to-all-start = ((bf16[16,16,256]{2,0,1:T(8,128)(2,1)}), bf16[16,16,256]{2,0,1:T(8,128)(2,1)S(1)}, u32[]{:S(2)}, u32[]{:S(2)}) async-start(bf16[16,16,256]{2,0,1:T(8,128)(2,1)} %bitcast.299), calls=%async_computation | async-start | bytes 262144 | tf_op jit(solution)/shard_map/all_to_all | solution.py:911
  65.2 11.7 %collective-permute-done.10 = bf16[4,16,1536]{2,1,0:T(8,128)(2,1)S(1)} collective-permute-done((bf16[4,16,1536]{2,1,0:T(8,128)(2,1)S(1)}, bf16[4,16,1536]{2,1,0:T(8,128)(2,1)S(1)}, u32[]{:S(2)}, u32[]{:S(2)}) %collective-permute-start.10) | collective-permute-done | bytes 196640 | tf_op jit(solution)/shard_map/ppermute | solution.py:512
  110.4 8.4 %collective-permute-done.15 = bf16[4,16,1536]{2,1,0:T(8,128)(2,1)S(1)} collective-permute-done((bf16[4,16,1536]{2,1,0:T(8,128)(2,1)S(1)}, bf16[4,16,1536]{2,1,0:T(8,128)(2,1)S(1)}, u32[]{:S(2)}, u32[]{:S(2)}) %collective-permute-start.15) | collective-permute-done | bytes 196640 | tf_op jit(solution)/shard_map/ppermute | solution.py:512
  121.8 53.1 %all-gather.3.cloned.1.call-done = bf16[55296,256]{1,0:T(8,128)(2,1)} async-done(((bf16[3456,256]{1,0:T(8,128)(2,1)}), bf16[55296,256]{1,0:T(8,128)(2,1)}) %all-gather.3.cloned.1.call-update) | async-done | bytes 28311568 | tf_op jit(solution)/shard_map/all_gather | solution.py:823
  191.0 18.9 %collective-permute-done.17.rest_1_ = bf16[3,256,768]{2,1,0:T(8,128)(2,1)S(1)} collective-permute-done((bf16[3,256,768]{2,1,0:T(8,128)(2,1)}, bf16[3,256,768]{2,1,0:T(8,128)(2,1)S(1)}, u32[]{:S(2)}, u32[]{:S(2)}) %collective-permute-start.17) | collective-permute-done | bytes 1179680 | tf_op jit(solution)/shard_map/ppermute | solution.py:512
  221.5 29.6 %collective-permute-done.21.rest_5_ = bf16[3,256,768]{2,1,0:T(8,128)(2,1)S(1)} collective-permute-done((bf16[3,256,768]{2,1,0:T(8,128)(2,1)S(1)}, bf16[3,256,768]{2,1,0:T(8,128)(2,1)S(1)}, u32[]{:S(2)}, u32[]{:S(2)}) %collective-permute-start.21) | collective-permute-done | bytes 1179680 | tf_op jit(solution)/shard_map/ppermute | solution.py:507
  259.5 23.5 %shard_map.222 = (bf16[256,768]{1,0:T(8,128)(2,1)}, f32[256,768]{1,0:T(8,128)}, f32[256,768]{1,0:T(8,128)}, f32[256,768]{1,0:T(8,128)}, f32[256,768]{1,0:T(8,128)}, /*index=5*/bf16[16,768]{1,0:T(8,128)(2,1)}) custom-call(s32[13]{0:T(128)} %convert_element_type.330.flag_ref, bf16[3,256,768]{2,1,0:T(8,128)(2,1)} %get-tuple-element.340.q_ref.rest_0_.k_ref.v_ref.refs_7_, ...), custom_call_target="tpu_custom_call" | custom-call | tf_op jit(solution)/shard_map/pallas_call | solution.py:478
  290.0 18.3 %collective-permute-done.25 = bf16[256,1536]{1,0:T(8,128)(2,1)S(1)} collective-permute-done((bf16[256,1536]{1,0:T(8,128)(2,1)}, bf16[256,1536]{1,0:T(8,128)(2,1)S(1)}, u32[]{:S(2)}, u32[]{:S(2)}) %collective-permute-start.25) | collective-permute-done | bytes 786464 | tf_op jit(solution)/shard_map/ppermute | solution.py:516
  313.7 11.3 %shard_map.224 = (f32[256,2048]{1,0:T(8,128)}, f32[256,2048]{1,0:T(8,128)}, bf16[256,2048]{1,0:T(8,128)(2,1)}, bf16[2048,256]{1,0:T(8,128)(2,1)}) custom-call(bf16[256,1536]{1,0:T(8,128)(2,1)} %get-tuple-element.346.b_ref.refs_13_, bf16[16,3456,256]{2,1,0:T(8,128)(2,1)} %bitcast.304, bf16[16,3456,256]{2,1,0:T(8,128)(2,1)} %bitcast.305), custom_call_target="tpu_custom_call" | custom-call | flops 3221225472 | bytes 12582912 | tf_op jit(solution)/shard_map/pallas_call | solution.py:478
  331.2 7.8 %shard_map.225.a_ref.refs_16_ = bf16[256,4096]{1,0:T(8,128)(2,1)} custom-call(bf16[256,1536]{1,0:T(8,128)(2,1)} %copy-done.35, bf16[16,3456,256]{2,1,0:T(8,128)(2,1)} %bitcast.306, f32[256,2048]{1,0:T(8,128)} %get-tuple-element.245.gate_ref, f32[256,2048]{1,0:T(8,128)} %get-tuple-element.246.up_ref), custom_call_target="tpu_custom_call" | custom-call | flops 1610612736 | bytes 6291456 | tf_op jit(solution)/shard_map/pallas_call | solution.py:478
  339.0 9.1 %shard_map.226.refs_17_ = bf16[256,1536]{1,0:T(8,128)(2,1)} custom-call(bf16[256,4096]{1,0:T(8,128)(2,1)} %shard_map.225.a_ref.refs_16_, bf16[16,3456,256]{2,1,0:T(8,128)(2,1)} %bitcast.307), custom_call_target="tpu_custom_call" | custom-call | flops 3221225472 | bytes 12582912 | tf_op jit(solution)/shard_map/pallas_call | solution.py:478
  356.4 10.8 %collective-permute-done.26 = bf16[256,1536]{1,0:T(8,128)(2,1)} collective-permute-done((bf16[256,1536]{1,0:T(8,128)(2,1)}, bf16[256,1536]{1,0:T(8,128)(2,1)}, u32[]{:S(2)}, u32[]{:S(2)}) %collective-permute-start.26) | collective-permute-done | bytes 786464 | tf_op jit(solution)/shard_map/ppermute | solution.py:516
  379.8 9.2 %collective-permute-start.28 = (bf16[1,288,768]{2,1,0:T(8,128)(2,1)}, bf16[1,288,768]{2,1,0:T(8,128)(2,1)S(1)}, u32[]{:S(2)}, u32[]{:S(2)}) collective-permute-start(bf16[1,288,768]{2,1,0:T(8,128)(2,1)} %get-tuple-element.353.d_self_ref.rest_9_.rest_18_.refs_20_), channel_id=1, source_target_pairs={{0,4},{2,6},{4,0},{6,2},{8,12},{10,14},{12,8},{14,10},{16,20},{18,... | collective-permute-start | bytes 1327112 | tf_op jit(solution)/shard_map/ppermute | solution.py:512
  402.5 7.1 shard_map.228.refs_21_
  423.0 16.3 %shard_map.229 = (bf16[256,384]{1,0:T(8,128)(2,1)}, f32[1,384]{1,0:T(1,128)}, f32[256,384]{1,0:T(8,128)}, f32[256,384]{1,0:T(8,128)}) custom-call(s32[13]{0:T(128)} %convert_element_type.330.flag_ref, bf16[3,256,768]{2,1,0:T(8,128)(2,1)} %get-tuple-element.340.q_ref.rest_0_.k_ref.v_ref.refs_7_, s32[256,1]{1,0:T(8,128)} %copy.307.own_ids_ref, ...), custom_call_target="tpu_custom_call" | custom-call | tf_op jit(solution)/shard_map/pallas_call | solution.py:478
  451.2 17.2 %shard_map.230 = (bf16[256,384]{1,0:T(8,128)(2,1)}, f32[1,384]{1,0:T(1,128)}, f32[256,384]{1,0:T(8,128)}, f32[256,384]{1,0:T(8,128)}) custom-call(s32[13]{0:T(128)} %convert_element_type.330.flag_ref, bf16[3,256,768]{2,1,0:T(8,128)(2,1)} %get-tuple-element.340.q_ref.rest_0_.k_ref.v_ref.refs_7_, s32[256,1]{1,0:T(8,128)} %copy.307.own_ids_ref, ...), custom_call_target="tpu_custom_call" | custom-call | tf_op jit(solution)/shard_map/pallas_call | solution.py:478
  472.2 8.7 %collective-permute-done.27.refs_31_ = f32[256,1536]{1,0:T(8,128)} collective-permute-done((f32[256,1536]{1,0:T(8,128)}, f32[256,1536]{1,0:T(8,128)}, u32[]{:S(2)}, u32[]{:S(2)}) %collective-permute-start.27) | collective-permute-done | bytes 1572896 | tf_op jit(solution)/shard_map/ppermute | solution.py:516
  490.5 21.7 %shard_map.231 = (bf16[256,1536]{1,0:T(8,128)(2,1)}, f32[1,768]{1,0:T(1,128)}) custom-call(s32[13]{0:T(128)} %convert_element_type.330.flag_ref, bf16[3,256,768]{2,1,0:T(8,128)(2,1)} %get-tuple-element.340.q_ref.rest_0_.k_ref.v_ref.refs_7_, bf16[3,256,768]{2,1,0:T(8,128)(2,1)} %get-tuple-element.340.q_ref.rest_0_.k_ref.v_ref.refs_7_, ...), custom_call_target="tpu_custom_call" | custom-call | tf_op jit(solution)/shard_map/pallas_call | solution.py:478
  527.1 6.9 shard_map.232.refs_40_
  567.7 7.4 %collective-permute-done.39 = bf16[256,1536]{1,0:T(8,128)(2,1)} collective-permute-done((bf16[256,1536]{1,0:T(8,128)(2,1)S(1)}, bf16[256,1536]{1,0:T(8,128)(2,1)}, u32[]{:S(2)}, u32[]{:S(2)}) %collective-permute-start.39) | collective-permute-done | bytes 786464 | tf_op jit(solution)/shard_map/ppermute | solution.py:516
  582.4 8.3 %collective-permute-start.46 = (bf16[1,16,1536]{2,1,0:T(8,128)(2,1)S(1)}, bf16[1,16,1536]{2,1,0:T(8,128)(2,1)S(1)}, u32[]{:S(2)}, u32[]{:S(2)}) collective-permute-start(bf16[1,16,1536]{2,1,0:T(8,128)(2,1)S(1)} %bitcast.361), channel_id=1, source_target_pairs={{0,16},{2,18},{4,20},{6,22},{8,24},{10,26},{12,28},{14,30},{16,0},... | collective-permute-start | bytes 147464 | tf_op jit(solution)/shard_map/ppermute | solution.py:512
  650.2 10.9 %collective-permute-done.60 = bf16[18,4608]{1,0:T(8,128)(2,1)S(1)} collective-permute-done((bf16[18,4608]{1,0:T(8,128)(2,1)S(1)}, bf16[18,4608]{1,0:T(8,128)(2,1)S(1)}, u32[]{:S(2)}, u32[]{:S(2)}) %collective-permute-start.60) | collective-permute-done | bytes 165920 | tf_op jit(solution)/shard_map/ppermute | solution.py:512
  682.4 7.2 shard_map.233.g_ref
  695.8 20.0 %shard_map.234 = (f32[12288,128]{1,0:T(8,128)}, f32[12288,128]{1,0:T(8,128)}, f32[12288,128]{1,0:T(8,128)}, f32[12288,128]{1,0:T(8,128)}, bf16[12288,128]{1,0:T(8,128)(2,1)}) custom-call(f32[1]{0:T(128)} %bitcast.138.clip_ref, f32[12288,128]{1,0:T(8,128)} %shard_map.233.g_ref, f32[12288,128]{1,0:T(8,128)} %bitcast.326, f32[12288,128]{1,0:T(8,128)} %bitcast.327, ...), custom_call_target="tpu_custom_call" | custom-call | flops 31457280 | bytes 59768832 | tf_op jit(solution)/shard_map/pallas_call | solution.py:478
  (676 shorter events, 355.4 us)
Async XLA Ops:
  7.2 167.6 %all-gather.3.cloned.1.call-start = ((), (), s32[]{:S(2)}) async-start(), calls=%async_computation.5 | async-start | bytes 30081024 | tf_op jit(solution)/shard_map/all_gather | solution.py:823
  14.6 31.5 %all-to-all-start = ((bf16[16,16,256]{2,0,1:T(8,128)(2,1)}), bf16[16,16,256]{2,0,1:T(8,128)(2,1)S(1)}, u32[]{:S(2)}, u32[]{:S(2)}) async-start(bf16[16,16,256]{2,0,1:T(8,128)(2,1)} %bitcast.299), calls=%async_computation | async-start | bytes 262144 | tf_op jit(solution)/shard_map/all_to_all | solution.py:911
  22.1 458.8 %reduce-scatter.3.cloned.1.call-start = ((), (), s32[]{:S(2)}) async-start(), calls=%async_computation.3 | async-start | bytes 6684672 | tf_op jit(solution)/shard_map/reduce_scatter | solution.py:820
  181.5 28.4 %collective-permute-start.17 = (bf16[3,256,768]{2,1,0:T(8,128)(2,1)}, bf16[3,256,768]{2,1,0:T(8,128)(2,1)S(1)}, u32[]{:S(2)}, u32[]{:S(2)}) collective-permute-start(bf16[3,256,768]{2,1,0:T(8,128)(2,1)} %get-tuple-element.340.q_ref.rest_0_.k_ref.v_ref.refs_7_), channel_id=1, source_target_pairs={{0,4},{2,6},{4,0},{6,2},{8,12},{10,14},{12,8},{14,10},{16,20},{18,... | collective-permute-start | bytes 3538952 | tf_op jit(solution)/shard_map/ppermute | solution.py:512
  182.7 29.9 %collective-permute-start.18 = (bf16[3,256,768]{2,1,0:T(8,128)(2,1)}, bf16[3,256,768]{2,1,0:T(8,128)(2,1)S(1)}, u32[]{:S(2)}, u32[]{:S(2)}) collective-permute-start(bf16[3,256,768]{2,1,0:T(8,128)(2,1)} %get-tuple-element.340.q_ref.rest_0_.k_ref.v_ref.refs_7_), channel_id=1, source_target_pairs={{8,0},{10,2},{12,4},{14,6},{16,8},{18,10},{20,12},{22,14},{24,16},... | collective-permute-start | bytes 3538952 | tf_op jit(solution)/shard_map/ppermute | solution.py:507
  184.0 29.9 %collective-permute-start.19 = (bf16[3,256,768]{2,1,0:T(8,128)(2,1)}, bf16[3,256,768]{2,1,0:T(8,128)(2,1)S(1)}, u32[]{:S(2)}, u32[]{:S(2)}) collective-permute-start(bf16[3,256,768]{2,1,0:T(8,128)(2,1)} %get-tuple-element.340.q_ref.rest_0_.k_ref.v_ref.refs_7_), channel_id=1, source_target_pairs={{0,8},{2,10},{4,12},{6,14},{8,16},{10,18},{12,20},{14,22},{16,24},... | collective-permute-start | bytes 3538952 | tf_op jit(solution)/shard_map/ppermute | solution.py:507
  215.1 36.0 %collective-permute-start.23 = (bf16[12,256,768]{2,1,0:T(8,128)(2,1)S(1)}, bf16[12,256,768]{2,1,0:T(8,128)(2,1)}, u32[]{:S(2)}, u32[]{:S(2)}) collective-permute-start(bf16[12,256,768]{2,1,0:T(8,128)(2,1)S(1)} %constant_dynamic-update-slice_fusion.refs_8_), channel_id=1, source_target_pairs={{0,2},{2,0},{4,6},{6,4},{8,10},{10,8},{12,14},{14,12},{16,18},{18,... | collective-permute-start | bytes 14155784 | tf_op jit(solution)/shard_map/ppermute | solution.py:512
  215.2 35.9 %collective-permute-start.21 = (bf16[3,256,768]{2,1,0:T(8,128)(2,1)S(1)}, bf16[3,256,768]{2,1,0:T(8,128)(2,1)S(1)}, u32[]{:S(2)}, u32[]{:S(2)}) collective-permute-start(bf16[3,256,768]{2,1,0:T(8,128)(2,1)S(1)} %collective-permute-done.17.rest_1_), channel_id=1, source_target_pairs={{8,0},{10,2},{12,4},{14,6},{16,8},{18,10},{20,12},{22,14},{24,16},... | collective-permute-start | bytes 3538952 | tf_op jit(solution)/shard_map/ppermute | solution.py:507
  216.5 34.6 %collective-permute-start.22 = (bf16[3,256,768]{2,1,0:T(8,128)(2,1)S(1)}, bf16[3,256,768]{2,1,0:T(8,128)(2,1)S(1)}, u32[]{:S(2)}, u32[]{:S(2)}) collective-permute-start(bf16[3,256,768]{2,1,0:T(8,128)(2,1)S(1)} %collective-permute-done.17.rest_1_), channel_id=1, source_target_pairs={{0,8},{2,10},{4,12},{6,14},{8,16},{10,18},{12,20},{14,22},{16,24},... | collective-permute-start | bytes 3538952 | tf_op jit(solution)/shard_map/ppermute | solution.py:507
  330.8 275.7 %reduce-scatter.5.cloned.1.call-start = ((), (), s32[]{:S(2)}) async-start(), calls=%async_computation.4 | async-start | bytes 13369344 | tf_op jit(solution)/shard_map/reduce_scatter | solution.py:820
  379.8 29.8 %collective-permute-start.28 = (bf16[1,288,768]{2,1,0:T(8,128)(2,1)}, bf16[1,288,768]{2,1,0:T(8,128)(2,1)S(1)}, u32[]{:S(2)}, u32[]{:S(2)}) collective-permute-start(bf16[1,288,768]{2,1,0:T(8,128)(2,1)} %get-tuple-element.353.d_self_ref.rest_9_.rest_18_.refs_20_), channel_id=1, source_target_pairs={{0,4},{2,6},{4,0},{6,2},{8,12},{10,14},{12,8},{14,10},{16,20},{18,... | collective-permute-start | bytes 1327112 | tf_op jit(solution)/shard_map/ppermute | solution.py:512
  389.0 22.7 %collective-permute-start.29 = (bf16[1,288,768]{2,1,0:T(8,128)(2,1)}, bf16[1,288,768]{2,1,0:T(8,128)(2,1)S(1)}, u32[]{:S(2)}, u32[]{:S(2)}) collective-permute-start(bf16[1,288,768]{2,1,0:T(8,128)(2,1)} %get-tuple-element.353.d_self_ref.rest_9_.rest_18_.refs_20_), channel_id=1, source_target_pairs={{8,0},{10,2},{12,4},{14,6},{16,8},{18,10},{20,12},{22,14},{24,16},... | collective-permute-start | bytes 1327112 | tf_op jit(solution)/shard_map/ppermute | solution.py:507
  414.2 25.5 %collective-permute-start.34 = (bf16[4,288,768]{2,1,0:T(8,128)(2,1)}, bf16[4,288,768]{2,1,0:T(8,128)(2,1)}, u32[]{:S(2)}, u32[]{:S(2)}) collective-permute-start(bf16[4,288,768]{2,1,0:T(8,128)(2,1)} %constant_dynamic-update-slice_fusion.12.refs_22_), channel_id=1, source_target_pairs={{0,2},{2,0},{4,6},{6,4},{8,10},{10,8},{12,14},{14,12},{16,18},{18,... | collective-permute-start | bytes 5308424 | tf_op jit(solution)/shard_map/ppermute | solution.py:512
  414.2 25.1 %collective-permute-start.32 = (bf16[1,288,768]{2,1,0:T(8,128)(2,1)S(1)}, bf16[1,288,768]{2,1,0:T(8,128)(2,1)S(1)}, u32[]{:S(2)}, u32[]{:S(2)}) collective-permute-start(bf16[1,288,768]{2,1,0:T(8,128)(2,1)S(1)} %collective-permute-done.28.rest_10_.rest_19_), channel_id=1, source_target_pairs={{8,0},{10,2},{12,4},{14,6},{16,8},{18,10},{20,12},{22,14},{24,16},... | collective-permute-start | bytes 1327112 | tf_op jit(solution)/shard_map/ppermute | solution.py:507
  415.5 24.2 %collective-permute-start.33 = (bf16[1,288,768]{2,1,0:T(8,128)(2,1)S(1)}, bf16[1,288,768]{2,1,0:T(8,128)(2,1)}, u32[]{:S(2)}, u32[]{:S(2)}) collective-permute-start(bf16[1,288,768]{2,1,0:T(8,128)(2,1)S(1)} %collective-permute-done.28.rest_10_.rest_19_), channel_id=1, source_target_pairs={{0,8},{2,10},{4,12},{6,14},{8,16},{10,18},{12,20},{14,22},{16,24},... | collective-permute-start | bytes 1327112 | tf_op jit(solution)/shard_map/ppermute | solution.py:507
  443.8 37.1 %collective-permute-start.27 = (f32[256,1536]{1,0:T(8,128)}, f32[256,1536]{1,0:T(8,128)}, u32[]{:S(2)}, u32[]{:S(2)}) collective-permute-start(f32[256,1536]{1,0:T(8,128)} %shard_map.228.refs_21_), channel_id=1, source_target_pairs={{0,1},{1,0},{2,3},{3,2},{4,5},{5,4},{6,7},{7,6},{8,9},{9,8},{10,11... | collective-permute-start | bytes 4718600 | tf_op jit(solution)/shard_map/ppermute | solution.py:516
  516.8 29.9 %collective-permute-start.43 = (bf16[4,48,1536]{2,1,0:T(8,128)(2,1)}, bf16[4,48,1536]{2,1,0:T(8,128)(2,1)}, u32[]{:S(2)}, u32[]{:S(2)}) collective-permute-start(bf16[4,48,1536]{2,1,0:T(8,128)(2,1)} %fusion.3.refs_28_), channel_id=1, source_target_pairs={{0,4},{2,6},{4,0},{6,2},{8,12},{10,14},{12,8},{14,10},{16,20},{18,... | collective-permute-start | bytes 1769480 | tf_op jit(solution)/shard_map/ppermute | solution.py:512
  558.7 40.7 %collective-permute-start.47 = (bf16[4,96,768]{2,1,0:T(8,128)(2,1)}, bf16[4,96,768]{2,1,0:T(8,128)(2,1)}, u32[]{:S(2)}, u32[]{:S(2)}) collective-permute-start(bf16[4,96,768]{2,1,0:T(8,128)(2,1)} %fusion.33.refs_37_), channel_id=1, source_target_pairs={{0,4},{2,6},{4,0},{6,2},{8,12},{10,14},{12,8},{14,10},{16,20},{18,... | collective-permute-start | bytes 1769480 | tf_op jit(solution)/shard_map/ppermute | solution.py:512
  559.5 37.7 %collective-permute-start.48 = (bf16[2,48,1536]{2,1,0:T(8,128)(2,1)}, bf16[2,48,1536]{2,1,0:T(8,128)(2,1)}, u32[]{:S(2)}, u32[]{:S(2)}) collective-permute-start(bf16[2,48,1536]{2,1,0:T(8,128)(2,1)} %fusion.57.refs_46_), channel_id=1, source_target_pairs={{0,8},{2,10},{4,12},{6,14},{8,0},{10,2},{12,4},{14,6},{16,24},{18,... | collective-permute-start | bytes 884744 | tf_op jit(solution)/shard_map/ppermute | solution.py:512
  563.8 42.3 %collective-permute-start.45 = (bf16[4,96,1536]{2,1,0:T(8,128)(2,1)}, bf16[4,96,1536]{2,1,0:T(8,128)(2,1)}, u32[]{:S(2)}, u32[]{:S(2)}) collective-permute-start(bf16[4,96,1536]{2,1,0:T(8,128)(2,1)} %fusion.1.refs_42_), channel_id=1, source_target_pairs={{0,4},{2,6},{4,0},{6,2},{8,12},{10,14},{12,8},{14,10},{16,20},{18,... | collective-permute-start | bytes 3538952 | tf_op jit(solution)/shard_map/ppermute | solution.py:512
  599.2 45.1 %collective-permute-start.57 = (bf16[1,48,1536]{2,1,0:T(8,128)(2,1)}, bf16[1,48,1536]{2,1,0:T(8,128)(2,1)}, u32[]{:S(2)}, u32[]{:S(2)}) collective-permute-start(bf16[1,48,1536]{2,1,0:T(8,128)(2,1)} %dynamic-slice_convert_fusion.3.refs_56_), channel_id=1, source_target_pairs={{0,16},{2,18},{4,20},{6,22},{8,24},{10,26},{12,28},{14,30},{16,0},... | collective-permute-start | bytes 442376 | tf_op jit(solution)/shard_map/ppermute | solution.py:512
  603.4 39.8 %collective-permute-start.53 = (bf16[2,16,1536]{2,1,0:T(8,128)(2,1)}, bf16[2,16,1536]{2,1,0:T(8,128)(2,1)}, u32[]{:S(2)}, u32[]{:S(2)}) collective-permute-start(bf16[2,16,1536]{2,1,0:T(8,128)(2,1)} %maximum_select_fusion.12.refs_59_), channel_id=1, source_target_pairs={{0,8},{2,10},{4,12},{6,14},{8,0},{10,2},{12,4},{14,6},{16,24},{18,... | collective-permute-start | bytes 294920 | tf_op jit(solution)/shard_map/ppermute | solution.py:512
  623.5 26.7 %collective-permute-start.52 = (bf16[1,96,768]{2,1,0:T(8,128)(2,1)S(1)}, bf16[1,96,768]{2,1,0:T(8,128)(2,1)S(1)}, u32[]{:S(2)}, u32[]{:S(2)}) collective-permute-start(bf16[1,96,768]{2,1,0:T(8,128)(2,1)S(1)} %dynamic-slice_convert_fusion.2.refs_65_), channel_id=1, source_target_pairs={{0,16},{2,18},{4,20},{6,22},{8,24},{10,26},{12,28},{14,30},{16,0},... | collective-permute-start | bytes 442376 | tf_op jit(solution)/shard_map/ppermute | solution.py:512
  635.0 31.5 %collective-permute-start.59 = (bf16[1,96,1536]{2,1,0:T(8,128)(2,1)S(1)}, bf16[1,96,1536]{2,1,0:T(8,128)(2,1)S(1)}, u32[]{:S(2)}, u32[]{:S(2)}) collective-permute-start(bf16[1,96,1536]{2,1,0:T(8,128)(2,1)S(1)} %dynamic-slice_convert_fusion.1.refs_67_), channel_id=1, source_target_pairs={{0,16},{2,18},{4,20},{6,22},{8,24},{10,26},{12,28},{14,30},{16,0},... | collective-permute-start | bytes 884744 | tf_op jit(solution)/shard_map/ppermute | solution.py:512
  (188 other events, 1820.5 us)
Sparse Core Ops, SparseCore 0:
  13.1 161.6 all-gather.2
  330.9 112.7 reduce-scatter.2
  448.3 158.1 reduce-scatter.4
